TPU v7x, 256 devices: a whole 4x4x8 slice. The times are simulated.
256 devices in a mesh: outer: 16 (over x, y), ctx: 16 (over z, core).
Axes of the slice: x: 4, y: 4, z: 8, core: 2. Of those that a mesh axis runs over, the one named last changes fastest.
Arguments:
- hidden_rows: float32 [2048, 8192], P('outer'), may hold values from -6 to 6
- query_weight: float32 [8192, 4096], P('outer', 'ctx'), may hold values from -0.0625 to 0.0625
- key_cache: float32 [4096, 512], P('ctx')
- value_cache: float32 [4096, 512], P('ctx'), may hold values from -6 to 6
- vertical_blocks: int32 [32, 16], replicated, may hold values from 0 to 63, as said below
- vertical_count: int32 [32], replicated, may hold values from 1 to 16
- slash_offsets: int32 [32, 16], replicated, may hold values from 0 to 63, as said below
- slash_count: int32 [32], replicated, may hold values from 1 to 16
- output_weight: float32 [4096, 8192], P('ctx', 'outer'), may hold values from -2.4 to 2.4
Outputs:
- mixed: float32 [2048, 8192], P('outer', 'ctx')
Inputs may be any that keep to these rules, and one draw needn't show every extreme that they name: `vertical_blocks`: slot 0 of every head holds block 0; slots at or past a head's vertical_count are unused. `slash_offsets`: slot 0 of every head holds offset 0; slots at or past a head's slash_count are unused.
All inputs are finite; a program needn't handle non-finite values.
Results may differ from a plain program's by a relative error of at most 0.0003.
Values sent between devices are 32-bit elements; how exact they have to be, the bound alone decides.
No kernel may reach another device: no remote copies, remote signals or barrier semaphores. Data moves between devices by JAX's collectives and lax.ppermute only.
A program may use at most 192 MiB of HBM per device.

v0:
```python
import math

import jax
import jax.numpy as jnp
from jax import lax
from jax.sharding import PartitionSpec as P

HD = 128
BLOCK = 64


HIGHEST = lax.Precision.HIGHEST
NEGATIVE = -1e30


def joined(value, axis, join):
    pieces = jax.tree.map(lambda part: lax.all_gather(part, axis), value)
    head = jax.tree.map(lambda part: part[0], pieces)
    tail = jax.tree.map(lambda part: part[1:], pieces)
    total, _ = lax.scan(lambda total, slab: (join(total, slab), None), head, tail)
    return total


def partial_attention(
    all_query,
    key_cache,
    value_cache,
    vertical_blocks,
    vertical_count,
    slash_offsets,
    slash_count,
    query_first,
    key_first,
    total_blocks,
):
    row_count = all_query.shape[0]
    head_count = vertical_blocks.shape[0]
    key_len = key_cache.shape[0]
    kv_heads = key_cache.shape[1] // HD
    group_size = head_count // kv_heads
    score_scale = 1.0 / math.sqrt(HD)
    key_pos = key_first + jnp.arange(key_len, dtype=jnp.int32)
    query_pos = query_first + jnp.arange(row_count, dtype=jnp.int32)
    vert_valid = (
        jnp.arange(vertical_blocks.shape[1], dtype=jnp.int32)[None, :] < vertical_count[:, None]
    )
    vert_mask = jnp.any(
        (vertical_blocks[:, :, None] == (key_pos // BLOCK)[None, None, :]) & vert_valid[:, :, None],
        axis=1,
    )
    slash_valid = (
        jnp.arange(slash_offsets.shape[1], dtype=jnp.int32)[None, :] < slash_count[:, None]
    )
    block_ids = jnp.arange(total_blocks, dtype=jnp.int32)
    slash_table = jnp.any(
        (slash_offsets[:, :, None] == block_ids[None, None, :]) & slash_valid[:, :, None], axis=1
    )
    distance = query_pos[:, None] - key_pos[None, :]
    causal = distance >= 0
    band_index = jnp.clip(distance // BLOCK, 0, total_blocks - 1)
    queries = all_query.reshape(row_count, head_count, HD)
    weighted_list = []
    maxima_list = []
    totals_list = []
    for group_index in range(kv_heads):
        head_low = group_index * group_size
        key_rows = key_cache[:, group_index * HD : (group_index + 1) * HD]
        value_rows = value_cache[:, group_index * HD : (group_index + 1) * HD]
        slash_hit = jnp.take(slash_table[head_low : head_low + group_size], band_index, axis=1)
        allowed = causal[None] & (
            vert_mask[head_low : head_low + group_size][:, None, :] | slash_hit
        )
        scores = (
            jnp.einsum(
                "rhd,kd->hrk",
                queries[:, head_low : head_low + group_size],
                key_rows,
                precision=HIGHEST,
            )
            * score_scale
        )
        row_max = jnp.max(jnp.where(allowed, scores, NEGATIVE), axis=2)
        weights = jnp.exp(jnp.where(allowed, scores - row_max[..., None], NEGATIVE))
        totals_list.append(jnp.sum(weights, axis=2).T)
        maxima_list.append(row_max.T)
        weighted_list.append(jnp.einsum("hrk,kd->rhd", weights, value_rows, precision=HIGHEST))
    return (
        jnp.concatenate(weighted_list, axis=1),
        jnp.concatenate(maxima_list, axis=1),
        jnp.concatenate(totals_list, axis=1),
    )


def merge_partials(left_part, right_part):
    left_out, left_max, left_total = left_part
    right_out, right_max, right_total = right_part
    highest = jnp.maximum(left_max, right_max)
    left_factor = jnp.exp(left_max - highest)
    right_factor = jnp.exp(right_max - highest)
    merged_out = left_out * left_factor[..., None] + right_out * right_factor[..., None]
    return (merged_out, highest, left_total * left_factor + right_total * right_factor)


def shards(
    hidden_rows,
    query_weight,
    key_cache,
    value_cache,
    vertical_blocks,
    vertical_count,
    slash_offsets,
    slash_count,
    output_weight,
):
    row_count = hidden_rows.shape[0]
    ctx_count = lax.axis_size("ctx")
    outer_count = lax.axis_size("outer")
    ctx_index = lax.axis_index("ctx")
    outer_index = lax.axis_index("outer")
    key_len = key_cache.shape[0]
    total_keys = key_len * ctx_count
    local_query = jnp.dot(
        hidden_rows,
        lax.all_gather(query_weight, "outer", axis=0, tiled=True),
        precision=HIGHEST,
        preferred_element_type=jnp.float32,
    )
    all_query = lax.all_gather(local_query, "ctx", axis=1, tiled=True)
    query_first = total_keys - row_count * outer_count + outer_index * row_count
    key_first = ctx_index * key_len
    weighted, row_max, row_total = partial_attention(
        all_query,
        key_cache,
        value_cache,
        vertical_blocks,
        vertical_count,
        slash_offsets,
        slash_count,
        query_first,
        key_first,
        total_keys // BLOCK,
    )
    own_heads = vertical_blocks.shape[0] // ctx_count
    merged_out, merged_max, merged_total = joined(
        (weighted, row_max, row_total), "ctx", merge_partials
    )
    own_weighted = lax.dynamic_slice_in_dim(merged_out, ctx_index * own_heads, own_heads, 1)
    own_totals = lax.dynamic_slice_in_dim(merged_total, ctx_index * own_heads, own_heads, 1)
    attended = own_weighted / own_totals[..., None]
    attended_flat = attended.reshape(row_count, own_heads * HD)
    partial_out = jnp.dot(
        attended_flat,
        lax.all_gather(output_weight, "outer", axis=1, tiled=True),
        precision=HIGHEST,
        preferred_element_type=jnp.float32,
    )
    return lax.psum_scatter(partial_out, "ctx", scatter_dimension=1, tiled=True)


def solution(mesh):
    placed = (
        P("outer", None),
        P("outer", "ctx"),
        P("ctx", None),
        P("ctx", None),
        P(),
        P(),
        P(),
        P(),
        P("ctx", "outer"),
    )
    return jax.shard_map(
        shards, mesh=mesh, in_specs=placed, out_specs=P("outer", "ctx"), check_vma=False
    )
```

profile of v0, /device:TPU:1, one launch (start us, length us, event | category | flops | bytes accessed | tf_op | source)
XLA Modules:
  0.0 953.3 jit_solution(7667908499529613311)
XLA Ops:
  7.3 82.1 %all-gather.8.cloned.1.call-done = f32[8192,256]{1,0:T(8,128)} async-done(((f32[512,256]{1,0:T(8,128)}), f32[8192,256]{1,0:T(8,128)}) %all-gather.8.cloned.1.call-update) | async-done | bytes 8388624 | tf_op jit(solution)/shard_map/all_gather | solution.py:124
  89.4 9.3 fusion.68
  100.1 111.8 %gather_fusion = pred[32768,8]{1,0:T(32,128)(4,1)} fusion(pred[8,64]{0,1:T(8,128)(4,1)S(1)} %copy.60, s32[32768]{0:T(1024)S(1)} %broadcast_clamp_fusion), kind=kCustom, calls=%fused_computation.clone | custom fusion | bytes 655360 | tf_op jit(solution)/shard_map/jit(_take)/gather | solution.py:69
  211.9 6.7 copy.78
  218.6 111.8 %gather_fusion.1 = pred[32768,8]{1,0:T(32,128)(4,1)} fusion(pred[8,64]{0,1:T(8,128)(4,1)S(1)} %copy.63, s32[32768]{0:T(1024)S(1)} %broadcast_clamp_fusion), kind=kCustom, calls=%fused_computation.1.clone | custom fusion | bytes 655360 | tf_op jit(solution)/shard_map/jit(_take)/gather | solution.py:69
  330.4 7.4 copy.79
  337.9 111.8 %gather_fusion.2 = pred[32768,8]{1,0:T(32,128)(4,1)} fusion(pred[8,64]{0,1:T(8,128)(4,1)S(1)} %copy.66, s32[32768]{0:T(1024)S(1)} %broadcast_clamp_fusion), kind=kCustom, calls=%fused_computation.2.clone | custom fusion | bytes 655360 | tf_op jit(solution)/shard_map/jit(_take)/gather | solution.py:69
  449.7 7.4 copy.80
  457.1 111.9 %gather_fusion.3 = pred[32768,8]{1,0:T(32,128)(4,1)} fusion(pred[8,64]{0,1:T(8,128)(4,1)S(1)} %copy.69, s32[32768]{0:T(1024)S(1)} %broadcast_clamp_fusion), kind=kCustom, calls=%fused_computation.3.clone | custom fusion | bytes 655360 | tf_op jit(solution)/shard_map/jit(_take)/gather | solution.py:69
  569.1 7.4 copy.81
  591.5 3.3 fusion.12
  594.8 19.1 %all-gather.2 = f32[2048,32]{0,1:T(8,128)S(1)} all-gather(f32[128,32]{0,1:T(8,128)S(1)} %pad_maximum_fusion.2), channel_id=4, replica_groups=mesh['outer'=16,'ctx'=16] {'ctx'}, dimensions={0}, use_global_device_ids=true | all-gather | bytes 278528 | tf_op jit(solution)/shard_map/all_gather | solution.py:17
  613.9 17.0 %all-gather.1 = f32[2048,32]{0,1:T(8,128)S(1)} all-gather(f32[128,32]{0,1:T(8,128)S(1)} %pad_maximum_fusion.1), channel_id=3, replica_groups=mesh['outer'=16,'ctx'=16] {'ctx'}, dimensions={0}, use_global_device_ids=true | all-gather | bytes 278528 | tf_op jit(solution)/shard_map/all_gather | solution.py:17
  632.8 134.8 %all-gather.14.cloned.1.call-done = f32[2048,32,128]{2,0,1:T(8,128)} async-done(((f32[128,32,128]{2,0,1:T(8,128)}), f32[2048,32,128]{2,0,1:T(8,128)}) %all-gather.14.cloned.1.call-update) | async-done | bytes 33554448 | tf_op jit(solution)/shard_map/all_gather | solution.py:17
  770.4 21.9 %slice.134 = f32[1920,32,128]{2,0,1:T(8,128)} slice(f32[2048,32,128]{2,0,1:T(8,128)} %all-gather.14.cloned.1.call-done), slice={[128:2048], [0:32], [0:128]} | slice | bytes 62914560 | tf_op jit(solution)/shard_map/slice | solution.py:19
  792.3 86.2 %while.14 = (s32[]{:T(128)}, f32[128,32,128]{2,1,0:T(8,128)S(1)}, f32[128,32]{1,0:T(8,128)S(1)}, f32[128,32]{1,0:T(8,128)S(1)}, f32[15,128,32]{2,1,0:T(8,128)}, ...) while((s32[]{:T(128)}, f32[128,32,128]{2,1,0:T(8,128)S(1)}, ...), condition=%wide.region_11.13_spmd, body=%wide.region_10.12_spmd.sunk | while | flops 1597442 | bytes 10649693 | solution.py:20
  795.0 3.0 fusion.75
  800.7 3.0 fusion.75
  806.4 3.0 fusion.75
  812.1 3.0 fusion.75
  817.9 3.0 fusion.75
  823.8 3.0 fusion.75
  878.8 10.1 %fusion.35 = f32[128,8192]{1,0:T(8,128)} fusion(f32[256,8192]{1,0:T(8,128)} %all-gather.12.cloned.1.call-done, f32[16,8,2,128]{3,2,1,0:T(2,128)S(1)} %bitcast.143), kind=kOutput, calls=%fused_computation.77 | convolution fusion | flops 3221225472 | bytes 12713984 | tf_op jit(solution)/shard_map/dot_general | solution.py:151
  888.9 57.7 %reduce-scatter.2.cloned.1.call-done = f32[128,512]{1,0:T(8,128)} async-done(((f32[128,8192]{1,0:T(8,128)}), f32[128,512]{1,0:T(8,128)}) %reduce-scatter.2.cloned.1.call-update) | async-done | bytes 262160 | tf_op jit(solution)/shard_map/reduce_scatter | solution.py:157
  (115 shorter events, 89.6 us)
Async XLA Ops:
  6.5 82.8 %all-gather.8.cloned.1.call-start = ((), (), s32[]{:S(2)}) async-start(), calls=%async_computation.1 | async-start | bytes 8912896 | tf_op jit(solution)/shard_map/all_gather | solution.py:124
  7.3 92.3 %copy-start.5 = (s32[32,16]{0,1:T(8,128)S(1)}, s32[32,16]{0,1:T(8,128)}, u32[]{:S(2)}) copy-start(s32[32,16]{0,1:T(8,128)} %param.19) | copy-start | bytes 6148
  7.3 92.4 %copy-start.7 = (s32[32]{0:T(128)S(1)}, s32[32]{0:T(128)}, u32[]{:S(2)}) copy-start(s32[32]{0:T(128)} %param.20) | copy-start | bytes 388
  7.3 569.8 %all-gather.10.cloned.1.call-start = ((), (), s32[]{:S(2)}) async-start(), calls=%async_computation.2 | async-start | bytes 2228224 | tf_op jit(solution)/shard_map/all_gather | solution.py:128
  98.7 668.8 %all-gather.14.cloned.1.call-start = ((), (), s32[]{:S(2)}) async-start(), calls=%async_computation.5 | async-start | bytes 35651584 | tf_op jit(solution)/shard_map/all_gather | solution.py:17
  457.0 119.4 %copy-start.6 = (s32[32,16]{0,1:T(8,128)S(1)}, s32[32,16]{0,1:T(8,128)}, u32[]{:S(2)}) copy-start(s32[32,16]{0,1:T(8,128)} %param.17) | copy-start | bytes 6148
  457.0 119.5 %copy-start.8 = (s32[32]{0:T(128)S(1)}, s32[32]{0:T(128)}, u32[]{:S(2)}) copy-start(s32[32]{0:T(128)} %param.18) | copy-start | bytes 388
  577.1 2.2 copy-start.4
  579.2 3.2 copy-start.1
  579.2 3.2 copy-start.2
  579.2 3.2 copy-start.3
  581.3 2.7 copy-start.9
  584.0 4.0 copy-start
  590.8 287.9 %all-gather.12.cloned.1.call-start = ((), (), s32[]{:S(2)}) async-start(), calls=%async_computation.3 | async-start | bytes 8912896 | tf_op jit(solution)/shard_map/all_gather | solution.py:153
  591.4 355.2 %reduce-scatter.2.cloned.1.call-start = ((), (), s32[]{:S(2)}) async-start(), calls=%async_computation.4 | async-start | bytes 4456448 | tf_op jit(solution)/shard_map/reduce_scatter | solution.py:157
  767.6 1.6 slice-start
Sparse Core Ops, SparseCore 0:
  9.8 79.5 all-gather.7
  98.9 39.9 all-gather.9
  591.0 176.5 all-gather.13
  769.9 73.7 all-gather.11
  889.0 57.4 reduce-scatter.1
where the time goes:
time: 961 us; the launch traced here: 953 us
  local copies, waits for them, and re-layouts  532 us (55%)
  waiting for transfers between devices  276 us (29%)
  other arithmetic  65.4 us (7%)
  blocking collectives  36.1 us (4%)
  matrix products  29.2 us (3%)
  between operations  13.7 us (1%)
    gather x8, local copies, waits for them, and re-layouts, partial_attention(): jnp.take(slash_table[head_low:head_low + group_size], band_index, axis=1)  476 us
    all_gather x1, waiting for transfers between devices, joined(): pieces = jax.tree.map(lambda part: lax.all_gather(part, axis), value)  135 us
    all_gather x1, waiting for transfers between devices, shards(): lax.all_gather(query_weight, 'outer', axis=0, tiled=True)  82.1 us
    reduce_scatter x1, waiting for transfers between devices, shards(): return lax.psum_scatter(partial_out, 'ctx', scatter_dimension=1, tiled=True)  57.7 us
    add x15, other arithmetic, merge_partials(): left_out * left_factor[..., None] + right_out * right_factor[..., None]  45.7 us
    all_gather x2, blocking collectives, joined(): pieces = jax.tree.map(lambda part: lax.all_gather(part, axis), value)  36.1 us
    dynamic_slice x15, local copies, waits for them, and re-layouts, joined(): lax.scan(lambda total, slab: (join(total, slab), None), head, tail)  26.4 us
    slice x3, local copies, waits for them, and re-layouts, joined(): tail = jax.tree.map(lambda part: part[1:], pieces)  21.9 us
  transfers between devices with their start and end apart: 5, of which 3 were waited for; matrix products, arithmetic and copies ran while one was open for 62% of the time, Pallas kernels for 0%

commit v1 on v0

v1 whole, which is shorter than its diff:
```python
import functools
import math

import jax
import jax.numpy as jnp
from jax import lax
from jax.experimental import pallas as pl
from jax.experimental.pallas import tpu as pltpu
from jax.sharding import Mesh
from jax.sharding import PartitionSpec as P

HD = 128
BLOCK = 64
NX, NY, NZ, NK = 4, 4, 8, 2
ALL = ("x", "y", "z", "k")
VMEM = pl.BlockSpec(memory_space=pltpu.VMEM)
SMEM = pl.BlockSpec(memory_space=pltpu.SMEM)


def split(value):
    high = value.astype(jnp.bfloat16)
    low = (value - high.astype(jnp.float32)).astype(jnp.bfloat16)
    return high, low


def dot3(left, right, dims):
    (lh, ll), (rh, rl) = left, right
    one = functools.partial(
        lax.dot_general, dimension_numbers=dims, preferred_element_type=jnp.float32
    )
    return one(lh, rh) + (one(lh, rl) + one(ll, rh))


MM = (((1,), (0,)), ((), ()))
MT = (((1,), (1,)), ((), ()))


def project_kernel(where, hidden, *refs):
    weights, out = refs[:8], refs[8]
    y, k = where[0], where[1]
    totals = [None, None]
    for shift in range(NY):
        owner = lax.rem(y - shift + NY, NY)
        left = split(hidden[:, pl.ds(pl.multiple_of(owner * 512, 512), 512)])
        for other in range(2):
            term = dot3(left, split(weights[2 * shift + other][...]), MM)
            totals[other] = term if totals[other] is None else totals[other] + term
    for other in range(2):
        core = k if other == 0 else 1 - k
        for b in range(2):
            out[2 * core + b] = totals[other][:, b * HD : (b + 1) * HD]


def project(where, hidden, weights):
    return pl.pallas_call(
        project_kernel,
        out_shape=jax.ShapeDtypeStruct((NX, 256, HD), jnp.float32),
        in_specs=[SMEM] + [VMEM] * 9,
        out_specs=VMEM,
        compiler_params=pltpu.CompilerParams(vmem_limit_bytes=40 << 20),
        cost_estimate=pl.CostEstimate(
            flops=6 * 256 * 2048 * 512, bytes_accessed=7 << 20, transcendentals=0
        ),
        name="project",
    )(where, hidden, *weights)


def attend_kernel(query, kv, low, up, out, scores):
    tiles = kv.shape[0]
    width = kv.shape[2]
    row = lax.broadcasted_iota(jnp.int32, (BLOCK, width), 0)
    col = lax.broadcasted_iota(jnp.int32, (BLOCK, width), 1)
    lower = row >= lax.rem(col, BLOCK)
    left = split(query[...] * (math.log2(math.e) / math.sqrt(HD)))
    top = None
    for tile in range(tiles):
        s = dot3(left, split(kv[tile, 0]), MT)
        cols = slice(tile * width, (tile + 1) * width)
        bias = jnp.concatenate(
            [
                jnp.where(lower, low[b : b + 1, cols], up[b : b + 1, cols])
                for b in range(low.shape[0])
            ],
            axis=0,
        )
        s = s + bias
        scores[tile] = s
        top = s if top is None else jnp.maximum(top, s)
    top = jnp.max(top, axis=1, keepdims=True)
    total, summed = None, None
    for tile in range(tiles):
        weight = jnp.exp2(scores[tile] - top)
        term = dot3(split(weight), split(kv[tile, 1]), MM)
        total = weight if total is None else total + weight
        summed = term if summed is None else summed + term
    out[...] = summed / jnp.sum(total, axis=1, keepdims=True)


def attend(query, kv, low, up):
    tiles, _, width, _ = kv.shape
    return pl.pallas_call(
        attend_kernel,
        out_shape=jax.ShapeDtypeStruct(query.shape, jnp.float32),
        in_specs=[VMEM] * 4,
        out_specs=VMEM,
        scratch_shapes=[pltpu.VMEM((tiles, query.shape[0], width), jnp.float32)],
        compiler_params=pltpu.CompilerParams(vmem_limit_bytes=48 << 20),
        cost_estimate=pl.CostEstimate(
            flops=12 * 256 * 4096 * HD, bytes_accessed=5 << 20, transcendentals=256 * 4096
        ),
        name="attend",
    )(query, kv, low, up)


def mix_kernel(attended, weights, out):
    for core in range(NK):
        total = None
        for y in range(NY):
            left = jnp.concatenate([attended[2 * y], attended[2 * y + 1]], axis=1)
            term = dot3(split(left), split(weights[2 * y + core]), MM)
            total = term if total is None else total + term
        for x in range(NX):
            out[x, :, core * 512 : (core + 1) * 512] = total[x * BLOCK : (x + 1) * BLOCK]


def mix(attended, weights):
    return pl.pallas_call(
        mix_kernel,
        out_shape=jax.ShapeDtypeStruct((NX, BLOCK, 1024), jnp.float32),
        in_specs=[VMEM] * 2,
        out_specs=VMEM,
        compiler_params=pltpu.CompilerParams(vmem_limit_bytes=40 << 20),
        cost_estimate=pl.CostEstimate(
            flops=6 * 256 * 1024 * 1024, bytes_accessed=6 << 20, transcendentals=0
        ),
        name="mix",
    )(attended, weights)


def allowed_rows(x, y, z, k, vertical_blocks, vertical_count, slash_offsets, slash_count):
    head = 8 * x + z
    slots = jnp.arange(vertical_blocks.shape[1], dtype=jnp.int32)
    used_v = slots < vertical_count[head]
    used_s = slots < slash_count[head]
    verticals = jnp.where(used_v, vertical_blocks[head], -1)
    slashes = jnp.where(used_s, slash_offsets[head], -1)
    query_block = 32 + 8 * jnp.arange(NX, dtype=jnp.int32) + 2 * y + k
    key_block = jnp.arange(64 * BLOCK, dtype=jnp.int32) // BLOCK
    offset = query_block[:, None] - key_block[None, :]
    vert = jnp.any(key_block[:, None] == verticals[None, :], axis=1)[None, :]
    low_slash = jnp.any(offset[:, :, None] == slashes, axis=2)
    up_slash = jnp.any((offset - 1)[:, :, None] == slashes, axis=2)
    low = (offset >= 0) & (vert | low_slash)
    up = (offset >= 1) & (vert | up_slash)
    return jnp.where(low, 0.0, -jnp.inf), jnp.where(up, 0.0, -jnp.inf)


def place(x, y, z, k):
    return ((x * NY + y) * NZ + z) * NK + k


CORES = [(0, 1), (1, 0)]
OTHERS = [
    (place(x, y, z, k), place(z >> 1, y, 4 * (z & 1) + x, k))
    for x in range(NX)
    for y in range(NY)
    for z in range(NZ)
    for k in range(NK)
]
FLIPPED = [(a * 16 + b, b * 16 + a) for a in range(16) for b in range(16)]


def shards(
    hidden_rows,
    query_weight,
    key_cache,
    value_cache,
    vertical_blocks,
    vertical_count,
    slash_offsets,
    slash_count,
    output_weight,
):
    x, y, z, k = (lax.axis_index(name) for name in ALL)
    kv_own = jnp.stack(
        [
            lax.dynamic_slice_in_dim(key_cache, x * HD, HD, 1),
            lax.dynamic_slice_in_dim(value_cache, x * HD, HD, 1),
        ]
    )
    kv = lax.all_gather(kv_own, ("z", "k"), axis=0)
    flipped = lax.ppermute(output_weight, ALL, FLIPPED)
    out_weight = lax.all_gather(flipped, ("y", "k"), axis=0)
    weights = []
    for shift in range(NY):
        piece = query_weight
        if shift:
            piece = lax.ppermute(
                query_weight, "y", [(i, (i + shift) % NY) for i in range(NY)]
            )
        weights += [piece, lax.ppermute(piece, "k", CORES)]
    half = lax.dynamic_slice_in_dim(hidden_rows, k * BLOCK, BLOCK, 0)
    half = half.reshape(BLOCK, NX, 2048).transpose(1, 0, 2)
    hidden = lax.all_to_all(half, "x", 0, 0).reshape(NX * BLOCK, 2048)
    partial = project(jnp.stack([y, k]).astype(jnp.int32), hidden, weights)
    summed = jnp.sum(lax.all_to_all(partial, "x", 0, 0), axis=0)
    query = lax.ppermute(summed, ALL, OTHERS)
    low, up = allowed_rows(
        x, y, z, k, vertical_blocks, vertical_count, slash_offsets, slash_count
    )
    attended = attend(query, kv, low, up)
    heads = lax.all_to_all(jnp.broadcast_to(attended, (NZ,) + attended.shape), "z", 0, 0)
    mixed = mix(heads, out_weight)
    rows = jnp.sum(lax.all_to_all(mixed, "x", 0, 0), axis=0)
    own = lax.dynamic_slice_in_dim(rows, k * 512, 512, 1)
    other = lax.ppermute(lax.dynamic_slice_in_dim(rows, (1 - k) * 512, 512, 1), "k", CORES)
    first = jnp.where(k == 0, own, other)
    second = jnp.where(k == 0, other, own)
    return jnp.concatenate([first, second], axis=0)


def solution(mesh):
    grid = Mesh(mesh.devices.reshape(NX, NY, NZ, NK), ALL)
    outer, ctx = ("x", "y"), ("z", "k")
    placed = (
        P(outer, None),
        P(outer, ctx),
        P(ctx, None),
        P(ctx, None),
        P(),
        P(),
        P(),
        P(),
        P(ctx, outer),
    )
    return jax.shard_map(
        shards, mesh=grid, in_specs=placed, out_specs=P(outer, ctx), check_vma=False
    )
```

time: 961 us -> 237 us (0.25)
  local copies, waits for them, and re-layouts: 532 us -> 22.4 us
  waiting for transfers between devices: 276 us -> 80.2 us
  starting transfers between devices: 0.63 us -> 103 us
  other arithmetic: 65.4 us -> 3.92 us
  blocking collectives: 36.1 us -> 0 us
  matrix products: 29.2 us -> 0 us
  Pallas kernels: 0 us -> 11 us
    gather x8 -> x0, local copies, waits for them, and re-layouts: 476 us -> none  [partial_attention(): jnp.take(slash_table[head_low:head_low + group_size], band_index, axis=1)]
    all_gather x4 -> x2, waiting for transfers between devices: 217 us -> 0.03 us  [the longest x1 0.02 us: shards(): kv = lax.all_gather(kv_own, ('z', 'k'), axis=0)]
    all_to_all x0 -> x4, starting transfers between devices: none -> 86.1 us  [the longest x1 56.9 us: shards(): hidden = lax.all_to_all(half, 'x', 0, 0).reshape(NX * BLOCK, 2048)]
    add x31 -> x1, other arithmetic: 59.3 us -> 0.01 us  [allowed_rows(): query_block = 32 + 8 * jnp.arange(NX, dtype=jnp.int32) + 2 * y + k]
    reduce_scatter x1 -> x0, waiting for transfers between devices: 57.7 us -> none  [shards(): return lax.psum_scatter(partial_out, 'ctx', scatter_dimension=1, tiled=True)]
    all_to_all x0 -> x4, waiting for transfers between devices: none -> 43.4 us  [the longest x1 25.7 us: shards(): lax.all_to_all(jnp.broadcast_to(attended, (NZ,) + attended.shape), 'z', 0...]
    ppermute x0 -> x10, waiting for transfers between devices: none -> 36.8 us  [the longest x3 28.2 us: shards(): lax.ppermute(query_weight, 'y', [(i, (i + shift) % NY) for i in range(NY)])]
    all_gather x2 -> x0, blocking collectives: 36.1 us -> none  [joined(): pieces = jax.tree.map(lambda part: lax.all_gather(part, axis), value)]
  transfers between devices with their start and end apart: 5 -> 16, of which waited for: 3 -> 8; matrix products, arithmetic and copies ran while one was open for 62% -> 6% of each run, Pallas kernels for 0% -> 4%
where the time goes in v1:
time: 237 us; the launch traced here: 235 us
  starting transfers between devices  103 us (43%)
  waiting for transfers between devices  80.2 us (34%)
  local copies, waits for them, and re-layouts  22.4 us (9%)
  between operations  13.6 us (6%)
  Pallas kernels  11 us (5%)
  other arithmetic  3.92 us (2%)
    all_to_all x1, starting transfers between devices, shards(): hidden = lax.all_to_all(half, 'x', 0, 0).reshape(NX * BLOCK, 2048)  56.9 us
    ppermute x3, waiting for transfers between devices, shards(): lax.ppermute(query_weight, 'y', [(i, (i + shift) % NY) for i in range(NY)])  28.2 us
    all_to_all x1, waiting for transfers between devices, shards(): lax.all_to_all(jnp.broadcast_to(attended, (NZ,) + attended.shape), 'z', 0...  25.7 us
    all_to_all x1, starting transfers between devices, shards(): lax.all_to_all(jnp.broadcast_to(attended, (NZ,) + attended.shape), 'z', 0...  20.9 us
    all_to_all x1, waiting for transfers between devices, shards(): rows = jnp.sum(lax.all_to_all(mixed, 'x', 0, 0), axis=0)  10.8 us
    unnamed x28, local copies, waits for them, and re-layouts  10.8 us
    ppermute x1, waiting for transfers between devices, shards(): flipped = lax.ppermute(output_weight, ALL, FLIPPED)  7.16 us
    all_to_all x1, waiting for transfers between devices, shards(): summed = jnp.sum(lax.all_to_all(partial, 'x', 0, 0), axis=0)  6.89 us
  transfers between devices with their start and end apart: 16, of which 8 were waited for; matrix products, arithmetic and copies ran while one was open for 6% of the time, Pallas kernels for 4%

profile of v1, /device:TPU:1, one launch (start us, length us, event | category | flops | bytes accessed | tf_op | source)
XLA Modules:
  0.0 234.7 jit_solution(17831063146586324396)
XLA Ops:
  8.3 4.6 %collective-permute-start.8 = (f32[256,512]{1,0:T(8,128)}, f32[256,512]{1,0:T(8,128)S(1)}, u32[]{:S(2)}, u32[]{:S(2)}) collective-permute-start(f32[256,512]{1,0:T(8,128)} %param.17), channel_id=1, source_target_pairs={{0,0},{1,16},{2,32},{3,48},{4,64},{5,80},{6,96},{7,112},{8,128},{9... | collective-permute-start | bytes 1572872 | tf_op jit(solution)/shard_map/ppermute | solution.py:192
  12.9 7.2 %collective-permute-done.8 = f32[256,512]{1,0:T(8,128)S(1)} collective-permute-done((f32[256,512]{1,0:T(8,128)}, f32[256,512]{1,0:T(8,128)S(1)}, u32[]{:S(2)}, u32[]{:S(2)}) %collective-permute-start.8) | collective-permute-done | bytes 524320 | tf_op jit(solution)/shard_map/ppermute | solution.py:192
  21.0 1.7 constant_dynamic-slice_fusion.1
  22.7 2.4 %reshape.110 = f32[64,4,2048]{2,1,0:T(4,128)} reshape(f32[64,8192]{1,0:T(8,128)S(1)} %constant_dynamic-slice_fusion.1) | data formatting | bytes 4194304 | tf_op jit(solution)/shard_map/reshape | solution.py:203
  25.2 4.2 %copy.12 = f32[4,64,2048]{2,1,0:T(8,128)} copy(f32[4,64,2048]{2,0,1:T(4,128)} %bitcast.15) | data formatting | bytes 4194304 | tf_op jit(solution)/shard_map/transpose | solution.py:203
  29.4 56.9 %all-to-all-start = ((f32[4,64,2048]{2,1,0:T(8,128)}), f32[4,64,2048]{2,1,0:T(8,128)S(1)}, u32[]{:S(2)}, u32[]{:S(2)}) async-start(f32[4,64,2048]{2,1,0:T(8,128)} %copy.12), calls=%async_computation | async-start | bytes 4194304 | tf_op jit(solution)/shard_map/all_to_all | solution.py:204
  86.4 2.6 %collective-permute-start.5 = (f32[512,256]{1,0:T(8,128)S(1)}, f32[512,256]{1,0:T(8,128)}, u32[]{:S(2)}, u32[]{:S(2)}) collective-permute-start(f32[512,256]{1,0:T(8,128)S(1)} %copy-done.1), channel_id=1, source_target_pairs={{0,48},{16,0},{32,16},{48,32},{1,49},{17,1},{33,17},{49,33},{2,50}... | collective-permute-start | bytes 1572872 | tf_op jit(solution)/shard_map/ppermute | solution.py:198
  89.0 1.8 collective-permute-start
  92.2 24.4 %collective-permute-done.1.refs_2_ = f32[512,256]{1,0:T(8,128)S(1)} collective-permute-done((f32[512,256]{1,0:T(8,128)S(1)}, f32[512,256]{1,0:T(8,128)S(1)}, u32[]{:S(2)}, u32[]{:S(2)}) %collective-permute-start.1) | collective-permute-done | bytes 524320 | tf_op jit(solution)/shard_map/ppermute | solution.py:198
  116.5 2.1 collective-permute-start.4
  118.6 3.9 %collective-permute-done.5.refs_6_ = f32[512,256]{1,0:T(8,128)} collective-permute-done((f32[512,256]{1,0:T(8,128)S(1)}, f32[512,256]{1,0:T(8,128)}, u32[]{:S(2)}, u32[]{:S(2)}) %collective-permute-start.5) | collective-permute-done | bytes 524320 | tf_op jit(solution)/shard_map/ppermute | solution.py:198
  127.5 1.1 copy-done.7
  128.5 4.0 %project.1 = f32[4,256,128]{2,1,0:T(8,128)} custom-call(s32[2]{0:T(128)S(1)} %pad_add_fusion.where, f32[256,2048]{1,0:T(8,128)S(1)} %bitcast.12, f32[512,256]{1,0:T(8,128)S(1)} %copy-done.1, f32[512,256]{1,0:T(8,128)} %collective-permute-done.refs_1_, f32[512,256]{1,0:T(8,128)S(1)} %collective-permute-done.1.refs_2_, f32[512,256]{1,0:T(8,128)S(1)} %copy-done.3, ...), custom_call_target="tpu_custom_call" | custom-call | flops 1610612736 | bytes 7340032 | tf_op jit(solution)/shard_map/project/pallas_call | solution.py:55
  132.6 4.8 %all-to-all-start.1 = ((f32[4,256,128]{2,1,0:T(8,128)}), f32[4,256,128]{2,1,0:T(8,128)S(1)}, u32[]{:S(2)}, u32[]{:S(2)}) async-start(f32[4,256,128]{2,1,0:T(8,128)} %project.1), calls=%async_computation.1 | async-start | bytes 1048576 | tf_op jit(solution)/shard_map/all_to_all | solution.py:206
  139.4 6.9 %all-to-all-done.1 = f32[4,256,128]{2,1,0:T(8,128)S(1)} async-done(((f32[4,256,128]{2,1,0:T(8,128)}), f32[4,256,128]{2,1,0:T(8,128)S(1)}, u32[]{:S(2)}, u32[]{:S(2)}) %all-to-all-start.1) | async-done | bytes 524320 | tf_op jit(solution)/shard_map/all_to_all | solution.py:206
  147.3 2.2 copy-done.8
  149.5 4.2 %attend.1 = f32[256,128]{1,0:T(8,128)S(1)} custom-call(f32[256,128]{1,0:T(8,128)S(1)} %collective-permute-done.7.query, f32[16,2,256,128]{3,2,1,0:T(8,128)S(1)} %bitcast.14, f32[4,4096]{1,0:T(4,128)S(1)} %get-tuple-element.10.low, f32[4,4096]{1,0:T(4,128)S(1)} %get-tuple-element.9.up), custom_call_target="tpu_custom_call" | custom-call | flops 1610612736 | bytes 5242880 | tf_op jit(solution)/shard_map/attend/pallas_call | solution.py:101
  154.8 20.9 %all-to-all-start.2 = ((f32[8,256,128]{2,1,0:T(8,128)}), f32[8,256,128]{2,1,0:T(8,128)S(1)}, u32[]{:S(2)}, u32[]{:S(2)}) async-start(f32[8,256,128]{2,1,0:T(8,128)} %broadcast_in_dim.33), calls=%async_computation.2 | async-start | bytes 2097152 | tf_op jit(solution)/shard_map/all_to_all | solution.py:212
  175.6 25.7 %all-to-all-done.2.attended = f32[8,256,128]{2,1,0:T(8,128)S(1)} async-done(((f32[8,256,128]{2,1,0:T(8,128)}), f32[8,256,128]{2,1,0:T(8,128)S(1)}, u32[]{:S(2)}, u32[]{:S(2)}) %all-to-all-start.2) | async-done | bytes 1048608 | tf_op jit(solution)/shard_map/all_to_all | solution.py:212
  201.4 2.2 copy-done
  203.5 2.8 %mix.1 = f32[4,64,1024]{2,1,0:T(8,128)} custom-call(f32[8,256,128]{2,1,0:T(8,128)S(1)} %all-to-all-done.2.attended, f32[8,256,512]{2,1,0:T(8,128)S(1)} %bitcast.13), custom_call_target="tpu_custom_call" | custom-call | flops 1610612736 | bytes 6291456 | tf_op jit(solution)/shard_map/mix/pallas_call | solution.py:127
  206.4 3.5 %all-to-all-start.3 = ((f32[4,64,1024]{2,1,0:T(8,128)}), f32[4,64,1024]{2,1,0:T(8,128)S(1)}, u32[]{:S(2)}, u32[]{:S(2)}) async-start(f32[4,64,1024]{2,1,0:T(8,128)} %mix.1), calls=%async_computation.3 | async-start | bytes 2097152 | tf_op jit(solution)/shard_map/all_to_all | solution.py:214
  209.9 10.8 %all-to-all-done.3 = f32[4,64,1024]{2,1,0:T(8,128)S(1)} async-done(((f32[4,64,1024]{2,1,0:T(8,128)}), f32[4,64,1024]{2,1,0:T(8,128)S(1)}, u32[]{:S(2)}, u32[]{:S(2)}) %all-to-all-start.3) | async-done | bytes 1048608 | tf_op jit(solution)/shard_map/all_to_all | solution.py:214
  220.8 5.3 %collective-permute-start.9 = (f32[64,512]{1,0:T(8,128)S(1)}, f32[64,512]{1,0:T(8,128)S(1)}, u32[]{:S(2)}, u32[]{:S(2)}) collective-permute-start(f32[64,512]{1,0:T(8,128)S(1)} %constant_dynamic-slice_fusion), channel_id=1, source_target_pairs={{0,1},{1,0},{2,3},{3,2},{4,5},{5,4},{6,7},{7,6},{8,9},{9,8},{10,11... | collective-permute-start | bytes 393224 | tf_op jit(solution)/shard_map/ppermute | solution.py:216
  (63 shorter events, 15.0 us)
Async XLA Ops:
  6.5 140.8 %all-gather.5.cloned.1.call-start = ((), (), s32[]{:S(2)}) async-start(), calls=%async_computation.4 | async-start | bytes 4456448 | tf_op jit(solution)/shard_map/all_gather | solution.py:191
  8.3 167.4 %all-gather.7.cloned.1.call-start = ((), (), s32[]{:S(2)}) async-start(), calls=%async_computation.5 | async-start | bytes 4718592 | tf_op jit(solution)/shard_map/all_gather | solution.py:193
  8.3 11.8 %collective-permute-start.8 = (f32[256,512]{1,0:T(8,128)}, f32[256,512]{1,0:T(8,128)S(1)}, u32[]{:S(2)}, u32[]{:S(2)}) collective-permute-start(f32[256,512]{1,0:T(8,128)} %param.17), channel_id=1, source_target_pairs={{0,0},{1,16},{2,32},{3,48},{4,64},{5,80},{6,96},{7,112},{8,128},{9... | collective-permute-start | bytes 1572872 | tf_op jit(solution)/shard_map/ppermute | solution.py:192
  29.4 56.9 %copy-start.1 = (f32[512,256]{1,0:T(8,128)S(1)}, f32[512,256]{1,0:T(8,128)}, u32[]{:S(2)}) copy-start(f32[512,256]{1,0:T(8,128)} %refs_0_.1) | copy-start | bytes 1572868
  29.4 61.4 %copy-start.12 = (s32[32]{0:T(128)S(1)}, s32[32]{0:T(128)}, u32[]{:S(2)}) copy-start(s32[32]{0:T(128)} %param.14) | copy-start | bytes 388
  29.4 61.9 %copy-start.10 = (s32[32,16]{0,1:T(8,128)S(1)}, s32[32,16]{0,1:T(8,128)}, u32[]{:S(2)}) copy-start(s32[32,16]{0,1:T(8,128)} %param.15) | copy-start | bytes 6148
  29.4 61.9 %copy-start.11 = (s32[32,16]{0,1:T(8,128)S(1)}, s32[32,16]{0,1:T(8,128)}, u32[]{:S(2)}) copy-start(s32[32,16]{0,1:T(8,128)} %param.13) | copy-start | bytes 6148
  29.4 96.0 %all-to-all-start = ((f32[4,64,2048]{2,1,0:T(8,128)}), f32[4,64,2048]{2,1,0:T(8,128)S(1)}, u32[]{:S(2)}, u32[]{:S(2)}) async-start(f32[4,64,2048]{2,1,0:T(8,128)} %copy.12), calls=%async_computation | async-start | bytes 4194304 | tf_op jit(solution)/shard_map/all_to_all | solution.py:204
  86.3 30.2 %collective-permute-start.1 = (f32[512,256]{1,0:T(8,128)S(1)}, f32[512,256]{1,0:T(8,128)S(1)}, u32[]{:S(2)}, u32[]{:S(2)}) collective-permute-start(f32[512,256]{1,0:T(8,128)S(1)} %copy-done.1), channel_id=1, source_target_pairs={{0,16},{16,32},{32,48},{48,0},{1,17},{17,33},{33,49},{49,1},{2,18}... | collective-permute-start | bytes 1572872 | tf_op jit(solution)/shard_map/ppermute | solution.py:198
  86.3 30.2 %collective-permute-start.3 = (f32[512,256]{1,0:T(8,128)S(1)}, f32[512,256]{1,0:T(8,128)}, u32[]{:S(2)}, u32[]{:S(2)}) collective-permute-start(f32[512,256]{1,0:T(8,128)S(1)} %copy-done.1), channel_id=1, source_target_pairs={{0,32},{16,48},{32,0},{48,16},{1,33},{17,49},{33,1},{49,17},{2,34}... | collective-permute-start | bytes 1572872 | tf_op jit(solution)/shard_map/ppermute | solution.py:198
  86.4 36.1 %collective-permute-start.5 = (f32[512,256]{1,0:T(8,128)S(1)}, f32[512,256]{1,0:T(8,128)}, u32[]{:S(2)}, u32[]{:S(2)}) collective-permute-start(f32[512,256]{1,0:T(8,128)S(1)} %copy-done.1), channel_id=1, source_target_pairs={{0,48},{16,0},{32,16},{48,32},{1,49},{17,1},{33,17},{49,33},{2,50}... | collective-permute-start | bytes 1572872 | tf_op jit(solution)/shard_map/ppermute | solution.py:198
  89.0 33.6 %collective-permute-start = (f32[512,256]{1,0:T(8,128)S(1)}, f32[512,256]{1,0:T(8,128)}, u32[]{:S(2)}, u32[]{:S(2)}) collective-permute-start(f32[512,256]{1,0:T(8,128)S(1)} %copy-done.1), channel_id=1, source_target_pairs={{0,1},{1,0},{2,3},{3,2},{4,5},{5,4},{6,7},{7,6},{8,9},{9,8},{10,11... | collective-permute-start | bytes 1572872 | tf_op jit(solution)/shard_map/ppermute | solution.py:201
  116.5 6.1 %collective-permute-start.2 = (f32[512,256]{1,0:T(8,128)S(1)}, f32[512,256]{1,0:T(8,128)S(1)}, u32[]{:S(2)}, u32[]{:S(2)}) collective-permute-start(f32[512,256]{1,0:T(8,128)S(1)} %collective-permute-done.1.refs_2_), channel_id=1, source_target_pairs={{0,1},{1,0},{2,3},{3,2},{4,5},{5,4},{6,7},{7,6},{8,9},{9,8},{10,11... | collective-permute-start | bytes 1572872 | tf_op jit(solution)/shard_map/ppermute | solution.py:201
  116.5 6.9 %collective-permute-start.4 = (f32[512,256]{1,0:T(8,128)}, f32[512,256]{1,0:T(8,128)S(1)}, u32[]{:S(2)}, u32[]{:S(2)}) collective-permute-start(f32[512,256]{1,0:T(8,128)} %collective-permute-done.3.refs_4_), channel_id=1, source_target_pairs={{0,1},{1,0},{2,3},{3,2},{4,5},{5,4},{6,7},{7,6},{8,9},{9,8},{10,11... | collective-permute-start | bytes 1572872 | tf_op jit(solution)/shard_map/ppermute | solution.py:201
  122.5 2.1 collective-permute-start.6
  127.5 1.1 copy-start.7
  128.5 9.0 %copy-start.13 = (s32[32]{0:T(128)S(1)}, s32[32]{0:T(128)}, u32[]{:S(2)}) copy-start(s32[32]{0:T(128)} %param.16) | copy-start | bytes 388
  132.6 13.7 %all-to-all-start.1 = ((f32[4,256,128]{2,1,0:T(8,128)}), f32[4,256,128]{2,1,0:T(8,128)S(1)}, u32[]{:S(2)}, u32[]{:S(2)}) async-start(f32[4,256,128]{2,1,0:T(8,128)} %project.1), calls=%async_computation.1 | async-start | bytes 1048576 | tf_op jit(solution)/shard_map/all_to_all | solution.py:206
  146.3 1.0 collective-permute-start.7
  147.3 2.2 copy-start.8
  154.8 46.6 %all-to-all-start.2 = ((f32[8,256,128]{2,1,0:T(8,128)}), f32[8,256,128]{2,1,0:T(8,128)S(1)}, u32[]{:S(2)}, u32[]{:S(2)}) async-start(f32[8,256,128]{2,1,0:T(8,128)} %broadcast_in_dim.33), calls=%async_computation.2 | async-start | bytes 2097152 | tf_op jit(solution)/shard_map/all_to_all | solution.py:212
  201.4 2.2 copy-start
  206.4 14.3 %all-to-all-start.3 = ((f32[4,64,1024]{2,1,0:T(8,128)}), f32[4,64,1024]{2,1,0:T(8,128)S(1)}, u32[]{:S(2)}, u32[]{:S(2)}) async-start(f32[4,64,1024]{2,1,0:T(8,128)} %mix.1), calls=%async_computation.3 | async-start | bytes 2097152 | tf_op jit(solution)/shard_map/all_to_all | solution.py:214
  220.8 6.3 %collective-permute-start.9 = (f32[64,512]{1,0:T(8,128)S(1)}, f32[64,512]{1,0:T(8,128)S(1)}, u32[]{:S(2)}, u32[]{:S(2)}) collective-permute-start(f32[64,512]{1,0:T(8,128)S(1)} %constant_dynamic-slice_fusion), channel_id=1, source_target_pairs={{0,1},{1,0},{2,3},{3,2},{4,5},{5,4},{6,7},{7,6},{8,9},{9,8},{10,11... | collective-permute-start | bytes 393224 | tf_op jit(solution)/shard_map/ppermute | solution.py:216
  (6 other events, 5.3 us)
Sparse Core Ops, SparseCore 0:
  9.2 79.3 all-gather.4
  90.4 41.2 all-gather.6

commit v2 on v1

v2 whole, which is shorter than its diff:
```python
import functools
import math

import jax
import jax.numpy as jnp
from jax import lax
from jax.experimental import pallas as pl
from jax.experimental.pallas import tpu as pltpu
from jax.sharding import Mesh
from jax.sharding import PartitionSpec as P

HD = 128
BLOCK = 64
NX, NY, NZ, NK = 4, 4, 8, 2
ALL = ("x", "y", "z", "k")
VMEM = pl.BlockSpec(memory_space=pltpu.VMEM)
SMEM = pl.BlockSpec(memory_space=pltpu.SMEM)
ANY = pl.BlockSpec(memory_space=pl.ANY)


def split(value):
    high = value.astype(jnp.bfloat16)
    low = (value - high.astype(jnp.float32)).astype(jnp.bfloat16)
    return high, low


def dot3(left, right, dims):
    (lh, ll), (rh, rl) = left, right
    one = functools.partial(
        lax.dot_general, dimension_numbers=dims, preferred_element_type=jnp.float32
    )
    return one(lh, rh) + (one(lh, rl) + one(ll, rh))


MM = (((1,), (0,)), ((), ()))
MT = (((1,), (1,)), ((), ()))


def pick_kernel(where, rows, out):
    out[0] = rows[...]


def pick(k, hidden_rows):
    return pl.pallas_call(
        pick_kernel,
        out_shape=jax.ShapeDtypeStruct((NX, BLOCK, 2048), jnp.float32),
        grid_spec=pltpu.PrefetchScalarGridSpec(
            num_scalar_prefetch=1,
            grid=(NX,),
            in_specs=[pl.BlockSpec((BLOCK, 2048), lambda i, where: (where[0], i))],
            out_specs=pl.BlockSpec((1, BLOCK, 2048), lambda i, where: (i, 0, 0)),
        ),
        name="pick",
    )(k, hidden_rows)


def project_kernel(hidden, weights, out, left_buf, right_buf, left_sem, right_sem):
    copies = []
    for y in range(NY):
        cols = pl.ds(y * 512, 512)
        copies.append(
            (
                pltpu.make_async_copy(hidden.at[:, :, cols], left_buf.at[y], left_sem.at[y]),
                pltpu.make_async_copy(
                    weights.at[pl.ds(2 * y, 2)], right_buf.at[y], right_sem.at[y]
                ),
            )
        )
        for copy in copies[y]:
            copy.start()
    totals = [None, None]
    for y in range(NY):
        for copy in copies[y]:
            copy.wait()
        left = split(left_buf[y].reshape(NX * BLOCK, 512))
        for core in range(NK):
            term = dot3(left, split(right_buf[y, core]), MM)
            totals[core] = term if totals[core] is None else totals[core] + term
    for core in range(NK):
        for b in range(2):
            out[2 * core + b] = totals[core][:, b * HD : (b + 1) * HD]


def project(hidden, weights):
    return pl.pallas_call(
        project_kernel,
        out_shape=jax.ShapeDtypeStruct((NX, NX * BLOCK, HD), jnp.float32),
        in_specs=[ANY, ANY],
        out_specs=VMEM,
        scratch_shapes=[
            pltpu.VMEM((NY, NX, BLOCK, 512), jnp.float32),
            pltpu.VMEM((NY, NK, 512, 256), jnp.float32),
            pltpu.SemaphoreType.DMA((NY,)),
            pltpu.SemaphoreType.DMA((NY,)),
        ],
        compiler_params=pltpu.CompilerParams(vmem_limit_bytes=32 << 20),
        cost_estimate=pl.CostEstimate(
            flops=6 * 256 * 2048 * 512, bytes_accessed=7 << 20, transcendentals=0
        ),
        name="project",
    )(hidden, weights)


def attend_kernel(partial, low, up, *refs):
    pieces, (out, kv, scores, sem) = refs[:8], refs[8:]
    tiles = len(pieces)
    copies = [
        pltpu.make_async_copy(piece, kv.at[tile], sem.at[tile])
        for tile, piece in enumerate(pieces)
    ]
    for copy in copies:
        copy.start()
    width = NZ * BLOCK
    row = lax.broadcasted_iota(jnp.int32, (BLOCK, width), 0)
    col = lax.broadcasted_iota(jnp.int32, (BLOCK, width), 1)
    lower = row >= lax.rem(col, BLOCK)
    query = (partial[0] + partial[1]) + (partial[2] + partial[3])
    left = split(query * (math.log2(math.e) / math.sqrt(HD)))
    top = None
    for tile in range(tiles):
        copies[tile].wait()
        s = dot3(left, split(kv[tile, :, 0].reshape(width, HD)), MT)
        cols = slice(tile * width, (tile + 1) * width)
        bias = jnp.concatenate(
            [
                jnp.where(lower, low[b : b + 1, cols], up[b : b + 1, cols])
                for b in range(NX)
            ],
            axis=0,
        )
        s = s + bias
        scores[tile] = s
        top = s if top is None else jnp.maximum(top, s)
    top = jnp.max(top, axis=1, keepdims=True)
    total, summed = None, None
    for tile in range(tiles):
        weight = jnp.exp2(scores[tile] - top)
        term = dot3(split(weight), split(kv[tile, :, 1].reshape(width, HD)), MM)
        total = weight if total is None else total + weight
        summed = term if summed is None else summed + term
    attended = summed / jnp.sum(total, axis=1, keepdims=True)
    for z in range(NZ):
        out[z] = attended


def attend(partial, low, up, pieces):
    rows = NX * BLOCK
    return pl.pallas_call(
        attend_kernel,
        out_shape=jax.ShapeDtypeStruct((NZ, rows, HD), jnp.float32),
        in_specs=[VMEM] * 3 + [ANY] * 8,
        out_specs=VMEM,
        scratch_shapes=[
            pltpu.VMEM((8, NZ, 2, BLOCK, HD), jnp.float32),
            pltpu.VMEM((8, rows, NZ * BLOCK), jnp.float32),
            pltpu.SemaphoreType.DMA((8,)),
        ],
        compiler_params=pltpu.CompilerParams(vmem_limit_bytes=48 << 20),
        cost_estimate=pl.CostEstimate(
            flops=12 * 256 * 4096 * HD, bytes_accessed=6 << 20, transcendentals=256 * 4096
        ),
        name="attend",
    )(partial, low, up, *pieces)


def mix_kernel(where, heads, weights, out, buf, sem):
    copies = []
    for step in range(8):
        copies.append(pltpu.make_async_copy(weights.at[step], buf.at[step], sem.at[step]))
        copies[step].start()
    totals = [None, None]
    swap = where[0]
    for step in range(8):
        y, core = step // 2, step % 2
        spot = (y + NY - (where[1] + core)) & 3
        left = jnp.concatenate(
            [heads[spot + 4 * swap], heads[spot + 4 * (1 - swap)]], axis=1
        )
        left = split(left)
        copies[step].wait()
        term = dot3(left, split(buf[step].reshape(2 * HD, 512)), MM)
        totals[core] = term if totals[core] is None else totals[core] + term
    for core in range(NK):
        for x in range(NX):
            out[2 * x + core] = totals[core][x * BLOCK : (x + 1) * BLOCK]


def mix(where, heads, weights):
    return pl.pallas_call(
        mix_kernel,
        out_shape=jax.ShapeDtypeStruct((NX * NK, BLOCK, 512), jnp.float32),
        in_specs=[SMEM, VMEM, ANY],
        out_specs=VMEM,
        scratch_shapes=[
            pltpu.VMEM((8, 2, HD, 512), jnp.float32),
            pltpu.SemaphoreType.DMA((8,)),
        ],
        compiler_params=pltpu.CompilerParams(vmem_limit_bytes=32 << 20),
        cost_estimate=pl.CostEstimate(
            flops=6 * 256 * 1024 * 1024, bytes_accessed=6 << 20, transcendentals=0
        ),
        name="mix",
    )(where, heads, weights)


def allowed_rows(
    head, key_block, query_block, vertical_blocks, vertical_count, slash_offsets, slash_count
):
    slots = jnp.arange(vertical_blocks.shape[1], dtype=jnp.int32)
    verticals = jnp.where(slots < vertical_count[head], vertical_blocks[head], -1)
    slashes = jnp.where(slots < slash_count[head], slash_offsets[head], -1)
    offset = query_block[:, None] - key_block[None, :]
    vert = jnp.any(key_block[:, None] == verticals[None, :], axis=1)[None, :]
    low_slash = jnp.any(offset[:, :, None] == slashes, axis=2)
    up_slash = jnp.any((offset - 1)[:, :, None] == slashes, axis=2)
    low = (offset >= 0) & (vert | low_slash)
    up = (offset >= 1) & (vert | up_slash)
    bias = jnp.where(jnp.stack([low, up]), 0.0, -jnp.inf)
    bias = jnp.repeat(bias, BLOCK, axis=2)
    return bias[0], bias[1]


def place(x, y, z, k):
    return ((x * NY + y) * NZ + z) * NK + k


def every():
    return [
        (x, y, z, k)
        for x in range(NX)
        for y in range(NY)
        for z in range(NZ)
        for k in range(NK)
    ]


CORES = [(0, 1), (1, 0)]


def row_moves(number):
    moves = []
    for x, y, z, k in every():
        half = number ^ (z >> 2)
        moves.append(
            (place(x, y, z, k), place(2 * k + half, (y + z) % NY, 2 * x + (y >> 1), y & 1))
        )
    return moves


def shards(
    hidden_rows,
    query_weight,
    key_cache,
    value_cache,
    vertical_blocks,
    vertical_count,
    slash_offsets,
    slash_count,
    output_weight,
):
    x, y, z, k = (lax.axis_index(name) for name in ALL)
    weights = lax.all_gather(query_weight, ("y", "k"), axis=0)
    quarters = [
        lax.dynamic_slice_in_dim(cache, y * BLOCK, BLOCK, 0)
        for cache in (key_cache, value_cache)
    ]
    sent = jnp.stack(
        [
            jnp.stack([quarter[:, (to // 2) * HD : (to // 2 + 1) * HD] for quarter in quarters])
            for to in range(NZ)
        ]
    )
    near = lax.all_to_all(sent, "z", 0, 0)
    halves = pick(k.reshape(1).astype(jnp.int32), hidden_rows)
    hidden = lax.all_to_all(halves, "x", 0, 0)
    pieces = []
    key_block = []
    for shift in range(NY):
        piece = near
        if shift:
            piece = lax.ppermute(near, "y", [(i, (i + shift) % NY) for i in range(NY)])
        pieces += [piece, lax.ppermute(piece, "k", CORES)]
        for core in (k, 1 - k):
            key_block.append(
                4 * (2 * jnp.arange(NZ, dtype=jnp.int32) + core) + (y - shift) % NY
            )
    rows, _ = lax.optimization_barrier((output_weight, near))
    moved = jnp.stack(
        [
            lax.ppermute(
                lax.dynamic_slice_in_dim(rows, (number ^ (z >> 2)) * HD, HD, 0),
                ALL,
                row_moves(number),
            )
            for number in range(2)
        ]
    )
    partial = project(hidden, weights)
    moved, partial = lax.optimization_barrier((moved, partial))
    out_weight = lax.all_gather(moved, ("y", "k"), axis=0)
    partial = lax.all_to_all(partial, "x", 0, 0)
    low, up = allowed_rows(
        4 * z + x,
        jnp.concatenate(key_block),
        32 + 8 * jnp.arange(NX, dtype=jnp.int32) + 2 * y + k,
        vertical_blocks,
        vertical_count,
        slash_offsets,
        slash_count,
    )
    heads = attend(partial, low, up, pieces)
    heads = lax.all_to_all(heads, "z", 0, 0)
    where = jnp.stack([x & 1, 2 * (z & 1)]).astype(jnp.int32)
    mixed = mix(where, heads, out_weight)
    mixed = lax.all_to_all(mixed, ("x", "k"), 0, 0)
    return jnp.sum(mixed.reshape(NX, NK * BLOCK, 512), axis=0)


def solution(mesh):
    grid = Mesh(mesh.devices.reshape(NX, NY, NZ, NK), ALL)
    outer, ctx = ("x", "y"), ("z", "k")
    placed = (
        P(outer, None),
        P(outer, ctx),
        P(ctx, None),
        P(ctx, None),
        P(),
        P(),
        P(),
        P(),
        P(ctx, outer),
    )
    return jax.shard_map(
        shards, mesh=grid, in_specs=placed, out_specs=P(outer, ctx), check_vma=False
    )
```

time: 237 us -> 250 us (1.055)
  starting transfers between devices: 103 us -> 46.2 us
  waiting for transfers between devices: 80.2 us -> 135 us
  blocking collectives: 0 us -> 20.2 us
  local copies, waits for them, and re-layouts: 22.4 us -> 7.08 us
  Pallas kernels: 11 us -> 18.1 us
  other arithmetic: 3.92 us -> 8.5 us
    all_to_all x4, starting transfers between devices: 86.1 us -> 20.2 us  [the longest x1 9.01 us: shards(): near = lax.all_to_all(sent, 'z', 0, 0)]
    ppermute x10 -> x9, waiting for transfers between devices: 36.8 us -> 84.7 us  [the longest x2 58.8 us: shards(): lax.ppermute(lax.dynamic_slice_in_dim(rows, (number ^ z >> 2) * HD, HD, 0...]
    all_to_all x0 -> x1, blocking collectives: none -> 20.2 us  [shards(): mixed = lax.all_to_all(mixed, ('x', 'k'), 0, 0)]
    ppermute x10 -> x9, starting transfers between devices: 17.3 us -> 26 us  [the longest x4 13.8 us: shards(): pieces += [piece, lax.ppermute(piece, 'k', CORES)]]
    pallas_call x3 -> x4, Pallas kernels: 11 us -> 18.1 us  [the longest x1 7.12 us: attend(): pl.pallas_call(attend_kernel, out_shape=jax.ShapeDtypeStruct((NZ, rows, H...]
    all_to_all x4, waiting for transfers between devices: 43.4 us -> 49.9 us  [the longest x1 26.8 us: shards(): heads = lax.all_to_all(heads, 'z', 0, 0)]
    unnamed x28 -> x14, local copies, waits for them, and re-layouts: 10.8 us -> 4.4 us
    unnamed x0 -> x7, other arithmetic: none -> 4.35 us
  transfers between devices with their start and end apart: 16 -> 15, of which waited for: 8 -> 6; matrix products, arithmetic and copies ran while one was open for 6% -> 4% of each run, Pallas kernels for 4% -> 4%
where the time goes in v2:
time: 250 us; the launch traced here: 249 us
  waiting for transfers between devices  135 us (54%)
  starting transfers between devices  46.2 us (18%)
  blocking collectives  20.2 us (8%)
  Pallas kernels  18.1 us (7%)
  between operations  13.7 us (5%)
  other arithmetic  8.5 us (3%)
  local copies, waits for them, and re-layouts  7.08 us (3%)
    ppermute x2, waiting for transfers between devices, shards(): lax.ppermute(lax.dynamic_slice_in_dim(rows, (number ^ z >> 2) * HD, HD, 0...  58.8 us
    all_to_all x1, waiting for transfers between devices, shards(): heads = lax.all_to_all(heads, 'z', 0, 0)  26.8 us
    ppermute x3, waiting for transfers between devices, shards(): piece = lax.ppermute(near, 'y', [(i, (i + shift) % NY) for i in range(NY)])  25.8 us
    all_to_all x1, blocking collectives, shards(): mixed = lax.all_to_all(mixed, ('x', 'k'), 0, 0)  20.2 us
    all_to_all x1, waiting for transfers between devices, shards(): near = lax.all_to_all(sent, 'z', 0, 0)  14 us
    ppermute x4, starting transfers between devices, shards(): pieces += [piece, lax.ppermute(piece, 'k', CORES)]  13.8 us
    all_to_all x1, waiting for transfers between devices, shards(): partial = lax.all_to_all(partial, 'x', 0, 0)  9.06 us
    all_to_all x1, starting transfers between devices, shards(): near = lax.all_to_all(sent, 'z', 0, 0)  9.01 us
  transfers between devices with their start and end apart: 15, of which 6 were waited for; matrix products, arithmetic and copies ran while one was open for 4% of the time, Pallas kernels for 4%

profile of v2, /device:TPU:1, one launch (start us, length us, event | category | flops | bytes accessed | tf_op | source)
XLA Modules:
  0.0 249.0 jit_solution(6899515226191852116)
XLA Ops:
  13.1 9.0 %all-to-all-start = ((f32[8,2,64,128]{3,2,1,0:T(8,128)}), f32[8,2,64,128]{3,2,1,0:T(8,128)S(1)}, u32[]{:S(2)}, u32[]{:S(2)}) async-start(f32[8,2,64,128]{3,2,1,0:T(8,128)} %fusion.1), calls=%async_computation | async-start | bytes 1048576 | tf_op jit(solution)/shard_map/all_to_all | solution.py:273
  22.2 3.9 %pick.1 = f32[4,64,2048]{2,1,0:T(8,128)} custom-call(s32[1]{0:T(128)} %bitcast.16.where, f32[128,8192]{1,0:T(8,128)} %rows.1), custom_call_target="tpu_custom_call" | custom-call | tf_op jit(solution)/shard_map/pick/pallas_call | solution.py:44
  26.1 14.0 %all-to-all-done.refs_0_ = f32[8,2,64,128]{3,2,1,0:T(8,128)S(1)} async-done(((f32[8,2,64,128]{3,2,1,0:T(8,128)}), f32[8,2,64,128]{3,2,1,0:T(8,128)S(1)}, u32[]{:S(2)}, u32[]{:S(2)}) %all-to-all-start) | async-done | bytes 524320 | tf_op jit(solution)/shard_map/all_to_all | solution.py:273
  40.1 4.0 %all-to-all-start.1 = ((f32[4,64,2048]{2,1,0:T(8,128)}), f32[4,64,2048]{2,1,0:T(8,128)S(1)}, u32[]{:S(2)}, u32[]{:S(2)}) async-start(f32[4,64,2048]{2,1,0:T(8,128)} %pick.1), calls=%async_computation.1 | async-start | bytes 4194304 | tf_op jit(solution)/shard_map/all_to_all | solution.py:275
  44.2 5.5 %collective-permute-start.1 = (f32[128,512]{1,0:T(8,128)S(1)}, f32[128,512]{1,0:T(8,128)S(1)}, u32[]{:S(2)}, u32[]{:S(2)}) collective-permute-start(f32[128,512]{1,0:T(8,128)S(1)} %get-tuple-element.14), channel_id=1, source_target_pairs={{0,64},{1,192},{2,80},{3,208},{4,96},{5,224},{6,112},{7,240},{8,0}... | collective-permute-start | bytes 786440 | tf_op jit(solution)/shard_map/ppermute | solution.py:290
  49.7 2.8 %collective-permute-start = (f32[128,512]{1,0:T(8,128)S(1)}, f32[128,512]{1,0:T(8,128)S(1)}, u32[]{:S(2)}, u32[]{:S(2)}) collective-permute-start(f32[128,512]{1,0:T(8,128)S(1)} %get-tuple-element.13), channel_id=1, source_target_pairs={{0,0},{1,128},{2,16},{3,144},{4,32},{5,160},{6,48},{7,176},{8,64},... | collective-permute-start | bytes 786440 | tf_op jit(solution)/shard_map/ppermute | solution.py:290
  52.5 36.2 %collective-permute-done.1 = f32[128,512]{1,0:T(8,128)S(1)} collective-permute-done((f32[128,512]{1,0:T(8,128)S(1)}, f32[128,512]{1,0:T(8,128)S(1)}, u32[]{:S(2)}, u32[]{:S(2)}) %collective-permute-start.1) | collective-permute-done | bytes 262176 | tf_op jit(solution)/shard_map/ppermute | solution.py:290
  88.7 22.6 %collective-permute-done = f32[128,512]{1,0:T(8,128)S(1)} collective-permute-done((f32[128,512]{1,0:T(8,128)S(1)}, f32[128,512]{1,0:T(8,128)S(1)}, u32[]{:S(2)}, u32[]{:S(2)}) %collective-permute-start) | collective-permute-done | bytes 262176 | tf_op jit(solution)/shard_map/ppermute | solution.py:290
  112.2 2.2 copy-done.1
  114.4 3.4 %project.1 = f32[4,256,128]{2,1,0:T(8,128)} custom-call(f32[4,64,2048]{2,1,0:T(8,128)S(1)} %all-to-all-done.1.hidden, f32[8,512,256]{2,1,0:T(8,128)S(1)} %bitcast.65), custom_call_target="tpu_custom_call" | custom-call | flops 1610612736 | bytes 7340032 | tf_op jit(solution)/shard_map/project/pallas_call | solution.py:85
  121.5 2.5 collective-permute-start.7
  124.8 2.0 collective-permute-start.2
  126.8 25.8 %collective-permute-done.3.refs_2_ = f32[8,2,64,128]{3,2,1,0:T(8,128)S(1)} collective-permute-done((f32[8,2,64,128]{3,2,1,0:T(8,128)S(1)}, f32[8,2,64,128]{3,2,1,0:T(8,128)S(1)}, u32[]{:S(2)}, u32[]{:S(2)}) %collective-permute-start.3) | collective-permute-done | bytes 524320 | tf_op jit(solution)/shard_map/ppermute | solution.py:281
  152.7 5.6 %collective-permute-start.4 = (f32[8,2,64,128]{3,2,1,0:T(8,128)S(1)}, f32[8,2,64,128]{3,2,1,0:T(8,128)}, u32[]{:S(2)}, u32[]{:S(2)}) collective-permute-start(f32[8,2,64,128]{3,2,1,0:T(8,128)S(1)} %collective-permute-done.3.refs_2_), channel_id=1, source_target_pairs={{0,1},{1,0},{2,3},{3,2},{4,5},{5,4},{6,7},{7,6},{8,9},{9,8},{10,11... | collective-permute-start | bytes 1572872 | tf_op jit(solution)/shard_map/ppermute | solution.py:282
  158.2 3.2 %collective-permute-start.6 = (f32[8,2,64,128]{3,2,1,0:T(8,128)S(1)}, f32[8,2,64,128]{3,2,1,0:T(8,128)}, u32[]{:S(2)}, u32[]{:S(2)}) collective-permute-start(f32[8,2,64,128]{3,2,1,0:T(8,128)S(1)} %collective-permute-done.5.refs_4_), channel_id=1, source_target_pairs={{0,1},{1,0},{2,3},{3,2},{4,5},{5,4},{6,7},{7,6},{8,9},{9,8},{10,11... | collective-permute-start | bytes 1572872 | tf_op jit(solution)/shard_map/ppermute | solution.py:282
  161.5 3.0 %collective-permute-start.8 = (f32[8,2,64,128]{3,2,1,0:T(8,128)S(1)}, f32[8,2,64,128]{3,2,1,0:T(8,128)}, u32[]{:S(2)}, u32[]{:S(2)}) collective-permute-start(f32[8,2,64,128]{3,2,1,0:T(8,128)S(1)} %collective-permute-done.7.refs_6_), channel_id=1, source_target_pairs={{0,1},{1,0},{2,3},{3,2},{4,5},{5,4},{6,7},{7,6},{8,9},{9,8},{10,11... | collective-permute-start | bytes 1572872 | tf_op jit(solution)/shard_map/ppermute | solution.py:282
  164.5 3.5 %all-to-all-start.2 = ((f32[4,256,128]{2,1,0:T(8,128)}), f32[4,256,128]{2,1,0:T(8,128)S(1)}, u32[]{:S(2)}, u32[]{:S(2)}) async-start(f32[4,256,128]{2,1,0:T(8,128)} %project.1), calls=%async_computation.2 | async-start | bytes 1048576 | tf_op jit(solution)/shard_map/all_to_all | solution.py:301
  168.5 9.1 %all-to-all-done.2.partial = f32[4,256,128]{2,1,0:T(8,128)S(1)} async-done(((f32[4,256,128]{2,1,0:T(8,128)}), f32[4,256,128]{2,1,0:T(8,128)S(1)}, u32[]{:S(2)}, u32[]{:S(2)}) %all-to-all-start.2) | async-done | bytes 524320 | tf_op jit(solution)/shard_map/all_to_all | solution.py:301
  177.6 7.1 %attend.1 = f32[8,256,128]{2,1,0:T(8,128)} custom-call(f32[4,256,128]{2,1,0:T(8,128)S(1)} %all-to-all-done.2.partial, f32[4,4096]{1,0:T(4,128)S(1)} %broadcast_in_dim.38.low, f32[4,4096]{1,0:T(4,128)S(1)} %broadcast_in_dim.40.up, f32[8,2,64,128]{3,2,1,0:T(8,128)S(1)} %all-to-all-done.refs_0_, f32[8,2,64,128]{3,2,1,0:T(8,128)} %collective-permute-done.2.refs_1_, ...), custom_call_target="tpu_custom_call" | custom-call | flops 1610612736 | bytes 6291456 | tf_op jit(solution)/shard_map/attend/pallas_call | solution.py:148
  184.7 3.7 %all-to-all-start.3 = ((f32[8,256,128]{2,1,0:T(8,128)}), f32[8,256,128]{2,1,0:T(8,128)S(1)}, u32[]{:S(2)}, u32[]{:S(2)}) async-start(f32[8,256,128]{2,1,0:T(8,128)} %attend.1), calls=%async_computation.3 | async-start | bytes 2097152 | tf_op jit(solution)/shard_map/all_to_all | solution.py:312
  188.5 26.8 %all-to-all-done.3.heads = f32[8,256,128]{2,1,0:T(8,128)S(1)} async-done(((f32[8,256,128]{2,1,0:T(8,128)}), f32[8,256,128]{2,1,0:T(8,128)S(1)}, u32[]{:S(2)}, u32[]{:S(2)}) %all-to-all-start.3) | async-done | bytes 1048608 | tf_op jit(solution)/shard_map/all_to_all | solution.py:312
  215.4 2.2 copy-done
  217.6 3.7 %mix.1 = f32[8,64,512]{2,1,0:T(8,128)S(1)} custom-call(s32[2]{0:T(128)S(1)} %pad_add_fusion.where, f32[8,256,128]{2,1,0:T(8,128)S(1)} %all-to-all-done.3.heads, f32[8,2,128,512]{3,2,1,0:T(8,128)S(1)} %bitcast.64), custom_call_target="tpu_custom_call" | custom-call | flops 1610612736 | bytes 6291456 | tf_op jit(solution)/shard_map/mix/pallas_call | solution.py:189
  221.2 20.2 %all_to_all.25 = f32[8,64,512]{2,1,0:T(8,128)S(1)} all-to-all(f32[8,64,512]{2,1,0:T(8,128)S(1)} %mix.1), channel_id=1, replica_groups=mesh['x'=4,'y'=4,'z'=8,'k'=2] {'x','k'}, dimensions={0} | all-to-all | bytes 2097152 | tf_op jit(solution)/shard_map/all_to_all | solution.py:315
  (60 shorter events, 13.3 us)
Async XLA Ops:
  6.5 105.6 %all-gather.5.cloned.1.call-start = ((), (), s32[]{:S(2)}) async-start(), calls=%async_computation.5 | async-start | bytes 4718592 | tf_op jit(solution)/shard_map/all_gather | solution.py:262
  13.1 27.0 %all-to-all-start = ((f32[8,2,64,128]{3,2,1,0:T(8,128)}), f32[8,2,64,128]{3,2,1,0:T(8,128)S(1)}, u32[]{:S(2)}, u32[]{:S(2)}) async-start(f32[8,2,64,128]{3,2,1,0:T(8,128)} %fusion.1), calls=%async_computation | async-start | bytes 1048576 | tf_op jit(solution)/shard_map/all_to_all | solution.py:273
  22.2 22.0 %copy-start.2 = (f32[256,512]{1,0:T(8,128)S(1)}, f32[256,512]{1,0:T(8,128)}, u32[]{:S(2)}) copy-start(f32[256,512]{1,0:T(8,128)} %param.17) | copy-start | bytes 1572868
  40.1 72.0 %all-to-all-start.1 = ((f32[4,64,2048]{2,1,0:T(8,128)}), f32[4,64,2048]{2,1,0:T(8,128)S(1)}, u32[]{:S(2)}, u32[]{:S(2)}) async-start(f32[4,64,2048]{2,1,0:T(8,128)} %pick.1), calls=%async_computation.1 | async-start | bytes 4194304 | tf_op jit(solution)/shard_map/all_to_all | solution.py:275
  44.1 171.2 %all-gather.7.cloned.1.call-start = ((), (), s32[]{:S(2)}) async-start(), calls=%async_computation.6 | async-start | bytes 4718592 | tf_op jit(solution)/shard_map/all_gather | solution.py:300
  44.2 44.5 %collective-permute-start.1 = (f32[128,512]{1,0:T(8,128)S(1)}, f32[128,512]{1,0:T(8,128)S(1)}, u32[]{:S(2)}, u32[]{:S(2)}) collective-permute-start(f32[128,512]{1,0:T(8,128)S(1)} %get-tuple-element.14), channel_id=1, source_target_pairs={{0,64},{1,192},{2,80},{3,208},{4,96},{5,224},{6,112},{7,240},{8,0}... | collective-permute-start | bytes 786440 | tf_op jit(solution)/shard_map/ppermute | solution.py:290
  49.7 61.6 %collective-permute-start = (f32[128,512]{1,0:T(8,128)S(1)}, f32[128,512]{1,0:T(8,128)S(1)}, u32[]{:S(2)}, u32[]{:S(2)}) collective-permute-start(f32[128,512]{1,0:T(8,128)S(1)} %get-tuple-element.13), channel_id=1, source_target_pairs={{0,0},{1,128},{2,16},{3,144},{4,32},{5,160},{6,48},{7,176},{8,64},... | collective-permute-start | bytes 786440 | tf_op jit(solution)/shard_map/ppermute | solution.py:290
  111.3 6.5 %copy-start.5 = (s32[32]{0:T(128)S(1)}, s32[32]{0:T(128)}, u32[]{:S(2)}) copy-start(s32[32]{0:T(128)} %param.14) | copy-start | bytes 388
  111.3 7.1 %copy-start.6 = (s32[32]{0:T(128)S(1)}, s32[32]{0:T(128)}, u32[]{:S(2)}) copy-start(s32[32]{0:T(128)} %param.16) | copy-start | bytes 388
  111.3 7.9 %copy-start.3 = (s32[32,16]{0,1:T(8,128)S(1)}, s32[32,16]{0,1:T(8,128)}, u32[]{:S(2)}) copy-start(s32[32,16]{0,1:T(8,128)} %param.15) | copy-start | bytes 6148
  111.3 7.9 %copy-start.4 = (s32[32,16]{0,1:T(8,128)S(1)}, s32[32,16]{0,1:T(8,128)}, u32[]{:S(2)}) copy-start(s32[32,16]{0,1:T(8,128)} %param.13) | copy-start | bytes 6148
  112.2 2.2 copy-start.1
  120.2 32.5 %collective-permute-start.3 = (f32[8,2,64,128]{3,2,1,0:T(8,128)S(1)}, f32[8,2,64,128]{3,2,1,0:T(8,128)S(1)}, u32[]{:S(2)}, u32[]{:S(2)}) collective-permute-start(f32[8,2,64,128]{3,2,1,0:T(8,128)S(1)} %all-to-all-done.refs_0_), channel_id=1, source_target_pairs={{0,16},{16,32},{32,48},{48,0},{1,17},{17,33},{33,49},{49,1},{2,18}... | collective-permute-start | bytes 1572872 | tf_op jit(solution)/shard_map/ppermute | solution.py:281
  121.5 36.7 %collective-permute-start.5 = (f32[8,2,64,128]{3,2,1,0:T(8,128)S(1)}, f32[8,2,64,128]{3,2,1,0:T(8,128)S(1)}, u32[]{:S(2)}, u32[]{:S(2)}) collective-permute-start(f32[8,2,64,128]{3,2,1,0:T(8,128)S(1)} %all-to-all-done.refs_0_), channel_id=1, source_target_pairs={{0,32},{16,48},{32,0},{48,16},{1,33},{17,49},{33,1},{49,17},{2,34}... | collective-permute-start | bytes 1572872 | tf_op jit(solution)/shard_map/ppermute | solution.py:281
  121.5 39.9 %collective-permute-start.7 = (f32[8,2,64,128]{3,2,1,0:T(8,128)S(1)}, f32[8,2,64,128]{3,2,1,0:T(8,128)S(1)}, u32[]{:S(2)}, u32[]{:S(2)}) collective-permute-start(f32[8,2,64,128]{3,2,1,0:T(8,128)S(1)} %all-to-all-done.refs_0_), channel_id=1, source_target_pairs={{0,48},{16,0},{32,16},{48,32},{1,49},{17,1},{33,17},{49,33},{2,50}... | collective-permute-start | bytes 1572872 | tf_op jit(solution)/shard_map/ppermute | solution.py:281
  124.8 43.6 %collective-permute-start.2 = (f32[8,2,64,128]{3,2,1,0:T(8,128)S(1)}, f32[8,2,64,128]{3,2,1,0:T(8,128)}, u32[]{:S(2)}, u32[]{:S(2)}) collective-permute-start(f32[8,2,64,128]{3,2,1,0:T(8,128)S(1)} %all-to-all-done.refs_0_), channel_id=1, source_target_pairs={{0,1},{1,0},{2,3},{3,2},{4,5},{5,4},{6,7},{7,6},{8,9},{9,8},{10,11... | collective-permute-start | bytes 1572872 | tf_op jit(solution)/shard_map/ppermute | solution.py:282
  152.7 15.8 %collective-permute-start.4 = (f32[8,2,64,128]{3,2,1,0:T(8,128)S(1)}, f32[8,2,64,128]{3,2,1,0:T(8,128)}, u32[]{:S(2)}, u32[]{:S(2)}) collective-permute-start(f32[8,2,64,128]{3,2,1,0:T(8,128)S(1)} %collective-permute-done.3.refs_2_), channel_id=1, source_target_pairs={{0,1},{1,0},{2,3},{3,2},{4,5},{5,4},{6,7},{7,6},{8,9},{9,8},{10,11... | collective-permute-start | bytes 1572872 | tf_op jit(solution)/shard_map/ppermute | solution.py:282
  158.2 10.3 %collective-permute-start.6 = (f32[8,2,64,128]{3,2,1,0:T(8,128)S(1)}, f32[8,2,64,128]{3,2,1,0:T(8,128)}, u32[]{:S(2)}, u32[]{:S(2)}) collective-permute-start(f32[8,2,64,128]{3,2,1,0:T(8,128)S(1)} %collective-permute-done.5.refs_4_), channel_id=1, source_target_pairs={{0,1},{1,0},{2,3},{3,2},{4,5},{5,4},{6,7},{7,6},{8,9},{9,8},{10,11... | collective-permute-start | bytes 1572872 | tf_op jit(solution)/shard_map/ppermute | solution.py:282
  161.5 7.0 %collective-permute-start.8 = (f32[8,2,64,128]{3,2,1,0:T(8,128)S(1)}, f32[8,2,64,128]{3,2,1,0:T(8,128)}, u32[]{:S(2)}, u32[]{:S(2)}) collective-permute-start(f32[8,2,64,128]{3,2,1,0:T(8,128)S(1)} %collective-permute-done.7.refs_6_), channel_id=1, source_target_pairs={{0,1},{1,0},{2,3},{3,2},{4,5},{5,4},{6,7},{7,6},{8,9},{9,8},{10,11... | collective-permute-start | bytes 1572872 | tf_op jit(solution)/shard_map/ppermute | solution.py:282
  164.5 13.1 %all-to-all-start.2 = ((f32[4,256,128]{2,1,0:T(8,128)}), f32[4,256,128]{2,1,0:T(8,128)S(1)}, u32[]{:S(2)}, u32[]{:S(2)}) async-start(f32[4,256,128]{2,1,0:T(8,128)} %project.1), calls=%async_computation.2 | async-start | bytes 1048576 | tf_op jit(solution)/shard_map/all_to_all | solution.py:301
  184.7 30.7 %all-to-all-start.3 = ((f32[8,256,128]{2,1,0:T(8,128)}), f32[8,256,128]{2,1,0:T(8,128)S(1)}, u32[]{:S(2)}, u32[]{:S(2)}) async-start(f32[8,256,128]{2,1,0:T(8,128)} %attend.1), calls=%async_computation.3 | async-start | bytes 2097152 | tf_op jit(solution)/shard_map/all_to_all | solution.py:312
  215.4 2.2 copy-start
Sparse Core Ops, SparseCore 0:
  9.2 38.8 all-gather.4
  117.9 47.3 all-gather.6

commit v3 on v2

--- a/solution.py
+++ b/solution.py
@@ -163,44 +163,47 @@
     )(partial, low, up, *pieces)
 
 
-def mix_kernel(where, heads, weights, out, buf, sem):
+def mix_kernel(heads, weights, out, buf, sem):
+    steps = NZ // 2
     copies = []
-    for step in range(8):
-        copies.append(pltpu.make_async_copy(weights.at[step], buf.at[step], sem.at[step]))
+    for step in range(steps):
+        copies.append(
+            pltpu.make_async_copy(
+                weights.at[:, pl.ds(2 * step, 2)], buf.at[step], sem.at[step]
+            )
+        )
         copies[step].start()
     totals = [None, None]
-    swap = where[0]
-    for step in range(8):
-        y, core = step // 2, step % 2
-        spot = (y + NY - (where[1] + core)) & 3
-        left = jnp.concatenate(
-            [heads[spot + 4 * swap], heads[spot + 4 * (1 - swap)]], axis=1
-        )
-        left = split(left)
+    for step in range(steps):
+        left = split(jnp.concatenate([heads[2 * step], heads[2 * step + 1]], axis=1))
         copies[step].wait()
-        term = dot3(left, split(buf[step].reshape(2 * HD, 512)), MM)
-        totals[core] = term if totals[core] is None else totals[core] + term
+        for core in range(NK):
+            right = jnp.concatenate(
+                [buf[step, :, z, core].reshape(HD, 512) for z in range(2)], axis=0
+            )
+            term = dot3(left, split(right), MM)
+            totals[core] = term if totals[core] is None else totals[core] + term
     for core in range(NK):
         for x in range(NX):
             out[2 * x + core] = totals[core][x * BLOCK : (x + 1) * BLOCK]
 
 
-def mix(where, heads, weights):
+def mix(heads, weights):
     return pl.pallas_call(
         mix_kernel,
         out_shape=jax.ShapeDtypeStruct((NX * NK, BLOCK, 512), jnp.float32),
-        in_specs=[SMEM, VMEM, ANY],
+        in_specs=[VMEM, ANY],
         out_specs=VMEM,
         scratch_shapes=[
-            pltpu.VMEM((8, 2, HD, 512), jnp.float32),
-            pltpu.SemaphoreType.DMA((8,)),
+            pltpu.VMEM((NZ // 2, 8, 2, NK, 16, 512), jnp.float32),
+            pltpu.SemaphoreType.DMA((NZ // 2,)),
         ],
         compiler_params=pltpu.CompilerParams(vmem_limit_bytes=32 << 20),
         cost_estimate=pl.CostEstimate(
             flops=6 * 256 * 1024 * 1024, bytes_accessed=6 << 20, transcendentals=0
         ),
         name="mix",
-    )(where, heads, weights)
+    )(heads, weights)
 
 
 def allowed_rows(
@@ -220,31 +223,7 @@
     return bias[0], bias[1]
 
 
-def place(x, y, z, k):
-    return ((x * NY + y) * NZ + z) * NK + k
-
-
-def every():
-    return [
-        (x, y, z, k)
-        for x in range(NX)
-        for y in range(NY)
-        for z in range(NZ)
-        for k in range(NK)
-    ]
-
-
 CORES = [(0, 1), (1, 0)]
-
-
-def row_moves(number):
-    moves = []
-    for x, y, z, k in every():
-        half = number ^ (z >> 2)
-        moves.append(
-            (place(x, y, z, k), place(2 * k + half, (y + z) % NY, 2 * x + (y >> 1), y & 1))
-        )
-    return moves
 
 
 def shards(
@@ -260,6 +239,12 @@
 ):
     x, y, z, k = (lax.axis_index(name) for name in ALL)
     weights = lax.all_gather(query_weight, ("y", "k"), axis=0)
+    rows = output_weight.reshape(2, NY, NK, 16, 512).transpose(2, 0, 1, 3, 4)
+    rows = lax.all_to_all(rows, "k", 0, 0)
+    rows = rows.reshape(NX * NY, 16, 512)
+    rows = lax.all_to_all(rows, ("x", "y"), 0, 0)
+    rows = lax.all_to_all(rows.reshape(NZ, NK, 16, 512), "z", 0, 0)
+    out_weight = lax.all_gather(rows, ("y", "k"), axis=0)
     quarters = [
         lax.dynamic_slice_in_dim(cache, y * BLOCK, BLOCK, 0)
         for cache in (key_cache, value_cache)
@@ -284,20 +269,7 @@
             key_block.append(
                 4 * (2 * jnp.arange(NZ, dtype=jnp.int32) + core) + (y - shift) % NY
             )
-    rows, _ = lax.optimization_barrier((output_weight, near))
-    moved = jnp.stack(
-        [
-            lax.ppermute(
-                lax.dynamic_slice_in_dim(rows, (number ^ (z >> 2)) * HD, HD, 0),
-                ALL,
-                row_moves(number),
-            )
-            for number in range(2)
-        ]
-    )
     partial = project(hidden, weights)
-    moved, partial = lax.optimization_barrier((moved, partial))
-    out_weight = lax.all_gather(moved, ("y", "k"), axis=0)
     partial = lax.all_to_all(partial, "x", 0, 0)
     low, up = allowed_rows(
         4 * z + x,
@@ -310,8 +282,7 @@
     )
     heads = attend(partial, low, up, pieces)
     heads = lax.all_to_all(heads, "z", 0, 0)
-    where = jnp.stack([x & 1, 2 * (z & 1)]).astype(jnp.int32)
-    mixed = mix(where, heads, out_weight)
+    mixed = mix(heads, out_weight)
     mixed = lax.all_to_all(mixed, ("x", "k"), 0, 0)
     return jnp.sum(mixed.reshape(NX, NK * BLOCK, 512), axis=0)
 

time: 250 us -> 201 us (0.80)
  waiting for transfers between devices: 135 us -> 49.7 us
  blocking collectives: 20.2 us -> 62.7 us
  starting transfers between devices: 46.2 us -> 41.1 us
    ppermute x2 -> x0, waiting for transfers between devices: 58.8 us -> none  [shards(): lax.ppermute(lax.dynamic_slice_in_dim(rows, (number ^ z >> 2) * HD, HD, 0...]
    all_to_all x0 -> x3, blocking collectives: none -> 44.7 us  [the longest x1 22.5 us: shards(): rows = lax.all_to_all(rows.reshape(NZ, NK, 16, 512), 'z', 0, 0)]
    ppermute x3, waiting for transfers between devices: 25.8 us -> 2.39 us  [shards(): piece = lax.ppermute(near, 'y', [(i, (i + shift) % NY) for i in range(NY)])]
    ppermute x2 -> x0, starting transfers between devices: 8.28 us -> none  [shards(): lax.ppermute(lax.dynamic_slice_in_dim(rows, (number ^ z >> 2) * HD, HD, 0...]
    ppermute x4, starting transfers between devices: 13.8 us -> 20 us  [shards(): pieces += [piece, lax.ppermute(piece, 'k', CORES)]]
    all_to_all x1, starting transfers between devices: 9.01 us -> 3.5 us  [shards(): near = lax.all_to_all(sent, 'z', 0, 0)]
    all_to_all x1, waiting for transfers between devices: 14 us -> 9.12 us  [shards(): near = lax.all_to_all(sent, 'z', 0, 0)]
  transfers between devices with their start and end apart: 15 -> 13, of which waited for: 6 -> 4; matrix products, arithmetic and copies ran while one was open for 4% -> 5% of each run, Pallas kernels for 4% -> 7%
where the time goes in v3:
time: 201 us; the launch traced here: 200 us
  blocking collectives  62.7 us (31%)
  waiting for transfers between devices  49.7 us (25%)
  starting transfers between devices  41.1 us (20%)
  Pallas kernels  16.9 us (8%)
  between operations  13.7 us (7%)
  local copies, waits for them, and re-layouts  8.14 us (4%)
  other arithmetic  7.56 us (4%)
    all_to_all x1, waiting for transfers between devices, shards(): heads = lax.all_to_all(heads, 'z', 0, 0)  29.2 us
    all_to_all x1, blocking collectives, shards(): rows = lax.all_to_all(rows.reshape(NZ, NK, 16, 512), 'z', 0, 0)  22.5 us
    ppermute x4, starting transfers between devices, shards(): pieces += [piece, lax.ppermute(piece, 'k', CORES)]  20 us
    all_to_all x1, blocking collectives, shards(): mixed = lax.all_to_all(mixed, ('x', 'k'), 0, 0)  18 us
    all_to_all x1, blocking collectives, shards(): rows = lax.all_to_all(rows, ('x', 'y'), 0, 0)  15.2 us
    all_to_all x1, waiting for transfers between devices, shards(): near = lax.all_to_all(sent, 'z', 0, 0)  9.12 us
    all_to_all x1, waiting for transfers between devices, shards(): partial = lax.all_to_all(partial, 'x', 0, 0)  8.24 us
    pallas_call x1, Pallas kernels, attend(): pl.pallas_call(attend_kernel, out_shape=jax.ShapeDtypeStruct((NZ, rows, H...  7.1 us
  transfers between devices with their start and end apart: 13, of which 4 were waited for; matrix products, arithmetic and copies ran while one was open for 5% of the time, Pallas kernels for 7%

profile of v3, /device:TPU:1, one launch (start us, length us, event | category | flops | bytes accessed | tf_op | source)
XLA Modules:
  0.0 199.8 jit_solution(10715064408296361959)
XLA Ops:
  7.3 1.1 copy.12
  8.4 7.0 %all_to_all.40 = f32[2,2,4,16,512]{4,3,2,1,0:T(8,128)S(1)} all-to-all(f32[2,2,4,16,512]{4,3,2,1,0:T(8,128)S(1)} %copy.12), channel_id=1, replica_groups=mesh['x'=4,'y'=4,'z'=8,'k'=2] {'k'}, dimensions={0} | all-to-all | bytes 1048576 | tf_op jit(solution)/shard_map/all_to_all | solution.py:243
  15.4 15.2 %all_to_all.41 = f32[16,16,512]{2,1,0:T(8,128)S(1)} all-to-all(f32[16,16,512]{2,1,0:T(8,128)S(1)} %bitcast.68), channel_id=1, replica_groups=mesh['x'=4,'y'=4,'z'=8,'k'=2] {'x','y'}, dimensions={0} | all-to-all | bytes 1048576 | tf_op jit(solution)/shard_map/all_to_all | solution.py:245
  30.6 22.5 %all_to_all.42 = f32[8,2,16,512]{3,2,1,0:T(8,128)} all-to-all(f32[8,2,16,512]{3,2,1,0:T(8,128)S(1)} %bitcast.69), channel_id=1, replica_groups=mesh['x'=4,'y'=4,'z'=8,'k'=2] {'z'}, dimensions={0} | all-to-all | bytes 1048576 | tf_op jit(solution)/shard_map/all_to_all | solution.py:246
  59.0 3.5 %all-to-all-start.2 = ((f32[8,2,64,128]{3,2,1,0:T(8,128)}), f32[8,2,64,128]{3,2,1,0:T(8,128)S(1)}, u32[]{:S(2)}, u32[]{:S(2)}) async-start(f32[8,2,64,128]{3,2,1,0:T(8,128)} %fusion.1), calls=%async_computation.2 | async-start | bytes 1048576 | tf_op jit(solution)/shard_map/all_to_all | solution.py:258
  62.6 4.0 %pick.1 = f32[4,64,2048]{2,1,0:T(8,128)} custom-call(s32[1]{0:T(128)} %bitcast.where, f32[128,8192]{1,0:T(8,128)} %rows.1), custom_call_target="tpu_custom_call" | custom-call | tf_op jit(solution)/shard_map/pick/pallas_call | solution.py:44
  66.5 9.1 %all-to-all-done.2.refs_0_ = f32[8,2,64,128]{3,2,1,0:T(8,128)S(1)} async-done(((f32[8,2,64,128]{3,2,1,0:T(8,128)}), f32[8,2,64,128]{3,2,1,0:T(8,128)S(1)}, u32[]{:S(2)}, u32[]{:S(2)}) %all-to-all-start.2) | async-done | bytes 524320 | tf_op jit(solution)/shard_map/all_to_all | solution.py:258
  75.7 3.6 %all-to-all-start = ((f32[4,64,2048]{2,1,0:T(8,128)}), f32[4,64,2048]{2,1,0:T(8,128)S(1)}, u32[]{:S(2)}, u32[]{:S(2)}) async-start(f32[4,64,2048]{2,1,0:T(8,128)} %pick.1), calls=%async_computation | async-start | bytes 4194304 | tf_op jit(solution)/shard_map/all_to_all | solution.py:260
  82.0 3.1 %collective-permute-start.3 = (f32[8,2,64,128]{3,2,1,0:T(8,128)S(1)}, f32[8,2,64,128]{3,2,1,0:T(8,128)}, u32[]{:S(2)}, u32[]{:S(2)}) collective-permute-start(f32[8,2,64,128]{3,2,1,0:T(8,128)S(1)} %all-to-all-done.2.refs_0_), channel_id=1, source_target_pairs={{0,32},{16,48},{32,0},{48,16},{1,33},{17,49},{33,1},{49,17},{2,34}... | collective-permute-start | bytes 1572872 | tf_op jit(solution)/shard_map/ppermute | solution.py:266
  85.1 1.0 collective-permute-start.5
  86.9 5.3 %collective-permute-start = (f32[8,2,64,128]{3,2,1,0:T(8,128)S(1)}, f32[8,2,64,128]{3,2,1,0:T(8,128)}, u32[]{:S(2)}, u32[]{:S(2)}) collective-permute-start(f32[8,2,64,128]{3,2,1,0:T(8,128)S(1)} %all-to-all-done.2.refs_0_), channel_id=1, source_target_pairs={{0,1},{1,0},{2,3},{3,2},{4,5},{5,4},{6,7},{7,6},{8,9},{9,8},{10,11... | collective-permute-start | bytes 1572872 | tf_op jit(solution)/shard_map/ppermute | solution.py:267
  92.2 9.5 %collective-permute-start.2 = (f32[8,2,64,128]{3,2,1,0:T(8,128)S(1)}, f32[8,2,64,128]{3,2,1,0:T(8,128)}, u32[]{:S(2)}, u32[]{:S(2)}) collective-permute-start(f32[8,2,64,128]{3,2,1,0:T(8,128)S(1)} %collective-permute-done.1.refs_2_), channel_id=1, source_target_pairs={{0,1},{1,0},{2,3},{3,2},{4,5},{5,4},{6,7},{7,6},{8,9},{9,8},{10,11... | collective-permute-start | bytes 1572872 | tf_op jit(solution)/shard_map/ppermute | solution.py:267
  101.7 2.4 %collective-permute-done.3.refs_4_ = f32[8,2,64,128]{3,2,1,0:T(8,128)} collective-permute-done((f32[8,2,64,128]{3,2,1,0:T(8,128)S(1)}, f32[8,2,64,128]{3,2,1,0:T(8,128)}, u32[]{:S(2)}, u32[]{:S(2)}) %collective-permute-start.3) | collective-permute-done | bytes 524320 | tf_op jit(solution)/shard_map/ppermute | solution.py:266
  104.1 5.3 %collective-permute-start.4 = (f32[8,2,64,128]{3,2,1,0:T(8,128)}, f32[8,2,64,128]{3,2,1,0:T(8,128)}, u32[]{:S(2)}, u32[]{:S(2)}) collective-permute-start(f32[8,2,64,128]{3,2,1,0:T(8,128)} %collective-permute-done.3.refs_4_), channel_id=1, source_target_pairs={{0,1},{1,0},{2,3},{3,2},{4,5},{5,4},{6,7},{7,6},{8,9},{9,8},{10,11... | collective-permute-start | bytes 1572872 | tf_op jit(solution)/shard_map/ppermute | solution.py:267
  109.4 2.2 %copy-done.1 = f32[4096,256]{1,0:T(8,128)S(1)} copy-done((f32[4096,256]{1,0:T(8,128)S(1)}, f32[4096,256]{1,0:T(8,128)}, u32[]{:S(2)}) %copy-start.1) | copy-done | bytes 4194328
  111.6 3.4 %project.1 = f32[4,256,128]{2,1,0:T(8,128)} custom-call(f32[4,64,2048]{2,1,0:T(8,128)S(1)} %all-to-all-done.hidden, f32[8,512,256]{2,1,0:T(8,128)S(1)} %bitcast.66), custom_call_target="tpu_custom_call" | custom-call | flops 1610612736 | bytes 7340032 | tf_op jit(solution)/shard_map/project/pallas_call | solution.py:85
  115.0 4.2 %all-to-all-start.1 = ((f32[4,256,128]{2,1,0:T(8,128)}), f32[4,256,128]{2,1,0:T(8,128)S(1)}, u32[]{:S(2)}, u32[]{:S(2)}) async-start(f32[4,256,128]{2,1,0:T(8,128)} %project.1), calls=%async_computation.1 | async-start | bytes 1048576 | tf_op jit(solution)/shard_map/all_to_all | solution.py:273
  119.7 8.2 %all-to-all-done.1.partial = f32[4,256,128]{2,1,0:T(8,128)S(1)} async-done(((f32[4,256,128]{2,1,0:T(8,128)}), f32[4,256,128]{2,1,0:T(8,128)S(1)}, u32[]{:S(2)}, u32[]{:S(2)}) %all-to-all-start.1) | async-done | bytes 524320 | tf_op jit(solution)/shard_map/all_to_all | solution.py:273
  127.9 7.1 %attend.1 = f32[8,256,128]{2,1,0:T(8,128)} custom-call(f32[4,256,128]{2,1,0:T(8,128)S(1)} %all-to-all-done.1.partial, f32[4,4096]{1,0:T(4,128)S(1)} %broadcast_in_dim.38.low, f32[4,4096]{1,0:T(4,128)S(1)} %broadcast_in_dim.40.up, f32[8,2,64,128]{3,2,1,0:T(8,128)S(1)} %all-to-all-done.2.refs_0_, f32[8,2,64,128]{3,2,1,0:T(8,128)} %collective-permute-done.refs_1_, ...), custom_call_target="tpu_custom_call" | custom-call | flops 1610612736 | bytes 6291456 | tf_op jit(solution)/shard_map/attend/pallas_call | solution.py:148
  135.0 5.3 %all-to-all-start.3 = ((f32[8,256,128]{2,1,0:T(8,128)}), f32[8,256,128]{2,1,0:T(8,128)S(1)}, u32[]{:S(2)}, u32[]{:S(2)}) async-start(f32[8,256,128]{2,1,0:T(8,128)} %attend.1), calls=%async_computation.3 | async-start | bytes 2097152 | tf_op jit(solution)/shard_map/all_to_all | solution.py:284
  140.3 29.2 %all-to-all-done.3.heads = f32[8,256,128]{2,1,0:T(8,128)S(1)} async-done(((f32[8,256,128]{2,1,0:T(8,128)}), f32[8,256,128]{2,1,0:T(8,128)S(1)}, u32[]{:S(2)}, u32[]{:S(2)}) %all-to-all-start.3) | async-done | bytes 1048608 | tf_op jit(solution)/shard_map/all_to_all | solution.py:284
  169.5 2.2 %copy-done = f32[64,2,16,512]{3,2,1,0:T(8,128)S(1)} copy-done((f32[64,2,16,512]{3,2,1,0:T(8,128)S(1)}, f32[64,2,16,512]{3,2,1,0:T(8,128)}, u32[]{:S(2)}) %copy-start) | copy-done | bytes 4194328
  171.7 2.5 %mix.1 = f32[8,64,512]{2,1,0:T(8,128)S(1)} custom-call(f32[8,256,128]{2,1,0:T(8,128)S(1)} %all-to-all-done.3.heads, f32[8,8,2,16,512]{4,3,2,1,0:T(8,128)S(1)} %bitcast.65), custom_call_target="tpu_custom_call" | custom-call | flops 1610612736 | bytes 6291456 | tf_op jit(solution)/shard_map/mix/pallas_call | solution.py:192
  174.1 18.0 %all_to_all.43 = f32[8,64,512]{2,1,0:T(8,128)S(1)} all-to-all(f32[8,64,512]{2,1,0:T(8,128)S(1)} %mix.1), channel_id=1, replica_groups=mesh['x'=4,'y'=4,'z'=8,'k'=2] {'x','k'}, dimensions={0} | all-to-all | bytes 2097152 | tf_op jit(solution)/shard_map/all_to_all | solution.py:286
  (55 shorter events, 11.4 us)
Async XLA Ops:
  6.5 102.9 %all-gather.5.cloned.1.call-start = ((), (), s32[]{:S(2)}) async-start(), calls=%async_computation.8 | async-start | bytes 4718592 | tf_op jit(solution)/shard_map/all_gather | solution.py:241
  7.3 133.0 %all-gather.7.cloned.1.call-start = ((), (), s32[]{:S(2)}) async-start(), calls=%async_computation.9 | async-start | bytes 4718592 | tf_op jit(solution)/shard_map/all_gather | solution.py:247
  59.0 16.6 %all-to-all-start.2 = ((f32[8,2,64,128]{3,2,1,0:T(8,128)}), f32[8,2,64,128]{3,2,1,0:T(8,128)S(1)}, u32[]{:S(2)}, u32[]{:S(2)}) async-start(f32[8,2,64,128]{3,2,1,0:T(8,128)} %fusion.1), calls=%async_computation.2 | async-start | bytes 1048576 | tf_op jit(solution)/shard_map/all_to_all | solution.py:258
  62.5 16.8 %copy-start.4 = (s32[32]{0:T(128)S(1)}, s32[32]{0:T(128)}, u32[]{:S(2)}) copy-start(s32[32]{0:T(128)} %param.14) | copy-start | bytes 388
  62.5 17.5 %copy-start.5 = (s32[32]{0:T(128)S(1)}, s32[32]{0:T(128)}, u32[]{:S(2)}) copy-start(s32[32]{0:T(128)} %param.16) | copy-start | bytes 388
  62.5 18.2 %copy-start.2 = (s32[32,16]{0,1:T(8,128)S(1)}, s32[32,16]{0,1:T(8,128)}, u32[]{:S(2)}) copy-start(s32[32,16]{0,1:T(8,128)} %param.15) | copy-start | bytes 6148
  62.5 18.2 %copy-start.3 = (s32[32,16]{0,1:T(8,128)S(1)}, s32[32,16]{0,1:T(8,128)}, u32[]{:S(2)}) copy-start(s32[32,16]{0,1:T(8,128)} %param.13) | copy-start | bytes 6148
  75.7 33.7 %all-to-all-start = ((f32[4,64,2048]{2,1,0:T(8,128)}), f32[4,64,2048]{2,1,0:T(8,128)S(1)}, u32[]{:S(2)}, u32[]{:S(2)}) async-start(f32[4,64,2048]{2,1,0:T(8,128)} %pick.1), calls=%async_computation | async-start | bytes 4194304 | tf_op jit(solution)/shard_map/all_to_all | solution.py:260
  81.7 10.5 %collective-permute-start.1 = (f32[8,2,64,128]{3,2,1,0:T(8,128)S(1)}, f32[8,2,64,128]{3,2,1,0:T(8,128)S(1)}, u32[]{:S(2)}, u32[]{:S(2)}) collective-permute-start(f32[8,2,64,128]{3,2,1,0:T(8,128)S(1)} %all-to-all-done.2.refs_0_), channel_id=1, source_target_pairs={{0,16},{16,32},{32,48},{48,0},{1,17},{17,33},{33,49},{49,1},{2,18}... | collective-permute-start | bytes 1572872 | tf_op jit(solution)/shard_map/ppermute | solution.py:266
  82.0 22.1 %collective-permute-start.3 = (f32[8,2,64,128]{3,2,1,0:T(8,128)S(1)}, f32[8,2,64,128]{3,2,1,0:T(8,128)}, u32[]{:S(2)}, u32[]{:S(2)}) collective-permute-start(f32[8,2,64,128]{3,2,1,0:T(8,128)S(1)} %all-to-all-done.2.refs_0_), channel_id=1, source_target_pairs={{0,32},{16,48},{32,0},{48,16},{1,33},{17,49},{33,1},{49,17},{2,34}... | collective-permute-start | bytes 1572872 | tf_op jit(solution)/shard_map/ppermute | solution.py:266
  85.1 24.2 %collective-permute-start.5 = (f32[8,2,64,128]{3,2,1,0:T(8,128)S(1)}, f32[8,2,64,128]{3,2,1,0:T(8,128)}, u32[]{:S(2)}, u32[]{:S(2)}) collective-permute-start(f32[8,2,64,128]{3,2,1,0:T(8,128)S(1)} %all-to-all-done.2.refs_0_), channel_id=1, source_target_pairs={{0,48},{16,0},{32,16},{48,32},{1,49},{17,1},{33,17},{49,33},{2,50}... | collective-permute-start | bytes 1572872 | tf_op jit(solution)/shard_map/ppermute | solution.py:266
  86.9 32.7 %collective-permute-start = (f32[8,2,64,128]{3,2,1,0:T(8,128)S(1)}, f32[8,2,64,128]{3,2,1,0:T(8,128)}, u32[]{:S(2)}, u32[]{:S(2)}) collective-permute-start(f32[8,2,64,128]{3,2,1,0:T(8,128)S(1)} %all-to-all-done.2.refs_0_), channel_id=1, source_target_pairs={{0,1},{1,0},{2,3},{3,2},{4,5},{5,4},{6,7},{7,6},{8,9},{9,8},{10,11... | collective-permute-start | bytes 1572872 | tf_op jit(solution)/shard_map/ppermute | solution.py:267
  92.2 27.4 %collective-permute-start.2 = (f32[8,2,64,128]{3,2,1,0:T(8,128)S(1)}, f32[8,2,64,128]{3,2,1,0:T(8,128)}, u32[]{:S(2)}, u32[]{:S(2)}) collective-permute-start(f32[8,2,64,128]{3,2,1,0:T(8,128)S(1)} %collective-permute-done.1.refs_2_), channel_id=1, source_target_pairs={{0,1},{1,0},{2,3},{3,2},{4,5},{5,4},{6,7},{7,6},{8,9},{9,8},{10,11... | collective-permute-start | bytes 1572872 | tf_op jit(solution)/shard_map/ppermute | solution.py:267
  104.1 15.5 %collective-permute-start.4 = (f32[8,2,64,128]{3,2,1,0:T(8,128)}, f32[8,2,64,128]{3,2,1,0:T(8,128)}, u32[]{:S(2)}, u32[]{:S(2)}) collective-permute-start(f32[8,2,64,128]{3,2,1,0:T(8,128)} %collective-permute-done.3.refs_4_), channel_id=1, source_target_pairs={{0,1},{1,0},{2,3},{3,2},{4,5},{5,4},{6,7},{7,6},{8,9},{9,8},{10,11... | collective-permute-start | bytes 1572872 | tf_op jit(solution)/shard_map/ppermute | solution.py:267
  109.4 10.3 %collective-permute-start.6 = (f32[8,2,64,128]{3,2,1,0:T(8,128)}, f32[8,2,64,128]{3,2,1,0:T(8,128)}, u32[]{:S(2)}, u32[]{:S(2)}) collective-permute-start(f32[8,2,64,128]{3,2,1,0:T(8,128)} %collective-permute-done.5.refs_6_), channel_id=1, source_target_pairs={{0,1},{1,0},{2,3},{3,2},{4,5},{5,4},{6,7},{7,6},{8,9},{9,8},{10,11... | collective-permute-start | bytes 1572872 | tf_op jit(solution)/shard_map/ppermute | solution.py:267
  109.4 2.2 %copy-start.1 = (f32[4096,256]{1,0:T(8,128)S(1)}, f32[4096,256]{1,0:T(8,128)}, u32[]{:S(2)}) copy-start(f32[4096,256]{1,0:T(8,128)} %all-gather.5.cloned.1.call-done) | copy-start | bytes 12582916
  115.0 12.9 %all-to-all-start.1 = ((f32[4,256,128]{2,1,0:T(8,128)}), f32[4,256,128]{2,1,0:T(8,128)S(1)}, u32[]{:S(2)}, u32[]{:S(2)}) async-start(f32[4,256,128]{2,1,0:T(8,128)} %project.1), calls=%async_computation.1 | async-start | bytes 1048576 | tf_op jit(solution)/shard_map/all_to_all | solution.py:273
  135.0 34.5 %all-to-all-start.3 = ((f32[8,256,128]{2,1,0:T(8,128)}), f32[8,256,128]{2,1,0:T(8,128)S(1)}, u32[]{:S(2)}, u32[]{:S(2)}) async-start(f32[8,256,128]{2,1,0:T(8,128)} %attend.1), calls=%async_computation.3 | async-start | bytes 2097152 | tf_op jit(solution)/shard_map/all_to_all | solution.py:284
  169.5 2.2 %copy-start = (f32[64,2,16,512]{3,2,1,0:T(8,128)S(1)}, f32[64,2,16,512]{3,2,1,0:T(8,128)}, u32[]{:S(2)}) copy-start(f32[64,2,16,512]{3,2,1,0:T(8,128)} %all-gather.7.cloned.1.call-done) | copy-start | bytes 12582916
Sparse Core Ops, SparseCore 0:
  9.2 40.6 all-gather.4
  53.2 33.3 all-gather.6

commit v4 on v3

--- a/solution.py
+++ b/solution.py
@@ -16,6 +16,7 @@
 VMEM = pl.BlockSpec(memory_space=pltpu.VMEM)
 SMEM = pl.BlockSpec(memory_space=pltpu.SMEM)
 ANY = pl.BlockSpec(memory_space=pl.ANY)
+HBM = pl.BlockSpec(memory_space=pltpu.HBM)
 
 
 def split(value):
@@ -36,38 +37,51 @@
 MT = (((1,), (1,)), ((), ()))
 
 
-def pick_kernel(where, rows, out):
-    out[0] = rows[...]
-
-
-def pick(k, hidden_rows):
+def pick_kernel(where, rows, *refs):
+    outs, sem = refs[:3], refs[3]
+    copies = []
+    for shift in range(1, NX):
+        cols = pl.multiple_of(lax.rem(where[0] + shift, NX) * 2048, 2048)
+        part = rows.at[pl.ds(pl.multiple_of(where[1] * BLOCK, BLOCK), BLOCK), pl.ds(cols, 2048)]
+        copies.append(pltpu.make_async_copy(part, outs[shift - 1], sem.at[shift - 1]))
+    for copy in copies:
+        copy.start()
+    for copy in copies:
+        copy.wait()
+
+
+def pick(where, hidden_rows):
     return pl.pallas_call(
         pick_kernel,
-        out_shape=jax.ShapeDtypeStruct((NX, BLOCK, 2048), jnp.float32),
-        grid_spec=pltpu.PrefetchScalarGridSpec(
-            num_scalar_prefetch=1,
-            grid=(NX,),
-            in_specs=[pl.BlockSpec((BLOCK, 2048), lambda i, where: (where[0], i))],
-            out_specs=pl.BlockSpec((1, BLOCK, 2048), lambda i, where: (i, 0, 0)),
-        ),
+        out_shape=[jax.ShapeDtypeStruct((BLOCK, 2048), jnp.float32)] * 3,
+        in_specs=[SMEM, HBM],
+        out_specs=[HBM] * 3,
+        scratch_shapes=[pltpu.SemaphoreType.DMA((3,))],
         name="pick",
-    )(k, hidden_rows)
-
-
-def project_kernel(hidden, weights, out, left_buf, right_buf, left_sem, right_sem):
+    )(where, hidden_rows)
+
+
+def project_kernel(where, rows, first, second, third, weights, out, left_buf, right_buf, sems):
+    x, k = where[0], where[1]
     copies = []
     for y in range(NY):
-        cols = pl.ds(y * 512, 512)
-        copies.append(
-            (
-                pltpu.make_async_copy(hidden.at[:, :, cols], left_buf.at[y], left_sem.at[y]),
-                pltpu.make_async_copy(
-                    weights.at[pl.ds(2 * y, 2)], right_buf.at[y], right_sem.at[y]
-                ),
+        own = rows.at[
+            pl.ds(pl.multiple_of(k * BLOCK, BLOCK), BLOCK),
+            pl.ds(pl.multiple_of(x * 2048 + y * 512, 512), 512),
+        ]
+        parts = [own] + [part.at[:, pl.ds(y * 512, 512)] for part in (first, second, third)]
+        group = [
+            pltpu.make_async_copy(
+                part, left_buf.at[y, lax.rem(x + NX - shift, NX)], sems.at[y, shift]
             )
+            for shift, part in enumerate(parts)
+        ]
+        group.append(
+            pltpu.make_async_copy(weights.at[pl.ds(2 * y, 2)], right_buf.at[y], sems.at[y, NX])
         )
-        for copy in copies[y]:
+        for copy in group:
             copy.start()
+        copies.append(group)
     totals = [None, None]
     for y in range(NY):
         for copy in copies[y]:
@@ -81,24 +95,23 @@
             out[2 * core + b] = totals[core][:, b * HD : (b + 1) * HD]
 
 
-def project(hidden, weights):
+def project(where, rows, moved, weights):
     return pl.pallas_call(
         project_kernel,
         out_shape=jax.ShapeDtypeStruct((NX, NX * BLOCK, HD), jnp.float32),
-        in_specs=[ANY, ANY],
+        in_specs=[SMEM, HBM, ANY, ANY, ANY, HBM],
         out_specs=VMEM,
         scratch_shapes=[
             pltpu.VMEM((NY, NX, BLOCK, 512), jnp.float32),
             pltpu.VMEM((NY, NK, 512, 256), jnp.float32),
-            pltpu.SemaphoreType.DMA((NY,)),
-            pltpu.SemaphoreType.DMA((NY,)),
+            pltpu.SemaphoreType.DMA((NY, NX + 1)),
         ],
         compiler_params=pltpu.CompilerParams(vmem_limit_bytes=32 << 20),
         cost_estimate=pl.CostEstimate(
             flops=6 * 256 * 2048 * 512, bytes_accessed=7 << 20, transcendentals=0
         ),
         name="project",
-    )(hidden, weights)
+    )(where, rows, *moved, weights)
 
 
 def attend_kernel(partial, low, up, *refs):
@@ -192,7 +205,7 @@
     return pl.pallas_call(
         mix_kernel,
         out_shape=jax.ShapeDtypeStruct((NX * NK, BLOCK, 512), jnp.float32),
-        in_specs=[VMEM, ANY],
+        in_specs=[VMEM, HBM],
         out_specs=VMEM,
         scratch_shapes=[
             pltpu.VMEM((NZ // 2, 8, 2, NK, 16, 512), jnp.float32),
@@ -238,13 +251,13 @@
     output_weight,
 ):
     x, y, z, k = (lax.axis_index(name) for name in ALL)
+    where = jnp.stack([x, k]).astype(jnp.int32)
     weights = lax.all_gather(query_weight, ("y", "k"), axis=0)
-    rows = output_weight.reshape(2, NY, NK, 16, 512).transpose(2, 0, 1, 3, 4)
-    rows = lax.all_to_all(rows, "k", 0, 0)
-    rows = rows.reshape(NX * NY, 16, 512)
-    rows = lax.all_to_all(rows, ("x", "y"), 0, 0)
-    rows = lax.all_to_all(rows.reshape(NZ, NK, 16, 512), "z", 0, 0)
-    out_weight = lax.all_gather(rows, ("y", "k"), axis=0)
+    picked = pick(where, hidden_rows)
+    hidden = [
+        lax.ppermute(part, "x", [(i, (i + shift) % NX) for i in range(NX)])
+        for shift, part in zip(range(1, NX), picked)
+    ]
     quarters = [
         lax.dynamic_slice_in_dim(cache, y * BLOCK, BLOCK, 0)
         for cache in (key_cache, value_cache)
@@ -255,9 +268,8 @@
             for to in range(NZ)
         ]
     )
+    sent, _ = lax.optimization_barrier((sent, picked[0]))
     near = lax.all_to_all(sent, "z", 0, 0)
-    halves = pick(k.reshape(1).astype(jnp.int32), hidden_rows)
-    hidden = lax.all_to_all(halves, "x", 0, 0)
     pieces = []
     key_block = []
     for shift in range(NY):
@@ -269,7 +281,18 @@
             key_block.append(
                 4 * (2 * jnp.arange(NZ, dtype=jnp.int32) + core) + (y - shift) % NY
             )
-    partial = project(hidden, weights)
+    rows = output_weight.reshape(2, NY, NK, 16, 512)
+    kept = lax.dynamic_index_in_dim(rows, k, 2, keepdims=False)
+    given = lax.dynamic_index_in_dim(rows, 1 - k, 2, keepdims=False)
+    taken = lax.ppermute(given, "k", CORES)
+    rows = jnp.where(k == 0, jnp.stack([kept, taken]), jnp.stack([taken, kept]))
+    rows, near = lax.optimization_barrier((rows, near))
+    rows = lax.all_to_all(rows.reshape(NX * NY, 16, 512), ("x", "y"), 0, 0)
+    rows, hidden = lax.optimization_barrier((rows, hidden))
+    rows = lax.all_to_all(rows.reshape(NZ, NK, 16, 512), "z", 0, 0)
+    out_weight = lax.all_gather(rows, ("y", "k"), axis=0)
+    hidden, pieces[2::2] = lax.optimization_barrier((hidden, pieces[2::2]))
+    partial = project(where, hidden_rows, hidden, weights)
     partial = lax.all_to_all(partial, "x", 0, 0)
     low, up = allowed_rows(
         4 * z + x,

time: 201 us -> 270 us (1.34)
  Pallas kernels: 16.9 us -> 62.3 us
  waiting for transfers between devices: 49.7 us -> 62.5 us
  blocking collectives: 62.7 us -> 73.6 us
    pallas_call x1, Pallas kernels: 3.97 us -> 49.4 us  [pick(): pl.pallas_call(pick_kernel, out_shape=[jax.ShapeDtypeStruct((BLOCK, 2048)...]
    ppermute x3, waiting for transfers between devices: 2.39 us -> 30.7 us  [shards(): piece = lax.ppermute(near, 'y', [(i, (i + shift) % NY) for i in range(NY)])]
    all_to_all x2 -> x1, waiting for transfers between devices: 29.2 us -> 7.53 us  [shards(): rows = lax.all_to_all(rows.reshape(NX * NY, 16, 512), ('x', 'y'), 0, 0)]
    ppermute x4, starting transfers between devices: 20 us -> 10.4 us  [shards(): pieces += [piece, lax.ppermute(piece, 'k', CORES)]]
    all_to_all x2 -> x1, blocking collectives: 22.2 us -> 29.7 us  [shards(): heads = lax.all_to_all(heads, 'z', 0, 0)]
    ppermute x0 -> x4, starting transfers between devices: none -> 5.87 us  [the longest x3 4.83 us: shards(): lax.ppermute(part, 'x', [(i, (i + shift) % NX) for i in range(NX)])]
    all_to_all x1, starting transfers between devices: 3.5 us -> 9.01 us  [shards(): near = lax.all_to_all(sent, 'z', 0, 0)]
    ppermute x0 -> x4, waiting for transfers between devices: none -> 3.46 us  [the longest x3 3.46 us: shards(): lax.ppermute(part, 'x', [(i, (i + shift) % NX) for i in range(NX)])]
  transfers between devices with their start and end apart: 13 -> 16, of which waited for: 4 -> 7; matrix products, arithmetic and copies ran while one was open for 5% -> 4% of each run, Pallas kernels for 7% -> 22%
where the time goes in v4:
time: 270 us; the launch traced here: 269 us
  blocking collectives  73.6 us (27%)
  waiting for transfers between devices  62.5 us (23%)
  Pallas kernels  62.3 us (23%)
  starting transfers between devices  38.7 us (14%)
  between operations  13.7 us (5%)
  local copies, waits for them, and re-layouts  9.36 us (3%)
  other arithmetic  9.27 us (3%)
    pallas_call x1, Pallas kernels, pick(): pl.pallas_call(pick_kernel, out_shape=[jax.ShapeDtypeStruct((BLOCK, 2048)...  49.4 us
    ppermute x3, waiting for transfers between devices, shards(): piece = lax.ppermute(near, 'y', [(i, (i + shift) % NY) for i in range(NY)])  30.7 us
    all_to_all x1, blocking collectives, shards(): heads = lax.all_to_all(heads, 'z', 0, 0)  29.7 us
    all_to_all x1, blocking collectives, shards(): rows = lax.all_to_all(rows.reshape(NZ, NK, 16, 512), 'z', 0, 0)  23.7 us
    all_to_all x1, blocking collectives, shards(): mixed = lax.all_to_all(mixed, ('x', 'k'), 0, 0)  20.1 us
    all_to_all x1, waiting for transfers between devices, shards(): near = lax.all_to_all(sent, 'z', 0, 0)  11.2 us
    ppermute x4, starting transfers between devices, shards(): pieces += [piece, lax.ppermute(piece, 'k', CORES)]  10.4 us
    all_to_all x1, starting transfers between devices, shards(): near = lax.all_to_all(sent, 'z', 0, 0)  9.01 us
  transfers between devices with their start and end apart: 16, of which 7 were waited for; matrix products, arithmetic and copies ran while one was open for 4% of the time, Pallas kernels for 22%

profile of v4, /device:TPU:1, one launch (start us, length us, event | category | flops | bytes accessed | tf_op | source)
XLA Modules:
  0.0 269.3 jit_solution(2876395351029738348)
XLA Ops:
  7.9 49.4 %pick.1 = (f32[64,2048]{1,0:T(8,128)}, f32[64,2048]{1,0:T(8,128)}, f32[64,2048]{1,0:T(8,128)}) custom-call(s32[2]{0:T(128)} %pad_add_fusion.where, f32[128,8192]{1,0:T(8,128)} %rows.3), custom_call_target="tpu_custom_call" | custom-call | tf_op jit(solution)/shard_map/pick/pallas_call | solution.py:54
  63.4 9.0 %all-to-all-start = ((f32[8,2,64,128]{3,2,1,0:T(8,128)}), f32[8,2,64,128]{3,2,1,0:T(8,128)S(1)}, u32[]{:S(2)}, u32[]{:S(2)}) async-start(f32[8,2,64,128]{3,2,1,0:T(8,128)} %fusion.1), calls=%async_computation | async-start | bytes 1048576 | tf_op jit(solution)/shard_map/all_to_all | solution.py:272
  74.7 2.5 collective-permute-start.2
  79.2 11.2 %all-to-all-done.refs_0_ = f32[8,2,64,128]{3,2,1,0:T(8,128)S(1)} async-done(((f32[8,2,64,128]{3,2,1,0:T(8,128)}), f32[8,2,64,128]{3,2,1,0:T(8,128)S(1)}, u32[]{:S(2)}, u32[]{:S(2)}) %all-to-all-start) | async-done | bytes 524320 | tf_op jit(solution)/shard_map/all_to_all | solution.py:272
  90.3 6.8 %all-to-all-start.1 = ((f32[16,16,512]{2,1,0:T(8,128)}), f32[16,16,512]{2,1,0:T(8,128)S(1)}, u32[]{:S(2)}, u32[]{:S(2)}) async-start(f32[16,16,512]{2,1,0:T(8,128)} %bitcast.18), calls=%async_computation.1 | async-start | bytes 1048576 | tf_op jit(solution)/shard_map/all_to_all | solution.py:290
  97.2 3.5 %collective-permute-done.2.second = f32[64,2048]{1,0:T(8,128)S(1)} collective-permute-done((f32[64,2048]{1,0:T(8,128)}, f32[64,2048]{1,0:T(8,128)S(1)}, u32[]{:S(2)}, u32[]{:S(2)}) %collective-permute-start.2) | collective-permute-done | bytes 524320 | tf_op jit(solution)/shard_map/ppermute | solution.py:258
  100.6 7.5 %all-to-all-done.1 = f32[16,16,512]{2,1,0:T(8,128)S(1)} async-done(((f32[16,16,512]{2,1,0:T(8,128)}), f32[16,16,512]{2,1,0:T(8,128)S(1)}, u32[]{:S(2)}, u32[]{:S(2)}) %all-to-all-start.1) | async-done | bytes 524320 | tf_op jit(solution)/shard_map/all_to_all | solution.py:290
  108.2 23.7 %all_to_all.30 = f32[8,2,16,512]{3,2,1,0:T(8,128)} all-to-all(f32[8,2,16,512]{3,2,1,0:T(8,128)S(1)} %bitcast.72), channel_id=1, replica_groups=mesh['x'=4,'y'=4,'z'=8,'k'=2] {'z'}, dimensions={0} | all-to-all | bytes 1048576 | tf_op jit(solution)/shard_map/all_to_all | solution.py:292
  135.1 2.3 collective-permute-start.6
  138.3 3.3 %collective-permute-start.7 = (f32[8,2,64,128]{3,2,1,0:T(8,128)S(1)}, f32[8,2,64,128]{3,2,1,0:T(8,128)}, u32[]{:S(2)}, u32[]{:S(2)}) collective-permute-start(f32[8,2,64,128]{3,2,1,0:T(8,128)S(1)} %all-to-all-done.refs_0_), channel_id=1, source_target_pairs={{0,1},{1,0},{2,3},{3,2},{4,5},{5,4},{6,7},{7,6},{8,9},{9,8},{10,11... | collective-permute-start | bytes 1572872 | tf_op jit(solution)/shard_map/ppermute | solution.py:279
  141.6 8.9 %collective-permute-done.4.refs_2_ = f32[8,2,64,128]{3,2,1,0:T(8,128)S(1)} collective-permute-done((f32[8,2,64,128]{3,2,1,0:T(8,128)S(1)}, f32[8,2,64,128]{3,2,1,0:T(8,128)S(1)}, u32[]{:S(2)}, u32[]{:S(2)}) %collective-permute-start.4) | collective-permute-done | bytes 524320 | tf_op jit(solution)/shard_map/ppermute | solution.py:278
  150.5 17.9 %collective-permute-done.5.refs_4_ = f32[8,2,64,128]{3,2,1,0:T(8,128)S(1)} collective-permute-done((f32[8,2,64,128]{3,2,1,0:T(8,128)S(1)}, f32[8,2,64,128]{3,2,1,0:T(8,128)S(1)}, u32[]{:S(2)}, u32[]{:S(2)}) %collective-permute-start.5) | collective-permute-done | bytes 524320 | tf_op jit(solution)/shard_map/ppermute | solution.py:278
  168.4 3.9 %collective-permute-done.6.refs_6_ = f32[8,2,64,128]{3,2,1,0:T(8,128)} collective-permute-done((f32[8,2,64,128]{3,2,1,0:T(8,128)S(1)}, f32[8,2,64,128]{3,2,1,0:T(8,128)}, u32[]{:S(2)}, u32[]{:S(2)}) %collective-permute-start.6) | collective-permute-done | bytes 524320 | tf_op jit(solution)/shard_map/ppermute | solution.py:278
  172.3 6.6 %collective-permute-start.8 = (f32[8,2,64,128]{3,2,1,0:T(8,128)S(1)}, f32[8,2,64,128]{3,2,1,0:T(8,128)}, u32[]{:S(2)}, u32[]{:S(2)}) collective-permute-start(f32[8,2,64,128]{3,2,1,0:T(8,128)S(1)} %collective-permute-done.4.refs_2_), channel_id=1, source_target_pairs={{0,1},{1,0},{2,3},{3,2},{4,5},{5,4},{6,7},{7,6},{8,9},{9,8},{10,11... | collective-permute-start | bytes 1572872 | tf_op jit(solution)/shard_map/ppermute | solution.py:279
  179.4 2.2 copy-done
  181.6 2.2 copy-done.2
  183.8 4.2 %project.1 = f32[4,256,128]{2,1,0:T(8,128)} custom-call(s32[2]{0:T(128)S(1)} %copy-done.3, f32[128,8192]{1,0:T(8,128)S(1)} %copy-done, f32[64,2048]{1,0:T(8,128)S(1)} %collective-permute-done.1.first, f32[64,2048]{1,0:T(8,128)S(1)} %collective-permute-done.2.second, f32[64,2048]{1,0:T(8,128)S(1)} %collective-permute-done.3.third, f32[8,512,256]{2,1,0:T(8,128)S(1)} %bitcast.70), custom_call_target="tpu_custom_call" | custom-call | flops 1610612736 | bytes 7340032 | tf_op jit(solution)/shard_map/project/pallas_call | solution.py:99
  188.0 3.7 %all-to-all-start.2 = ((f32[4,256,128]{2,1,0:T(8,128)}), f32[4,256,128]{2,1,0:T(8,128)S(1)}, u32[]{:S(2)}, u32[]{:S(2)}) async-start(f32[4,256,128]{2,1,0:T(8,128)} %project.1), calls=%async_computation.2 | async-start | bytes 1048576 | tf_op jit(solution)/shard_map/all_to_all | solution.py:296
  192.2 8.9 %all-to-all-done.2.partial = f32[4,256,128]{2,1,0:T(8,128)S(1)} async-done(((f32[4,256,128]{2,1,0:T(8,128)}), f32[4,256,128]{2,1,0:T(8,128)S(1)}, u32[]{:S(2)}, u32[]{:S(2)}) %all-to-all-start.2) | async-done | bytes 524320 | tf_op jit(solution)/shard_map/all_to_all | solution.py:296
  201.1 6.1 %attend.1 = f32[8,256,128]{2,1,0:T(8,128)S(1)} custom-call(f32[4,256,128]{2,1,0:T(8,128)S(1)} %all-to-all-done.2.partial, f32[4,4096]{1,0:T(4,128)S(1)} %broadcast_in_dim.38.low, f32[4,4096]{1,0:T(4,128)S(1)} %broadcast_in_dim.40.up, f32[8,2,64,128]{3,2,1,0:T(8,128)S(1)} %all-to-all-done.refs_0_, f32[8,2,64,128]{3,2,1,0:T(8,128)} %collective-permute-done.7.refs_1_, ...), custom_call_target="tpu_custom_call" | custom-call | flops 1610612736 | bytes 6291456 | tf_op jit(solution)/shard_map/attend/pallas_call | solution.py:161
  207.2 29.7 %all_to_all.31.heads = f32[8,256,128]{2,1,0:T(8,128)S(1)} all-to-all(f32[8,256,128]{2,1,0:T(8,128)S(1)} %attend.1), channel_id=1, replica_groups=mesh['x'=4,'y'=4,'z'=8,'k'=2] {'z'}, dimensions={0} | all-to-all | bytes 2097152 | tf_op jit(solution)/shard_map/all_to_all | solution.py:307
  236.9 2.2 copy-done.1
  239.1 2.5 mix.1
  241.6 20.1 %all_to_all.32 = f32[8,64,512]{2,1,0:T(8,128)S(1)} all-to-all(f32[8,64,512]{2,1,0:T(8,128)S(1)} %mix.1), channel_id=1, replica_groups=mesh['x'=4,'y'=4,'z'=8,'k'=2] {'x','k'}, dimensions={0} | all-to-all | bytes 2097152 | tf_op jit(solution)/shard_map/all_to_all | solution.py:309
  (68 shorter events, 17.5 us)
Async XLA Ops:
  6.5 65.9 %copy-start.4 = (f32[256,512]{1,0:T(8,128)S(1)}, f32[256,512]{1,0:T(8,128)}, u32[]{:S(2)}) copy-start(f32[256,512]{1,0:T(8,128)} %param.17) | copy-start | bytes 1572868
  6.5 172.8 %all-gather.5.cloned.1.call-start = ((), (), s32[]{:S(2)}) async-start(), calls=%async_computation.6 | async-start | bytes 4718592 | tf_op jit(solution)/shard_map/all_gather | solution.py:255
  57.4 74.6 %copy-start.7 = (s32[32]{0:T(128)S(1)}, s32[32]{0:T(128)}, u32[]{:S(2)}) copy-start(s32[32]{0:T(128)} %param.14) | copy-start | bytes 388
  57.4 75.3 %copy-start.8 = (s32[32]{0:T(128)S(1)}, s32[32]{0:T(128)}, u32[]{:S(2)}) copy-start(s32[32]{0:T(128)} %param.16) | copy-start | bytes 388
  57.4 76.1 %copy-start.5 = (s32[32,16]{0,1:T(8,128)S(1)}, s32[32,16]{0,1:T(8,128)}, u32[]{:S(2)}) copy-start(s32[32,16]{0,1:T(8,128)} %param.15) | copy-start | bytes 6148
  57.4 76.0 %copy-start.6 = (s32[32,16]{0,1:T(8,128)S(1)}, s32[32,16]{0,1:T(8,128)}, u32[]{:S(2)}) copy-start(s32[32,16]{0,1:T(8,128)} %param.13) | copy-start | bytes 6148
  57.4 122.0 %copy-start.3 = (s32[2]{0:T(128)S(1)}, s32[2]{0:T(128)}, u32[]{:S(2)}) copy-start(s32[2]{0:T(128)} %pad_add_fusion.where) | copy-start | bytes 28
  63.4 27.0 %all-to-all-start = ((f32[8,2,64,128]{3,2,1,0:T(8,128)}), f32[8,2,64,128]{3,2,1,0:T(8,128)S(1)}, u32[]{:S(2)}, u32[]{:S(2)}) async-start(f32[8,2,64,128]{3,2,1,0:T(8,128)} %fusion.1), calls=%async_computation | async-start | bytes 1048576 | tf_op jit(solution)/shard_map/all_to_all | solution.py:272
  72.4 5.9 %collective-permute-start = (f32[2,4,16,512]{3,2,1,0:T(8,128)S(1)}, f32[2,4,16,512]{3,2,1,0:T(8,128)S(1)}, u32[]{:S(2)}, u32[]{:S(2)}) collective-permute-start(f32[2,4,16,512]{3,2,1,0:T(8,128)S(1)} %get-tuple-element.46), channel_id=1, source_target_pairs={{0,1},{1,0},{2,3},{3,2},{4,5},{5,4},{6,7},{7,6},{8,9},{9,8},{10,11... | collective-permute-start | bytes 786440 | tf_op jit(solution)/shard_map/ppermute | solution.py:287
  73.5 23.7 %collective-permute-start.1 = (f32[64,2048]{1,0:T(8,128)}, f32[64,2048]{1,0:T(8,128)S(1)}, u32[]{:S(2)}, u32[]{:S(2)}) collective-permute-start(f32[64,2048]{1,0:T(8,128)} %get-tuple-element.20), channel_id=1, source_target_pairs={{0,64},{64,128},{128,192},{192,0},{1,65},{65,129},{129,193},{193,1... | collective-permute-start | bytes 1572872 | tf_op jit(solution)/shard_map/ppermute | solution.py:258
  74.7 25.9 %collective-permute-start.2 = (f32[64,2048]{1,0:T(8,128)}, f32[64,2048]{1,0:T(8,128)S(1)}, u32[]{:S(2)}, u32[]{:S(2)}) collective-permute-start(f32[64,2048]{1,0:T(8,128)} %get-tuple-element.23), channel_id=1, source_target_pairs={{0,128},{64,192},{128,0},{192,64},{1,129},{65,193},{129,1},{193,65... | collective-permute-start | bytes 1572872 | tf_op jit(solution)/shard_map/ppermute | solution.py:258
  77.2 23.5 %collective-permute-start.3 = (f32[64,2048]{1,0:T(8,128)}, f32[64,2048]{1,0:T(8,128)S(1)}, u32[]{:S(2)}, u32[]{:S(2)}) collective-permute-start(f32[64,2048]{1,0:T(8,128)} %get-tuple-element.24), channel_id=1, source_target_pairs={{0,192},{64,0},{128,64},{192,128},{1,193},{65,1},{129,65},{193,129... | collective-permute-start | bytes 1572872 | tf_op jit(solution)/shard_map/ppermute | solution.py:258
  90.3 17.8 %all-to-all-start.1 = ((f32[16,16,512]{2,1,0:T(8,128)}), f32[16,16,512]{2,1,0:T(8,128)S(1)}, u32[]{:S(2)}, u32[]{:S(2)}) async-start(f32[16,16,512]{2,1,0:T(8,128)} %bitcast.18), calls=%async_computation.1 | async-start | bytes 1048576 | tf_op jit(solution)/shard_map/all_to_all | solution.py:290
  97.1 139.8 %all-gather.7.cloned.1.call-start = ((), (), s32[]{:S(2)}) async-start(), calls=%async_computation.7 | async-start | bytes 4718592 | tf_op jit(solution)/shard_map/all_gather | solution.py:293
  134.4 16.1 %collective-permute-start.4 = (f32[8,2,64,128]{3,2,1,0:T(8,128)S(1)}, f32[8,2,64,128]{3,2,1,0:T(8,128)S(1)}, u32[]{:S(2)}, u32[]{:S(2)}) collective-permute-start(f32[8,2,64,128]{3,2,1,0:T(8,128)S(1)} %all-to-all-done.refs_0_), channel_id=1, source_target_pairs={{0,16},{16,32},{32,48},{48,0},{1,17},{17,33},{33,49},{49,1},{2,18}... | collective-permute-start | bytes 1572872 | tf_op jit(solution)/shard_map/ppermute | solution.py:278
  134.9 33.5 %collective-permute-start.5 = (f32[8,2,64,128]{3,2,1,0:T(8,128)S(1)}, f32[8,2,64,128]{3,2,1,0:T(8,128)S(1)}, u32[]{:S(2)}, u32[]{:S(2)}) collective-permute-start(f32[8,2,64,128]{3,2,1,0:T(8,128)S(1)} %all-to-all-done.refs_0_), channel_id=1, source_target_pairs={{0,32},{16,48},{32,0},{48,16},{1,33},{17,49},{33,1},{49,17},{2,34}... | collective-permute-start | bytes 1572872 | tf_op jit(solution)/shard_map/ppermute | solution.py:278
  135.1 37.2 %collective-permute-start.6 = (f32[8,2,64,128]{3,2,1,0:T(8,128)S(1)}, f32[8,2,64,128]{3,2,1,0:T(8,128)}, u32[]{:S(2)}, u32[]{:S(2)}) collective-permute-start(f32[8,2,64,128]{3,2,1,0:T(8,128)S(1)} %all-to-all-done.refs_0_), channel_id=1, source_target_pairs={{0,48},{16,0},{32,16},{48,32},{1,49},{17,1},{33,17},{49,33},{2,50}... | collective-permute-start | bytes 1572872 | tf_op jit(solution)/shard_map/ppermute | solution.py:278
  138.3 53.9 %collective-permute-start.7 = (f32[8,2,64,128]{3,2,1,0:T(8,128)S(1)}, f32[8,2,64,128]{3,2,1,0:T(8,128)}, u32[]{:S(2)}, u32[]{:S(2)}) collective-permute-start(f32[8,2,64,128]{3,2,1,0:T(8,128)S(1)} %all-to-all-done.refs_0_), channel_id=1, source_target_pairs={{0,1},{1,0},{2,3},{3,2},{4,5},{5,4},{6,7},{7,6},{8,9},{9,8},{10,11... | collective-permute-start | bytes 1572872 | tf_op jit(solution)/shard_map/ppermute | solution.py:279
  172.3 19.9 %collective-permute-start.8 = (f32[8,2,64,128]{3,2,1,0:T(8,128)S(1)}, f32[8,2,64,128]{3,2,1,0:T(8,128)}, u32[]{:S(2)}, u32[]{:S(2)}) collective-permute-start(f32[8,2,64,128]{3,2,1,0:T(8,128)S(1)} %collective-permute-done.4.refs_2_), channel_id=1, source_target_pairs={{0,1},{1,0},{2,3},{3,2},{4,5},{5,4},{6,7},{7,6},{8,9},{9,8},{10,11... | collective-permute-start | bytes 1572872 | tf_op jit(solution)/shard_map/ppermute | solution.py:279
  178.9 13.3 %collective-permute-start.9 = (f32[8,2,64,128]{3,2,1,0:T(8,128)S(1)}, f32[8,2,64,128]{3,2,1,0:T(8,128)}, u32[]{:S(2)}, u32[]{:S(2)}) collective-permute-start(f32[8,2,64,128]{3,2,1,0:T(8,128)S(1)} %collective-permute-done.5.refs_4_), channel_id=1, source_target_pairs={{0,1},{1,0},{2,3},{3,2},{4,5},{5,4},{6,7},{7,6},{8,9},{9,8},{10,11... | collective-permute-start | bytes 1572872 | tf_op jit(solution)/shard_map/ppermute | solution.py:279
  178.9 13.3 %collective-permute-start.10 = (f32[8,2,64,128]{3,2,1,0:T(8,128)}, f32[8,2,64,128]{3,2,1,0:T(8,128)}, u32[]{:S(2)}, u32[]{:S(2)}) collective-permute-start(f32[8,2,64,128]{3,2,1,0:T(8,128)} %collective-permute-done.6.refs_6_), channel_id=1, source_target_pairs={{0,1},{1,0},{2,3},{3,2},{4,5},{5,4},{6,7},{7,6},{8,9},{9,8},{10,11... | collective-permute-start | bytes 1572872 | tf_op jit(solution)/shard_map/ppermute | solution.py:279
  179.4 2.2 copy-start
  188.0 13.1 %all-to-all-start.2 = ((f32[4,256,128]{2,1,0:T(8,128)}), f32[4,256,128]{2,1,0:T(8,128)S(1)}, u32[]{:S(2)}, u32[]{:S(2)}) async-start(f32[4,256,128]{2,1,0:T(8,128)} %project.1), calls=%async_computation.2 | async-start | bytes 1048576 | tf_op jit(solution)/shard_map/all_to_all | solution.py:296
  236.9 2.2 copy-start.1
  (1 other events, 2.2 us)
Sparse Core Ops, SparseCore 0:
  9.2 38.8 all-gather.4
  132.0 47.4 all-gather.6

commit v5 on v4

--- a/solution.py
+++ b/solution.py
@@ -16,7 +16,7 @@
 VMEM = pl.BlockSpec(memory_space=pltpu.VMEM)
 SMEM = pl.BlockSpec(memory_space=pltpu.SMEM)
 ANY = pl.BlockSpec(memory_space=pl.ANY)
-HBM = pl.BlockSpec(memory_space=pltpu.HBM)
+LIMIT = 60 << 20
 
 
 def split(value):
@@ -42,7 +42,7 @@
     copies = []
     for shift in range(1, NX):
         cols = pl.multiple_of(lax.rem(where[0] + shift, NX) * 2048, 2048)
-        part = rows.at[pl.ds(pl.multiple_of(where[1] * BLOCK, BLOCK), BLOCK), pl.ds(cols, 2048)]
+        part = rows.at[pl.ds(pl.multiple_of(where[2] * BLOCK, BLOCK), BLOCK), pl.ds(cols, 2048)]
         copies.append(pltpu.make_async_copy(part, outs[shift - 1], sem.at[shift - 1]))
     for copy in copies:
         copy.start()
@@ -54,72 +54,83 @@
     return pl.pallas_call(
         pick_kernel,
         out_shape=[jax.ShapeDtypeStruct((BLOCK, 2048), jnp.float32)] * 3,
-        in_specs=[SMEM, HBM],
-        out_specs=[HBM] * 3,
+        in_specs=[SMEM, ANY],
+        out_specs=[VMEM] * 3,
         scratch_shapes=[pltpu.SemaphoreType.DMA((3,))],
+        compiler_params=pltpu.CompilerParams(vmem_limit_bytes=LIMIT),
         name="pick",
     )(where, hidden_rows)
 
 
-def project_kernel(where, rows, first, second, third, weights, out, left_buf, right_buf, sems):
-    x, k = where[0], where[1]
+def project_kernel(where, rows, *refs):
+    moved, weights, outs = refs[:3], refs[3:11], refs[11:15]
+    left_buf, right_buf, total_buf, sems = refs[15:]
+    x, y, k = where[0], where[1], where[2]
     copies = []
-    for y in range(NY):
+    for turn in range(NY):
+        slab = lax.rem(y + NY - turn, NY)
+        cols = pl.multiple_of(slab * 512, 512)
         own = rows.at[
             pl.ds(pl.multiple_of(k * BLOCK, BLOCK), BLOCK),
-            pl.ds(pl.multiple_of(x * 2048 + y * 512, 512), 512),
+            pl.ds(pl.multiple_of(x * 2048 + slab * 512, 512), 512),
         ]
-        parts = [own] + [part.at[:, pl.ds(y * 512, 512)] for part in (first, second, third)]
+        parts = [own] + [part.at[:, pl.ds(cols, 512)] for part in moved]
         group = [
             pltpu.make_async_copy(
-                part, left_buf.at[y, lax.rem(x + NX - shift, NX)], sems.at[y, shift]
+                part, left_buf.at[turn, lax.rem(x + NX - shift, NX)], sems.at[turn, shift]
             )
             for shift, part in enumerate(parts)
         ]
-        group.append(
-            pltpu.make_async_copy(weights.at[pl.ds(2 * y, 2)], right_buf.at[y], sems.at[y, NX])
-        )
+        group += [
+            pltpu.make_async_copy(
+                weights[2 * turn + other], right_buf.at[turn, other], sems.at[turn, NX + other]
+            )
+            for other in range(NK)
+        ]
         for copy in group:
             copy.start()
         copies.append(group)
     totals = [None, None]
-    for y in range(NY):
-        for copy in copies[y]:
+    for turn in range(NY):
+        for copy in copies[turn]:
             copy.wait()
-        left = split(left_buf[y].reshape(NX * BLOCK, 512))
-        for core in range(NK):
-            term = dot3(left, split(right_buf[y, core]), MM)
-            totals[core] = term if totals[core] is None else totals[core] + term
-    for core in range(NK):
+        left = split(left_buf[turn].reshape(NX * BLOCK, 512))
+        for other in range(NK):
+            term = dot3(left, split(right_buf[turn, other]), MM)
+            totals[other] = term if totals[other] is None else totals[other] + term
+    for other in range(NK):
+        core = k if other == 0 else 1 - k
         for b in range(2):
-            out[2 * core + b] = totals[core][:, b * HD : (b + 1) * HD]
+            total_buf[2 * core + b] = totals[other][:, b * HD : (b + 1) * HD]
+    for shift in range(NX):
+        outs[shift][...] = total_buf[lax.rem(x + shift, NX)]
 
 
 def project(where, rows, moved, weights):
     return pl.pallas_call(
         project_kernel,
-        out_shape=jax.ShapeDtypeStruct((NX, NX * BLOCK, HD), jnp.float32),
-        in_specs=[SMEM, HBM, ANY, ANY, ANY, HBM],
-        out_specs=VMEM,
+        out_shape=[jax.ShapeDtypeStruct((NX * BLOCK, HD), jnp.float32)] * NX,
+        in_specs=[SMEM] + [ANY] * 12,
+        out_specs=[VMEM] * NX,
         scratch_shapes=[
             pltpu.VMEM((NY, NX, BLOCK, 512), jnp.float32),
             pltpu.VMEM((NY, NK, 512, 256), jnp.float32),
-            pltpu.SemaphoreType.DMA((NY, NX + 1)),
+            pltpu.VMEM((NX, NX * BLOCK, HD), jnp.float32),
+            pltpu.SemaphoreType.DMA((NY, NX + NK)),
         ],
-        compiler_params=pltpu.CompilerParams(vmem_limit_bytes=32 << 20),
+        compiler_params=pltpu.CompilerParams(vmem_limit_bytes=LIMIT),
         cost_estimate=pl.CostEstimate(
             flops=6 * 256 * 2048 * 512, bytes_accessed=7 << 20, transcendentals=0
         ),
         name="project",
-    )(where, rows, *moved, weights)
-
-
-def attend_kernel(partial, low, up, *refs):
-    pieces, (out, kv, scores, sem) = refs[:8], refs[8:]
-    tiles = len(pieces)
+    )(where, rows, *moved, *weights)
+
+
+def attend_kernel(first, second, third, fourth, low, up, gathered, out, kv, scores, sem):
+    tiles = gathered.shape[0]
     copies = [
-        pltpu.make_async_copy(piece, kv.at[tile], sem.at[tile])
-        for tile, piece in enumerate(pieces)
+        pltpu.make_async_copy(gathered.at[tile], kv.at[tile], sem.at[tile])
+        for tile in range(tiles)
     ]
     for copy in copies:
         copy.start()
@@ -127,7 +138,7 @@
     row = lax.broadcasted_iota(jnp.int32, (BLOCK, width), 0)
     col = lax.broadcasted_iota(jnp.int32, (BLOCK, width), 1)
     lower = row >= lax.rem(col, BLOCK)
-    query = (partial[0] + partial[1]) + (partial[2] + partial[3])
+    query = (first[...] + second[...]) + (third[...] + fourth[...])
     left = split(query * (math.log2(math.e) / math.sqrt(HD)))
     top = None
     for tile in range(tiles):
@@ -156,24 +167,24 @@
         out[z] = attended
 
 
-def attend(partial, low, up, pieces):
+def attend(partial, low, up, gathered):
     rows = NX * BLOCK
     return pl.pallas_call(
         attend_kernel,
         out_shape=jax.ShapeDtypeStruct((NZ, rows, HD), jnp.float32),
-        in_specs=[VMEM] * 3 + [ANY] * 8,
+        in_specs=[VMEM] * 6 + [ANY],
         out_specs=VMEM,
         scratch_shapes=[
             pltpu.VMEM((8, NZ, 2, BLOCK, HD), jnp.float32),
             pltpu.VMEM((8, rows, NZ * BLOCK), jnp.float32),
             pltpu.SemaphoreType.DMA((8,)),
         ],
-        compiler_params=pltpu.CompilerParams(vmem_limit_bytes=48 << 20),
+        compiler_params=pltpu.CompilerParams(vmem_limit_bytes=LIMIT),
         cost_estimate=pl.CostEstimate(
             flops=12 * 256 * 4096 * HD, bytes_accessed=6 << 20, transcendentals=256 * 4096
         ),
         name="attend",
-    )(partial, low, up, *pieces)
+    )(*partial, low, up, gathered)
 
 
 def mix_kernel(heads, weights, out, buf, sem):
@@ -205,13 +216,13 @@
     return pl.pallas_call(
         mix_kernel,
         out_shape=jax.ShapeDtypeStruct((NX * NK, BLOCK, 512), jnp.float32),
-        in_specs=[VMEM, HBM],
+        in_specs=[VMEM, ANY],
         out_specs=VMEM,
         scratch_shapes=[
             pltpu.VMEM((NZ // 2, 8, 2, NK, 16, 512), jnp.float32),
             pltpu.SemaphoreType.DMA((NZ // 2,)),
         ],
-        compiler_params=pltpu.CompilerParams(vmem_limit_bytes=32 << 20),
+        compiler_params=pltpu.CompilerParams(vmem_limit_bytes=LIMIT),
         cost_estimate=pl.CostEstimate(
             flops=6 * 256 * 1024 * 1024, bytes_accessed=6 << 20, transcendentals=0
         ),
@@ -239,6 +250,11 @@
 CORES = [(0, 1), (1, 0)]
 
 
+def along(axis, value, shift):
+    count = lax.axis_size(axis)
+    return lax.ppermute(value, axis, [(i, (i + shift) % count) for i in range(count)])
+
+
 def shards(
     hidden_rows,
     query_weight,
@@ -251,13 +267,13 @@
     output_weight,
 ):
     x, y, z, k = (lax.axis_index(name) for name in ALL)
-    where = jnp.stack([x, k]).astype(jnp.int32)
-    weights = lax.all_gather(query_weight, ("y", "k"), axis=0)
+    where = jnp.stack([x, y, k]).astype(jnp.int32)
     picked = pick(where, hidden_rows)
-    hidden = [
-        lax.ppermute(part, "x", [(i, (i + shift) % NX) for i in range(NX)])
-        for shift, part in zip(range(1, NX), picked)
-    ]
+    hidden = [along("x", part, shift) for shift, part in enumerate(picked, 1)]
+    weights = []
+    for shift in range(NY):
+        piece = along("y", query_weight, shift) if shift else query_weight
+        weights += [piece, lax.ppermute(piece, "k", CORES)]
     quarters = [
         lax.dynamic_slice_in_dim(cache, y * BLOCK, BLOCK, 0)
         for cache in (key_cache, value_cache)
@@ -268,19 +284,8 @@
             for to in range(NZ)
         ]
     )
-    sent, _ = lax.optimization_barrier((sent, picked[0]))
     near = lax.all_to_all(sent, "z", 0, 0)
-    pieces = []
-    key_block = []
-    for shift in range(NY):
-        piece = near
-        if shift:
-            piece = lax.ppermute(near, "y", [(i, (i + shift) % NY) for i in range(NY)])
-        pieces += [piece, lax.ppermute(piece, "k", CORES)]
-        for core in (k, 1 - k):
-            key_block.append(
-                4 * (2 * jnp.arange(NZ, dtype=jnp.int32) + core) + (y - shift) % NY
-            )
+    kv = lax.all_gather(near, ("y", "k"), axis=0)
     rows = output_weight.reshape(2, NY, NK, 16, 512)
     kept = lax.dynamic_index_in_dim(rows, k, 2, keepdims=False)
     given = lax.dynamic_index_in_dim(rows, 1 - k, 2, keepdims=False)
@@ -288,22 +293,24 @@
     rows = jnp.where(k == 0, jnp.stack([kept, taken]), jnp.stack([taken, kept]))
     rows, near = lax.optimization_barrier((rows, near))
     rows = lax.all_to_all(rows.reshape(NX * NY, 16, 512), ("x", "y"), 0, 0)
-    rows, hidden = lax.optimization_barrier((rows, hidden))
+    rows, hidden, weights = lax.optimization_barrier((rows, hidden, weights))
     rows = lax.all_to_all(rows.reshape(NZ, NK, 16, 512), "z", 0, 0)
     out_weight = lax.all_gather(rows, ("y", "k"), axis=0)
-    hidden, pieces[2::2] = lax.optimization_barrier((hidden, pieces[2::2]))
     partial = project(where, hidden_rows, hidden, weights)
-    partial = lax.all_to_all(partial, "x", 0, 0)
+    partial = [partial[0]] + [along("x", partial[s], s) for s in range(1, NX)]
+    key_block = jnp.arange(NY, dtype=jnp.int32)[:, None, None]
+    key_block = key_block + 4 * jnp.arange(NK, dtype=jnp.int32)[None, :, None]
+    key_block = key_block + 8 * jnp.arange(NZ, dtype=jnp.int32)[None, None, :]
     low, up = allowed_rows(
         4 * z + x,
-        jnp.concatenate(key_block),
+        key_block.reshape(-1),
         32 + 8 * jnp.arange(NX, dtype=jnp.int32) + 2 * y + k,
         vertical_blocks,
         vertical_count,
         slash_offsets,
         slash_count,
     )
-    heads = attend(partial, low, up, pieces)
+    heads = attend(partial, low, up, kv)
     heads = lax.all_to_all(heads, "z", 0, 0)
     mixed = mix(heads, out_weight)
     mixed = lax.all_to_all(mixed, ("x", "k"), 0, 0)

time: 270 us -> 214 us (0.79)
  Pallas kernels: 62.3 us -> 22.7 us
  starting transfers between devices: 38.7 us -> 29.3 us
  blocking collectives: 73.6 us -> 65.7 us
  waiting for transfers between devices: 62.5 us -> 69.7 us
  other arithmetic: 9.27 us -> 4.26 us
    pallas_call x1, Pallas kernels: 49.4 us -> 3.23 us  [pick(): pl.pallas_call(pick_kernel, out_shape=[jax.ShapeDtypeStruct((BLOCK, 2048)...]
    all_to_all x2 -> x1, starting transfers between devices: 12.7 us -> 3.65 us  [shards(): heads = lax.all_to_all(heads, 'z', 0, 0)]
    all_to_all x1, blocking collectives: 23.7 us -> 17.6 us  [shards(): rows = lax.all_to_all(rows.reshape(NZ, NK, 16, 512), 'z', 0, 0)]
    unnamed x18 -> x26, local copies, waits for them, and re-layouts: 6.6 us -> 1.71 us
    all_to_all x1, blocking collectives: 29.7 us -> 24.9 us  [shards(): near = lax.all_to_all(sent, 'z', 0, 0)]
    unnamed x7, other arithmetic: 4.4 us -> 0.05 us
    all_to_all x1, blocking collectives: 20.1 us -> 23.2 us  [shards(): mixed = lax.all_to_all(mixed, ('x', 'k'), 0, 0)]
    pallas_call x1, Pallas kernels: 2.47 us -> 5.54 us  [mix(): pl.pallas_call(mix_kernel, out_shape=jax.ShapeDtypeStruct((NX * NK, BLOCK...]
  transfers between devices with their start and end apart: 16 -> 18, of which waited for: 7 -> 10; matrix products, arithmetic and copies ran while one was open for 4% -> 4% of each run, Pallas kernels for 22% -> 8%
where the time goes in v5:
time: 214 us; the launch traced here: 212 us
  waiting for transfers between devices  69.7 us (33%)
  blocking collectives  65.7 us (31%)
  starting transfers between devices  29.3 us (14%)
  Pallas kernels  22.7 us (11%)
  between operations  13.7 us (6%)
  local copies, waits for them, and re-layouts  6.8 us (3%)
  other arithmetic  4.26 us (2%)
    ppermute x9, waiting for transfers between devices, along(): lax.ppermute(value, axis, [(i, (i + shift) % count) for i in range(count)])  34.5 us
    all_to_all x1, blocking collectives, shards(): near = lax.all_to_all(sent, 'z', 0, 0)  24.9 us
    all_to_all x1, blocking collectives, shards(): mixed = lax.all_to_all(mixed, ('x', 'k'), 0, 0)  23.2 us
    all_to_all x1, waiting for transfers between devices, shards(): heads = lax.all_to_all(heads, 'z', 0, 0)  22.2 us
    all_to_all x1, blocking collectives, shards(): rows = lax.all_to_all(rows.reshape(NZ, NK, 16, 512), 'z', 0, 0)  17.6 us
    ppermute x9, starting transfers between devices, along(): lax.ppermute(value, axis, [(i, (i + shift) % count) for i in range(count)])  12 us
    all_to_all x1, waiting for transfers between devices, shards(): rows = lax.all_to_all(rows.reshape(NX * NY, 16, 512), ('x', 'y'), 0, 0)  10 us
    pallas_call x1, Pallas kernels, attend(): pl.pallas_call(attend_kernel, out_shape=jax.ShapeDtypeStruct((NZ, rows, H...  8.68 us
  transfers between devices with their start and end apart: 18, of which 10 were waited for; matrix products, arithmetic and copies ran while one was open for 4% of the time, Pallas kernels for 8%

profile of v5, /device:TPU:1, one launch (start us, length us, event | category | flops | bytes accessed | tf_op | source)
XLA Modules:
  0.0 212.2 jit_solution(6777516395786377327)
XLA Ops:
  7.6 24.9 %all_to_all.25 = f32[8,2,64,128]{3,2,1,0:T(8,128)} all-to-all(f32[8,2,64,128]{3,2,1,0:T(8,128)S(1)} %fusion.1), channel_id=1, replica_groups=mesh['x'=4,'y'=4,'z'=8,'k'=2] {'z'}, dimensions={0} | all-to-all | bytes 1048576 | tf_op jit(solution)/shard_map/all_to_all | solution.py:287
  33.7 2.5 %collective-permute-start = (f32[2,4,16,512]{3,2,1,0:T(8,128)S(1)}, f32[2,4,16,512]{3,2,1,0:T(8,128)S(1)}, u32[]{:S(2)}, u32[]{:S(2)}) collective-permute-start(f32[2,4,16,512]{3,2,1,0:T(8,128)S(1)} %get-tuple-element.56), channel_id=1, source_target_pairs={{0,1},{1,0},{2,3},{3,2},{4,5},{5,4},{6,7},{7,6},{8,9},{9,8},{10,11... | collective-permute-start | bytes 786440 | tf_op jit(solution)/shard_map/ppermute | solution.py:292
  36.8 3.2 %pick.1 = (f32[64,2048]{1,0:T(8,128)}, f32[64,2048]{1,0:T(8,128)}, f32[64,2048]{1,0:T(8,128)}) custom-call(s32[3]{0:T(128)} %pad_add_fusion.where, f32[128,8192]{1,0:T(8,128)} %rows.3), custom_call_target="tpu_custom_call" | custom-call | tf_op jit(solution)/shard_map/pick/pallas_call | solution.py:54
  41.4 2.5 %collective-permute-start.2 = (f32[64,2048]{1,0:T(8,128)}, f32[64,2048]{1,0:T(8,128)S(1)}, u32[]{:S(2)}, u32[]{:S(2)}) collective-permute-start(f32[64,2048]{1,0:T(8,128)} %get-tuple-element.27), channel_id=1, source_target_pairs={{0,128},{64,192},{128,0},{192,64},{1,129},{65,193},{129,1},{193,65... | collective-permute-start | bytes 1572872 | tf_op jit(solution)/shard_map/ppermute | solution.py:255
  43.8 2.7 %collective-permute-start.9 = (f32[512,256]{1,0:T(8,128)S(1)}, f32[512,256]{1,0:T(8,128)S(1)}, u32[]{:S(2)}, u32[]{:S(2)}) collective-permute-start(f32[512,256]{1,0:T(8,128)S(1)} %copy-done.1), channel_id=1, source_target_pairs={{0,48},{16,0},{32,16},{48,32},{1,49},{17,1},{33,17},{49,33},{2,50}... | collective-permute-start | bytes 1572872 | tf_op jit(solution)/shard_map/ppermute | solution.py:255
  46.6 1.6 collective-permute-start.7
  48.2 7.0 %collective-permute-done.1.refs_0_ = f32[64,2048]{1,0:T(8,128)S(1)} collective-permute-done((f32[64,2048]{1,0:T(8,128)}, f32[64,2048]{1,0:T(8,128)S(1)}, u32[]{:S(2)}, u32[]{:S(2)}) %collective-permute-start.1) | collective-permute-done | bytes 524320 | tf_op jit(solution)/shard_map/ppermute | solution.py:255
  55.9 11.4 %collective-permute-done.2.refs_1_ = f32[64,2048]{1,0:T(8,128)S(1)} collective-permute-done((f32[64,2048]{1,0:T(8,128)}, f32[64,2048]{1,0:T(8,128)S(1)}, u32[]{:S(2)}, u32[]{:S(2)}) %collective-permute-start.2) | collective-permute-done | bytes 524320 | tf_op jit(solution)/shard_map/ppermute | solution.py:255
  67.3 1.7 collective-permute-done.9.refs_9_
  69.1 2.8 %collective-permute-start.10 = (f32[512,256]{1,0:T(8,128)S(1)}, f32[512,256]{1,0:T(8,128)}, u32[]{:S(2)}, u32[]{:S(2)}) collective-permute-start(f32[512,256]{1,0:T(8,128)S(1)} %collective-permute-done.9.refs_9_), channel_id=1, source_target_pairs={{0,1},{1,0},{2,3},{3,2},{4,5},{5,4},{6,7},{7,6},{8,9},{9,8},{10,11... | collective-permute-start | bytes 1572872 | tf_op jit(solution)/shard_map/ppermute | solution.py:276
  72.9 2.7 %collective-permute-start.6 = (f32[512,256]{1,0:T(8,128)S(1)}, f32[512,256]{1,0:T(8,128)}, u32[]{:S(2)}, u32[]{:S(2)}) collective-permute-start(f32[512,256]{1,0:T(8,128)S(1)} %collective-permute-done.5.refs_5_), channel_id=1, source_target_pairs={{0,1},{1,0},{2,3},{3,2},{4,5},{5,4},{6,7},{7,6},{8,9},{9,8},{10,11... | collective-permute-start | bytes 1572872 | tf_op jit(solution)/shard_map/ppermute | solution.py:276
  75.7 10.9 %collective-permute-done.7.refs_7_ = f32[512,256]{1,0:T(8,128)} collective-permute-done((f32[512,256]{1,0:T(8,128)S(1)}, f32[512,256]{1,0:T(8,128)}, u32[]{:S(2)}, u32[]{:S(2)}) %collective-permute-start.7) | collective-permute-done | bytes 524320 | tf_op jit(solution)/shard_map/ppermute | solution.py:255
  88.2 4.0 %all-to-all-start.1 = ((f32[16,16,512]{2,1,0:T(8,128)}), f32[16,16,512]{2,1,0:T(8,128)S(1)}, u32[]{:S(2)}, u32[]{:S(2)}) async-start(f32[16,16,512]{2,1,0:T(8,128)} %bitcast.19), calls=%async_computation.1 | async-start | bytes 1048576 | tf_op jit(solution)/shard_map/all_to_all | solution.py:295
  92.4 10.0 %all-to-all-done.1 = f32[16,16,512]{2,1,0:T(8,128)S(1)} async-done(((f32[16,16,512]{2,1,0:T(8,128)}), f32[16,16,512]{2,1,0:T(8,128)S(1)}, u32[]{:S(2)}, u32[]{:S(2)}) %all-to-all-start.1) | async-done | bytes 524320 | tf_op jit(solution)/shard_map/all_to_all | solution.py:295
  102.4 17.6 %all_to_all.26 = f32[8,2,16,512]{3,2,1,0:T(8,128)} all-to-all(f32[8,2,16,512]{3,2,1,0:T(8,128)S(1)} %bitcast.72), channel_id=1, replica_groups=mesh['x'=4,'y'=4,'z'=8,'k'=2] {'z'}, dimensions={0} | all-to-all | bytes 1048576 | tf_op jit(solution)/shard_map/all_to_all | solution.py:297
  123.4 5.2 %project.1 = (f32[256,128]{1,0:T(8,128)}, f32[256,128]{1,0:T(8,128)}, f32[256,128]{1,0:T(8,128)}, f32[256,128]{1,0:T(8,128)}) custom-call(s32[3]{0:T(128)} %pad_add_fusion.where, f32[128,8192]{1,0:T(8,128)} %rows.3, f32[64,2048]{1,0:T(8,128)} %copy-done.2, f32[64,2048]{1,0:T(8,128)} %copy-done.3, f32[64,2048]{1,0:T(8,128)} %collective-permute-done.3.refs_2_, ...), custom_call_target="tpu_custom_call" | custom-call | flops 1610612736 | bytes 7340032 | tf_op jit(solution)/shard_map/project/pallas_call | solution.py:110
  129.8 2.4 %collective-permute-start.12 = (f32[256,128]{1,0:T(8,128)}, f32[256,128]{1,0:T(8,128)S(1)}, u32[]{:S(2)}, u32[]{:S(2)}) collective-permute-start(f32[256,128]{1,0:T(8,128)} %get-tuple-element.42), channel_id=1, source_target_pairs={{0,128},{64,192},{128,0},{192,64},{1,129},{65,193},{129,1},{193,65... | collective-permute-start | bytes 393224 | tf_op jit(solution)/shard_map/ppermute | solution.py:255
  134.2 2.0 collective-permute-done.12.third
  137.3 8.7 %attend.1 = f32[8,256,128]{2,1,0:T(8,128)} custom-call(f32[256,128]{1,0:T(8,128)} %get-tuple-element.40.first, f32[256,128]{1,0:T(8,128)} %copy-done.8, f32[256,128]{1,0:T(8,128)} %copy-done.9, f32[256,128]{1,0:T(8,128)} %copy-done.10, f32[4,4096]{1,0:T(4,128)} %broadcast_in_dim.39.low, f32[4,4096]{1,0:T(4,128)} %broadcast_in_dim.41.up, ...), custom_call_target="tpu_custom_call" | custom-call | flops 1610612736 | bytes 6291456 | tf_op jit(solution)/shard_map/attend/pallas_call | solution.py:172
  146.0 3.6 %all-to-all-start.2 = ((f32[8,256,128]{2,1,0:T(8,128)}), f32[8,256,128]{2,1,0:T(8,128)S(1)}, u32[]{:S(2)}, u32[]{:S(2)}) async-start(f32[8,256,128]{2,1,0:T(8,128)} %attend.1), calls=%async_computation.2 | async-start | bytes 2097152 | tf_op jit(solution)/shard_map/all_to_all | solution.py:314
  149.6 2.9 %all-gather.7.cloned.1.call-done = f32[64,2,16,512]{3,2,1,0:T(8,128)} async-done(((f32[8,2,16,512]{3,2,1,0:T(8,128)}), f32[64,2,16,512]{3,2,1,0:T(8,128)}) %all-gather.7.cloned.1.call-update) | async-done | bytes 4194320 | tf_op jit(solution)/shard_map/all_gather | solution.py:298
  152.5 22.2 %all-to-all-done.2.heads = f32[8,256,128]{2,1,0:T(8,128)S(1)} async-done(((f32[8,256,128]{2,1,0:T(8,128)}), f32[8,256,128]{2,1,0:T(8,128)S(1)}, u32[]{:S(2)}, u32[]{:S(2)}) %all-to-all-start.2) | async-done | bytes 1048608 | tf_op jit(solution)/shard_map/all_to_all | solution.py:314
  175.8 5.5 %mix.1 = f32[8,64,512]{2,1,0:T(8,128)} custom-call(f32[8,256,128]{2,1,0:T(8,128)} %copy-done, f32[8,8,2,16,512]{4,3,2,1,0:T(8,128)} %bitcast.70), custom_call_target="tpu_custom_call" | custom-call | flops 1610612736 | bytes 6291456 | tf_op jit(solution)/shard_map/mix/pallas_call | solution.py:216
  181.3 23.2 %all_to_all.27 = f32[8,64,512]{2,1,0:T(8,128)S(1)} all-to-all(f32[8,64,512]{2,1,0:T(8,128)} %mix.1), channel_id=1, replica_groups=mesh['x'=4,'y'=4,'z'=8,'k'=2] {'x','k'}, dimensions={0} | all-to-all | bytes 2097152 | tf_op jit(solution)/shard_map/all_to_all | solution.py:316
  (80 shorter events, 17.0 us)
Async XLA Ops:
  6.5 130.1 %all-gather.5.cloned.1.call-start = ((), (), s32[]{:S(2)}) async-start(), calls=%async_computation.5 | async-start | bytes 4718592 | tf_op jit(solution)/shard_map/all_gather | solution.py:288
  33.6 86.4 %copy-start.11 = (s32[32]{0:T(128)S(1)}, s32[32]{0:T(128)}, u32[]{:S(2)}) copy-start(s32[32]{0:T(128)} %param.14) | copy-start | bytes 388
  33.7 87.0 %copy-start.12 = (s32[32]{0:T(128)S(1)}, s32[32]{0:T(128)}, u32[]{:S(2)}) copy-start(s32[32]{0:T(128)} %param.16) | copy-start | bytes 388
  33.7 87.8 %copy-start.6 = (s32[32,16]{0,1:T(8,128)S(1)}, s32[32,16]{0,1:T(8,128)}, u32[]{:S(2)}) copy-start(s32[32,16]{0,1:T(8,128)} %param.15) | copy-start | bytes 6148
  33.7 87.8 %copy-start.7 = (s32[32,16]{0,1:T(8,128)S(1)}, s32[32,16]{0,1:T(8,128)}, u32[]{:S(2)}) copy-start(s32[32,16]{0,1:T(8,128)} %param.13) | copy-start | bytes 6148
  33.7 12.9 %collective-permute-start = (f32[2,4,16,512]{3,2,1,0:T(8,128)S(1)}, f32[2,4,16,512]{3,2,1,0:T(8,128)S(1)}, u32[]{:S(2)}, u32[]{:S(2)}) collective-permute-start(f32[2,4,16,512]{3,2,1,0:T(8,128)S(1)} %get-tuple-element.56), channel_id=1, source_target_pairs={{0,1},{1,0},{2,3},{3,2},{4,5},{5,4},{6,7},{7,6},{8,9},{9,8},{10,11... | collective-permute-start | bytes 786440 | tf_op jit(solution)/shard_map/ppermute | solution.py:292
  40.1 15.1 %collective-permute-start.1 = (f32[64,2048]{1,0:T(8,128)}, f32[64,2048]{1,0:T(8,128)S(1)}, u32[]{:S(2)}, u32[]{:S(2)}) collective-permute-start(f32[64,2048]{1,0:T(8,128)} %get-tuple-element.26), channel_id=1, source_target_pairs={{0,64},{64,128},{128,192},{192,0},{1,65},{65,129},{129,193},{193,1... | collective-permute-start | bytes 1572872 | tf_op jit(solution)/shard_map/ppermute | solution.py:255
  41.4 26.0 %collective-permute-start.2 = (f32[64,2048]{1,0:T(8,128)}, f32[64,2048]{1,0:T(8,128)S(1)}, u32[]{:S(2)}, u32[]{:S(2)}) collective-permute-start(f32[64,2048]{1,0:T(8,128)} %get-tuple-element.27), channel_id=1, source_target_pairs={{0,128},{64,192},{128,0},{192,64},{1,129},{65,193},{129,1},{193,65... | collective-permute-start | bytes 1572872 | tf_op jit(solution)/shard_map/ppermute | solution.py:255
  43.8 25.2 %collective-permute-start.9 = (f32[512,256]{1,0:T(8,128)S(1)}, f32[512,256]{1,0:T(8,128)S(1)}, u32[]{:S(2)}, u32[]{:S(2)}) collective-permute-start(f32[512,256]{1,0:T(8,128)S(1)} %copy-done.1), channel_id=1, source_target_pairs={{0,48},{16,0},{32,16},{48,32},{1,49},{17,1},{33,17},{49,33},{2,50}... | collective-permute-start | bytes 1572872 | tf_op jit(solution)/shard_map/ppermute | solution.py:255
  46.6 26.4 %collective-permute-start.5 = (f32[512,256]{1,0:T(8,128)S(1)}, f32[512,256]{1,0:T(8,128)S(1)}, u32[]{:S(2)}, u32[]{:S(2)}) collective-permute-start(f32[512,256]{1,0:T(8,128)S(1)} %copy-done.1), channel_id=1, source_target_pairs={{0,16},{16,32},{32,48},{48,0},{1,17},{17,33},{33,49},{49,1},{2,18}... | collective-permute-start | bytes 1572872 | tf_op jit(solution)/shard_map/ppermute | solution.py:255
  46.6 40.0 %collective-permute-start.7 = (f32[512,256]{1,0:T(8,128)S(1)}, f32[512,256]{1,0:T(8,128)}, u32[]{:S(2)}, u32[]{:S(2)}) collective-permute-start(f32[512,256]{1,0:T(8,128)S(1)} %copy-done.1), channel_id=1, source_target_pairs={{0,32},{16,48},{32,0},{48,16},{1,33},{17,49},{33,1},{49,17},{2,34}... | collective-permute-start | bytes 1572872 | tf_op jit(solution)/shard_map/ppermute | solution.py:255
  55.2 68.2 %copy-start.2 = (f32[64,2048]{1,0:T(8,128)}, f32[64,2048]{1,0:T(8,128)S(1)}, u32[]{:S(2)}) copy-start(f32[64,2048]{1,0:T(8,128)S(1)} %collective-permute-done.1.refs_0_) | copy-start | bytes 1572868
  55.2 37.1 %collective-permute-start.4 = (f32[512,256]{1,0:T(8,128)S(1)}, f32[512,256]{1,0:T(8,128)}, u32[]{:S(2)}, u32[]{:S(2)}) collective-permute-start(f32[512,256]{1,0:T(8,128)S(1)} %copy-done.1), channel_id=1, source_target_pairs={{0,1},{1,0},{2,3},{3,2},{4,5},{5,4},{6,7},{7,6},{8,9},{9,8},{10,11... | collective-permute-start | bytes 1572872 | tf_op jit(solution)/shard_map/ppermute | solution.py:276
  67.3 56.1 %copy-start.3 = (f32[64,2048]{1,0:T(8,128)}, f32[64,2048]{1,0:T(8,128)S(1)}, u32[]{:S(2)}) copy-start(f32[64,2048]{1,0:T(8,128)S(1)} %collective-permute-done.2.refs_1_) | copy-start | bytes 1572868
  67.3 25.0 %collective-permute-start.3 = (f32[64,2048]{1,0:T(8,128)}, f32[64,2048]{1,0:T(8,128)}, u32[]{:S(2)}, u32[]{:S(2)}) collective-permute-start(f32[64,2048]{1,0:T(8,128)} %get-tuple-element.28), channel_id=1, source_target_pairs={{0,192},{64,0},{128,64},{192,128},{1,193},{65,1},{129,65},{193,129... | collective-permute-start | bytes 1572872 | tf_op jit(solution)/shard_map/ppermute | solution.py:255
  69.1 23.3 %collective-permute-start.10 = (f32[512,256]{1,0:T(8,128)S(1)}, f32[512,256]{1,0:T(8,128)}, u32[]{:S(2)}, u32[]{:S(2)}) collective-permute-start(f32[512,256]{1,0:T(8,128)S(1)} %collective-permute-done.9.refs_9_), channel_id=1, source_target_pairs={{0,1},{1,0},{2,3},{3,2},{4,5},{5,4},{6,7},{7,6},{8,9},{9,8},{10,11... | collective-permute-start | bytes 1572872 | tf_op jit(solution)/shard_map/ppermute | solution.py:276
  72.9 19.4 %collective-permute-start.6 = (f32[512,256]{1,0:T(8,128)S(1)}, f32[512,256]{1,0:T(8,128)}, u32[]{:S(2)}, u32[]{:S(2)}) collective-permute-start(f32[512,256]{1,0:T(8,128)S(1)} %collective-permute-done.5.refs_5_), channel_id=1, source_target_pairs={{0,1},{1,0},{2,3},{3,2},{4,5},{5,4},{6,7},{7,6},{8,9},{9,8},{10,11... | collective-permute-start | bytes 1572872 | tf_op jit(solution)/shard_map/ppermute | solution.py:276
  86.5 5.8 %collective-permute-start.8 = (f32[512,256]{1,0:T(8,128)}, f32[512,256]{1,0:T(8,128)}, u32[]{:S(2)}, u32[]{:S(2)}) collective-permute-start(f32[512,256]{1,0:T(8,128)} %collective-permute-done.7.refs_7_), channel_id=1, source_target_pairs={{0,1},{1,0},{2,3},{3,2},{4,5},{5,4},{6,7},{7,6},{8,9},{9,8},{10,11... | collective-permute-start | bytes 1572872 | tf_op jit(solution)/shard_map/ppermute | solution.py:276
  88.2 14.2 %all-to-all-start.1 = ((f32[16,16,512]{2,1,0:T(8,128)}), f32[16,16,512]{2,1,0:T(8,128)S(1)}, u32[]{:S(2)}, u32[]{:S(2)}) async-start(f32[16,16,512]{2,1,0:T(8,128)} %bitcast.19), calls=%async_computation.1 | async-start | bytes 1048576 | tf_op jit(solution)/shard_map/all_to_all | solution.py:295
  92.3 60.3 %all-gather.7.cloned.1.call-start = ((), (), s32[]{:S(2)}) async-start(), calls=%async_computation.6 | async-start | bytes 4718592 | tf_op jit(solution)/shard_map/all_gather | solution.py:298
  128.7 5.6 %collective-permute-start.11 = (f32[256,128]{1,0:T(8,128)}, f32[256,128]{1,0:T(8,128)S(1)}, u32[]{:S(2)}, u32[]{:S(2)}) collective-permute-start(f32[256,128]{1,0:T(8,128)} %get-tuple-element.41), channel_id=1, source_target_pairs={{0,64},{64,128},{128,192},{192,0},{1,65},{65,129},{129,193},{193,1... | collective-permute-start | bytes 393224 | tf_op jit(solution)/shard_map/ppermute | solution.py:255
  129.8 6.4 %collective-permute-start.12 = (f32[256,128]{1,0:T(8,128)}, f32[256,128]{1,0:T(8,128)S(1)}, u32[]{:S(2)}, u32[]{:S(2)}) collective-permute-start(f32[256,128]{1,0:T(8,128)} %get-tuple-element.42), channel_id=1, source_target_pairs={{0,128},{64,192},{128,0},{192,64},{1,129},{65,193},{129,1},{193,65... | collective-permute-start | bytes 393224 | tf_op jit(solution)/shard_map/ppermute | solution.py:255
  132.2 4.4 %collective-permute-start.13 = (f32[256,128]{1,0:T(8,128)}, f32[256,128]{1,0:T(8,128)S(1)}, u32[]{:S(2)}, u32[]{:S(2)}) collective-permute-start(f32[256,128]{1,0:T(8,128)} %get-tuple-element.43), channel_id=1, source_target_pairs={{0,192},{64,0},{128,64},{192,128},{1,193},{65,1},{129,65},{193,129... | collective-permute-start | bytes 393224 | tf_op jit(solution)/shard_map/ppermute | solution.py:255
  146.0 28.8 %all-to-all-start.2 = ((f32[8,256,128]{2,1,0:T(8,128)}), f32[8,256,128]{2,1,0:T(8,128)S(1)}, u32[]{:S(2)}, u32[]{:S(2)}) async-start(f32[8,256,128]{2,1,0:T(8,128)} %attend.1), calls=%async_computation.2 | async-start | bytes 2097152 | tf_op jit(solution)/shard_map/all_to_all | solution.py:314
  (7 other events, 146.8 us)
Sparse Core Ops, SparseCore 0:
  32.7 48.7 all-gather.4
  120.1 32.3 all-gather.6

commit v6 on v4

--- a/solution.py
+++ b/solution.py
@@ -16,7 +16,7 @@
 VMEM = pl.BlockSpec(memory_space=pltpu.VMEM)
 SMEM = pl.BlockSpec(memory_space=pltpu.SMEM)
 ANY = pl.BlockSpec(memory_space=pl.ANY)
-HBM = pl.BlockSpec(memory_space=pltpu.HBM)
+LIMIT = 60 << 20
 
 
 def split(value):
@@ -54,14 +54,16 @@
     return pl.pallas_call(
         pick_kernel,
         out_shape=[jax.ShapeDtypeStruct((BLOCK, 2048), jnp.float32)] * 3,
-        in_specs=[SMEM, HBM],
-        out_specs=[HBM] * 3,
+        in_specs=[SMEM, ANY],
+        out_specs=[VMEM] * 3,
         scratch_shapes=[pltpu.SemaphoreType.DMA((3,))],
+        compiler_params=pltpu.CompilerParams(vmem_limit_bytes=LIMIT),
         name="pick",
     )(where, hidden_rows)
 
 
-def project_kernel(where, rows, first, second, third, weights, out, left_buf, right_buf, sems):
+def project_kernel(where, rows, first, second, third, weights, *refs):
+    outs, (left_buf, right_buf, total_buf, sems) = refs[:NX], refs[NX:]
     x, k = where[0], where[1]
     copies = []
     for y in range(NY):
@@ -92,21 +94,24 @@
             totals[core] = term if totals[core] is None else totals[core] + term
     for core in range(NK):
         for b in range(2):
-            out[2 * core + b] = totals[core][:, b * HD : (b + 1) * HD]
+            total_buf[2 * core + b] = totals[core][:, b * HD : (b + 1) * HD]
+    for shift in range(NX):
+        outs[shift][...] = total_buf[lax.rem(x + shift, NX)]
 
 
 def project(where, rows, moved, weights):
     return pl.pallas_call(
         project_kernel,
-        out_shape=jax.ShapeDtypeStruct((NX, NX * BLOCK, HD), jnp.float32),
-        in_specs=[SMEM, HBM, ANY, ANY, ANY, HBM],
-        out_specs=VMEM,
+        out_shape=[jax.ShapeDtypeStruct((NX * BLOCK, HD), jnp.float32)] * NX,
+        in_specs=[SMEM] + [ANY] * 5,
+        out_specs=[VMEM] * NX,
         scratch_shapes=[
             pltpu.VMEM((NY, NX, BLOCK, 512), jnp.float32),
             pltpu.VMEM((NY, NK, 512, 256), jnp.float32),
+            pltpu.VMEM((NX, NX * BLOCK, HD), jnp.float32),
             pltpu.SemaphoreType.DMA((NY, NX + 1)),
         ],
-        compiler_params=pltpu.CompilerParams(vmem_limit_bytes=32 << 20),
+        compiler_params=pltpu.CompilerParams(vmem_limit_bytes=LIMIT),
         cost_estimate=pl.CostEstimate(
             flops=6 * 256 * 2048 * 512, bytes_accessed=7 << 20, transcendentals=0
         ),
@@ -114,7 +119,7 @@
     )(where, rows, *moved, weights)
 
 
-def attend_kernel(partial, low, up, *refs):
+def attend_kernel(first, second, third, fourth, low, up, *refs):
     pieces, (out, kv, scores, sem) = refs[:8], refs[8:]
     tiles = len(pieces)
     copies = [
@@ -127,7 +132,7 @@
     row = lax.broadcasted_iota(jnp.int32, (BLOCK, width), 0)
     col = lax.broadcasted_iota(jnp.int32, (BLOCK, width), 1)
     lower = row >= lax.rem(col, BLOCK)
-    query = (partial[0] + partial[1]) + (partial[2] + partial[3])
+    query = (first[...] + second[...]) + (third[...] + fourth[...])
     left = split(query * (math.log2(math.e) / math.sqrt(HD)))
     top = None
     for tile in range(tiles):
@@ -161,22 +166,23 @@
     return pl.pallas_call(
         attend_kernel,
         out_shape=jax.ShapeDtypeStruct((NZ, rows, HD), jnp.float32),
-        in_specs=[VMEM] * 3 + [ANY] * 8,
+        in_specs=[VMEM] * 6 + [ANY] * 8,
         out_specs=VMEM,
         scratch_shapes=[
             pltpu.VMEM((8, NZ, 2, BLOCK, HD), jnp.float32),
             pltpu.VMEM((8, rows, NZ * BLOCK), jnp.float32),
             pltpu.SemaphoreType.DMA((8,)),
         ],
-        compiler_params=pltpu.CompilerParams(vmem_limit_bytes=48 << 20),
+        compiler_params=pltpu.CompilerParams(vmem_limit_bytes=LIMIT),
         cost_estimate=pl.CostEstimate(
             flops=12 * 256 * 4096 * HD, bytes_accessed=6 << 20, transcendentals=256 * 4096
         ),
         name="attend",
-    )(partial, low, up, *pieces)
-
-
-def mix_kernel(heads, weights, out, buf, sem):
+    )(*partial, low, up, *pieces)
+
+
+def mix_kernel(where, heads, weights, *refs):
+    outs, (total_buf, buf, sem) = refs[:NX], refs[NX:]
     steps = NZ // 2
     copies = []
     for step in range(steps):
@@ -198,25 +204,28 @@
             totals[core] = term if totals[core] is None else totals[core] + term
     for core in range(NK):
         for x in range(NX):
-            out[2 * x + core] = totals[core][x * BLOCK : (x + 1) * BLOCK]
-
-
-def mix(heads, weights):
+            total_buf[x, core] = totals[core][x * BLOCK : (x + 1) * BLOCK]
+    for shift in range(NX):
+        outs[shift][...] = total_buf[lax.rem(where[0] + shift, NX)]
+
+
+def mix(where, heads, weights):
     return pl.pallas_call(
         mix_kernel,
-        out_shape=jax.ShapeDtypeStruct((NX * NK, BLOCK, 512), jnp.float32),
-        in_specs=[VMEM, HBM],
-        out_specs=VMEM,
+        out_shape=[jax.ShapeDtypeStruct((NK, BLOCK, 512), jnp.float32)] * NX,
+        in_specs=[SMEM, VMEM, ANY],
+        out_specs=[VMEM] * NX,
         scratch_shapes=[
+            pltpu.VMEM((NX, NK, BLOCK, 512), jnp.float32),
             pltpu.VMEM((NZ // 2, 8, 2, NK, 16, 512), jnp.float32),
             pltpu.SemaphoreType.DMA((NZ // 2,)),
         ],
-        compiler_params=pltpu.CompilerParams(vmem_limit_bytes=32 << 20),
+        compiler_params=pltpu.CompilerParams(vmem_limit_bytes=LIMIT),
         cost_estimate=pl.CostEstimate(
             flops=6 * 256 * 1024 * 1024, bytes_accessed=6 << 20, transcendentals=0
         ),
         name="mix",
-    )(heads, weights)
+    )(where, heads, weights)
 
 
 def allowed_rows(
@@ -239,6 +248,11 @@
 CORES = [(0, 1), (1, 0)]
 
 
+def along(axis, value, shift):
+    count = lax.axis_size(axis)
+    return lax.ppermute(value, axis, [(i, (i + shift) % count) for i in range(count)])
+
+
 def shards(
     hidden_rows,
     query_weight,
@@ -254,10 +268,7 @@
     where = jnp.stack([x, k]).astype(jnp.int32)
     weights = lax.all_gather(query_weight, ("y", "k"), axis=0)
     picked = pick(where, hidden_rows)
-    hidden = [
-        lax.ppermute(part, "x", [(i, (i + shift) % NX) for i in range(NX)])
-        for shift, part in zip(range(1, NX), picked)
-    ]
+    hidden = [along("x", part, shift) for shift, part in enumerate(picked, 1)]
     quarters = [
         lax.dynamic_slice_in_dim(cache, y * BLOCK, BLOCK, 0)
         for cache in (key_cache, value_cache)
@@ -270,33 +281,28 @@
     )
     sent, _ = lax.optimization_barrier((sent, picked[0]))
     near = lax.all_to_all(sent, "z", 0, 0)
-    pieces = []
-    key_block = []
-    for shift in range(NY):
-        piece = near
-        if shift:
-            piece = lax.ppermute(near, "y", [(i, (i + shift) % NY) for i in range(NY)])
-        pieces += [piece, lax.ppermute(piece, "k", CORES)]
-        for core in (k, 1 - k):
-            key_block.append(
-                4 * (2 * jnp.arange(NZ, dtype=jnp.int32) + core) + (y - shift) % NY
-            )
     rows = output_weight.reshape(2, NY, NK, 16, 512)
     kept = lax.dynamic_index_in_dim(rows, k, 2, keepdims=False)
     given = lax.dynamic_index_in_dim(rows, 1 - k, 2, keepdims=False)
     taken = lax.ppermute(given, "k", CORES)
     rows = jnp.where(k == 0, jnp.stack([kept, taken]), jnp.stack([taken, kept]))
     rows, near = lax.optimization_barrier((rows, near))
+    quarters = [near] + [along("y", near, shift) for shift in range(1, NY)]
     rows = lax.all_to_all(rows.reshape(NX * NY, 16, 512), ("x", "y"), 0, 0)
-    rows, hidden = lax.optimization_barrier((rows, hidden))
+    rows, hidden, quarters = lax.optimization_barrier((rows, hidden, quarters))
     rows = lax.all_to_all(rows.reshape(NZ, NK, 16, 512), "z", 0, 0)
     out_weight = lax.all_gather(rows, ("y", "k"), axis=0)
-    hidden, pieces[2::2] = lax.optimization_barrier((hidden, pieces[2::2]))
+    pieces = []
+    for piece in quarters:
+        pieces += [piece, lax.ppermute(piece, "k", CORES)]
     partial = project(where, hidden_rows, hidden, weights)
-    partial = lax.all_to_all(partial, "x", 0, 0)
+    partial = [partial[0]] + [along("x", partial[s], s) for s in range(1, NX)]
+    key_block = (y - jnp.arange(NY, dtype=jnp.int32))[:, None, None] % NY
+    key_block = key_block + 4 * jnp.stack([k, 1 - k])[None, :, None]
+    key_block = key_block + 8 * jnp.arange(NZ, dtype=jnp.int32)[None, None, :]
     low, up = allowed_rows(
         4 * z + x,
-        jnp.concatenate(key_block),
+        key_block.reshape(-1),
         32 + 8 * jnp.arange(NX, dtype=jnp.int32) + 2 * y + k,
         vertical_blocks,
         vertical_count,
@@ -305,9 +311,13 @@
     )
     heads = attend(partial, low, up, pieces)
     heads = lax.all_to_all(heads, "z", 0, 0)
-    mixed = mix(heads, out_weight)
-    mixed = lax.all_to_all(mixed, ("x", "k"), 0, 0)
-    return jnp.sum(mixed.reshape(NX, NK * BLOCK, 512), axis=0)
+    mixed = mix(where, heads, out_weight)
+    mixed = [mixed[0]] + [along("x", mixed[s], s) for s in range(1, NX)]
+    mixed = (mixed[0] + mixed[1]) + (mixed[2] + mixed[3])
+    own = lax.dynamic_index_in_dim(mixed, k, 0, keepdims=False)
+    other = lax.dynamic_index_in_dim(mixed, 1 - k, 0, keepdims=False)
+    other = lax.ppermute(other, "k", CORES)
+    return jnp.concatenate([jnp.where(k == 0, own, other), jnp.where(k == 0, other, own)])
 
 
 def solution(mesh):

time: 270 us -> 191 us (0.71)
  Pallas kernels: 62.3 us -> 23 us
  blocking collectives: 73.6 us -> 49.8 us
  waiting for transfers between devices: 62.5 us -> 47.3 us
  local copies, waits for them, and re-layouts: 9.36 us -> 4.57 us
  starting transfers between devices: 38.7 us -> 41.8 us
    pallas_call x1, Pallas kernels: 49.4 us -> 3.21 us  [pick(): pl.pallas_call(pick_kernel, out_shape=[jax.ShapeDtypeStruct((BLOCK, 2048)...]
    all_to_all x1 -> x0, blocking collectives: 20.1 us -> none  [shards(): mixed = lax.all_to_all(mixed, ('x', 'k'), 0, 0)]
    ppermute x6 -> x13, waiting for transfers between devices: 34.2 us -> 14.1 us  [the longest x12 13.1 us: along(): lax.ppermute(value, axis, [(i, (i + shift) % count) for i in range(count)])]
    ppermute x6 -> x13, starting transfers between devices: 7.79 us -> 22.7 us  [the longest x12 19 us: along(): lax.ppermute(value, axis, [(i, (i + shift) % count) for i in range(count)])]
    all_to_all x1, waiting for transfers between devices: 7.53 us -> 21.5 us  [shards(): rows = lax.all_to_all(rows.reshape(NX * NY, 16, 512), ('x', 'y'), 0, 0)]
    all_to_all x1 -> x0, waiting for transfers between devices: 8.88 us -> none  [shards(): partial = lax.all_to_all(partial, 'x', 0, 0)]
    ppermute x4, starting transfers between devices: 10.4 us -> 4.5 us  [shards(): pieces += [piece, lax.ppermute(piece, 'k', CORES)]]
    unnamed x18 -> x26, local copies, waits for them, and re-layouts: 6.6 us -> 0.73 us
  transfers between devices with their start and end apart: 16 -> 22, of which waited for: 7 -> 8; matrix products, arithmetic and copies ran while one was open for 4% -> 6% of each run, Pallas kernels for 22% -> 9%
where the time goes in v6:
time: 191 us; the launch traced here: 190 us
  blocking collectives  49.8 us (26%)
  waiting for transfers between devices  47.3 us (25%)
  starting transfers between devices  41.8 us (22%)
  Pallas kernels  23 us (12%)
  between operations  13.7 us (7%)
  other arithmetic  10.3 us (5%)
  local copies, waits for them, and re-layouts  4.57 us (2%)
    all_to_all x1, blocking collectives, shards(): heads = lax.all_to_all(heads, 'z', 0, 0)  31 us
    all_to_all x1, waiting for transfers between devices, shards(): rows = lax.all_to_all(rows.reshape(NX * NY, 16, 512), ('x', 'y'), 0, 0)  21.5 us
    ppermute x12, starting transfers between devices, along(): lax.ppermute(value, axis, [(i, (i + shift) % count) for i in range(count)])  19 us
    all_to_all x1, blocking collectives, shards(): rows = lax.all_to_all(rows.reshape(NZ, NK, 16, 512), 'z', 0, 0)  18.7 us
    ppermute x12, waiting for transfers between devices, along(): lax.ppermute(value, axis, [(i, (i + shift) % count) for i in range(count)])  13.1 us
    all_to_all x1, waiting for transfers between devices, shards(): near = lax.all_to_all(sent, 'z', 0, 0)  10.9 us
    all_to_all x1, starting transfers between devices, shards(): near = lax.all_to_all(sent, 'z', 0, 0)  9.01 us
    pallas_call x1, Pallas kernels, attend(): pl.pallas_call(attend_kernel, out_shape=jax.ShapeDtypeStruct((NZ, rows, H...  8.59 us
  transfers between devices with their start and end apart: 22, of which 8 were waited for; matrix products, arithmetic and copies ran while one was open for 6% of the time, Pallas kernels for 9%

profile of v6, /device:TPU:1, one launch (start us, length us, event | category | flops | bytes accessed | tf_op | source)
XLA Modules:
  0.0 190.3 jit_solution(4249982211742439691)
XLA Ops:
  7.9 3.2 %pick.1 = (f32[64,2048]{1,0:T(8,128)}, f32[64,2048]{1,0:T(8,128)}, f32[64,2048]{1,0:T(8,128)}) custom-call(s32[2]{0:T(128)} %pad_add_fusion.where, f32[128,8192]{1,0:T(8,128)} %rows.3), custom_call_target="tpu_custom_call" | custom-call | tf_op jit(solution)/shard_map/pick/pallas_call | solution.py:54
  17.1 9.0 %all-to-all-start = ((f32[8,2,64,128]{3,2,1,0:T(8,128)}), f32[8,2,64,128]{3,2,1,0:T(8,128)S(1)}, u32[]{:S(2)}, u32[]{:S(2)}) async-start(f32[8,2,64,128]{3,2,1,0:T(8,128)} %fusion.1), calls=%async_computation | async-start | bytes 1048576 | tf_op jit(solution)/shard_map/all_to_all | solution.py:283
  26.1 1.2 collective-permute-start.1
  27.4 1.3 collective-permute-start
  28.7 2.5 %collective-permute-start.2 = (f32[64,2048]{1,0:T(8,128)}, f32[64,2048]{1,0:T(8,128)S(1)}, u32[]{:S(2)}, u32[]{:S(2)}) collective-permute-start(f32[64,2048]{1,0:T(8,128)} %get-tuple-element.30), channel_id=1, source_target_pairs={{0,128},{64,192},{128,0},{192,64},{1,129},{65,193},{129,1},{193,65... | collective-permute-start | bytes 1572872 | tf_op jit(solution)/shard_map/ppermute | solution.py:253
  33.2 10.9 %all-to-all-done.refs_0_ = f32[8,2,64,128]{3,2,1,0:T(8,128)S(1)} async-done(((f32[8,2,64,128]{3,2,1,0:T(8,128)}), f32[8,2,64,128]{3,2,1,0:T(8,128)S(1)}, u32[]{:S(2)}, u32[]{:S(2)}) %all-to-all-start) | async-done | bytes 524320 | tf_op jit(solution)/shard_map/all_to_all | solution.py:283
  44.1 1.3 collective-permute-start.4
  45.4 2.6 %collective-permute-start.5 = (f32[8,2,64,128]{3,2,1,0:T(8,128)S(1)}, f32[8,2,64,128]{3,2,1,0:T(8,128)}, u32[]{:S(2)}, u32[]{:S(2)}) collective-permute-start(f32[8,2,64,128]{3,2,1,0:T(8,128)S(1)} %all-to-all-done.refs_0_), channel_id=1, source_target_pairs={{0,32},{16,48},{32,0},{48,16},{1,33},{17,49},{33,1},{49,17},{2,34}... | collective-permute-start | bytes 1572872 | tf_op jit(solution)/shard_map/ppermute | solution.py:253
  49.1 4.2 %all-to-all-start.1 = ((f32[16,16,512]{2,1,0:T(8,128)}), f32[16,16,512]{2,1,0:T(8,128)S(1)}, u32[]{:S(2)}, u32[]{:S(2)}) async-start(f32[16,16,512]{2,1,0:T(8,128)} %bitcast.18), calls=%async_computation.1 | async-start | bytes 1048576 | tf_op jit(solution)/shard_map/all_to_all | solution.py:291
  54.3 21.5 %all-to-all-done.1 = f32[16,16,512]{2,1,0:T(8,128)S(1)} async-done(((f32[16,16,512]{2,1,0:T(8,128)}), f32[16,16,512]{2,1,0:T(8,128)S(1)}, u32[]{:S(2)}, u32[]{:S(2)}) %all-to-all-start.1) | async-done | bytes 524320 | tf_op jit(solution)/shard_map/all_to_all | solution.py:291
  75.8 18.7 %all_to_all.20 = f32[8,2,16,512]{3,2,1,0:T(8,128)} all-to-all(f32[8,2,16,512]{3,2,1,0:T(8,128)S(1)} %bitcast.73), channel_id=1, replica_groups=mesh['x'=4,'y'=4,'z'=8,'k'=2] {'z'}, dimensions={0} | all-to-all | bytes 1048576 | tf_op jit(solution)/shard_map/all_to_all | solution.py:293
  97.7 3.8 %collective-permute-start.10 = (f32[8,2,64,128]{3,2,1,0:T(8,128)S(1)}, f32[8,2,64,128]{3,2,1,0:T(8,128)}, u32[]{:S(2)}, u32[]{:S(2)}) collective-permute-start(f32[8,2,64,128]{3,2,1,0:T(8,128)S(1)} %all-to-all-done.refs_0_), channel_id=1, source_target_pairs={{0,1},{1,0},{2,3},{3,2},{4,5},{5,4},{6,7},{7,6},{8,9},{9,8},{10,11... | collective-permute-start | bytes 1572872 | tf_op jit(solution)/shard_map/ppermute | solution.py:297
  102.4 5.5 %project.1 = (f32[256,128]{1,0:T(8,128)}, f32[256,128]{1,0:T(8,128)}, f32[256,128]{1,0:T(8,128)}, f32[256,128]{1,0:T(8,128)}) custom-call(s32[2]{0:T(128)} %pad_add_fusion.where, f32[128,8192]{1,0:T(8,128)} %rows.3, f32[64,2048]{1,0:T(8,128)} %copy-done, f32[64,2048]{1,0:T(8,128)} %copy-done.1, f32[64,2048]{1,0:T(8,128)} %copy-done.2, f32[8,512,256]{2,1,0:T(8,128)} %bitcast.72), custom_call_target="tpu_custom_call" | custom-call | flops 1610612736 | bytes 7340032 | tf_op jit(solution)/shard_map/project/pallas_call | solution.py:103
  107.9 1.2 collective-permute-start.7
  109.2 2.4 %collective-permute-start.8 = (f32[256,128]{1,0:T(8,128)}, f32[256,128]{1,0:T(8,128)S(1)}, u32[]{:S(2)}, u32[]{:S(2)}) collective-permute-start(f32[256,128]{1,0:T(8,128)} %get-tuple-element.38), channel_id=1, source_target_pairs={{0,128},{64,192},{128,0},{192,64},{1,129},{65,193},{129,1},{193,65... | collective-permute-start | bytes 393224 | tf_op jit(solution)/shard_map/ppermute | solution.py:253
  114.4 3.3 %collective-permute-done.8.third = f32[256,128]{1,0:T(8,128)S(1)} collective-permute-done((f32[256,128]{1,0:T(8,128)}, f32[256,128]{1,0:T(8,128)S(1)}, u32[]{:S(2)}, u32[]{:S(2)}) %collective-permute-start.8) | collective-permute-done | bytes 131104 | tf_op jit(solution)/shard_map/ppermute | solution.py:253
  118.4 8.6 %attend.1 = f32[8,256,128]{2,1,0:T(8,128)} custom-call(f32[256,128]{1,0:T(8,128)} %get-tuple-element.36.first, f32[256,128]{1,0:T(8,128)} %copy-done.8, f32[256,128]{1,0:T(8,128)} %copy-done.9, f32[256,128]{1,0:T(8,128)} %copy-done.10, f32[4,4096]{1,0:T(4,128)} %broadcast_in_dim.39.low, f32[4,4096]{1,0:T(4,128)} %broadcast_in_dim.41.up, ...), custom_call_target="tpu_custom_call" | custom-call | flops 1610612736 | bytes 6291456 | tf_op jit(solution)/shard_map/attend/pallas_call | solution.py:166
  127.0 31.0 %all_to_all.21.heads = f32[8,256,128]{2,1,0:T(8,128)} all-to-all(f32[8,256,128]{2,1,0:T(8,128)} %attend.1), channel_id=1, replica_groups=mesh['x'=4,'y'=4,'z'=8,'k'=2] {'z'}, dimensions={0} | all-to-all | bytes 2097152 | tf_op jit(solution)/shard_map/all_to_all | solution.py:313
  158.1 5.6 %mix.1 = (f32[2,64,512]{2,1,0:T(8,128)}, f32[2,64,512]{2,1,0:T(8,128)}, f32[2,64,512]{2,1,0:T(8,128)}, f32[2,64,512]{2,1,0:T(8,128)}) custom-call(s32[2]{0:T(128)} %pad_add_fusion.where, f32[8,256,128]{2,1,0:T(8,128)} %all_to_all.21.heads, f32[8,8,2,16,512]{4,3,2,1,0:T(8,128)} %bitcast.76), custom_call_target="tpu_custom_call" | custom-call | flops 1610612736 | bytes 6291456 | tf_op jit(solution)/shard_map/mix/pallas_call | solution.py:213
  163.7 1.9 collective-permute-start.14
  165.6 1.9 %collective-permute-start.15 = (f32[2,64,512]{2,1,0:T(8,128)}, f32[2,64,512]{2,1,0:T(8,128)S(1)}, u32[]{:S(2)}, u32[]{:S(2)}) collective-permute-start(f32[2,64,512]{2,1,0:T(8,128)} %get-tuple-element.47), channel_id=1, source_target_pairs={{0,128},{64,192},{128,0},{192,64},{1,129},{65,193},{129,1},{193,65... | collective-permute-start | bytes 786440 | tf_op jit(solution)/shard_map/ppermute | solution.py:253
  168.1 2.4 %collective-permute-done.14 = f32[2,64,512]{2,1,0:T(8,128)S(1)} collective-permute-done((f32[2,64,512]{2,1,0:T(8,128)}, f32[2,64,512]{2,1,0:T(8,128)S(1)}, u32[]{:S(2)}, u32[]{:S(2)}) %collective-permute-start.14) | collective-permute-done | bytes 262176 | tf_op jit(solution)/shard_map/ppermute | solution.py:253
  170.4 6.3 %collective-permute-done.15 = f32[2,64,512]{2,1,0:T(8,128)S(1)} collective-permute-done((f32[2,64,512]{2,1,0:T(8,128)}, f32[2,64,512]{2,1,0:T(8,128)S(1)}, u32[]{:S(2)}, u32[]{:S(2)}) %collective-permute-start.15) | collective-permute-done | bytes 262176 | tf_op jit(solution)/shard_map/ppermute | solution.py:253
  178.1 3.7 %collective-permute-start.17 = (f32[64,512]{1,0:T(8,128)S(1)}, f32[64,512]{1,0:T(8,128)S(1)}, u32[]{:S(2)}, u32[]{:S(2)}) collective-permute-start(f32[64,512]{1,0:T(8,128)S(1)} %dynamic-slice_bitcast_fusion.2), channel_id=1, source_target_pairs={{0,1},{1,0},{2,3},{3,2},{4,5},{5,4},{6,7},{7,6},{8,9},{9,8},{10,11... | collective-permute-start | bytes 393224 | tf_op jit(solution)/shard_map/ppermute | solution.py:319
  (91 shorter events, 22.4 us)
Async XLA Ops:
  6.5 95.8 %all-gather.5.cloned.1.call-start = ((), (), s32[]{:S(2)}) async-start(), calls=%async_computation.4 | async-start | bytes 4718592 | tf_op jit(solution)/shard_map/all_gather | solution.py:269
  11.2 84.9 %copy-start.5 = (s32[32,16]{0,1:T(8,128)S(1)}, s32[32,16]{0,1:T(8,128)}, u32[]{:S(2)}) copy-start(s32[32,16]{0,1:T(8,128)} %param.15) | copy-start | bytes 6148
  11.2 84.9 %copy-start.6 = (s32[32,16]{0,1:T(8,128)S(1)}, s32[32,16]{0,1:T(8,128)}, u32[]{:S(2)}) copy-start(s32[32,16]{0,1:T(8,128)} %param.13) | copy-start | bytes 6148
  17.1 27.0 %all-to-all-start = ((f32[8,2,64,128]{3,2,1,0:T(8,128)}), f32[8,2,64,128]{3,2,1,0:T(8,128)S(1)}, u32[]{:S(2)}, u32[]{:S(2)}) async-start(f32[8,2,64,128]{3,2,1,0:T(8,128)} %fusion.1), calls=%async_computation | async-start | bytes 1048576 | tf_op jit(solution)/shard_map/all_to_all | solution.py:283
  26.1 21.9 %collective-permute-start.1 = (f32[64,2048]{1,0:T(8,128)}, f32[64,2048]{1,0:T(8,128)S(1)}, u32[]{:S(2)}, u32[]{:S(2)}) collective-permute-start(f32[64,2048]{1,0:T(8,128)} %get-tuple-element.27), channel_id=1, source_target_pairs={{0,64},{64,128},{128,192},{192,0},{1,65},{65,129},{129,193},{193,1... | collective-permute-start | bytes 1572872 | tf_op jit(solution)/shard_map/ppermute | solution.py:253
  27.4 4.9 %collective-permute-start = (f32[2,4,16,512]{3,2,1,0:T(8,128)S(1)}, f32[2,4,16,512]{3,2,1,0:T(8,128)S(1)}, u32[]{:S(2)}, u32[]{:S(2)}) collective-permute-start(f32[2,4,16,512]{3,2,1,0:T(8,128)S(1)} %get-tuple-element.60), channel_id=1, source_target_pairs={{0,1},{1,0},{2,3},{3,2},{4,5},{5,4},{6,7},{7,6},{8,9},{9,8},{10,11... | collective-permute-start | bytes 786440 | tf_op jit(solution)/shard_map/ppermute | solution.py:287
  28.7 24.7 %collective-permute-start.2 = (f32[64,2048]{1,0:T(8,128)}, f32[64,2048]{1,0:T(8,128)S(1)}, u32[]{:S(2)}, u32[]{:S(2)}) collective-permute-start(f32[64,2048]{1,0:T(8,128)} %get-tuple-element.30), channel_id=1, source_target_pairs={{0,128},{64,192},{128,0},{192,64},{1,129},{65,193},{129,1},{193,65... | collective-permute-start | bytes 1572872 | tf_op jit(solution)/shard_map/ppermute | solution.py:253
  31.2 23.1 %collective-permute-start.3 = (f32[64,2048]{1,0:T(8,128)}, f32[64,2048]{1,0:T(8,128)S(1)}, u32[]{:S(2)}, u32[]{:S(2)}) collective-permute-start(f32[64,2048]{1,0:T(8,128)} %get-tuple-element.31), channel_id=1, source_target_pairs={{0,192},{64,0},{128,64},{192,128},{1,193},{65,1},{129,65},{193,129... | collective-permute-start | bytes 1572872 | tf_op jit(solution)/shard_map/ppermute | solution.py:253
  44.1 31.7 %collective-permute-start.4 = (f32[8,2,64,128]{3,2,1,0:T(8,128)S(1)}, f32[8,2,64,128]{3,2,1,0:T(8,128)S(1)}, u32[]{:S(2)}, u32[]{:S(2)}) collective-permute-start(f32[8,2,64,128]{3,2,1,0:T(8,128)S(1)} %all-to-all-done.refs_0_), channel_id=1, source_target_pairs={{0,16},{16,32},{32,48},{48,0},{1,17},{17,33},{33,49},{49,1},{2,18}... | collective-permute-start | bytes 1572872 | tf_op jit(solution)/shard_map/ppermute | solution.py:253
  45.4 30.4 %collective-permute-start.5 = (f32[8,2,64,128]{3,2,1,0:T(8,128)S(1)}, f32[8,2,64,128]{3,2,1,0:T(8,128)}, u32[]{:S(2)}, u32[]{:S(2)}) collective-permute-start(f32[8,2,64,128]{3,2,1,0:T(8,128)S(1)} %all-to-all-done.refs_0_), channel_id=1, source_target_pairs={{0,32},{16,48},{32,0},{48,16},{1,33},{17,49},{33,1},{49,17},{2,34}... | collective-permute-start | bytes 1572872 | tf_op jit(solution)/shard_map/ppermute | solution.py:253
  48.0 27.8 %collective-permute-start.6 = (f32[8,2,64,128]{3,2,1,0:T(8,128)S(1)}, f32[8,2,64,128]{3,2,1,0:T(8,128)}, u32[]{:S(2)}, u32[]{:S(2)}) collective-permute-start(f32[8,2,64,128]{3,2,1,0:T(8,128)S(1)} %all-to-all-done.refs_0_), channel_id=1, source_target_pairs={{0,48},{16,0},{32,16},{48,32},{1,49},{17,1},{33,17},{49,33},{2,50}... | collective-permute-start | bytes 1572872 | tf_op jit(solution)/shard_map/ppermute | solution.py:253
  49.1 26.7 %all-to-all-start.1 = ((f32[16,16,512]{2,1,0:T(8,128)}), f32[16,16,512]{2,1,0:T(8,128)S(1)}, u32[]{:S(2)}, u32[]{:S(2)}) async-start(f32[16,16,512]{2,1,0:T(8,128)} %bitcast.18), calls=%async_computation.1 | async-start | bytes 1048576 | tf_op jit(solution)/shard_map/all_to_all | solution.py:291
  53.3 104.8 %all-gather.7.cloned.1.call-start = ((), (), s32[]{:S(2)}) async-start(), calls=%async_computation.5 | async-start | bytes 4718592 | tf_op jit(solution)/shard_map/all_gather | solution.py:294
  97.7 11.5 %collective-permute-start.10 = (f32[8,2,64,128]{3,2,1,0:T(8,128)S(1)}, f32[8,2,64,128]{3,2,1,0:T(8,128)}, u32[]{:S(2)}, u32[]{:S(2)}) collective-permute-start(f32[8,2,64,128]{3,2,1,0:T(8,128)S(1)} %all-to-all-done.refs_0_), channel_id=1, source_target_pairs={{0,1},{1,0},{2,3},{3,2},{4,5},{5,4},{6,7},{7,6},{8,9},{9,8},{10,11... | collective-permute-start | bytes 1572872 | tf_op jit(solution)/shard_map/ppermute | solution.py:297
  101.5 10.1 %collective-permute-start.11 = (f32[8,2,64,128]{3,2,1,0:T(8,128)S(1)}, f32[8,2,64,128]{3,2,1,0:T(8,128)}, u32[]{:S(2)}, u32[]{:S(2)}) collective-permute-start(f32[8,2,64,128]{3,2,1,0:T(8,128)S(1)} %collective-permute-done.4.refs_2_), channel_id=1, source_target_pairs={{0,1},{1,0},{2,3},{3,2},{4,5},{5,4},{6,7},{7,6},{8,9},{9,8},{10,11... | collective-permute-start | bytes 1572872 | tf_op jit(solution)/shard_map/ppermute | solution.py:297
  101.7 12.8 %collective-permute-start.12 = (f32[8,2,64,128]{3,2,1,0:T(8,128)}, f32[8,2,64,128]{3,2,1,0:T(8,128)}, u32[]{:S(2)}, u32[]{:S(2)}) collective-permute-start(f32[8,2,64,128]{3,2,1,0:T(8,128)} %collective-permute-done.5.refs_4_), channel_id=1, source_target_pairs={{0,1},{1,0},{2,3},{3,2},{4,5},{5,4},{6,7},{7,6},{8,9},{9,8},{10,11... | collective-permute-start | bytes 1572872 | tf_op jit(solution)/shard_map/ppermute | solution.py:297
  102.1 12.3 %collective-permute-start.13 = (f32[8,2,64,128]{3,2,1,0:T(8,128)}, f32[8,2,64,128]{3,2,1,0:T(8,128)}, u32[]{:S(2)}, u32[]{:S(2)}) collective-permute-start(f32[8,2,64,128]{3,2,1,0:T(8,128)} %collective-permute-done.6.refs_6_), channel_id=1, source_target_pairs={{0,1},{1,0},{2,3},{3,2},{4,5},{5,4},{6,7},{7,6},{8,9},{9,8},{10,11... | collective-permute-start | bytes 1572872 | tf_op jit(solution)/shard_map/ppermute | solution.py:297
  107.9 6.5 %collective-permute-start.7 = (f32[256,128]{1,0:T(8,128)}, f32[256,128]{1,0:T(8,128)S(1)}, u32[]{:S(2)}, u32[]{:S(2)}) collective-permute-start(f32[256,128]{1,0:T(8,128)} %get-tuple-element.37), channel_id=1, source_target_pairs={{0,64},{64,128},{128,192},{192,0},{1,65},{65,129},{129,193},{193,1... | collective-permute-start | bytes 393224 | tf_op jit(solution)/shard_map/ppermute | solution.py:253
  109.2 8.6 %collective-permute-start.8 = (f32[256,128]{1,0:T(8,128)}, f32[256,128]{1,0:T(8,128)S(1)}, u32[]{:S(2)}, u32[]{:S(2)}) collective-permute-start(f32[256,128]{1,0:T(8,128)} %get-tuple-element.38), channel_id=1, source_target_pairs={{0,128},{64,192},{128,0},{192,64},{1,129},{65,193},{129,1},{193,65... | collective-permute-start | bytes 393224 | tf_op jit(solution)/shard_map/ppermute | solution.py:253
  111.6 6.2 %collective-permute-start.9 = (f32[256,128]{1,0:T(8,128)}, f32[256,128]{1,0:T(8,128)S(1)}, u32[]{:S(2)}, u32[]{:S(2)}) collective-permute-start(f32[256,128]{1,0:T(8,128)} %get-tuple-element.39), channel_id=1, source_target_pairs={{0,192},{64,0},{128,64},{192,128},{1,193},{65,1},{129,65},{193,129... | collective-permute-start | bytes 393224 | tf_op jit(solution)/shard_map/ppermute | solution.py:253
  163.7 6.7 %collective-permute-start.14 = (f32[2,64,512]{2,1,0:T(8,128)}, f32[2,64,512]{2,1,0:T(8,128)S(1)}, u32[]{:S(2)}, u32[]{:S(2)}) collective-permute-start(f32[2,64,512]{2,1,0:T(8,128)} %get-tuple-element.46), channel_id=1, source_target_pairs={{0,64},{64,128},{128,192},{192,0},{1,65},{65,129},{129,193},{193,1... | collective-permute-start | bytes 786440 | tf_op jit(solution)/shard_map/ppermute | solution.py:253
  165.6 11.1 %collective-permute-start.15 = (f32[2,64,512]{2,1,0:T(8,128)}, f32[2,64,512]{2,1,0:T(8,128)S(1)}, u32[]{:S(2)}, u32[]{:S(2)}) collective-permute-start(f32[2,64,512]{2,1,0:T(8,128)} %get-tuple-element.47), channel_id=1, source_target_pairs={{0,128},{64,192},{128,0},{192,64},{1,129},{65,193},{129,1},{193,65... | collective-permute-start | bytes 786440 | tf_op jit(solution)/shard_map/ppermute | solution.py:253
  167.5 9.5 %collective-permute-start.16 = (f32[2,64,512]{2,1,0:T(8,128)}, f32[2,64,512]{2,1,0:T(8,128)S(1)}, u32[]{:S(2)}, u32[]{:S(2)}) collective-permute-start(f32[2,64,512]{2,1,0:T(8,128)} %get-tuple-element.48), channel_id=1, source_target_pairs={{0,192},{64,0},{128,64},{192,128},{1,193},{65,1},{129,65},{193,129... | collective-permute-start | bytes 786440 | tf_op jit(solution)/shard_map/ppermute | solution.py:253
  178.1 4.7 %collective-permute-start.17 = (f32[64,512]{1,0:T(8,128)S(1)}, f32[64,512]{1,0:T(8,128)S(1)}, u32[]{:S(2)}, u32[]{:S(2)}) collective-permute-start(f32[64,512]{1,0:T(8,128)S(1)} %dynamic-slice_bitcast_fusion.2), channel_id=1, source_target_pairs={{0,1},{1,0},{2,3},{3,2},{4,5},{5,4},{6,7},{7,6},{8,9},{9,8},{10,11... | collective-permute-start | bytes 393224 | tf_op jit(solution)/shard_map/ppermute | solution.py:319
  (11 other events, 440.4 us)
Sparse Core Ops, SparseCore 0:
  9.2 38.8 all-gather.4
  94.7 33.6 all-gather.6

commit v7 on v6

--- a/solution.py
+++ b/solution.py
@@ -1,4 +1,3 @@
-import functools
 import math
 
 import jax
@@ -25,24 +24,33 @@
     return high, low
 
 
+def dot(left, right, dims):
+    return lax.dot_general(left, right, dims, preferred_element_type=jnp.float32)
+
+
 def dot3(left, right, dims):
     (lh, ll), (rh, rl) = left, right
-    one = functools.partial(
-        lax.dot_general, dimension_numbers=dims, preferred_element_type=jnp.float32
-    )
-    return one(lh, rh) + (one(lh, rl) + one(ll, rh))
+    return dot(lh, rh, dims) + (dot(lh, rl, dims) + dot(ll, rh, dims))
 
 
 MM = (((1,), (0,)), ((), ()))
 MT = (((1,), (1,)), ((), ()))
 
 
-def pick_kernel(where, rows, *refs):
-    outs, sem = refs[:3], refs[3]
+def pick_kernel(where, rows, keys, values, *refs):
+    outs, sent, sem, kv_sem = refs[:3], refs[3], refs[4], refs[5]
+    x, y, k = where[0], where[1], where[2]
     copies = []
+    for to in range(NZ):
+        cols = pl.ds((to // 2) * HD, HD)
+        for index, cache in enumerate((keys, values)):
+            part = cache.at[pl.ds(pl.multiple_of(y * BLOCK, BLOCK), BLOCK), cols]
+            copies.append(
+                pltpu.make_async_copy(part, sent.at[to, index], kv_sem.at[2 * to + index])
+            )
     for shift in range(1, NX):
-        cols = pl.multiple_of(lax.rem(where[0] + shift, NX) * 2048, 2048)
-        part = rows.at[pl.ds(pl.multiple_of(where[1] * BLOCK, BLOCK), BLOCK), pl.ds(cols, 2048)]
+        cols = pl.multiple_of(lax.rem(x + shift, NX) * 2048, 2048)
+        part = rows.at[pl.ds(pl.multiple_of(k * BLOCK, BLOCK), BLOCK), pl.ds(cols, 2048)]
         copies.append(pltpu.make_async_copy(part, outs[shift - 1], sem.at[shift - 1]))
     for copy in copies:
         copy.start()
@@ -50,21 +58,22 @@
         copy.wait()
 
 
-def pick(where, hidden_rows):
+def pick(where, hidden_rows, key_cache, value_cache):
     return pl.pallas_call(
         pick_kernel,
-        out_shape=[jax.ShapeDtypeStruct((BLOCK, 2048), jnp.float32)] * 3,
-        in_specs=[SMEM, ANY],
-        out_specs=[VMEM] * 3,
-        scratch_shapes=[pltpu.SemaphoreType.DMA((3,))],
+        out_shape=[jax.ShapeDtypeStruct((BLOCK, 2048), jnp.float32)] * 3
+        + [jax.ShapeDtypeStruct((NZ, 2, BLOCK, HD), jnp.float32)],
+        in_specs=[SMEM, ANY, ANY, ANY],
+        out_specs=[VMEM] * 4,
+        scratch_shapes=[pltpu.SemaphoreType.DMA((3,)), pltpu.SemaphoreType.DMA((2 * NZ,))],
         compiler_params=pltpu.CompilerParams(vmem_limit_bytes=LIMIT),
         name="pick",
-    )(where, hidden_rows)
+    )(where, hidden_rows, key_cache, value_cache)
 
 
 def project_kernel(where, rows, first, second, third, weights, *refs):
     outs, (left_buf, right_buf, total_buf, sems) = refs[:NX], refs[NX:]
-    x, k = where[0], where[1]
+    x, k = where[0], where[2]
     copies = []
     for y in range(NY):
         own = rows.at[
@@ -119,12 +128,11 @@
     )(where, rows, *moved, weights)
 
 
-def attend_kernel(first, second, third, fourth, low, up, *refs):
-    pieces, (out, kv, scores, sem) = refs[:8], refs[8:]
-    tiles = len(pieces)
+def attend_kernel(first, second, third, fourth, low, up, gathered, out, kv, scores, sem):
+    tiles = gathered.shape[0]
     copies = [
-        pltpu.make_async_copy(piece, kv.at[tile], sem.at[tile])
-        for tile, piece in enumerate(pieces)
+        pltpu.make_async_copy(gathered.at[tile], kv.at[tile], sem.at[tile])
+        for tile in range(tiles)
     ]
     for copy in copies:
         copy.start()
@@ -133,11 +141,14 @@
     col = lax.broadcasted_iota(jnp.int32, (BLOCK, width), 1)
     lower = row >= lax.rem(col, BLOCK)
     query = (first[...] + second[...]) + (third[...] + fourth[...])
-    left = split(query * (math.log2(math.e) / math.sqrt(HD)))
+    high, low_part = split(query * (math.log2(math.e) / math.sqrt(HD)))
+    both = jnp.concatenate([high, low_part], axis=1)
     top = None
     for tile in range(tiles):
         copies[tile].wait()
-        s = dot3(left, split(kv[tile, :, 0].reshape(width, HD)), MT)
+        key_high, key_low = split(kv[tile, :, 0].reshape(width, HD))
+        s = dot(both, jnp.concatenate([key_high, key_high], axis=1), MT)
+        s = s + dot(high, key_low, MT)
         cols = slice(tile * width, (tile + 1) * width)
         bias = jnp.concatenate(
             [
@@ -153,7 +164,10 @@
     total, summed = None, None
     for tile in range(tiles):
         weight = jnp.exp2(scores[tile] - top)
-        term = dot3(split(weight), split(kv[tile, :, 1].reshape(width, HD)), MM)
+        weight_high, weight_low = split(weight)
+        value_high, value_low = split(kv[tile, :, 1].reshape(width, HD))
+        term = dot(weight_high, jnp.concatenate([value_high, value_low], axis=1), MM)
+        term = term[:, :HD] + (term[:, HD:] + dot(weight_low, value_high, MM))
         total = weight if total is None else total + weight
         summed = term if summed is None else summed + term
     attended = summed / jnp.sum(total, axis=1, keepdims=True)
@@ -161,12 +175,12 @@
         out[z] = attended
 
 
-def attend(partial, low, up, pieces):
+def attend(partial, low, up, gathered):
     rows = NX * BLOCK
     return pl.pallas_call(
         attend_kernel,
         out_shape=jax.ShapeDtypeStruct((NZ, rows, HD), jnp.float32),
-        in_specs=[VMEM] * 6 + [ANY] * 8,
+        in_specs=[VMEM] * 6 + [ANY],
         out_specs=VMEM,
         scratch_shapes=[
             pltpu.VMEM((8, NZ, 2, BLOCK, HD), jnp.float32),
@@ -178,7 +192,7 @@
             flops=12 * 256 * 4096 * HD, bytes_accessed=6 << 20, transcendentals=256 * 4096
         ),
         name="attend",
-    )(*partial, low, up, *pieces)
+    )(*partial, low, up, gathered)
 
 
 def mix_kernel(where, heads, weights, *refs):
@@ -265,21 +279,10 @@
     output_weight,
 ):
     x, y, z, k = (lax.axis_index(name) for name in ALL)
-    where = jnp.stack([x, k]).astype(jnp.int32)
+    where = jnp.stack([x, y, k]).astype(jnp.int32)
     weights = lax.all_gather(query_weight, ("y", "k"), axis=0)
-    picked = pick(where, hidden_rows)
-    hidden = [along("x", part, shift) for shift, part in enumerate(picked, 1)]
-    quarters = [
-        lax.dynamic_slice_in_dim(cache, y * BLOCK, BLOCK, 0)
-        for cache in (key_cache, value_cache)
-    ]
-    sent = jnp.stack(
-        [
-            jnp.stack([quarter[:, (to // 2) * HD : (to // 2 + 1) * HD] for quarter in quarters])
-            for to in range(NZ)
-        ]
-    )
-    sent, _ = lax.optimization_barrier((sent, picked[0]))
+    *picked, sent = pick(where, hidden_rows, key_cache, value_cache)
+    hidden = [along("x", piece, shift) for shift, piece in enumerate(picked, 1)]
     near = lax.all_to_all(sent, "z", 0, 0)
     rows = output_weight.reshape(2, NY, NK, 16, 512)
     kept = lax.dynamic_index_in_dim(rows, k, 2, keepdims=False)
@@ -287,18 +290,14 @@
     taken = lax.ppermute(given, "k", CORES)
     rows = jnp.where(k == 0, jnp.stack([kept, taken]), jnp.stack([taken, kept]))
     rows, near = lax.optimization_barrier((rows, near))
-    quarters = [near] + [along("y", near, shift) for shift in range(1, NY)]
     rows = lax.all_to_all(rows.reshape(NX * NY, 16, 512), ("x", "y"), 0, 0)
-    rows, hidden, quarters = lax.optimization_barrier((rows, hidden, quarters))
     rows = lax.all_to_all(rows.reshape(NZ, NK, 16, 512), "z", 0, 0)
+    kv = lax.all_gather(near, ("y", "k"), axis=0)
     out_weight = lax.all_gather(rows, ("y", "k"), axis=0)
-    pieces = []
-    for piece in quarters:
-        pieces += [piece, lax.ppermute(piece, "k", CORES)]
     partial = project(where, hidden_rows, hidden, weights)
     partial = [partial[0]] + [along("x", partial[s], s) for s in range(1, NX)]
-    key_block = (y - jnp.arange(NY, dtype=jnp.int32))[:, None, None] % NY
-    key_block = key_block + 4 * jnp.stack([k, 1 - k])[None, :, None]
+    key_block = jnp.arange(NY, dtype=jnp.int32)[:, None, None]
+    key_block = key_block + 4 * jnp.arange(NK, dtype=jnp.int32)[None, :, None]
     key_block = key_block + 8 * jnp.arange(NZ, dtype=jnp.int32)[None, None, :]
     low, up = allowed_rows(
         4 * z + x,
@@ -309,7 +308,7 @@
         slash_offsets,
         slash_count,
     )
-    heads = attend(partial, low, up, pieces)
+    heads = attend(partial, low, up, kv)
     heads = lax.all_to_all(heads, "z", 0, 0)
     mixed = mix(where, heads, out_weight)
     mixed = [mixed[0]] + [along("x", mixed[s], s) for s in range(1, NX)]

time: 191 us -> 190 us (level)
  waiting for transfers between devices: 47.3 us -> 81.4 us
  blocking collectives: 49.8 us -> 34.5 us
  starting transfers between devices: 41.8 us -> 26.7 us
  other arithmetic: 10.3 us -> 4.29 us
    ppermute x12 -> x9, waiting for transfers between devices: 13.1 us -> 36 us  [along(): lax.ppermute(value, axis, [(i, (i + shift) % count) for i in range(count)])]
    all_to_all x1, blocking collectives: 31 us -> 16.9 us  [shards(): rows = lax.all_to_all(rows.reshape(NX * NY, 16, 512), ('x', 'y'), 0, 0)]
    ppermute x12 -> x9, starting transfers between devices: 19 us -> 11.7 us  [along(): lax.ppermute(value, axis, [(i, (i + shift) % count) for i in range(count)])]
    all_to_all x1, waiting for transfers between devices: 21.5 us -> 26.8 us  [shards(): heads = lax.all_to_all(heads, 'z', 0, 0)]
    all_to_all x1, waiting for transfers between devices: 10.9 us -> 15.6 us  [shards(): near = lax.all_to_all(sent, 'z', 0, 0)]
    ppermute x4 -> x0, starting transfers between devices: 4.5 us -> none  [shards(): pieces += [piece, lax.ppermute(piece, 'k', CORES)]]
    unnamed x7 -> x0, other arithmetic: 4.38 us -> none
    unnamed x26 -> x32, local copies, waits for them, and re-layouts: 0.73 us -> 3.36 us
  transfers between devices with their start and end apart: 22 -> 16, of which waited for: 8 -> 12; matrix products, arithmetic and copies ran while one was open for 6% -> 3% of each run, Pallas kernels for 9% -> 9%
where the time goes in v7:
time: 190 us; the launch traced here: 189 us
  waiting for transfers between devices  81.4 us (43%)
  blocking collectives  34.5 us (18%)
  starting transfers between devices  26.7 us (14%)
  Pallas kernels  22.5 us (12%)
  between operations  13.4 us (7%)
  local copies, waits for them, and re-layouts  6.35 us (3%)
  other arithmetic  4.29 us (2%)
    ppermute x9, waiting for transfers between devices, along(): lax.ppermute(value, axis, [(i, (i + shift) % count) for i in range(count)])  36 us
    all_to_all x1, waiting for transfers between devices, shards(): heads = lax.all_to_all(heads, 'z', 0, 0)  26.8 us
    all_to_all x1, blocking collectives, shards(): rows = lax.all_to_all(rows.reshape(NZ, NK, 16, 512), 'z', 0, 0)  17.6 us
    all_to_all x1, blocking collectives, shards(): rows = lax.all_to_all(rows.reshape(NX * NY, 16, 512), ('x', 'y'), 0, 0)  16.9 us
    all_to_all x1, waiting for transfers between devices, shards(): near = lax.all_to_all(sent, 'z', 0, 0)  15.6 us
    ppermute x9, starting transfers between devices, along(): lax.ppermute(value, axis, [(i, (i + shift) % count) for i in range(count)])  11.7 us
    all_to_all x1, starting transfers between devices, shards(): near = lax.all_to_all(sent, 'z', 0, 0)  9.16 us
    pallas_call x1, Pallas kernels, attend(): pl.pallas_call(attend_kernel, out_shape=jax.ShapeDtypeStruct((NZ, rows, H...  7.5 us
  transfers between devices with their start and end apart: 16, of which 12 were waited for; matrix products, arithmetic and copies ran while one was open for 3% of the time, Pallas kernels for 9%

profile of v7, /device:TPU:1, one launch (start us, length us, event | category | flops | bytes accessed | tf_op | source)
XLA Modules:
  0.0 189.1 jit_solution(2520724657606106859)
XLA Ops:
  7.9 3.8 %pick.1 = (f32[64,2048]{1,0:T(8,128)}, f32[64,2048]{1,0:T(8,128)}, f32[64,2048]{1,0:T(8,128)}, f32[8,2,64,128]{3,2,1,0:T(8,128)}) custom-call(s32[3]{0:T(128)} %pad_add_fusion.where, f32[128,8192]{1,0:T(8,128)} %rows.3, f32[256,512]{1,0:T(8,128)} %keys.1, f32[256,512]{1,0:T(8,128)} %values.1), custom_call_target="tpu_custom_call" | custom-call | tf_op jit(solution)/shard_map/pick/pallas_call | solution.py:62
  11.8 9.2 %all-to-all-start = ((f32[8,2,64,128]{3,2,1,0:T(8,128)}), f32[8,2,64,128]{3,2,1,0:T(8,128)S(1)}, u32[]{:S(2)}, u32[]{:S(2)}) async-start(f32[8,2,64,128]{3,2,1,0:T(8,128)} %get-tuple-element.26), calls=%async_computation | async-start | bytes 1048576 | tf_op jit(solution)/shard_map/all_to_all | solution.py:286
  21.1 1.0 collective-permute-start.6
  22.1 1.2 collective-permute-done.6
  23.3 15.6 %all-to-all-done = f32[8,2,64,128]{3,2,1,0:T(8,128)S(1)} async-done(((f32[8,2,64,128]{3,2,1,0:T(8,128)}), f32[8,2,64,128]{3,2,1,0:T(8,128)S(1)}, u32[]{:S(2)}, u32[]{:S(2)}) %all-to-all-start) | async-done | bytes 524320 | tf_op jit(solution)/shard_map/all_to_all | solution.py:286
  39.8 16.9 %all_to_all.20 = f32[16,16,512]{2,1,0:T(8,128)S(1)} all-to-all(f32[16,16,512]{2,1,0:T(8,128)S(1)} %bitcast.34), channel_id=1, replica_groups=mesh['x'=4,'y'=4,'z'=8,'k'=2] {'x','y'}, dimensions={0} | all-to-all | bytes 1048576 | tf_op jit(solution)/shard_map/all_to_all | solution.py:293
  56.6 17.6 %all_to_all.21 = f32[8,2,16,512]{3,2,1,0:T(8,128)} all-to-all(f32[8,2,16,512]{3,2,1,0:T(8,128)S(1)} %bitcast.35), channel_id=1, replica_groups=mesh['x'=4,'y'=4,'z'=8,'k'=2] {'z'}, dimensions={0} | all-to-all | bytes 1048576 | tf_op jit(solution)/shard_map/all_to_all | solution.py:294
  74.4 2.3 %collective-permute-start.1 = (f32[64,2048]{1,0:T(8,128)S(1)}, f32[64,2048]{1,0:T(8,128)S(1)}, u32[]{:S(2)}, u32[]{:S(2)}) collective-permute-start(f32[64,2048]{1,0:T(8,128)S(1)} %copy-done.9), channel_id=1, source_target_pairs={{0,128},{64,192},{128,0},{192,64},{1,129},{65,193},{129,1},{193,65... | collective-permute-start | bytes 1572872 | tf_op jit(solution)/shard_map/ppermute | solution.py:267
  80.7 4.8 %collective-permute-done.first = f32[64,2048]{1,0:T(8,128)S(1)} collective-permute-done((f32[64,2048]{1,0:T(8,128)S(1)}, f32[64,2048]{1,0:T(8,128)S(1)}, u32[]{:S(2)}, u32[]{:S(2)}) %collective-permute-start) | collective-permute-done | bytes 524320 | tf_op jit(solution)/shard_map/ppermute | solution.py:267
  85.5 10.7 %collective-permute-done.1.second = f32[64,2048]{1,0:T(8,128)S(1)} collective-permute-done((f32[64,2048]{1,0:T(8,128)S(1)}, f32[64,2048]{1,0:T(8,128)S(1)}, u32[]{:S(2)}, u32[]{:S(2)}) %collective-permute-start.1) | collective-permute-done | bytes 524320 | tf_op jit(solution)/shard_map/ppermute | solution.py:267
  96.2 4.1 %collective-permute-done.2.third = f32[64,2048]{1,0:T(8,128)S(1)} collective-permute-done((f32[64,2048]{1,0:T(8,128)S(1)}, f32[64,2048]{1,0:T(8,128)S(1)}, u32[]{:S(2)}, u32[]{:S(2)}) %collective-permute-start.2) | collective-permute-done | bytes 524320 | tf_op jit(solution)/shard_map/ppermute | solution.py:267
  101.1 5.6 %project.1 = (f32[256,128]{1,0:T(8,128)}, f32[256,128]{1,0:T(8,128)}, f32[256,128]{1,0:T(8,128)}, f32[256,128]{1,0:T(8,128)}) custom-call(s32[3]{0:T(128)} %pad_add_fusion.where, f32[128,8192]{1,0:T(8,128)} %rows.3, f32[64,2048]{1,0:T(8,128)} %copy-done.2, f32[64,2048]{1,0:T(8,128)} %copy-done.3, f32[64,2048]{1,0:T(8,128)} %copy-done.4, f32[8,512,256]{2,1,0:T(8,128)} %bitcast.33), custom_call_target="tpu_custom_call" | custom-call | flops 1610612736 | bytes 7340032 | tf_op jit(solution)/shard_map/project/pallas_call | solution.py:112
  106.6 1.7 collective-permute-start.3
  108.3 3.2 %collective-permute-start.4 = (f32[256,128]{1,0:T(8,128)}, f32[256,128]{1,0:T(8,128)S(1)}, u32[]{:S(2)}, u32[]{:S(2)}) collective-permute-start(f32[256,128]{1,0:T(8,128)} %get-tuple-element.24), channel_id=1, source_target_pairs={{0,128},{64,192},{128,0},{192,64},{1,129},{65,193},{129,1},{193,65... | collective-permute-start | bytes 393224 | tf_op jit(solution)/shard_map/ppermute | solution.py:267
  113.4 4.1 %collective-permute-done.4.third = f32[256,128]{1,0:T(8,128)S(1)} collective-permute-done((f32[256,128]{1,0:T(8,128)}, f32[256,128]{1,0:T(8,128)S(1)}, u32[]{:S(2)}, u32[]{:S(2)}) %collective-permute-start.4) | collective-permute-done | bytes 131104 | tf_op jit(solution)/shard_map/ppermute | solution.py:267
  118.3 7.5 %attend.1 = f32[8,256,128]{2,1,0:T(8,128)} custom-call(f32[256,128]{1,0:T(8,128)} %get-tuple-element.22.first, f32[256,128]{1,0:T(8,128)} %copy-done.11, f32[256,128]{1,0:T(8,128)} %copy-done.12, f32[256,128]{1,0:T(8,128)} %copy-done.13, f32[4,4096]{1,0:T(4,128)} %broadcast_in_dim.39.low, f32[4,4096]{1,0:T(4,128)} %broadcast_in_dim.41.up, ...), custom_call_target="tpu_custom_call" | custom-call | flops 1610612736 | bytes 6291456 | tf_op jit(solution)/shard_map/attend/pallas_call | solution.py:180
  125.8 3.7 %all-to-all-start.1 = ((f32[8,256,128]{2,1,0:T(8,128)}), f32[8,256,128]{2,1,0:T(8,128)S(1)}, u32[]{:S(2)}, u32[]{:S(2)}) async-start(f32[8,256,128]{2,1,0:T(8,128)} %attend.1), calls=%async_computation.1 | async-start | bytes 2097152 | tf_op jit(solution)/shard_map/all_to_all | solution.py:312
  129.6 26.8 %all-to-all-done.1.heads = f32[8,256,128]{2,1,0:T(8,128)S(1)} async-done(((f32[8,256,128]{2,1,0:T(8,128)}), f32[8,256,128]{2,1,0:T(8,128)S(1)}, u32[]{:S(2)}, u32[]{:S(2)}) %all-to-all-start.1) | async-done | bytes 1048608 | tf_op jit(solution)/shard_map/all_to_all | solution.py:312
  157.4 5.7 %mix.1 = (f32[2,64,512]{2,1,0:T(8,128)}, f32[2,64,512]{2,1,0:T(8,128)}, f32[2,64,512]{2,1,0:T(8,128)}, f32[2,64,512]{2,1,0:T(8,128)}) custom-call(s32[3]{0:T(128)} %pad_add_fusion.where, f32[8,256,128]{2,1,0:T(8,128)} %copy-done.1, f32[8,8,2,16,512]{4,3,2,1,0:T(8,128)} %bitcast.38), custom_call_target="tpu_custom_call" | custom-call | flops 1610612736 | bytes 6291456 | tf_op jit(solution)/shard_map/mix/pallas_call | solution.py:227
  163.4 2.7 %collective-permute-start.9 = (f32[2,64,512]{2,1,0:T(8,128)}, f32[2,64,512]{2,1,0:T(8,128)S(1)}, u32[]{:S(2)}, u32[]{:S(2)}) collective-permute-start(f32[2,64,512]{2,1,0:T(8,128)} %get-tuple-element.32), channel_id=1, source_target_pairs={{0,192},{64,0},{128,64},{192,128},{1,193},{65,1},{129,65},{193,129... | collective-permute-start | bytes 786440 | tf_op jit(solution)/shard_map/ppermute | solution.py:267
  166.6 5.6 %collective-permute-done.8 = f32[2,64,512]{2,1,0:T(8,128)S(1)} collective-permute-done((f32[2,64,512]{2,1,0:T(8,128)}, f32[2,64,512]{2,1,0:T(8,128)S(1)}, u32[]{:S(2)}, u32[]{:S(2)}) %collective-permute-start.8) | collective-permute-done | bytes 262176 | tf_op jit(solution)/shard_map/ppermute | solution.py:267
  172.2 6.2 %collective-permute-done.9 = f32[2,64,512]{2,1,0:T(8,128)S(1)} collective-permute-done((f32[2,64,512]{2,1,0:T(8,128)}, f32[2,64,512]{2,1,0:T(8,128)S(1)}, u32[]{:S(2)}, u32[]{:S(2)}) %collective-permute-start.9) | collective-permute-done | bytes 262176 | tf_op jit(solution)/shard_map/ppermute | solution.py:267
  178.7 1.0 add_add_fusion
  179.8 1.1 collective-permute-start.10
  (76 shorter events, 13.8 us)
Async XLA Ops:
  6.5 93.7 %all-gather.7.cloned.1.call-start = ((), (), s32[]{:S(2)}) async-start(), calls=%async_computation.4 | async-start | bytes 4718592 | tf_op jit(solution)/shard_map/all_gather | solution.py:283
  11.7 62.6 %copy-start.10 = (f32[64,2048]{1,0:T(8,128)S(1)}, f32[64,2048]{1,0:T(8,128)}, u32[]{:S(2)}) copy-start(f32[64,2048]{1,0:T(8,128)} %get-tuple-element.19) | copy-start | bytes 1572868
  11.7 62.7 %copy-start.9 = (f32[64,2048]{1,0:T(8,128)S(1)}, f32[64,2048]{1,0:T(8,128)}, u32[]{:S(2)}) copy-start(f32[64,2048]{1,0:T(8,128)} %get-tuple-element.20) | copy-start | bytes 1572868
  11.7 65.0 %copy-start.8 = (f32[64,2048]{1,0:T(8,128)S(1)}, f32[64,2048]{1,0:T(8,128)}, u32[]{:S(2)}) copy-start(f32[64,2048]{1,0:T(8,128)} %get-tuple-element.21) | copy-start | bytes 1572868
  11.7 66.0 %copy-start.14 = (s32[32]{0:T(128)S(1)}, s32[32]{0:T(128)}, u32[]{:S(2)}) copy-start(s32[32]{0:T(128)} %param.14) | copy-start | bytes 388
  11.8 66.6 %copy-start.15 = (s32[32]{0:T(128)S(1)}, s32[32]{0:T(128)}, u32[]{:S(2)}) copy-start(s32[32]{0:T(128)} %param.16) | copy-start | bytes 388
  11.8 67.2 %copy-start.6 = (s32[32,16]{0,1:T(8,128)S(1)}, s32[32,16]{0,1:T(8,128)}, u32[]{:S(2)}) copy-start(s32[32,16]{0,1:T(8,128)} %param.15) | copy-start | bytes 6148
  11.8 67.2 %copy-start.7 = (s32[32,16]{0,1:T(8,128)S(1)}, s32[32,16]{0,1:T(8,128)}, u32[]{:S(2)}) copy-start(s32[32,16]{0,1:T(8,128)} %param.13) | copy-start | bytes 6148
  11.8 27.1 %all-to-all-start = ((f32[8,2,64,128]{3,2,1,0:T(8,128)}), f32[8,2,64,128]{3,2,1,0:T(8,128)S(1)}, u32[]{:S(2)}, u32[]{:S(2)}) async-start(f32[8,2,64,128]{3,2,1,0:T(8,128)} %get-tuple-element.26), calls=%async_computation | async-start | bytes 1048576 | tf_op jit(solution)/shard_map/all_to_all | solution.py:286
  20.9 96.6 %all-gather.9.cloned.1.call-start = ((), (), s32[]{:S(2)}) async-start(), calls=%async_computation.5 | async-start | bytes 4718592 | tf_op jit(solution)/shard_map/all_gather | solution.py:295
  21.1 2.2 %collective-permute-start.6 = (f32[2,4,16,512]{3,2,1,0:T(8,128)S(1)}, f32[2,4,16,512]{3,2,1,0:T(8,128)S(1)}, u32[]{:S(2)}, u32[]{:S(2)}) collective-permute-start(f32[2,4,16,512]{3,2,1,0:T(8,128)S(1)} %get-tuple-element.36), channel_id=1, source_target_pairs={{0,1},{1,0},{2,3},{3,2},{4,5},{5,4},{6,7},{7,6},{8,9},{9,8},{10,11... | collective-permute-start | bytes 786440 | tf_op jit(solution)/shard_map/ppermute | solution.py:290
  39.7 89.9 %all-gather.11.cloned.1.call-start = ((), (), s32[]{:S(2)}) async-start(), calls=%async_computation.6 | async-start | bytes 4718592 | tf_op jit(solution)/shard_map/all_gather | solution.py:296
  74.3 11.2 %collective-permute-start = (f32[64,2048]{1,0:T(8,128)S(1)}, f32[64,2048]{1,0:T(8,128)S(1)}, u32[]{:S(2)}, u32[]{:S(2)}) collective-permute-start(f32[64,2048]{1,0:T(8,128)S(1)} %copy-done.10), channel_id=1, source_target_pairs={{0,64},{64,128},{128,192},{192,0},{1,65},{65,129},{129,193},{193,1... | collective-permute-start | bytes 1572872 | tf_op jit(solution)/shard_map/ppermute | solution.py:267
  74.4 21.8 %collective-permute-start.1 = (f32[64,2048]{1,0:T(8,128)S(1)}, f32[64,2048]{1,0:T(8,128)S(1)}, u32[]{:S(2)}, u32[]{:S(2)}) collective-permute-start(f32[64,2048]{1,0:T(8,128)S(1)} %copy-done.9), channel_id=1, source_target_pairs={{0,128},{64,192},{128,0},{192,64},{1,129},{65,193},{129,1},{193,65... | collective-permute-start | bytes 1572872 | tf_op jit(solution)/shard_map/ppermute | solution.py:267
  76.7 23.5 %collective-permute-start.2 = (f32[64,2048]{1,0:T(8,128)S(1)}, f32[64,2048]{1,0:T(8,128)S(1)}, u32[]{:S(2)}, u32[]{:S(2)}) collective-permute-start(f32[64,2048]{1,0:T(8,128)S(1)} %copy-done.8), channel_id=1, source_target_pairs={{0,192},{64,0},{128,64},{192,128},{1,193},{65,1},{129,65},{193,129... | collective-permute-start | bytes 1572872 | tf_op jit(solution)/shard_map/ppermute | solution.py:267
  85.5 14.8 %copy-start.2 = (f32[64,2048]{1,0:T(8,128)}, f32[64,2048]{1,0:T(8,128)S(1)}, u32[]{:S(2)}) copy-start(f32[64,2048]{1,0:T(8,128)S(1)} %collective-permute-done.first) | copy-start | bytes 1572868
  106.6 6.8 %collective-permute-start.3 = (f32[256,128]{1,0:T(8,128)}, f32[256,128]{1,0:T(8,128)S(1)}, u32[]{:S(2)}, u32[]{:S(2)}) collective-permute-start(f32[256,128]{1,0:T(8,128)} %get-tuple-element.23), channel_id=1, source_target_pairs={{0,64},{64,128},{128,192},{192,0},{1,65},{65,129},{129,193},{193,1... | collective-permute-start | bytes 393224 | tf_op jit(solution)/shard_map/ppermute | solution.py:267
  108.3 9.3 %collective-permute-start.4 = (f32[256,128]{1,0:T(8,128)}, f32[256,128]{1,0:T(8,128)S(1)}, u32[]{:S(2)}, u32[]{:S(2)}) collective-permute-start(f32[256,128]{1,0:T(8,128)} %get-tuple-element.24), channel_id=1, source_target_pairs={{0,128},{64,192},{128,0},{192,64},{1,129},{65,193},{129,1},{193,65... | collective-permute-start | bytes 393224 | tf_op jit(solution)/shard_map/ppermute | solution.py:267
  111.5 6.1 %collective-permute-start.5 = (f32[256,128]{1,0:T(8,128)}, f32[256,128]{1,0:T(8,128)S(1)}, u32[]{:S(2)}, u32[]{:S(2)}) collective-permute-start(f32[256,128]{1,0:T(8,128)} %get-tuple-element.25), channel_id=1, source_target_pairs={{0,192},{64,0},{128,64},{192,128},{1,193},{65,1},{129,65},{193,129... | collective-permute-start | bytes 393224 | tf_op jit(solution)/shard_map/ppermute | solution.py:267
  125.8 30.6 %all-to-all-start.1 = ((f32[8,256,128]{2,1,0:T(8,128)}), f32[8,256,128]{2,1,0:T(8,128)S(1)}, u32[]{:S(2)}, u32[]{:S(2)}) async-start(f32[8,256,128]{2,1,0:T(8,128)} %attend.1), calls=%async_computation.1 | async-start | bytes 2097152 | tf_op jit(solution)/shard_map/all_to_all | solution.py:312
  163.1 9.1 %collective-permute-start.8 = (f32[2,64,512]{2,1,0:T(8,128)}, f32[2,64,512]{2,1,0:T(8,128)S(1)}, u32[]{:S(2)}, u32[]{:S(2)}) collective-permute-start(f32[2,64,512]{2,1,0:T(8,128)} %get-tuple-element.31), channel_id=1, source_target_pairs={{0,128},{64,192},{128,0},{192,64},{1,129},{65,193},{129,1},{193,65... | collective-permute-start | bytes 786440 | tf_op jit(solution)/shard_map/ppermute | solution.py:267
  163.4 15.0 %collective-permute-start.9 = (f32[2,64,512]{2,1,0:T(8,128)}, f32[2,64,512]{2,1,0:T(8,128)S(1)}, u32[]{:S(2)}, u32[]{:S(2)}) collective-permute-start(f32[2,64,512]{2,1,0:T(8,128)} %get-tuple-element.32), channel_id=1, source_target_pairs={{0,192},{64,0},{128,64},{192,128},{1,193},{65,1},{129,65},{193,129... | collective-permute-start | bytes 786440 | tf_op jit(solution)/shard_map/ppermute | solution.py:267
  166.1 12.6 %collective-permute-start.7 = (f32[2,64,512]{2,1,0:T(8,128)}, f32[2,64,512]{2,1,0:T(8,128)S(1)}, u32[]{:S(2)}, u32[]{:S(2)}) collective-permute-start(f32[2,64,512]{2,1,0:T(8,128)} %get-tuple-element.30), channel_id=1, source_target_pairs={{0,64},{64,128},{128,192},{192,0},{1,65},{65,129},{129,193},{193,1... | collective-permute-start | bytes 786440 | tf_op jit(solution)/shard_map/ppermute | solution.py:267
  179.8 2.1 %collective-permute-start.10 = (f32[64,512]{1,0:T(8,128)S(1)}, f32[64,512]{1,0:T(8,128)S(1)}, u32[]{:S(2)}, u32[]{:S(2)}) collective-permute-start(f32[64,512]{1,0:T(8,128)S(1)} %dynamic-slice_bitcast_fusion.2), channel_id=1, source_target_pairs={{0,1},{1,0},{2,3},{3,2},{4,5},{5,4},{6,7},{7,6},{8,9},{9,8},{10,11... | collective-permute-start | bytes 393224 | tf_op jit(solution)/shard_map/ppermute | solution.py:318
  (8 other events, 26.7 us)
Sparse Core Ops, SparseCore 0:
  9.2 38.8 all-gather.6
  50.0 40.2 all-gather.8
  92.2 34.6 all-gather.10

commit v8 on v7

--- a/solution.py
+++ b/solution.py
@@ -201,15 +201,20 @@
     copies = []
     for step in range(steps):
         copies.append(
-            pltpu.make_async_copy(
-                weights.at[:, pl.ds(2 * step, 2)], buf.at[step], sem.at[step]
-            )
+            [
+                pltpu.make_async_copy(
+                    weights.at[part, pl.ds(2 * step, 2)], buf.at[step, part], sem.at[step, part]
+                )
+                for part in range(8)
+            ]
         )
-        copies[step].start()
+        for copy in copies[step]:
+            copy.start()
     totals = [None, None]
     for step in range(steps):
         left = split(jnp.concatenate([heads[2 * step], heads[2 * step + 1]], axis=1))
-        copies[step].wait()
+        for copy in copies[step]:
+            copy.wait()
         for core in range(NK):
             right = jnp.concatenate(
                 [buf[step, :, z, core].reshape(HD, 512) for z in range(2)], axis=0
@@ -232,7 +237,7 @@
         scratch_shapes=[
             pltpu.VMEM((NX, NK, BLOCK, 512), jnp.float32),
             pltpu.VMEM((NZ // 2, 8, 2, NK, 16, 512), jnp.float32),
-            pltpu.SemaphoreType.DMA((NZ // 2,)),
+            pltpu.SemaphoreType.DMA((NZ // 2, 8)),
         ],
         compiler_params=pltpu.CompilerParams(vmem_limit_bytes=LIMIT),
         cost_estimate=pl.CostEstimate(
@@ -291,6 +296,7 @@
     rows = jnp.where(k == 0, jnp.stack([kept, taken]), jnp.stack([taken, kept]))
     rows, near = lax.optimization_barrier((rows, near))
     rows = lax.all_to_all(rows.reshape(NX * NY, 16, 512), ("x", "y"), 0, 0)
+    rows, hidden = lax.optimization_barrier((rows, hidden))
     rows = lax.all_to_all(rows.reshape(NZ, NK, 16, 512), "z", 0, 0)
     kv = lax.all_gather(near, ("y", "k"), axis=0)
     out_weight = lax.all_gather(rows, ("y", "k"), axis=0)

time: 190 us -> 184 us (0.968)
  blocking collectives: 34.5 us -> 17.5 us
  starting transfers between devices: 26.7 us -> 36.8 us
    all_to_all x1 -> x0, blocking collectives: 16.9 us -> none  [shards(): rows = lax.all_to_all(rows.reshape(NX * NY, 16, 512), ('x', 'y'), 0, 0)]
    ppermute x9, waiting for transfers between devices: 36 us -> 29.1 us  [along(): lax.ppermute(value, axis, [(i, (i + shift) % count) for i in range(count)])]
    all_to_all x0 -> x1, waiting for transfers between devices: none -> 6.7 us  [shards(): rows = lax.all_to_all(rows.reshape(NX * NY, 16, 512), ('x', 'y'), 0, 0)]
    all_to_all x0 -> x1, starting transfers between devices: none -> 4.34 us  [shards(): rows = lax.all_to_all(rows.reshape(NX * NY, 16, 512), ('x', 'y'), 0, 0)]
    all_to_all x1, waiting for transfers between devices: 26.8 us -> 23.1 us  [shards(): heads = lax.all_to_all(heads, 'z', 0, 0)]
    all_gather x1, waiting for transfers between devices: 0.02 us -> 3.72 us  [shards(): out_weight = lax.all_gather(rows, ('y', 'k'), axis=0)]
    ppermute x9, starting transfers between devices: 11.7 us -> 14.8 us  [along(): lax.ppermute(value, axis, [(i, (i + shift) % count) for i in range(count)])]
    ppermute x1, starting transfers between devices: 1.07 us -> 3.01 us  [shards(): other = lax.ppermute(other, 'k', CORES)]
  transfers between devices with their start and end apart: 16 -> 17, of which waited for: 12 -> 13; matrix products, arithmetic and copies ran while one was open for 3% -> 4% of each run, Pallas kernels for 9% -> 9%
where the time goes in v8:
time: 184 us; the launch traced here: 181 us
  waiting for transfers between devices  80.3 us (44%)
  starting transfers between devices  36.8 us (20%)
  Pallas kernels  22.6 us (12%)
  blocking collectives  17.5 us (10%)
  between operations  13.3 us (7%)
  local copies, waits for them, and re-layouts  5.65 us (3%)
  other arithmetic  5.15 us (3%)
    ppermute x9, waiting for transfers between devices, along(): lax.ppermute(value, axis, [(i, (i + shift) % count) for i in range(count)])  29.1 us
    all_to_all x1, waiting for transfers between devices, shards(): heads = lax.all_to_all(heads, 'z', 0, 0)  23.1 us
    all_to_all x1, blocking collectives, shards(): rows = lax.all_to_all(rows.reshape(NZ, NK, 16, 512), 'z', 0, 0)  17.5 us
    ppermute x9, starting transfers between devices, along(): lax.ppermute(value, axis, [(i, (i + shift) % count) for i in range(count)])  14.8 us
    all_to_all x1, waiting for transfers between devices, shards(): near = lax.all_to_all(sent, 'z', 0, 0)  14.8 us
    all_to_all x1, starting transfers between devices, shards(): near = lax.all_to_all(sent, 'z', 0, 0)  9.16 us
    pallas_call x1, Pallas kernels, attend(): pl.pallas_call(attend_kernel, out_shape=jax.ShapeDtypeStruct((NZ, rows, H...  7.5 us
    all_to_all x1, waiting for transfers between devices, shards(): rows = lax.all_to_all(rows.reshape(NX * NY, 16, 512), ('x', 'y'), 0, 0)  6.7 us
  transfers between devices with their start and end apart: 17, of which 13 were waited for; matrix products, arithmetic and copies ran while one was open for 4% of the time, Pallas kernels for 9%

profile of v8, /device:TPU:1, one launch (start us, length us, event | category | flops | bytes accessed | tf_op | source)
XLA Modules:
  0.0 181.3 jit_solution(2054446189988014500)
XLA Ops:
  7.9 3.8 %pick.1 = (f32[64,2048]{1,0:T(8,128)}, f32[64,2048]{1,0:T(8,128)}, f32[64,2048]{1,0:T(8,128)}, f32[8,2,64,128]{3,2,1,0:T(8,128)}) custom-call(s32[3]{0:T(128)} %pad_add_fusion.where, f32[128,8192]{1,0:T(8,128)} %rows.3, f32[256,512]{1,0:T(8,128)} %keys.1, f32[256,512]{1,0:T(8,128)} %values.1), custom_call_target="tpu_custom_call" | custom-call | tf_op jit(solution)/shard_map/pick/pallas_call | solution.py:62
  11.8 9.2 %all-to-all-start = ((f32[8,2,64,128]{3,2,1,0:T(8,128)}), f32[8,2,64,128]{3,2,1,0:T(8,128)S(1)}, u32[]{:S(2)}, u32[]{:S(2)}) async-start(f32[8,2,64,128]{3,2,1,0:T(8,128)} %get-tuple-element.23), calls=%async_computation | async-start | bytes 1048576 | tf_op jit(solution)/shard_map/all_to_all | solution.py:291
  24.1 14.8 %all-to-all-done = f32[8,2,64,128]{3,2,1,0:T(8,128)S(1)} async-done(((f32[8,2,64,128]{3,2,1,0:T(8,128)}), f32[8,2,64,128]{3,2,1,0:T(8,128)S(1)}, u32[]{:S(2)}, u32[]{:S(2)}) %all-to-all-start) | async-done | bytes 524320 | tf_op jit(solution)/shard_map/all_to_all | solution.py:291
  39.7 1.3 collective-permute-start.1
  41.0 2.5 %collective-permute-start.2 = (f32[64,2048]{1,0:T(8,128)}, f32[64,2048]{1,0:T(8,128)S(1)}, u32[]{:S(2)}, u32[]{:S(2)}) collective-permute-start(f32[64,2048]{1,0:T(8,128)} %get-tuple-element.26), channel_id=1, source_target_pairs={{0,128},{64,192},{128,0},{192,64},{1,129},{65,193},{129,1},{193,65... | collective-permute-start | bytes 1572872 | tf_op jit(solution)/shard_map/ppermute | solution.py:272
  44.6 4.3 %all-to-all-start.1 = ((f32[16,16,512]{2,1,0:T(8,128)}), f32[16,16,512]{2,1,0:T(8,128)S(1)}, u32[]{:S(2)}, u32[]{:S(2)}) async-start(f32[16,16,512]{2,1,0:T(8,128)} %bitcast.7), calls=%async_computation.1 | async-start | bytes 1048576 | tf_op jit(solution)/shard_map/all_to_all | solution.py:298
  49.0 5.2 %collective-permute-done.1.first = f32[64,2048]{1,0:T(8,128)S(1)} collective-permute-done((f32[64,2048]{1,0:T(8,128)}, f32[64,2048]{1,0:T(8,128)S(1)}, u32[]{:S(2)}, u32[]{:S(2)}) %collective-permute-start.1) | collective-permute-done | bytes 524320 | tf_op jit(solution)/shard_map/ppermute | solution.py:272
  54.2 12.3 %collective-permute-done.2.second = f32[64,2048]{1,0:T(8,128)S(1)} collective-permute-done((f32[64,2048]{1,0:T(8,128)}, f32[64,2048]{1,0:T(8,128)S(1)}, u32[]{:S(2)}, u32[]{:S(2)}) %collective-permute-start.2) | collective-permute-done | bytes 524320 | tf_op jit(solution)/shard_map/ppermute | solution.py:272
  66.5 6.7 %all-to-all-done.1 = f32[16,16,512]{2,1,0:T(8,128)S(1)} async-done(((f32[16,16,512]{2,1,0:T(8,128)}), f32[16,16,512]{2,1,0:T(8,128)S(1)}, u32[]{:S(2)}, u32[]{:S(2)}) %all-to-all-start.1) | async-done | bytes 524320 | tf_op jit(solution)/shard_map/all_to_all | solution.py:298
  73.2 17.5 %all_to_all.20 = f32[8,2,16,512]{3,2,1,0:T(8,128)} all-to-all(f32[8,2,16,512]{3,2,1,0:T(8,128)S(1)} %bitcast.34), channel_id=1, replica_groups=mesh['x'=4,'y'=4,'z'=8,'k'=2] {'z'}, dimensions={0} | all-to-all | bytes 1048576 | tf_op jit(solution)/shard_map/all_to_all | solution.py:300
  94.2 5.3 %project.1 = (f32[256,128]{1,0:T(8,128)}, f32[256,128]{1,0:T(8,128)}, f32[256,128]{1,0:T(8,128)}, f32[256,128]{1,0:T(8,128)}) custom-call(s32[3]{0:T(128)} %pad_add_fusion.where, f32[128,8192]{1,0:T(8,128)} %rows.3, f32[64,2048]{1,0:T(8,128)} %copy-done.2, f32[64,2048]{1,0:T(8,128)} %copy-done.3, f32[64,2048]{1,0:T(8,128)} %copy-done.4, f32[8,512,256]{2,1,0:T(8,128)} %bitcast.33), custom_call_target="tpu_custom_call" | custom-call | flops 1610612736 | bytes 7340032 | tf_op jit(solution)/shard_map/project/pallas_call | solution.py:112
  100.4 4.3 %collective-permute-start.5 = (f32[256,128]{1,0:T(8,128)}, f32[256,128]{1,0:T(8,128)S(1)}, u32[]{:S(2)}, u32[]{:S(2)}) collective-permute-start(f32[256,128]{1,0:T(8,128)} %get-tuple-element.33), channel_id=1, source_target_pairs={{0,128},{64,192},{128,0},{192,64},{1,129},{65,193},{129,1},{193,65... | collective-permute-start | bytes 393224 | tf_op jit(solution)/shard_map/ppermute | solution.py:272
  106.4 2.4 %collective-permute-done.5.third = f32[256,128]{1,0:T(8,128)S(1)} collective-permute-done((f32[256,128]{1,0:T(8,128)}, f32[256,128]{1,0:T(8,128)S(1)}, u32[]{:S(2)}, u32[]{:S(2)}) %collective-permute-start.5) | collective-permute-done | bytes 131104 | tf_op jit(solution)/shard_map/ppermute | solution.py:272
  109.8 7.5 %attend.1 = f32[8,256,128]{2,1,0:T(8,128)} custom-call(f32[256,128]{1,0:T(8,128)} %get-tuple-element.31.first, f32[256,128]{1,0:T(8,128)} %copy-done.8, f32[256,128]{1,0:T(8,128)} %copy-done.9, f32[256,128]{1,0:T(8,128)} %copy-done.10, f32[4,4096]{1,0:T(4,128)} %broadcast_in_dim.39.low, f32[4,4096]{1,0:T(4,128)} %broadcast_in_dim.41.up, ...), custom_call_target="tpu_custom_call" | custom-call | flops 1610612736 | bytes 6291456 | tf_op jit(solution)/shard_map/attend/pallas_call | solution.py:180
  117.3 4.3 %all-to-all-start.2 = ((f32[8,256,128]{2,1,0:T(8,128)}), f32[8,256,128]{2,1,0:T(8,128)S(1)}, u32[]{:S(2)}, u32[]{:S(2)}) async-start(f32[8,256,128]{2,1,0:T(8,128)} %attend.1), calls=%async_computation.2 | async-start | bytes 2097152 | tf_op jit(solution)/shard_map/all_to_all | solution.py:318
  121.7 3.7 %all-gather.11.cloned.1.call-done = f32[64,2,16,512]{3,2,1,0:T(8,128)} async-done(((f32[8,2,16,512]{3,2,1,0:T(8,128)}), f32[64,2,16,512]{3,2,1,0:T(8,128)}) %all-gather.11.cloned.1.call-update) | async-done | bytes 4194320 | tf_op jit(solution)/shard_map/all_gather | solution.py:302
  125.4 23.1 %all-to-all-done.2.heads = f32[8,256,128]{2,1,0:T(8,128)S(1)} async-done(((f32[8,256,128]{2,1,0:T(8,128)}), f32[8,256,128]{2,1,0:T(8,128)S(1)}, u32[]{:S(2)}, u32[]{:S(2)}) %all-to-all-start.2) | async-done | bytes 1048608 | tf_op jit(solution)/shard_map/all_to_all | solution.py:318
  149.5 6.0 %mix.1 = (f32[2,64,512]{2,1,0:T(8,128)}, f32[2,64,512]{2,1,0:T(8,128)}, f32[2,64,512]{2,1,0:T(8,128)}, f32[2,64,512]{2,1,0:T(8,128)}) custom-call(s32[3]{0:T(128)} %pad_add_fusion.where, f32[8,256,128]{2,1,0:T(8,128)} %copy-done.1, f32[8,8,2,16,512]{4,3,2,1,0:T(8,128)} %bitcast.38), custom_call_target="tpu_custom_call" | custom-call | flops 1610612736 | bytes 6291456 | tf_op jit(solution)/shard_map/mix/pallas_call | solution.py:232
  155.5 2.2 %collective-permute-start.7 = (f32[2,64,512]{2,1,0:T(8,128)}, f32[2,64,512]{2,1,0:T(8,128)S(1)}, u32[]{:S(2)}, u32[]{:S(2)}) collective-permute-start(f32[2,64,512]{2,1,0:T(8,128)} %get-tuple-element.38), channel_id=1, source_target_pairs={{0,64},{64,128},{128,192},{192,0},{1,65},{65,129},{129,193},{193,1... | collective-permute-start | bytes 786440 | tf_op jit(solution)/shard_map/ppermute | solution.py:272
  158.6 1.6 collective-permute-start.9
  160.2 2.0 %collective-permute-done.7 = f32[2,64,512]{2,1,0:T(8,128)S(1)} collective-permute-done((f32[2,64,512]{2,1,0:T(8,128)}, f32[2,64,512]{2,1,0:T(8,128)S(1)}, u32[]{:S(2)}, u32[]{:S(2)}) %collective-permute-start.7) | collective-permute-done | bytes 262176 | tf_op jit(solution)/shard_map/ppermute | solution.py:272
  162.2 5.2 %collective-permute-done.8 = f32[2,64,512]{2,1,0:T(8,128)S(1)} collective-permute-done((f32[2,64,512]{2,1,0:T(8,128)}, f32[2,64,512]{2,1,0:T(8,128)S(1)}, u32[]{:S(2)}, u32[]{:S(2)}) %collective-permute-start.8) | collective-permute-done | bytes 262176 | tf_op jit(solution)/shard_map/ppermute | solution.py:272
  167.4 1.6 collective-permute-done.9
  170.0 3.0 %collective-permute-start.10 = (f32[64,512]{1,0:T(8,128)S(1)}, f32[64,512]{1,0:T(8,128)S(1)}, u32[]{:S(2)}, u32[]{:S(2)}) collective-permute-start(f32[64,512]{1,0:T(8,128)S(1)} %dynamic-slice_bitcast_fusion.2), channel_id=1, source_target_pairs={{0,1},{1,0},{2,3},{3,2},{4,5},{5,4},{6,7},{7,6},{8,9},{9,8},{10,11... | collective-permute-start | bytes 393224 | tf_op jit(solution)/shard_map/ppermute | solution.py:324
  (71 shorter events, 18.3 us)
Async XLA Ops:
  6.5 87.6 %all-gather.7.cloned.1.call-start = ((), (), s32[]{:S(2)}) async-start(), calls=%async_computation.4 | async-start | bytes 4718592 | tf_op jit(solution)/shard_map/all_gather | solution.py:288
  11.7 79.1 %copy-start.11 = (s32[32]{0:T(128)S(1)}, s32[32]{0:T(128)}, u32[]{:S(2)}) copy-start(s32[32]{0:T(128)} %param.14) | copy-start | bytes 388
  11.7 79.7 %copy-start.12 = (s32[32]{0:T(128)S(1)}, s32[32]{0:T(128)}, u32[]{:S(2)}) copy-start(s32[32]{0:T(128)} %param.16) | copy-start | bytes 388
  11.7 80.5 %copy-start.6 = (s32[32,16]{0,1:T(8,128)S(1)}, s32[32,16]{0,1:T(8,128)}, u32[]{:S(2)}) copy-start(s32[32,16]{0,1:T(8,128)} %param.15) | copy-start | bytes 6148
  11.7 80.5 %copy-start.7 = (s32[32,16]{0,1:T(8,128)S(1)}, s32[32,16]{0,1:T(8,128)}, u32[]{:S(2)}) copy-start(s32[32,16]{0,1:T(8,128)} %param.13) | copy-start | bytes 6148
  11.8 27.1 %all-to-all-start = ((f32[8,2,64,128]{3,2,1,0:T(8,128)}), f32[8,2,64,128]{3,2,1,0:T(8,128)S(1)}, u32[]{:S(2)}, u32[]{:S(2)}) async-start(f32[8,2,64,128]{3,2,1,0:T(8,128)} %get-tuple-element.23), calls=%async_computation | async-start | bytes 1048576 | tf_op jit(solution)/shard_map/all_to_all | solution.py:291
  20.9 88.2 %all-gather.9.cloned.1.call-start = ((), (), s32[]{:S(2)}) async-start(), calls=%async_computation.5 | async-start | bytes 4718592 | tf_op jit(solution)/shard_map/all_gather | solution.py:301
  21.0 2.2 %collective-permute-start = (f32[2,4,16,512]{3,2,1,0:T(8,128)S(1)}, f32[2,4,16,512]{3,2,1,0:T(8,128)S(1)}, u32[]{:S(2)}, u32[]{:S(2)}) collective-permute-start(f32[2,4,16,512]{3,2,1,0:T(8,128)S(1)} %get-tuple-element.44), channel_id=1, source_target_pairs={{0,1},{1,0},{2,3},{3,2},{4,5},{5,4},{6,7},{7,6},{8,9},{9,8},{10,11... | collective-permute-start | bytes 786440 | tf_op jit(solution)/shard_map/ppermute | solution.py:295
  39.7 14.5 %collective-permute-start.1 = (f32[64,2048]{1,0:T(8,128)}, f32[64,2048]{1,0:T(8,128)S(1)}, u32[]{:S(2)}, u32[]{:S(2)}) collective-permute-start(f32[64,2048]{1,0:T(8,128)} %get-tuple-element.25), channel_id=1, source_target_pairs={{0,64},{64,128},{128,192},{192,0},{1,65},{65,129},{129,193},{193,1... | collective-permute-start | bytes 1572872 | tf_op jit(solution)/shard_map/ppermute | solution.py:272
  41.0 25.5 %collective-permute-start.2 = (f32[64,2048]{1,0:T(8,128)}, f32[64,2048]{1,0:T(8,128)S(1)}, u32[]{:S(2)}, u32[]{:S(2)}) collective-permute-start(f32[64,2048]{1,0:T(8,128)} %get-tuple-element.26), channel_id=1, source_target_pairs={{0,128},{64,192},{128,0},{192,64},{1,129},{65,193},{129,1},{193,65... | collective-permute-start | bytes 1572872 | tf_op jit(solution)/shard_map/ppermute | solution.py:272
  43.5 23.1 %collective-permute-start.3 = (f32[64,2048]{1,0:T(8,128)}, f32[64,2048]{1,0:T(8,128)S(1)}, u32[]{:S(2)}, u32[]{:S(2)}) collective-permute-start(f32[64,2048]{1,0:T(8,128)} %get-tuple-element.27), channel_id=1, source_target_pairs={{0,192},{64,0},{128,64},{192,128},{1,193},{65,1},{129,65},{193,129... | collective-permute-start | bytes 1572872 | tf_op jit(solution)/shard_map/ppermute | solution.py:272
  44.6 28.6 %all-to-all-start.1 = ((f32[16,16,512]{2,1,0:T(8,128)}), f32[16,16,512]{2,1,0:T(8,128)S(1)}, u32[]{:S(2)}, u32[]{:S(2)}) async-start(f32[16,16,512]{2,1,0:T(8,128)} %bitcast.7), calls=%async_computation.1 | async-start | bytes 1048576 | tf_op jit(solution)/shard_map/all_to_all | solution.py:298
  49.0 76.4 %all-gather.11.cloned.1.call-start = ((), (), s32[]{:S(2)}) async-start(), calls=%async_computation.6 | async-start | bytes 4718592 | tf_op jit(solution)/shard_map/all_gather | solution.py:302
  54.2 39.9 %copy-start.2 = (f32[64,2048]{1,0:T(8,128)}, f32[64,2048]{1,0:T(8,128)S(1)}, u32[]{:S(2)}) copy-start(f32[64,2048]{1,0:T(8,128)S(1)} %collective-permute-done.1.first) | copy-start | bytes 1572868
  66.5 27.7 %copy-start.3 = (f32[64,2048]{1,0:T(8,128)}, f32[64,2048]{1,0:T(8,128)S(1)}, u32[]{:S(2)}) copy-start(f32[64,2048]{1,0:T(8,128)S(1)} %collective-permute-done.2.second) | copy-start | bytes 1572868
  66.5 27.7 %copy-start.4 = (f32[64,2048]{1,0:T(8,128)}, f32[64,2048]{1,0:T(8,128)S(1)}, u32[]{:S(2)}) copy-start(f32[64,2048]{1,0:T(8,128)S(1)} %collective-permute-done.3.third) | copy-start | bytes 1572868
  99.5 6.9 %collective-permute-start.4 = (f32[256,128]{1,0:T(8,128)}, f32[256,128]{1,0:T(8,128)S(1)}, u32[]{:S(2)}, u32[]{:S(2)}) collective-permute-start(f32[256,128]{1,0:T(8,128)} %get-tuple-element.32), channel_id=1, source_target_pairs={{0,64},{64,128},{128,192},{192,0},{1,65},{65,129},{129,193},{193,1... | collective-permute-start | bytes 393224 | tf_op jit(solution)/shard_map/ppermute | solution.py:272
  100.4 8.4 %collective-permute-start.5 = (f32[256,128]{1,0:T(8,128)}, f32[256,128]{1,0:T(8,128)S(1)}, u32[]{:S(2)}, u32[]{:S(2)}) collective-permute-start(f32[256,128]{1,0:T(8,128)} %get-tuple-element.33), channel_id=1, source_target_pairs={{0,128},{64,192},{128,0},{192,64},{1,129},{65,193},{129,1},{193,65... | collective-permute-start | bytes 393224 | tf_op jit(solution)/shard_map/ppermute | solution.py:272
  104.7 4.5 %collective-permute-start.6 = (f32[256,128]{1,0:T(8,128)}, f32[256,128]{1,0:T(8,128)S(1)}, u32[]{:S(2)}, u32[]{:S(2)}) collective-permute-start(f32[256,128]{1,0:T(8,128)} %get-tuple-element.34), channel_id=1, source_target_pairs={{0,192},{64,0},{128,64},{192,128},{1,193},{65,1},{129,65},{193,129... | collective-permute-start | bytes 393224 | tf_op jit(solution)/shard_map/ppermute | solution.py:272
  117.3 31.1 %all-to-all-start.2 = ((f32[8,256,128]{2,1,0:T(8,128)}), f32[8,256,128]{2,1,0:T(8,128)S(1)}, u32[]{:S(2)}, u32[]{:S(2)}) async-start(f32[8,256,128]{2,1,0:T(8,128)} %attend.1), calls=%async_computation.2 | async-start | bytes 2097152 | tf_op jit(solution)/shard_map/all_to_all | solution.py:318
  155.5 6.7 %collective-permute-start.7 = (f32[2,64,512]{2,1,0:T(8,128)}, f32[2,64,512]{2,1,0:T(8,128)S(1)}, u32[]{:S(2)}, u32[]{:S(2)}) collective-permute-start(f32[2,64,512]{2,1,0:T(8,128)} %get-tuple-element.38), channel_id=1, source_target_pairs={{0,64},{64,128},{128,192},{192,0},{1,65},{65,129},{129,193},{193,1... | collective-permute-start | bytes 786440 | tf_op jit(solution)/shard_map/ppermute | solution.py:272
  157.7 9.7 %collective-permute-start.8 = (f32[2,64,512]{2,1,0:T(8,128)}, f32[2,64,512]{2,1,0:T(8,128)S(1)}, u32[]{:S(2)}, u32[]{:S(2)}) collective-permute-start(f32[2,64,512]{2,1,0:T(8,128)} %get-tuple-element.39), channel_id=1, source_target_pairs={{0,128},{64,192},{128,0},{192,64},{1,129},{65,193},{129,1},{193,65... | collective-permute-start | bytes 786440 | tf_op jit(solution)/shard_map/ppermute | solution.py:272
  158.6 10.4 %collective-permute-start.9 = (f32[2,64,512]{2,1,0:T(8,128)}, f32[2,64,512]{2,1,0:T(8,128)S(1)}, u32[]{:S(2)}, u32[]{:S(2)}) collective-permute-start(f32[2,64,512]{2,1,0:T(8,128)} %get-tuple-element.40), channel_id=1, source_target_pairs={{0,192},{64,0},{128,64},{192,128},{1,193},{65,1},{129,65},{193,129... | collective-permute-start | bytes 786440 | tf_op jit(solution)/shard_map/ppermute | solution.py:272
  170.0 4.0 %collective-permute-start.10 = (f32[64,512]{1,0:T(8,128)S(1)}, f32[64,512]{1,0:T(8,128)S(1)}, u32[]{:S(2)}, u32[]{:S(2)}) collective-permute-start(f32[64,512]{1,0:T(8,128)S(1)} %dynamic-slice_bitcast_fusion.2), channel_id=1, source_target_pairs={{0,1},{1,0},{2,3},{3,2},{4,5},{5,4},{6,7},{7,6},{8,9},{9,8},{10,11... | collective-permute-start | bytes 393224 | tf_op jit(solution)/shard_map/ppermute | solution.py:324
  (6 other events, 20.4 us)
Sparse Core Ops, SparseCore 0:
  9.2 38.8 all-gather.6
  50.0 39.0 all-gather.8
  90.9 34.3 all-gather.10

commit v9 on v8

--- a/solution.py
+++ b/solution.py
@@ -37,17 +37,10 @@
 MT = (((1,), (1,)), ((), ()))
 
 
-def pick_kernel(where, rows, keys, values, *refs):
-    outs, sent, sem, kv_sem = refs[:3], refs[3], refs[4], refs[5]
-    x, y, k = where[0], where[1], where[2]
+def pick_kernel(where, rows, *refs):
+    outs, sem = refs[:3], refs[3]
+    x, k = where[0], where[2]
     copies = []
-    for to in range(NZ):
-        cols = pl.ds((to // 2) * HD, HD)
-        for index, cache in enumerate((keys, values)):
-            part = cache.at[pl.ds(pl.multiple_of(y * BLOCK, BLOCK), BLOCK), cols]
-            copies.append(
-                pltpu.make_async_copy(part, sent.at[to, index], kv_sem.at[2 * to + index])
-            )
     for shift in range(1, NX):
         cols = pl.multiple_of(lax.rem(x + shift, NX) * 2048, 2048)
         part = rows.at[pl.ds(pl.multiple_of(k * BLOCK, BLOCK), BLOCK), pl.ds(cols, 2048)]
@@ -58,17 +51,44 @@
         copy.wait()
 
 
-def pick(where, hidden_rows, key_cache, value_cache):
+def pick(where, hidden_rows):
     return pl.pallas_call(
         pick_kernel,
-        out_shape=[jax.ShapeDtypeStruct((BLOCK, 2048), jnp.float32)] * 3
-        + [jax.ShapeDtypeStruct((NZ, 2, BLOCK, HD), jnp.float32)],
-        in_specs=[SMEM, ANY, ANY, ANY],
-        out_specs=[VMEM] * 4,
-        scratch_shapes=[pltpu.SemaphoreType.DMA((3,)), pltpu.SemaphoreType.DMA((2 * NZ,))],
+        out_shape=[jax.ShapeDtypeStruct((BLOCK, 2048), jnp.float32)] * 3,
+        in_specs=[SMEM, ANY],
+        out_specs=[VMEM] * 3,
+        scratch_shapes=[pltpu.SemaphoreType.DMA((3,))],
         compiler_params=pltpu.CompilerParams(vmem_limit_bytes=LIMIT),
         name="pick",
-    )(where, hidden_rows, key_cache, value_cache)
+    )(where, hidden_rows)
+
+
+def pick_keys_kernel(where, keys, values, out, sem):
+    y = where[1]
+    copies = []
+    for to in range(NZ):
+        for index, cache in enumerate((keys, values)):
+            part = cache.at[
+                pl.ds(pl.multiple_of(y * BLOCK, BLOCK), BLOCK), pl.ds((to // 2) * HD, HD)
+            ]
+            copies.append(pltpu.make_async_copy(part, out.at[to, index], sem.at[2 * to + index]))
+    for copy in copies:
+        copy.start()
+    for copy in copies:
+        copy.wait()
+
+
+def pick_keys(where, key_cache, value_cache):
+    return pl.pallas_call(
+        pick_keys_kernel,
+        out_shape=jax.ShapeDtypeStruct((NZ, 2, BLOCK, HD), jnp.float32),
+        in_specs=[SMEM, ANY, ANY],
+        out_specs=VMEM,
+        scratch_shapes=[pltpu.SemaphoreType.DMA((2 * NZ,))],
+        compiler_params=pltpu.CompilerParams(vmem_limit_bytes=56 << 20),
+        cost_estimate=pl.CostEstimate(flops=0, bytes_accessed=64 << 20, transcendentals=0),
+        name="pick_keys",
+    )(where, key_cache, value_cache)
 
 
 def project_kernel(where, rows, first, second, third, weights, *refs):
@@ -286,22 +306,23 @@
     x, y, z, k = (lax.axis_index(name) for name in ALL)
     where = jnp.stack([x, y, k]).astype(jnp.int32)
     weights = lax.all_gather(query_weight, ("y", "k"), axis=0)
-    *picked, sent = pick(where, hidden_rows, key_cache, value_cache)
+    picked = pick(where, hidden_rows)
     hidden = [along("x", piece, shift) for shift, piece in enumerate(picked, 1)]
-    near = lax.all_to_all(sent, "z", 0, 0)
+    behind, picked = lax.optimization_barrier((where, picked))
+    near = lax.all_to_all(pick_keys(behind, key_cache, value_cache), "z", 0, 0)
     rows = output_weight.reshape(2, NY, NK, 16, 512)
     kept = lax.dynamic_index_in_dim(rows, k, 2, keepdims=False)
     given = lax.dynamic_index_in_dim(rows, 1 - k, 2, keepdims=False)
     taken = lax.ppermute(given, "k", CORES)
     rows = jnp.where(k == 0, jnp.stack([kept, taken]), jnp.stack([taken, kept]))
-    rows, near = lax.optimization_barrier((rows, near))
+    rows, near, hidden = lax.optimization_barrier((rows, near, hidden))
     rows = lax.all_to_all(rows.reshape(NX * NY, 16, 512), ("x", "y"), 0, 0)
-    rows, hidden = lax.optimization_barrier((rows, hidden))
-    rows = lax.all_to_all(rows.reshape(NZ, NK, 16, 512), "z", 0, 0)
     kv = lax.all_gather(near, ("y", "k"), axis=0)
-    out_weight = lax.all_gather(rows, ("y", "k"), axis=0)
     partial = project(where, hidden_rows, hidden, weights)
     partial = [partial[0]] + [along("x", partial[s], s) for s in range(1, NX)]
+    rows, partial = lax.optimization_barrier((rows, partial))
+    rows = lax.all_to_all(rows.reshape(NZ, NK, 16, 512), "z", 0, 0)
+    out_weight = lax.all_gather(rows, ("y", "k"), axis=0)
     key_block = jnp.arange(NY, dtype=jnp.int32)[:, None, None]
     key_block = key_block + 4 * jnp.arange(NK, dtype=jnp.int32)[None, :, None]
     key_block = key_block + 8 * jnp.arange(NZ, dtype=jnp.int32)[None, None, :]

time: 184 us -> 168 us (0.913); the launches traced: 181 us -> 167 us
  waiting for transfers between devices: 80.3 us -> 31.8 us
  blocking collectives: 17.5 us -> 49.7 us
  Pallas kernels: 22.6 us -> 24.8 us
    all_to_all x2 -> x1, waiting for transfers between devices: 37.9 us -> 0.01 us  [shards(): near = lax.all_to_all(pick_keys(behind, key_cache, value_cache), 'z', 0, 0)]
    all_to_all x0 -> x1, blocking collectives: none -> 28.5 us  [shards(): heads = lax.all_to_all(heads, 'z', 0, 0)]
    all_to_all x1, waiting for transfers between devices: 6.7 us -> 0.01 us  [shards(): rows = lax.all_to_all(rows.reshape(NX * NY, 16, 512), ('x', 'y'), 0, 0)]
    all_to_all x2 -> x1, starting transfers between devices: 13.5 us -> 9.03 us  [shards(): near = lax.all_to_all(pick_keys(behind, key_cache, value_cache), 'z', 0, 0)]
    all_gather x1, waiting for transfers between devices: 3.72 us -> 0.01 us  [shards(): out_weight = lax.all_gather(rows, ('y', 'k'), axis=0)]
    all_to_all x1, blocking collectives: 17.5 us -> 21.2 us  [shards(): rows = lax.all_to_all(rows.reshape(NZ, NK, 16, 512), 'z', 0, 0)]
    ppermute x1, starting transfers between devices: 3.01 us -> 6.64 us  [shards(): other = lax.ppermute(other, 'k', CORES)]
    all_to_all x1, starting transfers between devices: 4.34 us -> 7.28 us  [shards(): rows = lax.all_to_all(rows.reshape(NX * NY, 16, 512), ('x', 'y'), 0, 0)]
  transfers between devices with their start and end apart: 17 -> 16, of which waited for: 13 -> 10; matrix products, arithmetic and copies ran while one was open for 4% -> 4% of each run, Pallas kernels for 9% -> 11%
where the time goes in v9:
time: 168 us; the launch traced here: 167 us
  blocking collectives  49.7 us (30%)
  starting transfers between devices  38.4 us (23%)
  waiting for transfers between devices  31.8 us (19%)
  Pallas kernels  24.8 us (15%)
  between operations  13.3 us (8%)
  other arithmetic  5.21 us (3%)
  local copies, waits for them, and re-layouts  4.09 us (2%)
    ppermute x9, waiting for transfers between devices, along(): lax.ppermute(value, axis, [(i, (i + shift) % count) for i in range(count)])  28.9 us
    all_to_all x1, blocking collectives, shards(): heads = lax.all_to_all(heads, 'z', 0, 0)  28.5 us
    all_to_all x1, blocking collectives, shards(): rows = lax.all_to_all(rows.reshape(NZ, NK, 16, 512), 'z', 0, 0)  21.2 us
    ppermute x9, starting transfers between devices, along(): lax.ppermute(value, axis, [(i, (i + shift) % count) for i in range(count)])  13.5 us
    all_to_all x1, starting transfers between devices, shards(): near = lax.all_to_all(pick_keys(behind, key_cache, value_cache), 'z', 0, 0)  9.03 us
    pallas_call x1, Pallas kernels, attend(): pl.pallas_call(attend_kernel, out_shape=jax.ShapeDtypeStruct((NZ, rows, H...  7.48 us
    all_to_all x1, starting transfers between devices, shards(): rows = lax.all_to_all(rows.reshape(NX * NY, 16, 512), ('x', 'y'), 0, 0)  7.28 us
    ppermute x1, starting transfers between devices, shards(): other = lax.ppermute(other, 'k', CORES)  6.64 us
  transfers between devices with their start and end apart: 16, of which 10 were waited for; matrix products, arithmetic and copies ran while one was open for 4% of the time, Pallas kernels for 11%

profile of v9, /device:TPU:1, one launch (start us, length us, event | category | flops | bytes accessed | tf_op | source)
XLA Modules:
  0.0 167.4 jit_solution(5304341618951110482)
XLA Ops:
  7.9 3.2 %pick.1 = (f32[64,2048]{1,0:T(8,128)}, f32[64,2048]{1,0:T(8,128)}, f32[64,2048]{1,0:T(8,128)}) custom-call(s32[3]{0:T(128)} %pad_add_fusion.where, f32[128,8192]{1,0:T(8,128)} %rows.3), custom_call_target="tpu_custom_call" | custom-call | tf_op jit(solution)/shard_map/pick/pallas_call | solution.py:55
  11.2 2.7 %pick_keys.1 = f32[8,2,64,128]{3,2,1,0:T(8,128)} custom-call(s32[3]{0:T(128)} %pad_add_fusion.where, f32[256,512]{1,0:T(8,128)} %keys.1, f32[256,512]{1,0:T(8,128)} %values.1), custom_call_target="tpu_custom_call" | custom-call | bytes 67108864 | tf_op jit(solution)/shard_map/pick_keys/pallas_call | solution.py:82
  13.8 9.0 %all-to-all-start = ((f32[8,2,64,128]{3,2,1,0:T(8,128)}), f32[8,2,64,128]{3,2,1,0:T(8,128)S(1)}, u32[]{:S(2)}, u32[]{:S(2)}) async-start(f32[8,2,64,128]{3,2,1,0:T(8,128)} %pick_keys.1), calls=%async_computation | async-start | bytes 1048576 | tf_op jit(solution)/shard_map/all_to_all | solution.py:312
  22.9 1.3 collective-permute-start.1
  24.2 2.5 %collective-permute-start.2 = (f32[64,2048]{1,0:T(8,128)}, f32[64,2048]{1,0:T(8,128)S(1)}, u32[]{:S(2)}, u32[]{:S(2)}) collective-permute-start(f32[64,2048]{1,0:T(8,128)} %get-tuple-element.28), channel_id=1, source_target_pairs={{0,128},{64,192},{128,0},{192,64},{1,129},{65,193},{129,1},{193,65... | collective-permute-start | bytes 1572872 | tf_op jit(solution)/shard_map/ppermute | solution.py:292
  26.7 1.2 collective-permute-start.3
  27.9 1.9 %collective-permute-start = (f32[2,4,16,512]{3,2,1,0:T(8,128)S(1)}, f32[2,4,16,512]{3,2,1,0:T(8,128)S(1)}, u32[]{:S(2)}, u32[]{:S(2)}) collective-permute-start(f32[2,4,16,512]{3,2,1,0:T(8,128)S(1)} %get-tuple-element.52), channel_id=1, source_target_pairs={{0,1},{1,0},{2,3},{3,2},{4,5},{5,4},{6,7},{7,6},{8,9},{9,8},{10,11... | collective-permute-start | bytes 786440 | tf_op jit(solution)/shard_map/ppermute | solution.py:316
  29.7 1.2 collective-permute-done
  31.8 5.2 %collective-permute-done.1.first = f32[64,2048]{1,0:T(8,128)S(1)} collective-permute-done((f32[64,2048]{1,0:T(8,128)}, f32[64,2048]{1,0:T(8,128)S(1)}, u32[]{:S(2)}, u32[]{:S(2)}) %collective-permute-start.1) | collective-permute-done | bytes 524320 | tf_op jit(solution)/shard_map/ppermute | solution.py:292
  37.0 12.1 %collective-permute-done.2.second = f32[64,2048]{1,0:T(8,128)S(1)} collective-permute-done((f32[64,2048]{1,0:T(8,128)}, f32[64,2048]{1,0:T(8,128)S(1)}, u32[]{:S(2)}, u32[]{:S(2)}) %collective-permute-start.2) | collective-permute-done | bytes 524320 | tf_op jit(solution)/shard_map/ppermute | solution.py:292
  50.2 7.3 %all-to-all-start.1 = ((f32[16,16,512]{2,1,0:T(8,128)}), f32[16,16,512]{2,1,0:T(8,128)S(1)}, u32[]{:S(2)}, u32[]{:S(2)}) async-start(f32[16,16,512]{2,1,0:T(8,128)} %bitcast.7), calls=%async_computation.1 | async-start | bytes 1048576 | tf_op jit(solution)/shard_map/all_to_all | solution.py:319
  57.6 5.4 %project.1 = (f32[256,128]{1,0:T(8,128)}, f32[256,128]{1,0:T(8,128)}, f32[256,128]{1,0:T(8,128)}, f32[256,128]{1,0:T(8,128)}) custom-call(s32[3]{0:T(128)} %pad_add_fusion.where, f32[128,8192]{1,0:T(8,128)} %rows.3, f32[64,2048]{1,0:T(8,128)} %copy-done.1, f32[64,2048]{1,0:T(8,128)} %copy-done.2, f32[64,2048]{1,0:T(8,128)} %copy-done.3, f32[8,512,256]{2,1,0:T(8,128)} %bitcast.33), custom_call_target="tpu_custom_call" | custom-call | flops 1610612736 | bytes 7340032 | tf_op jit(solution)/shard_map/project/pallas_call | solution.py:132
  63.0 1.4 collective-permute-start.4
  64.4 2.4 %collective-permute-start.5 = (f32[256,128]{1,0:T(8,128)}, f32[256,128]{1,0:T(8,128)S(1)}, u32[]{:S(2)}, u32[]{:S(2)}) collective-permute-start(f32[256,128]{1,0:T(8,128)} %get-tuple-element.37), channel_id=1, source_target_pairs={{0,128},{64,192},{128,0},{192,64},{1,129},{65,193},{129,1},{193,65... | collective-permute-start | bytes 393224 | tf_op jit(solution)/shard_map/ppermute | solution.py:292
  66.8 1.2 collective-permute-start.6
  68.8 2.9 %collective-permute-done.5.third = f32[256,128]{1,0:T(8,128)S(1)} collective-permute-done((f32[256,128]{1,0:T(8,128)}, f32[256,128]{1,0:T(8,128)S(1)}, u32[]{:S(2)}, u32[]{:S(2)}) %collective-permute-start.5) | collective-permute-done | bytes 131104 | tf_op jit(solution)/shard_map/ppermute | solution.py:292
  72.7 21.2 %all_to_all.20 = f32[8,2,16,512]{3,2,1,0:T(8,128)} all-to-all(f32[8,2,16,512]{3,2,1,0:T(8,128)S(1)} %bitcast.34), channel_id=1, replica_groups=mesh['x'=4,'y'=4,'z'=8,'k'=2] {'z'}, dimensions={0} | all-to-all | bytes 1048576 | tf_op jit(solution)/shard_map/all_to_all | solution.py:324
  98.9 7.5 %attend.1 = f32[8,256,128]{2,1,0:T(8,128)} custom-call(f32[256,128]{1,0:T(8,128)} %get-tuple-element.39.first, f32[256,128]{1,0:T(8,128)} %copy-done.7, f32[256,128]{1,0:T(8,128)} %copy-done.8, f32[256,128]{1,0:T(8,128)} %copy-done.9, f32[4,4096]{1,0:T(4,128)} %broadcast_in_dim.39.low, f32[4,4096]{1,0:T(4,128)} %broadcast_in_dim.41.up, ...), custom_call_target="tpu_custom_call" | custom-call | flops 1610612736 | bytes 6291456 | tf_op jit(solution)/shard_map/attend/pallas_call | solution.py:200
  106.4 28.5 %all_to_all.21.heads = f32[8,256,128]{2,1,0:T(8,128)} all-to-all(f32[8,256,128]{2,1,0:T(8,128)} %attend.1), channel_id=1, replica_groups=mesh['x'=4,'y'=4,'z'=8,'k'=2] {'z'}, dimensions={0} | all-to-all | bytes 2097152 | tf_op jit(solution)/shard_map/all_to_all | solution.py:339
  134.9 6.0 %mix.1 = (f32[2,64,512]{2,1,0:T(8,128)}, f32[2,64,512]{2,1,0:T(8,128)}, f32[2,64,512]{2,1,0:T(8,128)}, f32[2,64,512]{2,1,0:T(8,128)}) custom-call(s32[3]{0:T(128)} %pad_add_fusion.where, f32[8,256,128]{2,1,0:T(8,128)} %all_to_all.21.heads, f32[8,8,2,16,512]{4,3,2,1,0:T(8,128)} %bitcast.38), custom_call_target="tpu_custom_call" | custom-call | flops 1610612736 | bytes 6291456 | tf_op jit(solution)/shard_map/mix/pallas_call | solution.py:252
  141.0 3.5 %collective-permute-start.8 = (f32[2,64,512]{2,1,0:T(8,128)}, f32[2,64,512]{2,1,0:T(8,128)S(1)}, u32[]{:S(2)}, u32[]{:S(2)}) collective-permute-start(f32[2,64,512]{2,1,0:T(8,128)} %get-tuple-element.47), channel_id=1, source_target_pairs={{0,128},{64,192},{128,0},{192,64},{1,129},{65,193},{129,1},{193,65... | collective-permute-start | bytes 786440 | tf_op jit(solution)/shard_map/ppermute | solution.py:292
  144.5 3.2 %collective-permute-done.7 = f32[2,64,512]{2,1,0:T(8,128)S(1)} collective-permute-done((f32[2,64,512]{2,1,0:T(8,128)}, f32[2,64,512]{2,1,0:T(8,128)S(1)}, u32[]{:S(2)}, u32[]{:S(2)}) %collective-permute-start.7) | collective-permute-done | bytes 262176 | tf_op jit(solution)/shard_map/ppermute | solution.py:292
  147.7 3.7 %collective-permute-done.8 = f32[2,64,512]{2,1,0:T(8,128)S(1)} collective-permute-done((f32[2,64,512]{2,1,0:T(8,128)}, f32[2,64,512]{2,1,0:T(8,128)S(1)}, u32[]{:S(2)}, u32[]{:S(2)}) %collective-permute-start.8) | collective-permute-done | bytes 262176 | tf_op jit(solution)/shard_map/ppermute | solution.py:292
  152.5 6.6 %collective-permute-start.10 = (f32[64,512]{1,0:T(8,128)S(1)}, f32[64,512]{1,0:T(8,128)S(1)}, u32[]{:S(2)}, u32[]{:S(2)}) collective-permute-start(f32[64,512]{1,0:T(8,128)S(1)} %dynamic-slice_bitcast_fusion.2), channel_id=1, source_target_pairs={{0,1},{1,0},{2,3},{3,2},{4,5},{5,4},{6,7},{7,6},{8,9},{9,8},{10,11... | collective-permute-start | bytes 393224 | tf_op jit(solution)/shard_map/ppermute | solution.py:345
  (69 shorter events, 13.1 us)
Async XLA Ops:
  6.5 21.3 %copy-start.4 = (f32[256,512]{1,0:T(8,128)S(1)}, f32[256,512]{1,0:T(8,128)}, u32[]{:S(2)}) copy-start(f32[256,512]{1,0:T(8,128)} %param.17) | copy-start | bytes 1572868
  6.5 51.0 %all-gather.7.cloned.1.call-start = ((), (), s32[]{:S(2)}) async-start(), calls=%async_computation.4 | async-start | bytes 4718592 | tf_op jit(solution)/shard_map/all_gather | solution.py:308
  13.8 35.3 %all-to-all-start = ((f32[8,2,64,128]{3,2,1,0:T(8,128)}), f32[8,2,64,128]{3,2,1,0:T(8,128)S(1)}, u32[]{:S(2)}, u32[]{:S(2)}) async-start(f32[8,2,64,128]{3,2,1,0:T(8,128)} %pick_keys.1), calls=%async_computation | async-start | bytes 1048576 | tf_op jit(solution)/shard_map/all_to_all | solution.py:312
  22.9 76.0 %all-gather.9.cloned.1.call-start = ((), (), s32[]{:S(2)}) async-start(), calls=%async_computation.5 | async-start | bytes 4718592 | tf_op jit(solution)/shard_map/all_gather | solution.py:320
  22.9 14.1 %collective-permute-start.1 = (f32[64,2048]{1,0:T(8,128)}, f32[64,2048]{1,0:T(8,128)S(1)}, u32[]{:S(2)}, u32[]{:S(2)}) collective-permute-start(f32[64,2048]{1,0:T(8,128)} %get-tuple-element.27), channel_id=1, source_target_pairs={{0,64},{64,128},{128,192},{192,0},{1,65},{65,129},{129,193},{193,1... | collective-permute-start | bytes 1572872 | tf_op jit(solution)/shard_map/ppermute | solution.py:292
  24.2 24.9 %collective-permute-start.2 = (f32[64,2048]{1,0:T(8,128)}, f32[64,2048]{1,0:T(8,128)S(1)}, u32[]{:S(2)}, u32[]{:S(2)}) collective-permute-start(f32[64,2048]{1,0:T(8,128)} %get-tuple-element.28), channel_id=1, source_target_pairs={{0,128},{64,192},{128,0},{192,64},{1,129},{65,193},{129,1},{193,65... | collective-permute-start | bytes 1572872 | tf_op jit(solution)/shard_map/ppermute | solution.py:292
  26.7 22.5 %collective-permute-start.3 = (f32[64,2048]{1,0:T(8,128)}, f32[64,2048]{1,0:T(8,128)S(1)}, u32[]{:S(2)}, u32[]{:S(2)}) collective-permute-start(f32[64,2048]{1,0:T(8,128)} %get-tuple-element.29), channel_id=1, source_target_pairs={{0,192},{64,0},{128,64},{192,128},{1,193},{65,1},{129,65},{193,129... | collective-permute-start | bytes 1572872 | tf_op jit(solution)/shard_map/ppermute | solution.py:292
  27.9 3.0 %collective-permute-start = (f32[2,4,16,512]{3,2,1,0:T(8,128)S(1)}, f32[2,4,16,512]{3,2,1,0:T(8,128)S(1)}, u32[]{:S(2)}, u32[]{:S(2)}) collective-permute-start(f32[2,4,16,512]{3,2,1,0:T(8,128)S(1)} %get-tuple-element.52), channel_id=1, source_target_pairs={{0,1},{1,0},{2,3},{3,2},{4,5},{5,4},{6,7},{7,6},{8,9},{9,8},{10,11... | collective-permute-start | bytes 786440 | tf_op jit(solution)/shard_map/ppermute | solution.py:316
  50.2 17.9 %all-to-all-start.1 = ((f32[16,16,512]{2,1,0:T(8,128)}), f32[16,16,512]{2,1,0:T(8,128)S(1)}, u32[]{:S(2)}, u32[]{:S(2)}) async-start(f32[16,16,512]{2,1,0:T(8,128)} %bitcast.7), calls=%async_computation.1 | async-start | bytes 1048576 | tf_op jit(solution)/shard_map/all_to_all | solution.py:319
  57.4 77.5 %all-gather.11.cloned.1.call-start = ((), (), s32[]{:S(2)}) async-start(), calls=%async_computation.6 | async-start | bytes 4718592 | tf_op jit(solution)/shard_map/all_gather | solution.py:325
  57.5 36.4 %copy-start.10 = (s32[32]{0:T(128)S(1)}, s32[32]{0:T(128)}, u32[]{:S(2)}) copy-start(s32[32]{0:T(128)} %param.14) | copy-start | bytes 388
  57.6 37.0 %copy-start.11 = (s32[32]{0:T(128)S(1)}, s32[32]{0:T(128)}, u32[]{:S(2)}) copy-start(s32[32]{0:T(128)} %param.16) | copy-start | bytes 388
  57.6 37.8 %copy-start.5 = (s32[32,16]{0,1:T(8,128)S(1)}, s32[32,16]{0,1:T(8,128)}, u32[]{:S(2)}) copy-start(s32[32,16]{0,1:T(8,128)} %param.15) | copy-start | bytes 6148
  57.6 37.8 %copy-start.6 = (s32[32,16]{0,1:T(8,128)S(1)}, s32[32,16]{0,1:T(8,128)}, u32[]{:S(2)}) copy-start(s32[32,16]{0,1:T(8,128)} %param.13) | copy-start | bytes 6148
  63.0 5.8 %collective-permute-start.4 = (f32[256,128]{1,0:T(8,128)}, f32[256,128]{1,0:T(8,128)S(1)}, u32[]{:S(2)}, u32[]{:S(2)}) collective-permute-start(f32[256,128]{1,0:T(8,128)} %get-tuple-element.36), channel_id=1, source_target_pairs={{0,64},{64,128},{128,192},{192,0},{1,65},{65,129},{129,193},{193,1... | collective-permute-start | bytes 393224 | tf_op jit(solution)/shard_map/ppermute | solution.py:292
  64.4 7.2 %collective-permute-start.5 = (f32[256,128]{1,0:T(8,128)}, f32[256,128]{1,0:T(8,128)S(1)}, u32[]{:S(2)}, u32[]{:S(2)}) collective-permute-start(f32[256,128]{1,0:T(8,128)} %get-tuple-element.37), channel_id=1, source_target_pairs={{0,128},{64,192},{128,0},{192,64},{1,129},{65,193},{129,1},{193,65... | collective-permute-start | bytes 393224 | tf_op jit(solution)/shard_map/ppermute | solution.py:292
  66.8 5.8 %collective-permute-start.6 = (f32[256,128]{1,0:T(8,128)}, f32[256,128]{1,0:T(8,128)S(1)}, u32[]{:S(2)}, u32[]{:S(2)}) collective-permute-start(f32[256,128]{1,0:T(8,128)} %get-tuple-element.38), channel_id=1, source_target_pairs={{0,192},{64,0},{128,64},{192,128},{1,193},{65,1},{129,65},{193,129... | collective-permute-start | bytes 393224 | tf_op jit(solution)/shard_map/ppermute | solution.py:292
  68.8 30.1 %copy-start.7 = (f32[256,128]{1,0:T(8,128)}, f32[256,128]{1,0:T(8,128)S(1)}, u32[]{:S(2)}) copy-start(f32[256,128]{1,0:T(8,128)S(1)} %collective-permute-done.4.second) | copy-start | bytes 393220
  71.7 27.3 %copy-start.8 = (f32[256,128]{1,0:T(8,128)}, f32[256,128]{1,0:T(8,128)S(1)}, u32[]{:S(2)}) copy-start(f32[256,128]{1,0:T(8,128)S(1)} %collective-permute-done.5.third) | copy-start | bytes 393220
  72.7 26.3 %copy-start.9 = (f32[256,128]{1,0:T(8,128)}, f32[256,128]{1,0:T(8,128)S(1)}, u32[]{:S(2)}) copy-start(f32[256,128]{1,0:T(8,128)S(1)} %collective-permute-done.6.fourth) | copy-start | bytes 393220
  140.9 6.7 %collective-permute-start.7 = (f32[2,64,512]{2,1,0:T(8,128)}, f32[2,64,512]{2,1,0:T(8,128)S(1)}, u32[]{:S(2)}, u32[]{:S(2)}) collective-permute-start(f32[2,64,512]{2,1,0:T(8,128)} %get-tuple-element.46), channel_id=1, source_target_pairs={{0,64},{64,128},{128,192},{192,0},{1,65},{65,129},{129,193},{193,1... | collective-permute-start | bytes 786440 | tf_op jit(solution)/shard_map/ppermute | solution.py:292
  141.0 10.3 %collective-permute-start.8 = (f32[2,64,512]{2,1,0:T(8,128)}, f32[2,64,512]{2,1,0:T(8,128)S(1)}, u32[]{:S(2)}, u32[]{:S(2)}) collective-permute-start(f32[2,64,512]{2,1,0:T(8,128)} %get-tuple-element.47), channel_id=1, source_target_pairs={{0,128},{64,192},{128,0},{192,64},{1,129},{65,193},{129,1},{193,65... | collective-permute-start | bytes 786440 | tf_op jit(solution)/shard_map/ppermute | solution.py:292
  144.5 6.9 %collective-permute-start.9 = (f32[2,64,512]{2,1,0:T(8,128)}, f32[2,64,512]{2,1,0:T(8,128)S(1)}, u32[]{:S(2)}, u32[]{:S(2)}) collective-permute-start(f32[2,64,512]{2,1,0:T(8,128)} %get-tuple-element.48), channel_id=1, source_target_pairs={{0,192},{64,0},{128,64},{192,128},{1,193},{65,1},{129,65},{193,129... | collective-permute-start | bytes 786440 | tf_op jit(solution)/shard_map/ppermute | solution.py:292
  152.5 7.6 %collective-permute-start.10 = (f32[64,512]{1,0:T(8,128)S(1)}, f32[64,512]{1,0:T(8,128)S(1)}, u32[]{:S(2)}, u32[]{:S(2)}) collective-permute-start(f32[64,512]{1,0:T(8,128)S(1)} %dynamic-slice_bitcast_fusion.2), channel_id=1, source_target_pairs={{0,1},{1,0},{2,3},{3,2},{4,5},{5,4},{6,7},{7,6},{8,9},{9,8},{10,11... | collective-permute-start | bytes 393224 | tf_op jit(solution)/shard_map/ppermute | solution.py:345
  (4 other events, 38.3 us)
Sparse Core Ops, SparseCore 0:
  9.2 38.8 all-gather.6
  50.3 37.4 all-gather.8
  94.0 33.4 all-gather.10

commit v10 on v9

--- a/solution.py
+++ b/solution.py
@@ -45,8 +45,8 @@
         cols = pl.multiple_of(lax.rem(x + shift, NX) * 2048, 2048)
         part = rows.at[pl.ds(pl.multiple_of(k * BLOCK, BLOCK), BLOCK), pl.ds(cols, 2048)]
         copies.append(pltpu.make_async_copy(part, outs[shift - 1], sem.at[shift - 1]))
-    for copy in copies:
-        copy.start()
+    for number, copy in enumerate(copies):
+        copy.start(priority=number % 2)
     for copy in copies:
         copy.wait()
 
@@ -72,8 +72,8 @@
                 pl.ds(pl.multiple_of(y * BLOCK, BLOCK), BLOCK), pl.ds((to // 2) * HD, HD)
             ]
             copies.append(pltpu.make_async_copy(part, out.at[to, index], sem.at[2 * to + index]))
-    for copy in copies:
-        copy.start()
+    for number, copy in enumerate(copies):
+        copy.start(priority=number % 2)
     for copy in copies:
         copy.wait()
 
@@ -110,8 +110,8 @@
         group.append(
             pltpu.make_async_copy(weights.at[pl.ds(2 * y, 2)], right_buf.at[y], sems.at[y, NX])
         )
-        for copy in group:
-            copy.start()
+        for number, copy in enumerate(group):
+            copy.start(priority=number % 2)
         copies.append(group)
     totals = [None, None]
     for y in range(NY):
@@ -154,8 +154,8 @@
         pltpu.make_async_copy(gathered.at[tile], kv.at[tile], sem.at[tile])
         for tile in range(tiles)
     ]
-    for copy in copies:
-        copy.start()
+    for tile, copy in enumerate(copies):
+        copy.start(priority=tile % 2)
     width = NZ * BLOCK
     row = lax.broadcasted_iota(jnp.int32, (BLOCK, width), 0)
     col = lax.broadcasted_iota(jnp.int32, (BLOCK, width), 1)
@@ -228,8 +228,8 @@
                 for part in range(8)
             ]
         )
-        for copy in copies[step]:
-            copy.start()
+        for number, copy in enumerate(copies[step]):
+            copy.start(priority=number % 2)
     totals = [None, None]
     for step in range(steps):
         left = split(jnp.concatenate([heads[2 * step], heads[2 * step + 1]], axis=1))
@@ -308,7 +308,7 @@
     weights = lax.all_gather(query_weight, ("y", "k"), axis=0)
     picked = pick(where, hidden_rows)
     hidden = [along("x", piece, shift) for shift, piece in enumerate(picked, 1)]
-    behind, picked = lax.optimization_barrier((where, picked))
+    behind, hidden[0] = lax.optimization_barrier((where, hidden[0]))
     near = lax.all_to_all(pick_keys(behind, key_cache, value_cache), "z", 0, 0)
     rows = output_weight.reshape(2, NY, NK, 16, 512)
     kept = lax.dynamic_index_in_dim(rows, k, 2, keepdims=False)
@@ -318,11 +318,6 @@
     rows, near, hidden = lax.optimization_barrier((rows, near, hidden))
     rows = lax.all_to_all(rows.reshape(NX * NY, 16, 512), ("x", "y"), 0, 0)
     kv = lax.all_gather(near, ("y", "k"), axis=0)
-    partial = project(where, hidden_rows, hidden, weights)
-    partial = [partial[0]] + [along("x", partial[s], s) for s in range(1, NX)]
-    rows, partial = lax.optimization_barrier((rows, partial))
-    rows = lax.all_to_all(rows.reshape(NZ, NK, 16, 512), "z", 0, 0)
-    out_weight = lax.all_gather(rows, ("y", "k"), axis=0)
     key_block = jnp.arange(NY, dtype=jnp.int32)[:, None, None]
     key_block = key_block + 4 * jnp.arange(NK, dtype=jnp.int32)[None, :, None]
     key_block = key_block + 8 * jnp.arange(NZ, dtype=jnp.int32)[None, None, :]
@@ -335,6 +330,11 @@
         slash_offsets,
         slash_count,
     )
+    partial = project(where, hidden_rows, hidden, weights)
+    partial = [partial[0]] + [along("x", partial[s], s) for s in range(1, NX)]
+    rows, partial, low, up = lax.optimization_barrier((rows, partial, low, up))
+    rows = lax.all_to_all(rows.reshape(NZ, NK, 16, 512), "z", 0, 0)
+    out_weight = lax.all_gather(rows, ("y", "k"), axis=0)
     heads = attend(partial, low, up, kv)
     heads = lax.all_to_all(heads, "z", 0, 0)
     mixed = mix(where, heads, out_weight)

time: 168 us -> 181 us (1.077)
  waiting for transfers between devices: 31.8 us -> 41.4 us
  Pallas kernels: 24.8 us -> 26.9 us
  starting transfers between devices: 38.4 us -> 40.3 us
    ppermute x9, waiting for transfers between devices: 28.9 us -> 38.2 us  [along(): lax.ppermute(value, axis, [(i, (i + shift) % count) for i in range(count)])]
  transfers between devices with their start and end apart: 16 -> 16, of which waited for: 10 -> 9; matrix products, arithmetic and copies ran while one was open for 4% -> 4% of each run, Pallas kernels for 11% -> 11%
where the time goes in v10:
time: 181 us
  blocking collectives  49.5 us (27%)
  waiting for transfers between devices  41.4 us (23%)
  starting transfers between devices  40.3 us (22%)
  Pallas kernels  26.9 us (15%)
  between operations  13.3 us (7%)
  other arithmetic  5.19 us (3%)
  local copies, waits for them, and re-layouts  4 us (2%)
    ppermute x9, waiting for transfers between devices, along(): lax.ppermute(value, axis, [(i, (i + shift) % count) for i in range(count)])  38.2 us
    all_to_all x1, blocking collectives, shards(): heads = lax.all_to_all(heads, 'z', 0, 0)  28.5 us
    all_to_all x1, blocking collectives, shards(): rows = lax.all_to_all(rows.reshape(NZ, NK, 16, 512), 'z', 0, 0)  21 us
    ppermute x9, starting transfers between devices, along(): lax.ppermute(value, axis, [(i, (i + shift) % count) for i in range(count)])  13.5 us
    all_to_all x1, starting transfers between devices, shards(): near = lax.all_to_all(pick_keys(behind, key_cache, value_cache), 'z', 0, 0)  10.3 us
    pallas_call x1, Pallas kernels, attend(): pl.pallas_call(attend_kernel, out_shape=jax.ShapeDtypeStruct((NZ, rows, H...  7.81 us
    all_to_all x1, starting transfers between devices, shards(): rows = lax.all_to_all(rows.reshape(NX * NY, 16, 512), ('x', 'y'), 0, 0)  7.33 us
    pallas_call x1, Pallas kernels, project(): pl.pallas_call(project_kernel, out_shape=[jax.ShapeDtypeStruct((NX * BLOC...  6.53 us
  transfers between devices with their start and end apart: 16, of which 9 were waited for; matrix products, arithmetic and copies ran while one was open for 4% of the time, Pallas kernels for 11%

profile of v10, /device:TPU:1, one launch (start us, length us, event | category | flops | bytes accessed | tf_op | source)
XLA Modules:
  0.0 180.5 jit_solution(12947960594725060874)
XLA Ops:
  7.9 3.4 %pick.1 = (f32[64,2048]{1,0:T(8,128)}, f32[64,2048]{1,0:T(8,128)}, f32[64,2048]{1,0:T(8,128)}) custom-call(s32[3]{0:T(128)} %pad_add_fusion.where, f32[128,8192]{1,0:T(8,128)} %rows.3), custom_call_target="tpu_custom_call" | custom-call | tf_op jit(solution)/shard_map/pick/pallas_call | solution.py:55
  11.3 2.1 %collective-permute-start.1 = (f32[64,2048]{1,0:T(8,128)}, f32[64,2048]{1,0:T(8,128)S(1)}, u32[]{:S(2)}, u32[]{:S(2)}) collective-permute-start(f32[64,2048]{1,0:T(8,128)} %get-tuple-element.30), channel_id=1, source_target_pairs={{0,64},{64,128},{128,192},{192,0},{1,65},{65,129},{129,193},{193,1... | collective-permute-start | bytes 1572872 | tf_op jit(solution)/shard_map/ppermute | solution.py:292
  13.4 10.8 %collective-permute-done.1.first = f32[64,2048]{1,0:T(8,128)S(1)} collective-permute-done((f32[64,2048]{1,0:T(8,128)}, f32[64,2048]{1,0:T(8,128)S(1)}, u32[]{:S(2)}, u32[]{:S(2)}) %collective-permute-start.1) | collective-permute-done | bytes 524320 | tf_op jit(solution)/shard_map/ppermute | solution.py:292
  24.3 2.7 %pick_keys.1 = f32[8,2,64,128]{3,2,1,0:T(8,128)} custom-call(s32[3]{0:T(128)} %pad_add_fusion.where, f32[256,512]{1,0:T(8,128)} %keys.1, f32[256,512]{1,0:T(8,128)} %values.1), custom_call_target="tpu_custom_call" | custom-call | bytes 67108864 | tf_op jit(solution)/shard_map/pick_keys/pallas_call | solution.py:82
  26.9 10.3 %all-to-all-start = ((f32[8,2,64,128]{3,2,1,0:T(8,128)}), f32[8,2,64,128]{3,2,1,0:T(8,128)S(1)}, u32[]{:S(2)}, u32[]{:S(2)}) async-start(f32[8,2,64,128]{3,2,1,0:T(8,128)} %pick_keys.1), calls=%async_computation | async-start | bytes 1048576 | tf_op jit(solution)/shard_map/all_to_all | solution.py:312
  37.3 1.6 collective-permute-start.2
  39.8 2.5 %collective-permute-start = (f32[2,4,16,512]{3,2,1,0:T(8,128)S(1)}, f32[2,4,16,512]{3,2,1,0:T(8,128)S(1)}, u32[]{:S(2)}, u32[]{:S(2)}) collective-permute-start(f32[2,4,16,512]{3,2,1,0:T(8,128)S(1)} %get-tuple-element.58), channel_id=1, source_target_pairs={{0,1},{1,0},{2,3},{3,2},{4,5},{5,4},{6,7},{7,6},{8,9},{9,8},{10,11... | collective-permute-start | bytes 786440 | tf_op jit(solution)/shard_map/ppermute | solution.py:316
  42.3 1.3 collective-permute-done
  44.5 6.2 %collective-permute-done.2.second = f32[64,2048]{1,0:T(8,128)S(1)} collective-permute-done((f32[64,2048]{1,0:T(8,128)}, f32[64,2048]{1,0:T(8,128)S(1)}, u32[]{:S(2)}, u32[]{:S(2)}) %collective-permute-start.2) | collective-permute-done | bytes 524320 | tf_op jit(solution)/shard_map/ppermute | solution.py:292
  50.7 11.4 %collective-permute-done.3.third = f32[64,2048]{1,0:T(8,128)S(1)} collective-permute-done((f32[64,2048]{1,0:T(8,128)}, f32[64,2048]{1,0:T(8,128)S(1)}, u32[]{:S(2)}, u32[]{:S(2)}) %collective-permute-start.3) | collective-permute-done | bytes 524320 | tf_op jit(solution)/shard_map/ppermute | solution.py:292
  66.3 7.3 %all-to-all-start.1 = ((f32[16,16,512]{2,1,0:T(8,128)}), f32[16,16,512]{2,1,0:T(8,128)S(1)}, u32[]{:S(2)}, u32[]{:S(2)}) async-start(f32[16,16,512]{2,1,0:T(8,128)} %bitcast.7), calls=%async_computation.1 | async-start | bytes 1048576 | tf_op jit(solution)/shard_map/all_to_all | solution.py:319
  73.8 6.5 %project.1 = (f32[256,128]{1,0:T(8,128)}, f32[256,128]{1,0:T(8,128)}, f32[256,128]{1,0:T(8,128)}, f32[256,128]{1,0:T(8,128)}) custom-call(s32[3]{0:T(128)} %pad_add_fusion.where, f32[128,8192]{1,0:T(8,128)} %rows.3, f32[64,2048]{1,0:T(8,128)} %copy-done.1, f32[64,2048]{1,0:T(8,128)} %copy-done.2, f32[64,2048]{1,0:T(8,128)} %copy-done.3, f32[8,512,256]{2,1,0:T(8,128)} %bitcast.33), custom_call_target="tpu_custom_call" | custom-call | flops 1610612736 | bytes 7340032 | tf_op jit(solution)/shard_map/project/pallas_call | solution.py:132
  80.4 1.4 collective-permute-start.4
  81.8 2.4 %collective-permute-start.5 = (f32[256,128]{1,0:T(8,128)}, f32[256,128]{1,0:T(8,128)S(1)}, u32[]{:S(2)}, u32[]{:S(2)}) collective-permute-start(f32[256,128]{1,0:T(8,128)} %get-tuple-element.41), channel_id=1, source_target_pairs={{0,128},{64,192},{128,0},{192,64},{1,129},{65,193},{129,1},{193,65... | collective-permute-start | bytes 393224 | tf_op jit(solution)/shard_map/ppermute | solution.py:292
  84.2 1.2 collective-permute-start.6
  87.0 2.2 %collective-permute-done.5.third = f32[256,128]{1,0:T(8,128)S(1)} collective-permute-done((f32[256,128]{1,0:T(8,128)}, f32[256,128]{1,0:T(8,128)S(1)}, u32[]{:S(2)}, u32[]{:S(2)}) %collective-permute-start.5) | collective-permute-done | bytes 131104 | tf_op jit(solution)/shard_map/ppermute | solution.py:292
  89.9 21.0 %all_to_all.20 = f32[8,2,16,512]{3,2,1,0:T(8,128)} all-to-all(f32[8,2,16,512]{3,2,1,0:T(8,128)S(1)} %bitcast.34), channel_id=1, replica_groups=mesh['x'=4,'y'=4,'z'=8,'k'=2] {'z'}, dimensions={0} | all-to-all | bytes 1048576 | tf_op jit(solution)/shard_map/all_to_all | solution.py:336
  111.0 7.8 %attend.1 = f32[8,256,128]{2,1,0:T(8,128)} custom-call(f32[256,128]{1,0:T(8,128)} %get-tuple-element.43.first, f32[256,128]{1,0:T(8,128)} %copy-done.7, f32[256,128]{1,0:T(8,128)} %copy-done.8, f32[256,128]{1,0:T(8,128)} %copy-done.9, f32[4,4096]{1,0:T(4,128)} %broadcast_in_dim.39.low, f32[4,4096]{1,0:T(4,128)} %broadcast_in_dim.41.up, ...), custom_call_target="tpu_custom_call" | custom-call | flops 1610612736 | bytes 6291456 | tf_op jit(solution)/shard_map/attend/pallas_call | solution.py:200
  118.8 28.5 %all_to_all.21.heads = f32[8,256,128]{2,1,0:T(8,128)} all-to-all(f32[8,256,128]{2,1,0:T(8,128)} %attend.1), channel_id=1, replica_groups=mesh['x'=4,'y'=4,'z'=8,'k'=2] {'z'}, dimensions={0} | all-to-all | bytes 2097152 | tf_op jit(solution)/shard_map/all_to_all | solution.py:339
  147.3 6.5 %mix.1 = (f32[2,64,512]{2,1,0:T(8,128)}, f32[2,64,512]{2,1,0:T(8,128)}, f32[2,64,512]{2,1,0:T(8,128)}, f32[2,64,512]{2,1,0:T(8,128)}) custom-call(s32[3]{0:T(128)} %pad_add_fusion.where, f32[8,256,128]{2,1,0:T(8,128)} %all_to_all.21.heads, f32[8,8,2,16,512]{4,3,2,1,0:T(8,128)} %bitcast.38), custom_call_target="tpu_custom_call" | custom-call | flops 1610612736 | bytes 6291456 | tf_op jit(solution)/shard_map/mix/pallas_call | solution.py:252
  154.0 3.7 %collective-permute-start.8 = (f32[2,64,512]{2,1,0:T(8,128)}, f32[2,64,512]{2,1,0:T(8,128)S(1)}, u32[]{:S(2)}, u32[]{:S(2)}) collective-permute-start(f32[2,64,512]{2,1,0:T(8,128)} %get-tuple-element.53), channel_id=1, source_target_pairs={{0,128},{64,192},{128,0},{192,64},{1,129},{65,193},{129,1},{193,65... | collective-permute-start | bytes 786440 | tf_op jit(solution)/shard_map/ppermute | solution.py:292
  157.8 2.8 %collective-permute-done.7 = f32[2,64,512]{2,1,0:T(8,128)S(1)} collective-permute-done((f32[2,64,512]{2,1,0:T(8,128)}, f32[2,64,512]{2,1,0:T(8,128)S(1)}, u32[]{:S(2)}, u32[]{:S(2)}) %collective-permute-start.7) | collective-permute-done | bytes 262176 | tf_op jit(solution)/shard_map/ppermute | solution.py:292
  160.6 4.1 %collective-permute-done.8 = f32[2,64,512]{2,1,0:T(8,128)S(1)} collective-permute-done((f32[2,64,512]{2,1,0:T(8,128)}, f32[2,64,512]{2,1,0:T(8,128)S(1)}, u32[]{:S(2)}, u32[]{:S(2)}) %collective-permute-start.8) | collective-permute-done | bytes 262176 | tf_op jit(solution)/shard_map/ppermute | solution.py:292
  165.7 6.5 %collective-permute-start.10 = (f32[64,512]{1,0:T(8,128)S(1)}, f32[64,512]{1,0:T(8,128)S(1)}, u32[]{:S(2)}, u32[]{:S(2)}) collective-permute-start(f32[64,512]{1,0:T(8,128)S(1)} %dynamic-slice_bitcast_fusion.2), channel_id=1, source_target_pairs={{0,1},{1,0},{2,3},{3,2},{4,5},{5,4},{6,7},{7,6},{8,9},{9,8},{10,11... | collective-permute-start | bytes 393224 | tf_op jit(solution)/shard_map/ppermute | solution.py:345
  (69 shorter events, 12.8 us)
Async XLA Ops:
  6.5 33.2 %copy-start.4 = (f32[256,512]{1,0:T(8,128)S(1)}, f32[256,512]{1,0:T(8,128)}, u32[]{:S(2)}) copy-start(f32[256,512]{1,0:T(8,128)} %param.17) | copy-start | bytes 1572868
  6.5 67.3 %all-gather.7.cloned.1.call-start = ((), (), s32[]{:S(2)}) async-start(), calls=%async_computation.4 | async-start | bytes 4718592 | tf_op jit(solution)/shard_map/all_gather | solution.py:308
  7.9 55.2 %copy-start.10 = (s32[32]{0:T(128)S(1)}, s32[32]{0:T(128)}, u32[]{:S(2)}) copy-start(s32[32]{0:T(128)} %param.14) | copy-start | bytes 388
  7.9 55.8 %copy-start.11 = (s32[32]{0:T(128)S(1)}, s32[32]{0:T(128)}, u32[]{:S(2)}) copy-start(s32[32]{0:T(128)} %param.16) | copy-start | bytes 388
  7.9 56.6 %copy-start.5 = (s32[32,16]{0,1:T(8,128)S(1)}, s32[32,16]{0,1:T(8,128)}, u32[]{:S(2)}) copy-start(s32[32,16]{0,1:T(8,128)} %param.15) | copy-start | bytes 6148
  7.9 56.6 %copy-start.6 = (s32[32,16]{0,1:T(8,128)S(1)}, s32[32,16]{0,1:T(8,128)}, u32[]{:S(2)}) copy-start(s32[32,16]{0,1:T(8,128)} %param.13) | copy-start | bytes 6148
  11.3 12.9 %collective-permute-start.1 = (f32[64,2048]{1,0:T(8,128)}, f32[64,2048]{1,0:T(8,128)S(1)}, u32[]{:S(2)}, u32[]{:S(2)}) collective-permute-start(f32[64,2048]{1,0:T(8,128)} %get-tuple-element.30), channel_id=1, source_target_pairs={{0,64},{64,128},{128,192},{192,0},{1,65},{65,129},{129,193},{193,1... | collective-permute-start | bytes 1572872 | tf_op jit(solution)/shard_map/ppermute | solution.py:292
  24.3 49.5 %copy-start.1 = (f32[64,2048]{1,0:T(8,128)}, f32[64,2048]{1,0:T(8,128)S(1)}, u32[]{:S(2)}) copy-start(f32[64,2048]{1,0:T(8,128)S(1)} %collective-permute-done.1.first) | copy-start | bytes 1572868
  26.9 35.2 %all-to-all-start = ((f32[8,2,64,128]{3,2,1,0:T(8,128)}), f32[8,2,64,128]{3,2,1,0:T(8,128)S(1)}, u32[]{:S(2)}, u32[]{:S(2)}) async-start(f32[8,2,64,128]{3,2,1,0:T(8,128)} %pick_keys.1), calls=%async_computation | async-start | bytes 1048576 | tf_op jit(solution)/shard_map/all_to_all | solution.py:312
  37.2 73.7 %all-gather.9.cloned.1.call-start = ((), (), s32[]{:S(2)}) async-start(), calls=%async_computation.5 | async-start | bytes 4718592 | tf_op jit(solution)/shard_map/all_gather | solution.py:320
  37.3 13.4 %collective-permute-start.2 = (f32[64,2048]{1,0:T(8,128)}, f32[64,2048]{1,0:T(8,128)S(1)}, u32[]{:S(2)}, u32[]{:S(2)}) collective-permute-start(f32[64,2048]{1,0:T(8,128)} %get-tuple-element.33), channel_id=1, source_target_pairs={{0,128},{64,192},{128,0},{192,64},{1,129},{65,193},{129,1},{193,65... | collective-permute-start | bytes 1572872 | tf_op jit(solution)/shard_map/ppermute | solution.py:292
  38.9 23.2 %collective-permute-start.3 = (f32[64,2048]{1,0:T(8,128)}, f32[64,2048]{1,0:T(8,128)S(1)}, u32[]{:S(2)}, u32[]{:S(2)}) collective-permute-start(f32[64,2048]{1,0:T(8,128)} %get-tuple-element.34), channel_id=1, source_target_pairs={{0,192},{64,0},{128,64},{192,128},{1,193},{65,1},{129,65},{193,129... | collective-permute-start | bytes 1572872 | tf_op jit(solution)/shard_map/ppermute | solution.py:292
  39.8 3.8 %collective-permute-start = (f32[2,4,16,512]{3,2,1,0:T(8,128)S(1)}, f32[2,4,16,512]{3,2,1,0:T(8,128)S(1)}, u32[]{:S(2)}, u32[]{:S(2)}) collective-permute-start(f32[2,4,16,512]{3,2,1,0:T(8,128)S(1)} %get-tuple-element.58), channel_id=1, source_target_pairs={{0,1},{1,0},{2,3},{3,2},{4,5},{5,4},{6,7},{7,6},{8,9},{9,8},{10,11... | collective-permute-start | bytes 786440 | tf_op jit(solution)/shard_map/ppermute | solution.py:316
  50.7 23.1 %copy-start.2 = (f32[64,2048]{1,0:T(8,128)}, f32[64,2048]{1,0:T(8,128)S(1)}, u32[]{:S(2)}) copy-start(f32[64,2048]{1,0:T(8,128)S(1)} %collective-permute-done.2.second) | copy-start | bytes 1572868
  66.3 20.7 %all-to-all-start.1 = ((f32[16,16,512]{2,1,0:T(8,128)}), f32[16,16,512]{2,1,0:T(8,128)S(1)}, u32[]{:S(2)}, u32[]{:S(2)}) async-start(f32[16,16,512]{2,1,0:T(8,128)} %bitcast.7), calls=%async_computation.1 | async-start | bytes 1048576 | tf_op jit(solution)/shard_map/all_to_all | solution.py:319
  73.6 73.7 %all-gather.11.cloned.1.call-start = ((), (), s32[]{:S(2)}) async-start(), calls=%async_computation.6 | async-start | bytes 4718592 | tf_op jit(solution)/shard_map/all_gather | solution.py:337
  80.4 6.7 %collective-permute-start.4 = (f32[256,128]{1,0:T(8,128)}, f32[256,128]{1,0:T(8,128)S(1)}, u32[]{:S(2)}, u32[]{:S(2)}) collective-permute-start(f32[256,128]{1,0:T(8,128)} %get-tuple-element.40), channel_id=1, source_target_pairs={{0,64},{64,128},{128,192},{192,0},{1,65},{65,129},{129,193},{193,1... | collective-permute-start | bytes 393224 | tf_op jit(solution)/shard_map/ppermute | solution.py:292
  81.8 7.5 %collective-permute-start.5 = (f32[256,128]{1,0:T(8,128)}, f32[256,128]{1,0:T(8,128)S(1)}, u32[]{:S(2)}, u32[]{:S(2)}) collective-permute-start(f32[256,128]{1,0:T(8,128)} %get-tuple-element.41), channel_id=1, source_target_pairs={{0,128},{64,192},{128,0},{192,64},{1,129},{65,193},{129,1},{193,65... | collective-permute-start | bytes 393224 | tf_op jit(solution)/shard_map/ppermute | solution.py:292
  84.2 5.8 %collective-permute-start.6 = (f32[256,128]{1,0:T(8,128)}, f32[256,128]{1,0:T(8,128)S(1)}, u32[]{:S(2)}, u32[]{:S(2)}) collective-permute-start(f32[256,128]{1,0:T(8,128)} %get-tuple-element.42), channel_id=1, source_target_pairs={{0,192},{64,0},{128,64},{192,128},{1,193},{65,1},{129,65},{193,129... | collective-permute-start | bytes 393224 | tf_op jit(solution)/shard_map/ppermute | solution.py:292
  87.0 24.0 %copy-start.7 = (f32[256,128]{1,0:T(8,128)}, f32[256,128]{1,0:T(8,128)S(1)}, u32[]{:S(2)}) copy-start(f32[256,128]{1,0:T(8,128)S(1)} %collective-permute-done.4.second) | copy-start | bytes 393220
  153.8 6.7 %collective-permute-start.7 = (f32[2,64,512]{2,1,0:T(8,128)}, f32[2,64,512]{2,1,0:T(8,128)S(1)}, u32[]{:S(2)}, u32[]{:S(2)}) collective-permute-start(f32[2,64,512]{2,1,0:T(8,128)} %get-tuple-element.52), channel_id=1, source_target_pairs={{0,64},{64,128},{128,192},{192,0},{1,65},{65,129},{129,193},{193,1... | collective-permute-start | bytes 786440 | tf_op jit(solution)/shard_map/ppermute | solution.py:292
  154.0 10.6 %collective-permute-start.8 = (f32[2,64,512]{2,1,0:T(8,128)}, f32[2,64,512]{2,1,0:T(8,128)S(1)}, u32[]{:S(2)}, u32[]{:S(2)}) collective-permute-start(f32[2,64,512]{2,1,0:T(8,128)} %get-tuple-element.53), channel_id=1, source_target_pairs={{0,128},{64,192},{128,0},{192,64},{1,129},{65,193},{129,1},{193,65... | collective-permute-start | bytes 786440 | tf_op jit(solution)/shard_map/ppermute | solution.py:292
  157.8 6.9 %collective-permute-start.9 = (f32[2,64,512]{2,1,0:T(8,128)}, f32[2,64,512]{2,1,0:T(8,128)S(1)}, u32[]{:S(2)}, u32[]{:S(2)}) collective-permute-start(f32[2,64,512]{2,1,0:T(8,128)} %get-tuple-element.54), channel_id=1, source_target_pairs={{0,192},{64,0},{128,64},{192,128},{1,193},{65,1},{129,65},{193,129... | collective-permute-start | bytes 786440 | tf_op jit(solution)/shard_map/ppermute | solution.py:292
  165.7 7.5 %collective-permute-start.10 = (f32[64,512]{1,0:T(8,128)S(1)}, f32[64,512]{1,0:T(8,128)S(1)}, u32[]{:S(2)}, u32[]{:S(2)}) collective-permute-start(f32[64,512]{1,0:T(8,128)S(1)} %dynamic-slice_bitcast_fusion.2), channel_id=1, source_target_pairs={{0,1},{1,0},{2,3},{3,2},{4,5},{5,4},{6,7},{7,6},{8,9},{9,8},{10,11... | collective-permute-start | bytes 393224 | tf_op jit(solution)/shard_map/ppermute | solution.py:345
  (4 other events, 55.4 us)
Sparse Core Ops, SparseCore 0:
  9.2 38.8 all-gather.6
  63.2 39.9 all-gather.8
  111.1 34.1 all-gather.10

commit v11 on v9

--- a/solution.py
+++ b/solution.py
@@ -318,11 +318,6 @@
     rows, near, hidden = lax.optimization_barrier((rows, near, hidden))
     rows = lax.all_to_all(rows.reshape(NX * NY, 16, 512), ("x", "y"), 0, 0)
     kv = lax.all_gather(near, ("y", "k"), axis=0)
-    partial = project(where, hidden_rows, hidden, weights)
-    partial = [partial[0]] + [along("x", partial[s], s) for s in range(1, NX)]
-    rows, partial = lax.optimization_barrier((rows, partial))
-    rows = lax.all_to_all(rows.reshape(NZ, NK, 16, 512), "z", 0, 0)
-    out_weight = lax.all_gather(rows, ("y", "k"), axis=0)
     key_block = jnp.arange(NY, dtype=jnp.int32)[:, None, None]
     key_block = key_block + 4 * jnp.arange(NK, dtype=jnp.int32)[None, :, None]
     key_block = key_block + 8 * jnp.arange(NZ, dtype=jnp.int32)[None, None, :]
@@ -335,6 +330,11 @@
         slash_offsets,
         slash_count,
     )
+    partial = project(where, hidden_rows, hidden, weights)
+    rows, partial, low, up = lax.optimization_barrier((rows, partial, low, up))
+    partial = [partial[0]] + [along("x", partial[s], s) for s in range(1, NX)]
+    rows = lax.all_to_all(rows.reshape(NZ, NK, 16, 512), "z", 0, 0)
+    out_weight = lax.all_gather(rows, ("y", "k"), axis=0)
     heads = attend(partial, low, up, kv)
     heads = lax.all_to_all(heads, "z", 0, 0)
     mixed = mix(where, heads, out_weight)

time: 168 us -> 169 us (level)
  blocking collectives: 49.7 us -> 47.9 us
  waiting for transfers between devices: 31.8 us -> 33.6 us
    all_to_all x1, waiting for transfers between devices: 0.01 us -> 2.54 us  [shards(): rows = lax.all_to_all(rows.reshape(NX * NY, 16, 512), ('x', 'y'), 0, 0)]
    ppermute x9, starting transfers between devices: 13.5 us -> 11.6 us  [along(): lax.ppermute(value, axis, [(i, (i + shift) % count) for i in range(count)])]
    ppermute x1, starting transfers between devices: 6.64 us -> 8.4 us  [shards(): other = lax.ppermute(other, 'k', CORES)]
  transfers between devices with their start and end apart: 16 -> 16, of which waited for: 10 -> 9; matrix products, arithmetic and copies ran while one was open for 4% -> 4% of each run, Pallas kernels for 11% -> 11%
where the time goes in v11:
time: 169 us; the launch traced here: 168 us
  blocking collectives  47.9 us (28%)
  starting transfers between devices  38.3 us (23%)
  waiting for transfers between devices  33.6 us (20%)
  Pallas kernels  25.3 us (15%)
  between operations  13.3 us (8%)
  other arithmetic  5.2 us (3%)
  local copies, waits for them, and re-layouts  4.69 us (3%)
    ppermute x9, waiting for transfers between devices, along(): lax.ppermute(value, axis, [(i, (i + shift) % count) for i in range(count)])  28.2 us
    all_to_all x1, blocking collectives, shards(): heads = lax.all_to_all(heads, 'z', 0, 0)  27 us
    all_to_all x1, blocking collectives, shards(): rows = lax.all_to_all(rows.reshape(NZ, NK, 16, 512), 'z', 0, 0)  20.8 us
    ppermute x9, starting transfers between devices, along(): lax.ppermute(value, axis, [(i, (i + shift) % count) for i in range(count)])  11.6 us
    all_to_all x1, starting transfers between devices, shards(): near = lax.all_to_all(pick_keys(behind, key_cache, value_cache), 'z', 0, 0)  9.03 us
    ppermute x1, starting transfers between devices, shards(): other = lax.ppermute(other, 'k', CORES)  8.4 us
    pallas_call x1, Pallas kernels, attend(): pl.pallas_call(attend_kernel, out_shape=jax.ShapeDtypeStruct((NZ, rows, H...  7.51 us
    all_to_all x1, starting transfers between devices, shards(): rows = lax.all_to_all(rows.reshape(NX * NY, 16, 512), ('x', 'y'), 0, 0)  7.28 us
  transfers between devices with their start and end apart: 16, of which 9 were waited for; matrix products, arithmetic and copies ran while one was open for 4% of the time, Pallas kernels for 11%

profile of v11, /device:TPU:1, one launch (start us, length us, event | category | flops | bytes accessed | tf_op | source)
XLA Modules:
  0.0 168.2 jit_solution(15082495115385245580)
XLA Ops:
  7.9 3.4 %pick.1 = (f32[64,2048]{1,0:T(8,128)}, f32[64,2048]{1,0:T(8,128)}, f32[64,2048]{1,0:T(8,128)}) custom-call(s32[3]{0:T(128)} %pad_add_fusion.where, f32[128,8192]{1,0:T(8,128)} %rows.3), custom_call_target="tpu_custom_call" | custom-call | tf_op jit(solution)/shard_map/pick/pallas_call | solution.py:55
  11.3 2.6 %pick_keys.1 = f32[8,2,64,128]{3,2,1,0:T(8,128)} custom-call(s32[3]{0:T(128)} %pad_add_fusion.where, f32[256,512]{1,0:T(8,128)} %keys.1, f32[256,512]{1,0:T(8,128)} %values.1), custom_call_target="tpu_custom_call" | custom-call | bytes 67108864 | tf_op jit(solution)/shard_map/pick_keys/pallas_call | solution.py:82
  14.0 9.0 %all-to-all-start = ((f32[8,2,64,128]{3,2,1,0:T(8,128)}), f32[8,2,64,128]{3,2,1,0:T(8,128)S(1)}, u32[]{:S(2)}, u32[]{:S(2)}) async-start(f32[8,2,64,128]{3,2,1,0:T(8,128)} %pick_keys.1), calls=%async_computation | async-start | bytes 1048576 | tf_op jit(solution)/shard_map/all_to_all | solution.py:312
  23.0 1.3 collective-permute-start.1
  24.3 2.5 %collective-permute-start.2 = (f32[64,2048]{1,0:T(8,128)}, f32[64,2048]{1,0:T(8,128)S(1)}, u32[]{:S(2)}, u32[]{:S(2)}) collective-permute-start(f32[64,2048]{1,0:T(8,128)} %get-tuple-element.30), channel_id=1, source_target_pairs={{0,128},{64,192},{128,0},{192,64},{1,129},{65,193},{129,1},{193,65... | collective-permute-start | bytes 1572872 | tf_op jit(solution)/shard_map/ppermute | solution.py:292
  26.8 1.2 collective-permute-start.3
  28.0 1.9 %collective-permute-start = (f32[2,4,16,512]{3,2,1,0:T(8,128)S(1)}, f32[2,4,16,512]{3,2,1,0:T(8,128)S(1)}, u32[]{:S(2)}, u32[]{:S(2)}) collective-permute-start(f32[2,4,16,512]{3,2,1,0:T(8,128)S(1)} %get-tuple-element.56), channel_id=1, source_target_pairs={{0,1},{1,0},{2,3},{3,2},{4,5},{5,4},{6,7},{7,6},{8,9},{9,8},{10,11... | collective-permute-start | bytes 786440 | tf_op jit(solution)/shard_map/ppermute | solution.py:316
  29.9 1.2 collective-permute-done
  31.9 5.2 %collective-permute-done.1.first = f32[64,2048]{1,0:T(8,128)S(1)} collective-permute-done((f32[64,2048]{1,0:T(8,128)}, f32[64,2048]{1,0:T(8,128)S(1)}, u32[]{:S(2)}, u32[]{:S(2)}) %collective-permute-start.1) | collective-permute-done | bytes 524320 | tf_op jit(solution)/shard_map/ppermute | solution.py:292
  37.1 12.1 %collective-permute-done.2.second = f32[64,2048]{1,0:T(8,128)S(1)} collective-permute-done((f32[64,2048]{1,0:T(8,128)}, f32[64,2048]{1,0:T(8,128)S(1)}, u32[]{:S(2)}, u32[]{:S(2)}) %collective-permute-start.2) | collective-permute-done | bytes 524320 | tf_op jit(solution)/shard_map/ppermute | solution.py:292
  53.5 7.3 %all-to-all-start.1 = ((f32[16,16,512]{2,1,0:T(8,128)}), f32[16,16,512]{2,1,0:T(8,128)S(1)}, u32[]{:S(2)}, u32[]{:S(2)}) async-start(f32[16,16,512]{2,1,0:T(8,128)} %bitcast.7), calls=%async_computation.1 | async-start | bytes 1048576 | tf_op jit(solution)/shard_map/all_to_all | solution.py:319
  62.6 5.8 %project.1 = (f32[256,128]{1,0:T(8,128)}, f32[256,128]{1,0:T(8,128)}, f32[256,128]{1,0:T(8,128)}, f32[256,128]{1,0:T(8,128)}) custom-call(s32[3]{0:T(128)} %pad_add_fusion.where, f32[128,8192]{1,0:T(8,128)} %rows.3, f32[64,2048]{1,0:T(8,128)} %copy-done.1, f32[64,2048]{1,0:T(8,128)} %copy-done.2, f32[64,2048]{1,0:T(8,128)} %copy-done.3, f32[8,512,256]{2,1,0:T(8,128)} %bitcast.33), custom_call_target="tpu_custom_call" | custom-call | flops 1610612736 | bytes 7340032 | tf_op jit(solution)/shard_map/project/pallas_call | solution.py:132
  68.4 2.5 %all-to-all-done.1 = f32[16,16,512]{2,1,0:T(8,128)S(1)} async-done(((f32[16,16,512]{2,1,0:T(8,128)}), f32[16,16,512]{2,1,0:T(8,128)S(1)}, u32[]{:S(2)}, u32[]{:S(2)}) %all-to-all-start.1) | async-done | bytes 524320 | tf_op jit(solution)/shard_map/all_to_all | solution.py:319
  71.0 20.8 %all_to_all.20 = f32[8,2,16,512]{3,2,1,0:T(8,128)} all-to-all(f32[8,2,16,512]{3,2,1,0:T(8,128)S(1)} %bitcast.34), channel_id=1, replica_groups=mesh['x'=4,'y'=4,'z'=8,'k'=2] {'z'}, dimensions={0} | all-to-all | bytes 1048576 | tf_op jit(solution)/shard_map/all_to_all | solution.py:336
  91.9 2.2 %collective-permute-start.5 = (f32[256,128]{1,0:T(8,128)}, f32[256,128]{1,0:T(8,128)S(1)}, u32[]{:S(2)}, u32[]{:S(2)}) collective-permute-start(f32[256,128]{1,0:T(8,128)} %get-tuple-element.43), channel_id=1, source_target_pairs={{0,128},{64,192},{128,0},{192,64},{1,129},{65,193},{129,1},{193,65... | collective-permute-start | bytes 393224 | tf_op jit(solution)/shard_map/ppermute | solution.py:292
  94.6 3.9 %collective-permute-done.4.second = f32[256,128]{1,0:T(8,128)S(1)} collective-permute-done((f32[256,128]{1,0:T(8,128)}, f32[256,128]{1,0:T(8,128)S(1)}, u32[]{:S(2)}, u32[]{:S(2)}) %collective-permute-start.4) | collective-permute-done | bytes 131104 | tf_op jit(solution)/shard_map/ppermute | solution.py:292
  99.8 7.5 %attend.1 = f32[8,256,128]{2,1,0:T(8,128)} custom-call(f32[256,128]{1,0:T(8,128)} %get-tuple-element.41.first, f32[256,128]{1,0:T(8,128)} %copy-done.7, f32[256,128]{1,0:T(8,128)} %copy-done.8, f32[256,128]{1,0:T(8,128)} %copy-done.9, f32[4,4096]{1,0:T(4,128)} %broadcast_in_dim.39.low, f32[4,4096]{1,0:T(4,128)} %broadcast_in_dim.41.up, ...), custom_call_target="tpu_custom_call" | custom-call | flops 1610612736 | bytes 6291456 | tf_op jit(solution)/shard_map/attend/pallas_call | solution.py:200
  107.3 27.0 %all_to_all.21.heads = f32[8,256,128]{2,1,0:T(8,128)} all-to-all(f32[8,256,128]{2,1,0:T(8,128)} %attend.1), channel_id=1, replica_groups=mesh['x'=4,'y'=4,'z'=8,'k'=2] {'z'}, dimensions={0} | all-to-all | bytes 2097152 | tf_op jit(solution)/shard_map/all_to_all | solution.py:339
  134.3 6.0 %mix.1 = (f32[2,64,512]{2,1,0:T(8,128)}, f32[2,64,512]{2,1,0:T(8,128)}, f32[2,64,512]{2,1,0:T(8,128)}, f32[2,64,512]{2,1,0:T(8,128)}) custom-call(s32[3]{0:T(128)} %pad_add_fusion.where, f32[8,256,128]{2,1,0:T(8,128)} %all_to_all.21.heads, f32[8,8,2,16,512]{4,3,2,1,0:T(8,128)} %bitcast.38), custom_call_target="tpu_custom_call" | custom-call | flops 1610612736 | bytes 6291456 | tf_op jit(solution)/shard_map/mix/pallas_call | solution.py:252
  140.8 2.9 %collective-permute-start.8 = (f32[2,64,512]{2,1,0:T(8,128)}, f32[2,64,512]{2,1,0:T(8,128)S(1)}, u32[]{:S(2)}, u32[]{:S(2)}) collective-permute-start(f32[2,64,512]{2,1,0:T(8,128)} %get-tuple-element.51), channel_id=1, source_target_pairs={{0,128},{64,192},{128,0},{192,64},{1,129},{65,193},{129,1},{193,65... | collective-permute-start | bytes 786440 | tf_op jit(solution)/shard_map/ppermute | solution.py:292
  144.2 2.8 %collective-permute-done.7 = f32[2,64,512]{2,1,0:T(8,128)S(1)} collective-permute-done((f32[2,64,512]{2,1,0:T(8,128)}, f32[2,64,512]{2,1,0:T(8,128)S(1)}, u32[]{:S(2)}, u32[]{:S(2)}) %collective-permute-start.7) | collective-permute-done | bytes 262176 | tf_op jit(solution)/shard_map/ppermute | solution.py:292
  147.1 3.4 %collective-permute-done.8 = f32[2,64,512]{2,1,0:T(8,128)S(1)} collective-permute-done((f32[2,64,512]{2,1,0:T(8,128)}, f32[2,64,512]{2,1,0:T(8,128)S(1)}, u32[]{:S(2)}, u32[]{:S(2)}) %collective-permute-start.8) | collective-permute-done | bytes 262176 | tf_op jit(solution)/shard_map/ppermute | solution.py:292
  150.5 1.0 add_add_fusion
  151.6 8.4 %collective-permute-start.10 = (f32[64,512]{1,0:T(8,128)S(1)}, f32[64,512]{1,0:T(8,128)S(1)}, u32[]{:S(2)}, u32[]{:S(2)}) collective-permute-start(f32[64,512]{1,0:T(8,128)S(1)} %dynamic-slice_bitcast_fusion.2), channel_id=1, source_target_pairs={{0,1},{1,0},{2,3},{3,2},{4,5},{5,4},{6,7},{7,6},{8,9},{9,8},{10,11... | collective-permute-start | bytes 393224 | tf_op jit(solution)/shard_map/ppermute | solution.py:345
  (69 shorter events, 12.9 us)
Async XLA Ops:
  6.5 21.4 %copy-start.4 = (f32[256,512]{1,0:T(8,128)S(1)}, f32[256,512]{1,0:T(8,128)}, u32[]{:S(2)}) copy-start(f32[256,512]{1,0:T(8,128)} %param.17) | copy-start | bytes 1572868
  6.5 56.0 %all-gather.7.cloned.1.call-start = ((), (), s32[]{:S(2)}) async-start(), calls=%async_computation.4 | async-start | bytes 4718592 | tf_op jit(solution)/shard_map/all_gather | solution.py:308
  7.9 42.3 %copy-start.10 = (s32[32]{0:T(128)S(1)}, s32[32]{0:T(128)}, u32[]{:S(2)}) copy-start(s32[32]{0:T(128)} %param.14) | copy-start | bytes 388
  7.9 43.0 %copy-start.11 = (s32[32]{0:T(128)S(1)}, s32[32]{0:T(128)}, u32[]{:S(2)}) copy-start(s32[32]{0:T(128)} %param.16) | copy-start | bytes 388
  7.9 43.8 %copy-start.5 = (s32[32,16]{0,1:T(8,128)S(1)}, s32[32,16]{0,1:T(8,128)}, u32[]{:S(2)}) copy-start(s32[32,16]{0,1:T(8,128)} %param.15) | copy-start | bytes 6148
  7.9 43.8 %copy-start.6 = (s32[32,16]{0,1:T(8,128)S(1)}, s32[32,16]{0,1:T(8,128)}, u32[]{:S(2)}) copy-start(s32[32,16]{0,1:T(8,128)} %param.13) | copy-start | bytes 6148
  14.0 35.3 %all-to-all-start = ((f32[8,2,64,128]{3,2,1,0:T(8,128)}), f32[8,2,64,128]{3,2,1,0:T(8,128)S(1)}, u32[]{:S(2)}, u32[]{:S(2)}) async-start(f32[8,2,64,128]{3,2,1,0:T(8,128)} %pick_keys.1), calls=%async_computation | async-start | bytes 1048576 | tf_op jit(solution)/shard_map/all_to_all | solution.py:312
  23.0 76.2 %all-gather.9.cloned.1.call-start = ((), (), s32[]{:S(2)}) async-start(), calls=%async_computation.5 | async-start | bytes 4718592 | tf_op jit(solution)/shard_map/all_gather | solution.py:320
  23.0 14.1 %collective-permute-start.1 = (f32[64,2048]{1,0:T(8,128)}, f32[64,2048]{1,0:T(8,128)S(1)}, u32[]{:S(2)}, u32[]{:S(2)}) collective-permute-start(f32[64,2048]{1,0:T(8,128)} %get-tuple-element.29), channel_id=1, source_target_pairs={{0,64},{64,128},{128,192},{192,0},{1,65},{65,129},{129,193},{193,1... | collective-permute-start | bytes 1572872 | tf_op jit(solution)/shard_map/ppermute | solution.py:292
  24.3 24.9 %collective-permute-start.2 = (f32[64,2048]{1,0:T(8,128)}, f32[64,2048]{1,0:T(8,128)S(1)}, u32[]{:S(2)}, u32[]{:S(2)}) collective-permute-start(f32[64,2048]{1,0:T(8,128)} %get-tuple-element.30), channel_id=1, source_target_pairs={{0,128},{64,192},{128,0},{192,64},{1,129},{65,193},{129,1},{193,65... | collective-permute-start | bytes 1572872 | tf_op jit(solution)/shard_map/ppermute | solution.py:292
  26.8 22.5 %collective-permute-start.3 = (f32[64,2048]{1,0:T(8,128)}, f32[64,2048]{1,0:T(8,128)S(1)}, u32[]{:S(2)}, u32[]{:S(2)}) collective-permute-start(f32[64,2048]{1,0:T(8,128)} %get-tuple-element.31), channel_id=1, source_target_pairs={{0,192},{64,0},{128,64},{192,128},{1,193},{65,1},{129,65},{193,129... | collective-permute-start | bytes 1572872 | tf_op jit(solution)/shard_map/ppermute | solution.py:292
  28.0 3.0 %collective-permute-start = (f32[2,4,16,512]{3,2,1,0:T(8,128)S(1)}, f32[2,4,16,512]{3,2,1,0:T(8,128)S(1)}, u32[]{:S(2)}, u32[]{:S(2)}) collective-permute-start(f32[2,4,16,512]{3,2,1,0:T(8,128)S(1)} %get-tuple-element.56), channel_id=1, source_target_pairs={{0,1},{1,0},{2,3},{3,2},{4,5},{5,4},{6,7},{7,6},{8,9},{9,8},{10,11... | collective-permute-start | bytes 786440 | tf_op jit(solution)/shard_map/ppermute | solution.py:316
  37.1 25.5 %copy-start.1 = (f32[64,2048]{1,0:T(8,128)}, f32[64,2048]{1,0:T(8,128)S(1)}, u32[]{:S(2)}) copy-start(f32[64,2048]{1,0:T(8,128)S(1)} %collective-permute-done.1.first) | copy-start | bytes 1572868
  49.2 13.4 %copy-start.2 = (f32[64,2048]{1,0:T(8,128)}, f32[64,2048]{1,0:T(8,128)S(1)}, u32[]{:S(2)}) copy-start(f32[64,2048]{1,0:T(8,128)S(1)} %collective-permute-done.2.second) | copy-start | bytes 1572868
  49.3 13.3 %copy-start.3 = (f32[64,2048]{1,0:T(8,128)}, f32[64,2048]{1,0:T(8,128)S(1)}, u32[]{:S(2)}) copy-start(f32[64,2048]{1,0:T(8,128)S(1)} %collective-permute-done.3.third) | copy-start | bytes 1572868
  53.5 17.5 %all-to-all-start.1 = ((f32[16,16,512]{2,1,0:T(8,128)}), f32[16,16,512]{2,1,0:T(8,128)S(1)}, u32[]{:S(2)}, u32[]{:S(2)}) async-start(f32[16,16,512]{2,1,0:T(8,128)} %bitcast.7), calls=%async_computation.1 | async-start | bytes 1048576 | tf_op jit(solution)/shard_map/all_to_all | solution.py:319
  60.8 73.6 %all-gather.11.cloned.1.call-start = ((), (), s32[]{:S(2)}) async-start(), calls=%async_computation.6 | async-start | bytes 4718592 | tf_op jit(solution)/shard_map/all_gather | solution.py:337
  91.8 6.7 %collective-permute-start.4 = (f32[256,128]{1,0:T(8,128)}, f32[256,128]{1,0:T(8,128)S(1)}, u32[]{:S(2)}, u32[]{:S(2)}) collective-permute-start(f32[256,128]{1,0:T(8,128)} %get-tuple-element.42), channel_id=1, source_target_pairs={{0,64},{64,128},{128,192},{192,0},{1,65},{65,129},{129,193},{193,1... | collective-permute-start | bytes 393224 | tf_op jit(solution)/shard_map/ppermute | solution.py:292
  91.9 6.6 %collective-permute-start.5 = (f32[256,128]{1,0:T(8,128)}, f32[256,128]{1,0:T(8,128)S(1)}, u32[]{:S(2)}, u32[]{:S(2)}) collective-permute-start(f32[256,128]{1,0:T(8,128)} %get-tuple-element.43), channel_id=1, source_target_pairs={{0,128},{64,192},{128,0},{192,64},{1,129},{65,193},{129,1},{193,65... | collective-permute-start | bytes 393224 | tf_op jit(solution)/shard_map/ppermute | solution.py:292
  94.1 5.1 %collective-permute-start.6 = (f32[256,128]{1,0:T(8,128)}, f32[256,128]{1,0:T(8,128)S(1)}, u32[]{:S(2)}, u32[]{:S(2)}) collective-permute-start(f32[256,128]{1,0:T(8,128)} %get-tuple-element.44), channel_id=1, source_target_pairs={{0,192},{64,0},{128,64},{192,128},{1,193},{65,1},{129,65},{193,129... | collective-permute-start | bytes 393224 | tf_op jit(solution)/shard_map/ppermute | solution.py:292
  140.3 6.7 %collective-permute-start.7 = (f32[2,64,512]{2,1,0:T(8,128)}, f32[2,64,512]{2,1,0:T(8,128)S(1)}, u32[]{:S(2)}, u32[]{:S(2)}) collective-permute-start(f32[2,64,512]{2,1,0:T(8,128)} %get-tuple-element.50), channel_id=1, source_target_pairs={{0,64},{64,128},{128,192},{192,0},{1,65},{65,129},{129,193},{193,1... | collective-permute-start | bytes 786440 | tf_op jit(solution)/shard_map/ppermute | solution.py:292
  140.8 9.7 %collective-permute-start.8 = (f32[2,64,512]{2,1,0:T(8,128)}, f32[2,64,512]{2,1,0:T(8,128)S(1)}, u32[]{:S(2)}, u32[]{:S(2)}) collective-permute-start(f32[2,64,512]{2,1,0:T(8,128)} %get-tuple-element.51), channel_id=1, source_target_pairs={{0,128},{64,192},{128,0},{192,64},{1,129},{65,193},{129,1},{193,65... | collective-permute-start | bytes 786440 | tf_op jit(solution)/shard_map/ppermute | solution.py:292
  143.7 6.8 %collective-permute-start.9 = (f32[2,64,512]{2,1,0:T(8,128)}, f32[2,64,512]{2,1,0:T(8,128)S(1)}, u32[]{:S(2)}, u32[]{:S(2)}) collective-permute-start(f32[2,64,512]{2,1,0:T(8,128)} %get-tuple-element.52), channel_id=1, source_target_pairs={{0,192},{64,0},{128,64},{192,128},{1,193},{65,1},{129,65},{193,129... | collective-permute-start | bytes 786440 | tf_op jit(solution)/shard_map/ppermute | solution.py:292
  151.6 9.4 %collective-permute-start.10 = (f32[64,512]{1,0:T(8,128)S(1)}, f32[64,512]{1,0:T(8,128)S(1)}, u32[]{:S(2)}, u32[]{:S(2)}) collective-permute-start(f32[64,512]{1,0:T(8,128)S(1)} %dynamic-slice_bitcast_fusion.2), channel_id=1, source_target_pairs={{0,1},{1,0},{2,3},{3,2},{4,5},{5,4},{6,7},{7,6},{8,9},{9,8},{10,11... | collective-permute-start | bytes 393224 | tf_op jit(solution)/shard_map/ppermute | solution.py:345
  (4 other events, 3.0 us)
Sparse Core Ops, SparseCore 0:
  9.2 38.8 all-gather.6
  50.4 39.9 all-gather.8
  92.2 33.1 all-gather.10

commit v12 on v11

--- a/solution.py
+++ b/solution.py
@@ -216,28 +216,13 @@
 
 
 def mix_kernel(where, heads, weights, *refs):
-    outs, (total_buf, buf, sem) = refs[:NX], refs[NX:]
-    steps = NZ // 2
-    copies = []
-    for step in range(steps):
-        copies.append(
-            [
-                pltpu.make_async_copy(
-                    weights.at[part, pl.ds(2 * step, 2)], buf.at[step, part], sem.at[step, part]
-                )
-                for part in range(8)
-            ]
-        )
-        for copy in copies[step]:
-            copy.start()
+    outs, total_buf = refs[:NX], refs[NX]
     totals = [None, None]
-    for step in range(steps):
+    for step in range(NZ // 2):
         left = split(jnp.concatenate([heads[2 * step], heads[2 * step + 1]], axis=1))
-        for copy in copies[step]:
-            copy.wait()
         for core in range(NK):
             right = jnp.concatenate(
-                [buf[step, :, z, core].reshape(HD, 512) for z in range(2)], axis=0
+                [weights[:, 2 * step + z, core].reshape(HD, 512) for z in range(2)], axis=0
             )
             term = dot3(left, split(right), MM)
             totals[core] = term if totals[core] is None else totals[core] + term
@@ -252,14 +237,10 @@
     return pl.pallas_call(
         mix_kernel,
         out_shape=[jax.ShapeDtypeStruct((NK, BLOCK, 512), jnp.float32)] * NX,
-        in_specs=[SMEM, VMEM, ANY],
+        in_specs=[SMEM, VMEM, VMEM],
         out_specs=[VMEM] * NX,
-        scratch_shapes=[
-            pltpu.VMEM((NX, NK, BLOCK, 512), jnp.float32),
-            pltpu.VMEM((NZ // 2, 8, 2, NK, 16, 512), jnp.float32),
-            pltpu.SemaphoreType.DMA((NZ // 2, 8)),
-        ],
-        compiler_params=pltpu.CompilerParams(vmem_limit_bytes=LIMIT),
+        scratch_shapes=[pltpu.VMEM((NX, NK, BLOCK, 512), jnp.float32)],
+        compiler_params=pltpu.CompilerParams(vmem_limit_bytes=24 << 20),
         cost_estimate=pl.CostEstimate(
             flops=6 * 256 * 1024 * 1024, bytes_accessed=6 << 20, transcendentals=0
         ),
@@ -331,8 +312,8 @@
         slash_count,
     )
     partial = project(where, hidden_rows, hidden, weights)
+    partial = [partial[0]] + [along("x", partial[s], s) for s in range(1, NX)]
     rows, partial, low, up = lax.optimization_barrier((rows, partial, low, up))
-    partial = [partial[0]] + [along("x", partial[s], s) for s in range(1, NX)]
     rows = lax.all_to_all(rows.reshape(NZ, NK, 16, 512), "z", 0, 0)
     out_weight = lax.all_gather(rows, ("y", "k"), axis=0)
     heads = attend(partial, low, up, kv)

time: 169 us -> 163 us (0.964)
  Pallas kernels: 25.3 us -> 21.3 us
  waiting for transfers between devices: 33.6 us -> 29.8 us
    pallas_call x1, Pallas kernels: 5.99 us -> 2.47 us  [mix(): pl.pallas_call(mix_kernel, out_shape=[jax.ShapeDtypeStruct((NK, BLOCK, 51...]
    all_to_all x1, waiting for transfers between devices: 2.54 us -> 0.01 us  [shards(): rows = lax.all_to_all(rows.reshape(NX * NY, 16, 512), ('x', 'y'), 0, 0)]
    ppermute x9, starting transfers between devices: 11.6 us -> 13.5 us  [along(): lax.ppermute(value, axis, [(i, (i + shift) % count) for i in range(count)])]
    ppermute x1, starting transfers between devices: 8.4 us -> 6.67 us  [shards(): other = lax.ppermute(other, 'k', CORES)]
  transfers between devices with their start and end apart: 16 -> 16, of which waited for: 9 -> 8; matrix products, arithmetic and copies ran while one was open for 4% -> 4% of each run, Pallas kernels for 11% -> 12%
where the time goes in v12:
time: 163 us; the launch traced here: 162 us
  blocking collectives  48.6 us (30%)
  starting transfers between devices  38.5 us (24%)
  waiting for transfers between devices  29.8 us (18%)
  Pallas kernels  21.3 us (13%)
  between operations  13.4 us (8%)
  local copies, waits for them, and re-layouts  6.22 us (4%)
  other arithmetic  4.2 us (3%)
    all_to_all x1, blocking collectives, shards(): heads = lax.all_to_all(heads, 'z', 0, 0)  27.7 us
    ppermute x9, waiting for transfers between devices, along(): lax.ppermute(value, axis, [(i, (i + shift) % count) for i in range(count)])  26.8 us
    all_to_all x1, blocking collectives, shards(): rows = lax.all_to_all(rows.reshape(NZ, NK, 16, 512), 'z', 0, 0)  20.9 us
    ppermute x9, starting transfers between devices, along(): lax.ppermute(value, axis, [(i, (i + shift) % count) for i in range(count)])  13.5 us
    all_to_all x1, starting transfers between devices, shards(): near = lax.all_to_all(pick_keys(behind, key_cache, value_cache), 'z', 0, 0)  9.03 us
    pallas_call x1, Pallas kernels, attend(): pl.pallas_call(attend_kernel, out_shape=jax.ShapeDtypeStruct((NZ, rows, H...  7.47 us
    all_to_all x1, starting transfers between devices, shards(): rows = lax.all_to_all(rows.reshape(NX * NY, 16, 512), ('x', 'y'), 0, 0)  7.31 us
    ppermute x1, starting transfers between devices, shards(): other = lax.ppermute(other, 'k', CORES)  6.67 us
  transfers between devices with their start and end apart: 16, of which 8 were waited for; matrix products, arithmetic and copies ran while one was open for 4% of the time, Pallas kernels for 12%

profile of v12, /device:TPU:1, one launch (start us, length us, event | category | flops | bytes accessed | tf_op | source)
XLA Modules:
  0.0 162.0 jit_solution(14903415050097385352)
XLA Ops:
  7.9 3.4 %pick.1 = (f32[64,2048]{1,0:T(8,128)}, f32[64,2048]{1,0:T(8,128)}, f32[64,2048]{1,0:T(8,128)}) custom-call(s32[3]{0:T(128)} %pad_add_fusion.where, f32[128,8192]{1,0:T(8,128)} %rows.3), custom_call_target="tpu_custom_call" | custom-call | tf_op jit(solution)/shard_map/pick/pallas_call | solution.py:55
  11.3 2.6 %pick_keys.1 = f32[8,2,64,128]{3,2,1,0:T(8,128)} custom-call(s32[3]{0:T(128)} %pad_add_fusion.where, f32[256,512]{1,0:T(8,128)} %keys.1, f32[256,512]{1,0:T(8,128)} %values.1), custom_call_target="tpu_custom_call" | custom-call | bytes 67108864 | tf_op jit(solution)/shard_map/pick_keys/pallas_call | solution.py:82
  13.9 9.0 %all-to-all-start = ((f32[8,2,64,128]{3,2,1,0:T(8,128)}), f32[8,2,64,128]{3,2,1,0:T(8,128)S(1)}, u32[]{:S(2)}, u32[]{:S(2)}) async-start(f32[8,2,64,128]{3,2,1,0:T(8,128)} %pick_keys.1), calls=%async_computation | async-start | bytes 1048576 | tf_op jit(solution)/shard_map/all_to_all | solution.py:293
  23.0 1.3 collective-permute-start.1
  24.3 2.5 %collective-permute-start.2 = (f32[64,2048]{1,0:T(8,128)}, f32[64,2048]{1,0:T(8,128)S(1)}, u32[]{:S(2)}, u32[]{:S(2)}) collective-permute-start(f32[64,2048]{1,0:T(8,128)} %get-tuple-element.30), channel_id=1, source_target_pairs={{0,128},{64,192},{128,0},{192,64},{1,129},{65,193},{129,1},{193,65... | collective-permute-start | bytes 1572872 | tf_op jit(solution)/shard_map/ppermute | solution.py:273
  27.9 1.9 %collective-permute-start = (f32[2,4,16,512]{3,2,1,0:T(8,128)S(1)}, f32[2,4,16,512]{3,2,1,0:T(8,128)S(1)}, u32[]{:S(2)}, u32[]{:S(2)}) collective-permute-start(f32[2,4,16,512]{3,2,1,0:T(8,128)S(1)} %get-tuple-element.56), channel_id=1, source_target_pairs={{0,1},{1,0},{2,3},{3,2},{4,5},{5,4},{6,7},{7,6},{8,9},{9,8},{10,11... | collective-permute-start | bytes 786440 | tf_op jit(solution)/shard_map/ppermute | solution.py:297
  29.8 1.2 collective-permute-done
  31.8 5.2 %collective-permute-done.1.first = f32[64,2048]{1,0:T(8,128)S(1)} collective-permute-done((f32[64,2048]{1,0:T(8,128)}, f32[64,2048]{1,0:T(8,128)S(1)}, u32[]{:S(2)}, u32[]{:S(2)}) %collective-permute-start.1) | collective-permute-done | bytes 524320 | tf_op jit(solution)/shard_map/ppermute | solution.py:273
  37.1 12.1 %collective-permute-done.2.second = f32[64,2048]{1,0:T(8,128)S(1)} collective-permute-done((f32[64,2048]{1,0:T(8,128)}, f32[64,2048]{1,0:T(8,128)S(1)}, u32[]{:S(2)}, u32[]{:S(2)}) %collective-permute-start.2) | collective-permute-done | bytes 524320 | tf_op jit(solution)/shard_map/ppermute | solution.py:273
  53.4 7.3 %all-to-all-start.1 = ((f32[16,16,512]{2,1,0:T(8,128)}), f32[16,16,512]{2,1,0:T(8,128)S(1)}, u32[]{:S(2)}, u32[]{:S(2)}) async-start(f32[16,16,512]{2,1,0:T(8,128)} %bitcast.7), calls=%async_computation.1 | async-start | bytes 1048576 | tf_op jit(solution)/shard_map/all_to_all | solution.py:300
  60.9 5.4 %project.1 = (f32[256,128]{1,0:T(8,128)}, f32[256,128]{1,0:T(8,128)}, f32[256,128]{1,0:T(8,128)}, f32[256,128]{1,0:T(8,128)}) custom-call(s32[3]{0:T(128)} %pad_add_fusion.where, f32[128,8192]{1,0:T(8,128)} %rows.3, f32[64,2048]{1,0:T(8,128)} %copy-done.3, f32[64,2048]{1,0:T(8,128)} %copy-done.4, f32[64,2048]{1,0:T(8,128)} %copy-done.5, f32[8,512,256]{2,1,0:T(8,128)} %bitcast.34), custom_call_target="tpu_custom_call" | custom-call | flops 1610612736 | bytes 7340032 | tf_op jit(solution)/shard_map/project/pallas_call | solution.py:132
  66.3 1.4 collective-permute-start.4
  67.7 2.4 %collective-permute-start.5 = (f32[256,128]{1,0:T(8,128)}, f32[256,128]{1,0:T(8,128)S(1)}, u32[]{:S(2)}, u32[]{:S(2)}) collective-permute-start(f32[256,128]{1,0:T(8,128)} %get-tuple-element.39), channel_id=1, source_target_pairs={{0,128},{64,192},{128,0},{192,64},{1,129},{65,193},{129,1},{193,65... | collective-permute-start | bytes 393224 | tf_op jit(solution)/shard_map/ppermute | solution.py:273
  70.1 1.2 collective-permute-start.6
  73.0 1.8 %collective-permute-done.5.third = f32[256,128]{1,0:T(8,128)S(1)} collective-permute-done((f32[256,128]{1,0:T(8,128)}, f32[256,128]{1,0:T(8,128)S(1)}, u32[]{:S(2)}, u32[]{:S(2)}) %collective-permute-start.5) | collective-permute-done | bytes 131104 | tf_op jit(solution)/shard_map/ppermute | solution.py:273
  75.8 20.9 %all_to_all.20 = f32[8,2,16,512]{3,2,1,0:T(8,128)} all-to-all(f32[8,2,16,512]{3,2,1,0:T(8,128)S(1)} %bitcast.35), channel_id=1, replica_groups=mesh['x'=4,'y'=4,'z'=8,'k'=2] {'z'}, dimensions={0} | all-to-all | bytes 1048576 | tf_op jit(solution)/shard_map/all_to_all | solution.py:317
  96.8 7.5 %attend.1 = f32[8,256,128]{2,1,0:T(8,128)} custom-call(f32[256,128]{1,0:T(8,128)} %get-tuple-element.41.first, f32[256,128]{1,0:T(8,128)} %copy-done.9, f32[256,128]{1,0:T(8,128)} %copy-done.10, f32[256,128]{1,0:T(8,128)} %copy-done.11, f32[4,4096]{1,0:T(4,128)} %broadcast_in_dim.39.low, f32[4,4096]{1,0:T(4,128)} %broadcast_in_dim.41.up, ...), custom_call_target="tpu_custom_call" | custom-call | flops 1610612736 | bytes 6291456 | tf_op jit(solution)/shard_map/attend/pallas_call | solution.py:200
  104.3 27.7 %all_to_all.21.heads = f32[8,256,128]{2,1,0:T(8,128)S(1)} all-to-all(f32[8,256,128]{2,1,0:T(8,128)} %attend.1), channel_id=1, replica_groups=mesh['x'=4,'y'=4,'z'=8,'k'=2] {'z'}, dimensions={0} | all-to-all | bytes 2097152 | tf_op jit(solution)/shard_map/all_to_all | solution.py:320
  132.0 2.2 %copy-done.1 = f32[64,2,16,512]{3,2,1,0:T(8,128)S(1)} copy-done((f32[64,2,16,512]{3,2,1,0:T(8,128)S(1)}, f32[64,2,16,512]{3,2,1,0:T(8,128)}, u32[]{:S(2)}) %copy-start.1) | copy-done | bytes 4194328
  134.2 2.5 %mix.1 = (f32[2,64,512]{2,1,0:T(8,128)S(1)}, f32[2,64,512]{2,1,0:T(8,128)S(1)}, f32[2,64,512]{2,1,0:T(8,128)S(1)}, f32[2,64,512]{2,1,0:T(8,128)S(1)}) custom-call(s32[3]{0:T(128)S(1)} %copy-done, f32[8,256,128]{2,1,0:T(8,128)S(1)} %all_to_all.21.heads, f32[8,8,2,16,512]{4,3,2,1,0:T(8,128)S(1)} %bitcast.33), custom_call_target="tpu_custom_call" | custom-call | flops 1610612736 | bytes 6291456 | tf_op jit(solution)/shard_map/mix/pallas_call | solution.py:237
  136.7 3.6 %collective-permute-start.8 = (f32[2,64,512]{2,1,0:T(8,128)S(1)}, f32[2,64,512]{2,1,0:T(8,128)S(1)}, u32[]{:S(2)}, u32[]{:S(2)}) collective-permute-start(f32[2,64,512]{2,1,0:T(8,128)S(1)} %get-tuple-element.51), channel_id=1, source_target_pairs={{0,128},{64,192},{128,0},{192,64},{1,129},{65,193},{129,1},{193,65... | collective-permute-start | bytes 786440 | tf_op jit(solution)/shard_map/ppermute | solution.py:273
  140.3 2.9 %collective-permute-done.7 = f32[2,64,512]{2,1,0:T(8,128)S(1)} collective-permute-done((f32[2,64,512]{2,1,0:T(8,128)S(1)}, f32[2,64,512]{2,1,0:T(8,128)S(1)}, u32[]{:S(2)}, u32[]{:S(2)}) %collective-permute-start.7) | collective-permute-done | bytes 262176 | tf_op jit(solution)/shard_map/ppermute | solution.py:273
  143.2 3.8 %collective-permute-done.8 = f32[2,64,512]{2,1,0:T(8,128)S(1)} collective-permute-done((f32[2,64,512]{2,1,0:T(8,128)S(1)}, f32[2,64,512]{2,1,0:T(8,128)S(1)}, u32[]{:S(2)}, u32[]{:S(2)}) %collective-permute-start.8) | collective-permute-done | bytes 262176 | tf_op jit(solution)/shard_map/ppermute | solution.py:273
  147.1 6.7 %collective-permute-start.10 = (f32[64,512]{1,0:T(8,128)S(1)}, f32[64,512]{1,0:T(8,128)S(1)}, u32[]{:S(2)}, u32[]{:S(2)}) collective-permute-start(f32[64,512]{1,0:T(8,128)S(1)} %dynamic-slice_bitcast_fusion.2), channel_id=1, source_target_pairs={{0,1},{1,0},{2,3},{3,2},{4,5},{5,4},{6,7},{7,6},{8,9},{9,8},{10,11... | collective-permute-start | bytes 393224 | tf_op jit(solution)/shard_map/ppermute | solution.py:326
  (73 shorter events, 12.4 us)
Async XLA Ops:
  6.5 54.3 %all-gather.7.cloned.1.call-start = ((), (), s32[]{:S(2)}) async-start(), calls=%async_computation.4 | async-start | bytes 4718592 | tf_op jit(solution)/shard_map/all_gather | solution.py:289
  7.9 42.3 %copy-start.12 = (s32[32]{0:T(128)S(1)}, s32[32]{0:T(128)}, u32[]{:S(2)}) copy-start(s32[32]{0:T(128)} %param.14) | copy-start | bytes 388
  7.9 42.9 %copy-start.13 = (s32[32]{0:T(128)S(1)}, s32[32]{0:T(128)}, u32[]{:S(2)}) copy-start(s32[32]{0:T(128)} %param.16) | copy-start | bytes 388
  7.9 43.8 %copy-start.7 = (s32[32,16]{0,1:T(8,128)S(1)}, s32[32,16]{0,1:T(8,128)}, u32[]{:S(2)}) copy-start(s32[32,16]{0,1:T(8,128)} %param.15) | copy-start | bytes 6148
  7.9 43.8 %copy-start.8 = (s32[32,16]{0,1:T(8,128)S(1)}, s32[32,16]{0,1:T(8,128)}, u32[]{:S(2)}) copy-start(s32[32,16]{0,1:T(8,128)} %param.13) | copy-start | bytes 6148
  13.9 35.3 %all-to-all-start = ((f32[8,2,64,128]{3,2,1,0:T(8,128)}), f32[8,2,64,128]{3,2,1,0:T(8,128)S(1)}, u32[]{:S(2)}, u32[]{:S(2)}) async-start(f32[8,2,64,128]{3,2,1,0:T(8,128)} %pick_keys.1), calls=%async_computation | async-start | bytes 1048576 | tf_op jit(solution)/shard_map/all_to_all | solution.py:293
  22.9 73.8 %all-gather.9.cloned.1.call-start = ((), (), s32[]{:S(2)}) async-start(), calls=%async_computation.5 | async-start | bytes 4718592 | tf_op jit(solution)/shard_map/all_gather | solution.py:301
  23.0 14.1 %collective-permute-start.1 = (f32[64,2048]{1,0:T(8,128)}, f32[64,2048]{1,0:T(8,128)S(1)}, u32[]{:S(2)}, u32[]{:S(2)}) collective-permute-start(f32[64,2048]{1,0:T(8,128)} %get-tuple-element.29), channel_id=1, source_target_pairs={{0,64},{64,128},{128,192},{192,0},{1,65},{65,129},{129,193},{193,1... | collective-permute-start | bytes 1572872 | tf_op jit(solution)/shard_map/ppermute | solution.py:273
  24.3 24.9 %collective-permute-start.2 = (f32[64,2048]{1,0:T(8,128)}, f32[64,2048]{1,0:T(8,128)S(1)}, u32[]{:S(2)}, u32[]{:S(2)}) collective-permute-start(f32[64,2048]{1,0:T(8,128)} %get-tuple-element.30), channel_id=1, source_target_pairs={{0,128},{64,192},{128,0},{192,64},{1,129},{65,193},{129,1},{193,65... | collective-permute-start | bytes 1572872 | tf_op jit(solution)/shard_map/ppermute | solution.py:273
  26.7 22.5 %collective-permute-start.3 = (f32[64,2048]{1,0:T(8,128)}, f32[64,2048]{1,0:T(8,128)S(1)}, u32[]{:S(2)}, u32[]{:S(2)}) collective-permute-start(f32[64,2048]{1,0:T(8,128)} %get-tuple-element.31), channel_id=1, source_target_pairs={{0,192},{64,0},{128,64},{192,128},{1,193},{65,1},{129,65},{193,129... | collective-permute-start | bytes 1572872 | tf_op jit(solution)/shard_map/ppermute | solution.py:273
  27.9 3.0 %collective-permute-start = (f32[2,4,16,512]{3,2,1,0:T(8,128)S(1)}, f32[2,4,16,512]{3,2,1,0:T(8,128)S(1)}, u32[]{:S(2)}, u32[]{:S(2)}) collective-permute-start(f32[2,4,16,512]{3,2,1,0:T(8,128)S(1)} %get-tuple-element.56), channel_id=1, source_target_pairs={{0,1},{1,0},{2,3},{3,2},{4,5},{5,4},{6,7},{7,6},{8,9},{9,8},{10,11... | collective-permute-start | bytes 786440 | tf_op jit(solution)/shard_map/ppermute | solution.py:297
  37.1 23.8 %copy-start.3 = (f32[64,2048]{1,0:T(8,128)}, f32[64,2048]{1,0:T(8,128)S(1)}, u32[]{:S(2)}) copy-start(f32[64,2048]{1,0:T(8,128)S(1)} %collective-permute-done.1.first) | copy-start | bytes 1572868
  53.4 19.6 %all-to-all-start.1 = ((f32[16,16,512]{2,1,0:T(8,128)}), f32[16,16,512]{2,1,0:T(8,128)S(1)}, u32[]{:S(2)}, u32[]{:S(2)}) async-start(f32[16,16,512]{2,1,0:T(8,128)} %bitcast.7), calls=%async_computation.1 | async-start | bytes 1048576 | tf_op jit(solution)/shard_map/all_to_all | solution.py:300
  60.7 71.2 %all-gather.11.cloned.1.call-start = ((), (), s32[]{:S(2)}) async-start(), calls=%async_computation.6 | async-start | bytes 4718592 | tf_op jit(solution)/shard_map/all_gather | solution.py:318
  66.3 6.7 %collective-permute-start.4 = (f32[256,128]{1,0:T(8,128)}, f32[256,128]{1,0:T(8,128)S(1)}, u32[]{:S(2)}, u32[]{:S(2)}) collective-permute-start(f32[256,128]{1,0:T(8,128)} %get-tuple-element.38), channel_id=1, source_target_pairs={{0,64},{64,128},{128,192},{192,0},{1,65},{65,129},{129,193},{193,1... | collective-permute-start | bytes 393224 | tf_op jit(solution)/shard_map/ppermute | solution.py:273
  67.7 7.0 %collective-permute-start.5 = (f32[256,128]{1,0:T(8,128)}, f32[256,128]{1,0:T(8,128)S(1)}, u32[]{:S(2)}, u32[]{:S(2)}) collective-permute-start(f32[256,128]{1,0:T(8,128)} %get-tuple-element.39), channel_id=1, source_target_pairs={{0,128},{64,192},{128,0},{192,64},{1,129},{65,193},{129,1},{193,65... | collective-permute-start | bytes 393224 | tf_op jit(solution)/shard_map/ppermute | solution.py:273
  70.1 5.7 %collective-permute-start.6 = (f32[256,128]{1,0:T(8,128)}, f32[256,128]{1,0:T(8,128)S(1)}, u32[]{:S(2)}, u32[]{:S(2)}) collective-permute-start(f32[256,128]{1,0:T(8,128)} %get-tuple-element.40), channel_id=1, source_target_pairs={{0,192},{64,0},{128,64},{192,128},{1,193},{65,1},{129,65},{193,129... | collective-permute-start | bytes 393224 | tf_op jit(solution)/shard_map/ppermute | solution.py:273
  73.0 23.8 %copy-start.9 = (f32[256,128]{1,0:T(8,128)}, f32[256,128]{1,0:T(8,128)S(1)}, u32[]{:S(2)}) copy-start(f32[256,128]{1,0:T(8,128)S(1)} %collective-permute-done.4.second) | copy-start | bytes 393220
  74.8 22.1 %copy-start.10 = (f32[256,128]{1,0:T(8,128)}, f32[256,128]{1,0:T(8,128)S(1)}, u32[]{:S(2)}) copy-start(f32[256,128]{1,0:T(8,128)S(1)} %collective-permute-done.5.third) | copy-start | bytes 393220
  96.7 35.2 %copy-start = (s32[3]{0:T(128)S(1)}, s32[3]{0:T(128)}, u32[]{:S(2)}) copy-start(s32[3]{0:T(128)} %pad_add_fusion.where) | copy-start | bytes 40
  136.7 6.5 %collective-permute-start.7 = (f32[2,64,512]{2,1,0:T(8,128)S(1)}, f32[2,64,512]{2,1,0:T(8,128)S(1)}, u32[]{:S(2)}, u32[]{:S(2)}) collective-permute-start(f32[2,64,512]{2,1,0:T(8,128)S(1)} %get-tuple-element.50), channel_id=1, source_target_pairs={{0,64},{64,128},{128,192},{192,0},{1,65},{65,129},{129,193},{193,1... | collective-permute-start | bytes 786440 | tf_op jit(solution)/shard_map/ppermute | solution.py:273
  136.7 10.2 %collective-permute-start.8 = (f32[2,64,512]{2,1,0:T(8,128)S(1)}, f32[2,64,512]{2,1,0:T(8,128)S(1)}, u32[]{:S(2)}, u32[]{:S(2)}) collective-permute-start(f32[2,64,512]{2,1,0:T(8,128)S(1)} %get-tuple-element.51), channel_id=1, source_target_pairs={{0,128},{64,192},{128,0},{192,64},{1,129},{65,193},{129,1},{193,65... | collective-permute-start | bytes 786440 | tf_op jit(solution)/shard_map/ppermute | solution.py:273
  140.3 6.6 %collective-permute-start.9 = (f32[2,64,512]{2,1,0:T(8,128)S(1)}, f32[2,64,512]{2,1,0:T(8,128)S(1)}, u32[]{:S(2)}, u32[]{:S(2)}) collective-permute-start(f32[2,64,512]{2,1,0:T(8,128)S(1)} %get-tuple-element.52), channel_id=1, source_target_pairs={{0,192},{64,0},{128,64},{192,128},{1,193},{65,1},{129,65},{193,129... | collective-permute-start | bytes 786440 | tf_op jit(solution)/shard_map/ppermute | solution.py:273
  147.1 7.7 %collective-permute-start.10 = (f32[64,512]{1,0:T(8,128)S(1)}, f32[64,512]{1,0:T(8,128)S(1)}, u32[]{:S(2)}, u32[]{:S(2)}) collective-permute-start(f32[64,512]{1,0:T(8,128)S(1)} %dynamic-slice_bitcast_fusion.2), channel_id=1, source_target_pairs={{0,1},{1,0},{2,3},{3,2},{4,5},{5,4},{6,7},{7,6},{8,9},{9,8},{10,11... | collective-permute-start | bytes 393224 | tf_op jit(solution)/shard_map/ppermute | solution.py:326
  (6 other events, 68.9 us)
Sparse Core Ops, SparseCore 0:
  9.2 38.8 all-gather.6
  50.3 39.9 all-gather.8
  96.9 33.5 all-gather.10

commit v13 on v12

--- a/solution.py
+++ b/solution.py
@@ -63,15 +63,20 @@
     )(where, hidden_rows)
 
 
-def pick_keys_kernel(where, keys, values, out, sem):
-    y = where[1]
+def pick_keys_kernel(where, keys, values, *refs):
+    outs, sem = refs[:NZ], refs[NZ]
+    y, z = where[1], where[3]
     copies = []
-    for to in range(NZ):
+    for shift in range(NZ):
+        head = lax.rem(z + shift, NZ) // 2
         for index, cache in enumerate((keys, values)):
             part = cache.at[
-                pl.ds(pl.multiple_of(y * BLOCK, BLOCK), BLOCK), pl.ds((to // 2) * HD, HD)
+                pl.ds(pl.multiple_of(y * BLOCK, BLOCK), BLOCK),
+                pl.ds(pl.multiple_of(head * HD, HD), HD),
             ]
-            copies.append(pltpu.make_async_copy(part, out.at[to, index], sem.at[2 * to + index]))
+            copies.append(
+                pltpu.make_async_copy(part, outs[shift].at[index], sem.at[2 * shift + index])
+            )
     for copy in copies:
         copy.start()
     for copy in copies:
@@ -81,9 +86,9 @@
 def pick_keys(where, key_cache, value_cache):
     return pl.pallas_call(
         pick_keys_kernel,
-        out_shape=jax.ShapeDtypeStruct((NZ, 2, BLOCK, HD), jnp.float32),
+        out_shape=[jax.ShapeDtypeStruct((2, BLOCK, HD), jnp.float32)] * NZ,
         in_specs=[SMEM, ANY, ANY],
-        out_specs=VMEM,
+        out_specs=[VMEM] * NZ,
         scratch_shapes=[pltpu.SemaphoreType.DMA((2 * NZ,))],
         compiler_params=pltpu.CompilerParams(vmem_limit_bytes=56 << 20),
         cost_estimate=pl.CostEstimate(flops=0, bytes_accessed=64 << 20, transcendentals=0),
@@ -285,12 +290,13 @@
     output_weight,
 ):
     x, y, z, k = (lax.axis_index(name) for name in ALL)
-    where = jnp.stack([x, y, k]).astype(jnp.int32)
+    where = jnp.stack([x, y, k, z]).astype(jnp.int32)
     weights = lax.all_gather(query_weight, ("y", "k"), axis=0)
     picked = pick(where, hidden_rows)
     hidden = [along("x", piece, shift) for shift, piece in enumerate(picked, 1)]
     behind, picked = lax.optimization_barrier((where, picked))
-    near = lax.all_to_all(pick_keys(behind, key_cache, value_cache), "z", 0, 0)
+    near = pick_keys(behind, key_cache, value_cache)
+    near = jnp.stack([near[0]] + [along("z", near[s], s) for s in range(1, NZ)])
     rows = output_weight.reshape(2, NY, NK, 16, 512)
     kept = lax.dynamic_index_in_dim(rows, k, 2, keepdims=False)
     given = lax.dynamic_index_in_dim(rows, 1 - k, 2, keepdims=False)
@@ -301,7 +307,7 @@
     kv = lax.all_gather(near, ("y", "k"), axis=0)
     key_block = jnp.arange(NY, dtype=jnp.int32)[:, None, None]
     key_block = key_block + 4 * jnp.arange(NK, dtype=jnp.int32)[None, :, None]
-    key_block = key_block + 8 * jnp.arange(NZ, dtype=jnp.int32)[None, None, :]
+    key_block = key_block + 8 * ((z - jnp.arange(NZ, dtype=jnp.int32))[None, None, :] % NZ)
     low, up = allowed_rows(
         4 * z + x,
         key_block.reshape(-1),

time: 163 us -> 158 us (0.969)
  starting transfers between devices: 38.5 us -> 49.6 us
  waiting for transfers between devices: 29.8 us -> 20 us
  blocking collectives: 48.6 us -> 42.7 us
    ppermute x9 -> x16, starting transfers between devices: 13.5 us -> 32.7 us  [along(): lax.ppermute(value, axis, [(i, (i + shift) % count) for i in range(count)])]
    ppermute x9 -> x16, waiting for transfers between devices: 26.8 us -> 15.8 us  [along(): lax.ppermute(value, axis, [(i, (i + shift) % count) for i in range(count)])]
    all_to_all x1 -> x0, starting transfers between devices: 9.03 us -> none  [shards(): near = lax.all_to_all(pick_keys(behind, key_cache, value_cache), 'z', 0, 0)]
    all_to_all x1, blocking collectives: 20.9 us -> 16.3 us  [shards(): rows = lax.all_to_all(rows.reshape(NZ, NK, 16, 512), 'z', 0, 0)]
    ppermute x1, starting transfers between devices: 1.88 us -> 3.61 us  [shards(): taken = lax.ppermute(given, 'k', CORES)]
  transfers between devices with their start and end apart: 16 -> 22, of which waited for: 8 -> 12; matrix products, arithmetic and copies ran while one was open for 4% -> 5% of each run, Pallas kernels for 12% -> 12%
where the time goes in v13:
time: 158 us
  starting transfers between devices  49.6 us (31%)
  blocking collectives  42.7 us (27%)
  Pallas kernels  21.5 us (14%)
  waiting for transfers between devices  20 us (13%)
  between operations  13.4 us (8%)
  local copies, waits for them, and re-layouts  6.21 us (4%)
  other arithmetic  4.19 us (3%)
    ppermute x16, starting transfers between devices, along(): lax.ppermute(value, axis, [(i, (i + shift) % count) for i in range(count)])  32.7 us
    all_to_all x1, blocking collectives, shards(): heads = lax.all_to_all(heads, 'z', 0, 0)  26.4 us
    all_to_all x1, blocking collectives, shards(): rows = lax.all_to_all(rows.reshape(NZ, NK, 16, 512), 'z', 0, 0)  16.3 us
    ppermute x16, waiting for transfers between devices, along(): lax.ppermute(value, axis, [(i, (i + shift) % count) for i in range(count)])  15.8 us
    pallas_call x1, Pallas kernels, attend(): pl.pallas_call(attend_kernel, out_shape=jax.ShapeDtypeStruct((NZ, rows, H...  7.44 us
    ppermute x1, starting transfers between devices, shards(): other = lax.ppermute(other, 'k', CORES)  6.64 us
    all_to_all x1, starting transfers between devices, shards(): rows = lax.all_to_all(rows.reshape(NX * NY, 16, 512), ('x', 'y'), 0, 0)  6.59 us
    pallas_call x1, Pallas kernels, project(): pl.pallas_call(project_kernel, out_shape=[jax.ShapeDtypeStruct((NX * BLOC...  5.59 us
  transfers between devices with their start and end apart: 22, of which 12 were waited for; matrix products, arithmetic and copies ran while one was open for 5% of the time, Pallas kernels for 12%

profile of v13, /device:TPU:1, one launch (start us, length us, event | category | flops | bytes accessed | tf_op | source)
XLA Modules:
  0.0 157.6 jit_solution(8041677481011177752)
XLA Ops:
  8.0 3.4 %pick.1 = (f32[64,2048]{1,0:T(8,128)}, f32[64,2048]{1,0:T(8,128)}, f32[64,2048]{1,0:T(8,128)}) custom-call(s32[4]{0:T(128)} %pad_add_fusion.where, f32[128,8192]{1,0:T(8,128)} %rows.3), custom_call_target="tpu_custom_call" | custom-call | tf_op jit(solution)/shard_map/pick/pallas_call | solution.py:55
  11.4 3.4 %collective-permute-start.10 = (f32[64,2048]{1,0:T(8,128)}, f32[64,2048]{1,0:T(8,128)S(1)}, u32[]{:S(2)}, u32[]{:S(2)}) collective-permute-start(f32[64,2048]{1,0:T(8,128)} %get-tuple-element.39), channel_id=1, source_target_pairs={{0,192},{64,0},{128,64},{192,128},{1,193},{65,1},{129,65},{193,129... | collective-permute-start | bytes 1572872 | tf_op jit(solution)/shard_map/ppermute | solution.py:278
  14.7 1.7 %collective-permute-start.9 = (f32[64,2048]{1,0:T(8,128)}, f32[64,2048]{1,0:T(8,128)S(1)}, u32[]{:S(2)}, u32[]{:S(2)}) collective-permute-start(f32[64,2048]{1,0:T(8,128)} %get-tuple-element.38), channel_id=1, source_target_pairs={{0,128},{64,192},{128,0},{192,64},{1,129},{65,193},{129,1},{193,65... | collective-permute-start | bytes 1572872 | tf_op jit(solution)/shard_map/ppermute | solution.py:278
  16.5 2.6 %pick_keys.1 = (f32[2,64,128]{2,1,0:T(8,128)}, f32[2,64,128]{2,1,0:T(8,128)}, f32[2,64,128]{2,1,0:T(8,128)}, f32[2,64,128]{2,1,0:T(8,128)}, f32[2,64,128]{2,1,0:...) custom-call(s32[4]{0:T(128)} %pad_add_fusion.where, f32[256,512]{1,0:T(8,128)} %keys.1, ...), custom_call_target="tpu_custom_call" | custom-call | bytes 67108864 | tf_op jit(solution)/shard_map/pick_keys/pallas_call | solution.py:87
  19.1 1.7 %collective-permute-start.1 = (f32[2,64,128]{2,1,0:T(8,128)}, f32[2,64,128]{2,1,0:T(8,128)S(1)}, u32[]{:S(2)}, u32[]{:S(2)}) collective-permute-start(f32[2,64,128]{2,1,0:T(8,128)} %get-tuple-element.42), channel_id=1, source_target_pairs={{0,2},{2,4},{4,6},{6,8},{8,10},{10,12},{12,14},{14,0},{1,3},{3,5},... | collective-permute-start | bytes 196616 | tf_op jit(solution)/shard_map/ppermute | solution.py:278
  20.8 3.0 %collective-permute-start.2 = (f32[2,64,128]{2,1,0:T(8,128)}, f32[2,64,128]{2,1,0:T(8,128)S(1)}, u32[]{:S(2)}, u32[]{:S(2)}) collective-permute-start(f32[2,64,128]{2,1,0:T(8,128)} %get-tuple-element.43), channel_id=1, source_target_pairs={{0,4},{2,6},{4,8},{6,10},{8,12},{10,14},{12,0},{14,2},{1,5},{3,7},... | collective-permute-start | bytes 196616 | tf_op jit(solution)/shard_map/ppermute | solution.py:278
  24.7 2.2 %collective-permute-done.1 = f32[2,64,128]{2,1,0:T(8,128)S(1)} collective-permute-done((f32[2,64,128]{2,1,0:T(8,128)}, f32[2,64,128]{2,1,0:T(8,128)S(1)}, u32[]{:S(2)}, u32[]{:S(2)}) %collective-permute-start.1) | collective-permute-done | bytes 65568 | tf_op jit(solution)/shard_map/ppermute | solution.py:278
  29.2 3.7 %collective-permute-start.4 = (f32[2,64,128]{2,1,0:T(8,128)}, f32[2,64,128]{2,1,0:T(8,128)S(1)}, u32[]{:S(2)}, u32[]{:S(2)}) collective-permute-start(f32[2,64,128]{2,1,0:T(8,128)} %get-tuple-element.45), channel_id=1, source_target_pairs={{0,8},{2,10},{4,12},{6,14},{8,0},{10,2},{12,4},{14,6},{1,9},{3,11}... | collective-permute-start | bytes 196616 | tf_op jit(solution)/shard_map/ppermute | solution.py:278
  34.0 2.7 %collective-permute-start.5 = (f32[2,64,128]{2,1,0:T(8,128)}, f32[2,64,128]{2,1,0:T(8,128)S(1)}, u32[]{:S(2)}, u32[]{:S(2)}) collective-permute-start(f32[2,64,128]{2,1,0:T(8,128)} %get-tuple-element.46), channel_id=1, source_target_pairs={{0,10},{2,12},{4,14},{6,0},{8,2},{10,4},{12,6},{14,8},{1,11},{3,13... | collective-permute-start | bytes 196616 | tf_op jit(solution)/shard_map/ppermute | solution.py:278
  37.6 2.4 %collective-permute-start.6 = (f32[2,64,128]{2,1,0:T(8,128)}, f32[2,64,128]{2,1,0:T(8,128)S(1)}, u32[]{:S(2)}, u32[]{:S(2)}) collective-permute-start(f32[2,64,128]{2,1,0:T(8,128)} %get-tuple-element.47), channel_id=1, source_target_pairs={{0,12},{2,14},{4,0},{6,2},{8,4},{10,6},{12,8},{14,10},{1,13},{3,15... | collective-permute-start | bytes 196616 | tf_op jit(solution)/shard_map/ppermute | solution.py:278
  40.0 2.6 %collective-permute-start.7 = (f32[2,64,128]{2,1,0:T(8,128)}, f32[2,64,128]{2,1,0:T(8,128)S(1)}, u32[]{:S(2)}, u32[]{:S(2)}) collective-permute-start(f32[2,64,128]{2,1,0:T(8,128)} %get-tuple-element.48), channel_id=1, source_target_pairs={{0,14},{2,0},{4,2},{6,4},{8,6},{10,8},{12,10},{14,12},{1,15},{3,1}... | collective-permute-start | bytes 196616 | tf_op jit(solution)/shard_map/ppermute | solution.py:278
  42.5 2.9 %collective-permute-done.6 = f32[2,64,128]{2,1,0:T(8,128)S(1)} collective-permute-done((f32[2,64,128]{2,1,0:T(8,128)}, f32[2,64,128]{2,1,0:T(8,128)S(1)}, u32[]{:S(2)}, u32[]{:S(2)}) %collective-permute-start.6) | collective-permute-done | bytes 65568 | tf_op jit(solution)/shard_map/ppermute | solution.py:278
  45.4 3.6 %collective-permute-start = (f32[2,4,16,512]{3,2,1,0:T(8,128)S(1)}, f32[2,4,16,512]{3,2,1,0:T(8,128)S(1)}, u32[]{:S(2)}, u32[]{:S(2)}) collective-permute-start(f32[2,4,16,512]{3,2,1,0:T(8,128)S(1)} %get-tuple-element.72), channel_id=1, source_target_pairs={{0,1},{1,0},{2,3},{3,2},{4,5},{5,4},{6,7},{7,6},{8,9},{9,8},{10,11... | collective-permute-start | bytes 786440 | tf_op jit(solution)/shard_map/ppermute | solution.py:303
  54.3 6.6 %all-to-all-start = ((f32[16,16,512]{2,1,0:T(8,128)}), f32[16,16,512]{2,1,0:T(8,128)S(1)}, u32[]{:S(2)}, u32[]{:S(2)}) async-start(f32[16,16,512]{2,1,0:T(8,128)} %bitcast.16), calls=%async_computation | async-start | bytes 1048576 | tf_op jit(solution)/shard_map/all_to_all | solution.py:306
  61.1 5.6 %project.1 = (f32[256,128]{1,0:T(8,128)}, f32[256,128]{1,0:T(8,128)}, f32[256,128]{1,0:T(8,128)}, f32[256,128]{1,0:T(8,128)}) custom-call(s32[4]{0:T(128)} %pad_add_fusion.where, f32[128,8192]{1,0:T(8,128)} %rows.3, f32[64,2048]{1,0:T(8,128)} %copy-done.4, f32[64,2048]{1,0:T(8,128)} %copy-done.5, f32[64,2048]{1,0:T(8,128)} %copy-done.3, f32[8,512,256]{2,1,0:T(8,128)} %bitcast.51), custom_call_target="tpu_custom_call" | custom-call | flops 1610612736 | bytes 7340032 | tf_op jit(solution)/shard_map/project/pallas_call | solution.py:137
  68.1 2.4 %collective-permute-start.12 = (f32[256,128]{1,0:T(8,128)}, f32[256,128]{1,0:T(8,128)S(1)}, u32[]{:S(2)}, u32[]{:S(2)}) collective-permute-start(f32[256,128]{1,0:T(8,128)} %get-tuple-element.55), channel_id=1, source_target_pairs={{0,128},{64,192},{128,0},{192,64},{1,129},{65,193},{129,1},{193,65... | collective-permute-start | bytes 393224 | tf_op jit(solution)/shard_map/ppermute | solution.py:278
  76.0 16.3 %all_to_all.15 = f32[8,2,16,512]{3,2,1,0:T(8,128)} all-to-all(f32[8,2,16,512]{3,2,1,0:T(8,128)S(1)} %bitcast.52), channel_id=1, replica_groups=mesh['x'=4,'y'=4,'z'=8,'k'=2] {'z'}, dimensions={0} | all-to-all | bytes 1048576 | tf_op jit(solution)/shard_map/all_to_all | solution.py:323
  92.5 7.4 %attend.1 = f32[8,256,128]{2,1,0:T(8,128)} custom-call(f32[256,128]{1,0:T(8,128)} %get-tuple-element.57.first, f32[256,128]{1,0:T(8,128)} %copy-done.9, f32[256,128]{1,0:T(8,128)} %copy-done.10, f32[256,128]{1,0:T(8,128)} %copy-done.11, f32[4,4096]{1,0:T(4,128)} %broadcast_in_dim.39.low, f32[4,4096]{1,0:T(4,128)} %broadcast_in_dim.41.up, ...), custom_call_target="tpu_custom_call" | custom-call | flops 1610612736 | bytes 6291456 | tf_op jit(solution)/shard_map/attend/pallas_call | solution.py:205
  99.9 26.4 %all_to_all.16.heads = f32[8,256,128]{2,1,0:T(8,128)S(1)} all-to-all(f32[8,256,128]{2,1,0:T(8,128)} %attend.1), channel_id=1, replica_groups=mesh['x'=4,'y'=4,'z'=8,'k'=2] {'z'}, dimensions={0} | all-to-all | bytes 2097152 | tf_op jit(solution)/shard_map/all_to_all | solution.py:326
  127.6 2.2 %copy-done.1 = f32[64,2,16,512]{3,2,1,0:T(8,128)S(1)} copy-done((f32[64,2,16,512]{3,2,1,0:T(8,128)S(1)}, f32[64,2,16,512]{3,2,1,0:T(8,128)}, u32[]{:S(2)}) %copy-start.1) | copy-done | bytes 4194328
  129.8 2.5 %mix.1 = (f32[2,64,512]{2,1,0:T(8,128)S(1)}, f32[2,64,512]{2,1,0:T(8,128)S(1)}, f32[2,64,512]{2,1,0:T(8,128)S(1)}, f32[2,64,512]{2,1,0:T(8,128)S(1)}) custom-call(s32[4]{0:T(128)S(1)} %copy-done, f32[8,256,128]{2,1,0:T(8,128)S(1)} %all_to_all.16.heads, f32[8,8,2,16,512]{4,3,2,1,0:T(8,128)S(1)} %bitcast.50), custom_call_target="tpu_custom_call" | custom-call | flops 1610612736 | bytes 6291456 | tf_op jit(solution)/shard_map/mix/pallas_call | solution.py:242
  133.6 2.4 %collective-permute-start.15 = (f32[2,64,512]{2,1,0:T(8,128)S(1)}, f32[2,64,512]{2,1,0:T(8,128)S(1)}, u32[]{:S(2)}, u32[]{:S(2)}) collective-permute-start(f32[2,64,512]{2,1,0:T(8,128)S(1)} %get-tuple-element.67), channel_id=1, source_target_pairs={{0,128},{64,192},{128,0},{192,64},{1,129},{65,193},{129,1},{193,65... | collective-permute-start | bytes 786440 | tf_op jit(solution)/shard_map/ppermute | solution.py:278
  138.8 3.8 %collective-permute-done.15 = f32[2,64,512]{2,1,0:T(8,128)S(1)} collective-permute-done((f32[2,64,512]{2,1,0:T(8,128)S(1)}, f32[2,64,512]{2,1,0:T(8,128)S(1)}, u32[]{:S(2)}, u32[]{:S(2)}) %collective-permute-start.15) | collective-permute-done | bytes 262176 | tf_op jit(solution)/shard_map/ppermute | solution.py:278
  142.7 6.6 %collective-permute-start.17 = (f32[64,512]{1,0:T(8,128)S(1)}, f32[64,512]{1,0:T(8,128)S(1)}, u32[]{:S(2)}, u32[]{:S(2)}) collective-permute-start(f32[64,512]{1,0:T(8,128)S(1)} %dynamic-slice_bitcast_fusion.2), channel_id=1, source_target_pairs={{0,1},{1,0},{2,3},{3,2},{4,5},{5,4},{6,7},{7,6},{8,9},{9,8},{10,11... | collective-permute-start | bytes 393224 | tf_op jit(solution)/shard_map/ppermute | solution.py:332
  (93 shorter events, 26.2 us)
Async XLA Ops:
  6.5 54.5 %all-gather.7.cloned.1.call-start = ((), (), s32[]{:S(2)}) async-start(), calls=%async_computation.3 | async-start | bytes 4718592 | tf_op jit(solution)/shard_map/all_gather | solution.py:294
  7.3 85.2 %all-gather.9.cloned.1.call-start = ((), (), s32[]{:S(2)}) async-start(), calls=%async_computation.4 | async-start | bytes 4718592 | tf_op jit(solution)/shard_map/all_gather | solution.py:307
  8.0 44.6 %copy-start.7 = (s32[32,16]{0,1:T(8,128)S(1)}, s32[32,16]{0,1:T(8,128)}, u32[]{:S(2)}) copy-start(s32[32,16]{0,1:T(8,128)} %param.15) | copy-start | bytes 6148
  8.0 44.6 %copy-start.8 = (s32[32,16]{0,1:T(8,128)S(1)}, s32[32,16]{0,1:T(8,128)}, u32[]{:S(2)}) copy-start(s32[32,16]{0,1:T(8,128)} %param.13) | copy-start | bytes 6148
  11.4 39.7 %collective-permute-start.10 = (f32[64,2048]{1,0:T(8,128)}, f32[64,2048]{1,0:T(8,128)S(1)}, u32[]{:S(2)}, u32[]{:S(2)}) collective-permute-start(f32[64,2048]{1,0:T(8,128)} %get-tuple-element.39), channel_id=1, source_target_pairs={{0,192},{64,0},{128,64},{192,128},{1,193},{65,1},{129,65},{193,129... | collective-permute-start | bytes 1572872 | tf_op jit(solution)/shard_map/ppermute | solution.py:278
  14.7 36.3 %collective-permute-start.8 = (f32[64,2048]{1,0:T(8,128)}, f32[64,2048]{1,0:T(8,128)S(1)}, u32[]{:S(2)}, u32[]{:S(2)}) collective-permute-start(f32[64,2048]{1,0:T(8,128)} %get-tuple-element.37), channel_id=1, source_target_pairs={{0,64},{64,128},{128,192},{192,0},{1,65},{65,129},{129,193},{193,1... | collective-permute-start | bytes 1572872 | tf_op jit(solution)/shard_map/ppermute | solution.py:278
  14.7 36.3 %collective-permute-start.9 = (f32[64,2048]{1,0:T(8,128)}, f32[64,2048]{1,0:T(8,128)S(1)}, u32[]{:S(2)}, u32[]{:S(2)}) collective-permute-start(f32[64,2048]{1,0:T(8,128)} %get-tuple-element.38), channel_id=1, source_target_pairs={{0,128},{64,192},{128,0},{192,64},{1,129},{65,193},{129,1},{193,65... | collective-permute-start | bytes 1572872 | tf_op jit(solution)/shard_map/ppermute | solution.py:278
  19.1 7.8 %collective-permute-start.1 = (f32[2,64,128]{2,1,0:T(8,128)}, f32[2,64,128]{2,1,0:T(8,128)S(1)}, u32[]{:S(2)}, u32[]{:S(2)}) collective-permute-start(f32[2,64,128]{2,1,0:T(8,128)} %get-tuple-element.42), channel_id=1, source_target_pairs={{0,2},{2,4},{4,6},{6,8},{8,10},{10,12},{12,14},{14,0},{1,3},{3,5},... | collective-permute-start | bytes 196616 | tf_op jit(solution)/shard_map/ppermute | solution.py:278
  20.8 8.4 %collective-permute-start.2 = (f32[2,64,128]{2,1,0:T(8,128)}, f32[2,64,128]{2,1,0:T(8,128)S(1)}, u32[]{:S(2)}, u32[]{:S(2)}) collective-permute-start(f32[2,64,128]{2,1,0:T(8,128)} %get-tuple-element.43), channel_id=1, source_target_pairs={{0,4},{2,6},{4,8},{6,10},{8,12},{10,14},{12,0},{14,2},{1,5},{3,7},... | collective-permute-start | bytes 196616 | tf_op jit(solution)/shard_map/ppermute | solution.py:278
  26.9 7.1 %collective-permute-start.3 = (f32[2,64,128]{2,1,0:T(8,128)}, f32[2,64,128]{2,1,0:T(8,128)S(1)}, u32[]{:S(2)}, u32[]{:S(2)}) collective-permute-start(f32[2,64,128]{2,1,0:T(8,128)} %get-tuple-element.44), channel_id=1, source_target_pairs={{0,6},{2,8},{4,10},{6,12},{8,14},{10,0},{12,2},{14,4},{1,7},{3,9},... | collective-permute-start | bytes 196616 | tf_op jit(solution)/shard_map/ppermute | solution.py:278
  29.2 8.4 %collective-permute-start.4 = (f32[2,64,128]{2,1,0:T(8,128)}, f32[2,64,128]{2,1,0:T(8,128)S(1)}, u32[]{:S(2)}, u32[]{:S(2)}) collective-permute-start(f32[2,64,128]{2,1,0:T(8,128)} %get-tuple-element.45), channel_id=1, source_target_pairs={{0,8},{2,10},{4,12},{6,14},{8,0},{10,2},{12,4},{14,6},{1,9},{3,11}... | collective-permute-start | bytes 196616 | tf_op jit(solution)/shard_map/ppermute | solution.py:278
  34.0 6.0 %collective-permute-start.5 = (f32[2,64,128]{2,1,0:T(8,128)}, f32[2,64,128]{2,1,0:T(8,128)S(1)}, u32[]{:S(2)}, u32[]{:S(2)}) collective-permute-start(f32[2,64,128]{2,1,0:T(8,128)} %get-tuple-element.46), channel_id=1, source_target_pairs={{0,10},{2,12},{4,14},{6,0},{8,2},{10,4},{12,6},{14,8},{1,11},{3,13... | collective-permute-start | bytes 196616 | tf_op jit(solution)/shard_map/ppermute | solution.py:278
  37.6 7.8 %collective-permute-start.6 = (f32[2,64,128]{2,1,0:T(8,128)}, f32[2,64,128]{2,1,0:T(8,128)S(1)}, u32[]{:S(2)}, u32[]{:S(2)}) collective-permute-start(f32[2,64,128]{2,1,0:T(8,128)} %get-tuple-element.47), channel_id=1, source_target_pairs={{0,12},{2,14},{4,0},{6,2},{8,4},{10,6},{12,8},{14,10},{1,13},{3,15... | collective-permute-start | bytes 196616 | tf_op jit(solution)/shard_map/ppermute | solution.py:278
  40.0 9.1 %collective-permute-start.7 = (f32[2,64,128]{2,1,0:T(8,128)}, f32[2,64,128]{2,1,0:T(8,128)S(1)}, u32[]{:S(2)}, u32[]{:S(2)}) collective-permute-start(f32[2,64,128]{2,1,0:T(8,128)} %get-tuple-element.48), channel_id=1, source_target_pairs={{0,14},{2,0},{4,2},{6,4},{8,6},{10,8},{12,10},{14,12},{1,15},{3,1}... | collective-permute-start | bytes 196616 | tf_op jit(solution)/shard_map/ppermute | solution.py:278
  45.4 4.8 %collective-permute-start = (f32[2,4,16,512]{3,2,1,0:T(8,128)S(1)}, f32[2,4,16,512]{3,2,1,0:T(8,128)S(1)}, u32[]{:S(2)}, u32[]{:S(2)}) collective-permute-start(f32[2,4,16,512]{3,2,1,0:T(8,128)S(1)} %get-tuple-element.72), channel_id=1, source_target_pairs={{0,1},{1,0},{2,3},{3,2},{4,5},{5,4},{6,7},{7,6},{8,9},{9,8},{10,11... | collective-permute-start | bytes 786440 | tf_op jit(solution)/shard_map/ppermute | solution.py:303
  54.3 19.1 %all-to-all-start = ((f32[16,16,512]{2,1,0:T(8,128)}), f32[16,16,512]{2,1,0:T(8,128)S(1)}, u32[]{:S(2)}, u32[]{:S(2)}) async-start(f32[16,16,512]{2,1,0:T(8,128)} %bitcast.16), calls=%async_computation | async-start | bytes 1048576 | tf_op jit(solution)/shard_map/all_to_all | solution.py:306
  60.9 66.7 %all-gather.11.cloned.1.call-start = ((), (), s32[]{:S(2)}) async-start(), calls=%async_computation.5 | async-start | bytes 4718592 | tf_op jit(solution)/shard_map/all_gather | solution.py:324
  66.7 6.7 %collective-permute-start.11 = (f32[256,128]{1,0:T(8,128)}, f32[256,128]{1,0:T(8,128)S(1)}, u32[]{:S(2)}, u32[]{:S(2)}) collective-permute-start(f32[256,128]{1,0:T(8,128)} %get-tuple-element.54), channel_id=1, source_target_pairs={{0,64},{64,128},{128,192},{192,0},{1,65},{65,129},{129,193},{193,1... | collective-permute-start | bytes 393224 | tf_op jit(solution)/shard_map/ppermute | solution.py:278
  68.1 6.9 %collective-permute-start.12 = (f32[256,128]{1,0:T(8,128)}, f32[256,128]{1,0:T(8,128)S(1)}, u32[]{:S(2)}, u32[]{:S(2)}) collective-permute-start(f32[256,128]{1,0:T(8,128)} %get-tuple-element.55), channel_id=1, source_target_pairs={{0,128},{64,192},{128,0},{192,64},{1,129},{65,193},{129,1},{193,65... | collective-permute-start | bytes 393224 | tf_op jit(solution)/shard_map/ppermute | solution.py:278
  70.5 5.5 %collective-permute-start.13 = (f32[256,128]{1,0:T(8,128)}, f32[256,128]{1,0:T(8,128)S(1)}, u32[]{:S(2)}, u32[]{:S(2)}) collective-permute-start(f32[256,128]{1,0:T(8,128)} %get-tuple-element.56), channel_id=1, source_target_pairs={{0,192},{64,0},{128,64},{192,128},{1,193},{65,1},{129,65},{193,129... | collective-permute-start | bytes 393224 | tf_op jit(solution)/shard_map/ppermute | solution.py:278
  132.3 6.5 %collective-permute-start.14 = (f32[2,64,512]{2,1,0:T(8,128)S(1)}, f32[2,64,512]{2,1,0:T(8,128)S(1)}, u32[]{:S(2)}, u32[]{:S(2)}) collective-permute-start(f32[2,64,512]{2,1,0:T(8,128)S(1)} %get-tuple-element.66), channel_id=1, source_target_pairs={{0,64},{64,128},{128,192},{192,0},{1,65},{65,129},{129,193},{193,1... | collective-permute-start | bytes 786440 | tf_op jit(solution)/shard_map/ppermute | solution.py:278
  133.6 9.0 %collective-permute-start.15 = (f32[2,64,512]{2,1,0:T(8,128)S(1)}, f32[2,64,512]{2,1,0:T(8,128)S(1)}, u32[]{:S(2)}, u32[]{:S(2)}) collective-permute-start(f32[2,64,512]{2,1,0:T(8,128)S(1)} %get-tuple-element.67), channel_id=1, source_target_pairs={{0,128},{64,192},{128,0},{192,64},{1,129},{65,193},{129,1},{193,65... | collective-permute-start | bytes 786440 | tf_op jit(solution)/shard_map/ppermute | solution.py:278
  136.0 6.6 %collective-permute-start.16 = (f32[2,64,512]{2,1,0:T(8,128)S(1)}, f32[2,64,512]{2,1,0:T(8,128)S(1)}, u32[]{:S(2)}, u32[]{:S(2)}) collective-permute-start(f32[2,64,512]{2,1,0:T(8,128)S(1)} %get-tuple-element.68), channel_id=1, source_target_pairs={{0,192},{64,0},{128,64},{192,128},{1,193},{65,1},{129,65},{193,129... | collective-permute-start | bytes 786440 | tf_op jit(solution)/shard_map/ppermute | solution.py:278
  142.7 7.6 %collective-permute-start.17 = (f32[64,512]{1,0:T(8,128)S(1)}, f32[64,512]{1,0:T(8,128)S(1)}, u32[]{:S(2)}, u32[]{:S(2)}) collective-permute-start(f32[64,512]{1,0:T(8,128)S(1)} %dynamic-slice_bitcast_fusion.2), channel_id=1, source_target_pairs={{0,1},{1,0},{2,3},{3,2},{4,5},{5,4},{6,7},{7,6},{8,9},{9,8},{10,11... | collective-permute-start | bytes 393224 | tf_op jit(solution)/shard_map/ppermute | solution.py:332
  (12 other events, 227.6 us)
Sparse Core Ops, SparseCore 0:
  9.2 38.8 all-gather.6
  51.2 39.0 all-gather.8
  92.5 35.0 all-gather.10

commit v14 on v13

--- a/solution.py
+++ b/solution.py
@@ -64,18 +64,18 @@
 
 
 def pick_keys_kernel(where, keys, values, *refs):
-    outs, sem = refs[:NZ], refs[NZ]
+    outs, sem = refs[: NZ // 2], refs[NZ // 2]
     y, z = where[1], where[3]
     copies = []
-    for shift in range(NZ):
-        head = lax.rem(z + shift, NZ) // 2
+    for turn in range(NZ // 2):
+        head = lax.rem(z + 2 * turn, NZ) // 2
         for index, cache in enumerate((keys, values)):
             part = cache.at[
                 pl.ds(pl.multiple_of(y * BLOCK, BLOCK), BLOCK),
                 pl.ds(pl.multiple_of(head * HD, HD), HD),
             ]
             copies.append(
-                pltpu.make_async_copy(part, outs[shift].at[index], sem.at[2 * shift + index])
+                pltpu.make_async_copy(part, outs[turn].at[index], sem.at[2 * turn + index])
             )
     for copy in copies:
         copy.start()
@@ -86,10 +86,10 @@
 def pick_keys(where, key_cache, value_cache):
     return pl.pallas_call(
         pick_keys_kernel,
-        out_shape=[jax.ShapeDtypeStruct((2, BLOCK, HD), jnp.float32)] * NZ,
+        out_shape=[jax.ShapeDtypeStruct((2, BLOCK, HD), jnp.float32)] * (NZ // 2),
         in_specs=[SMEM, ANY, ANY],
-        out_specs=[VMEM] * NZ,
-        scratch_shapes=[pltpu.SemaphoreType.DMA((2 * NZ,))],
+        out_specs=[VMEM] * (NZ // 2),
+        scratch_shapes=[pltpu.SemaphoreType.DMA((NZ,))],
         compiler_params=pltpu.CompilerParams(vmem_limit_bytes=56 << 20),
         cost_estimate=pl.CostEstimate(flops=0, bytes_accessed=64 << 20, transcendentals=0),
         name="pick_keys",
@@ -296,7 +296,8 @@
     hidden = [along("x", piece, shift) for shift, piece in enumerate(picked, 1)]
     behind, picked = lax.optimization_barrier((where, picked))
     near = pick_keys(behind, key_cache, value_cache)
-    near = jnp.stack([near[0]] + [along("z", near[s], s) for s in range(1, NZ)])
+    near = jnp.stack([near[0]] + [along("z", near[t], 2 * t) for t in range(1, NZ // 2)])
+    near = jnp.concatenate([near, lax.ppermute(near, "z", [(i, i ^ 1) for i in range(NZ)])])
     rows = output_weight.reshape(2, NY, NK, 16, 512)
     kept = lax.dynamic_index_in_dim(rows, k, 2, keepdims=False)
     given = lax.dynamic_index_in_dim(rows, 1 - k, 2, keepdims=False)
@@ -307,7 +308,9 @@
     kv = lax.all_gather(near, ("y", "k"), axis=0)
     key_block = jnp.arange(NY, dtype=jnp.int32)[:, None, None]
     key_block = key_block + 4 * jnp.arange(NK, dtype=jnp.int32)[None, :, None]
-    key_block = key_block + 8 * ((z - jnp.arange(NZ, dtype=jnp.int32))[None, None, :] % NZ)
+    turns = 2 * jnp.arange(NZ // 2, dtype=jnp.int32)
+    along_z = jnp.concatenate([z - turns, (z ^ 1) - turns]) % NZ
+    key_block = key_block + 8 * along_z[None, None, :]
     low, up = allowed_rows(
         4 * z + x,
         key_block.reshape(-1),

time: 158 us -> 158 us (level)
  starting transfers between devices: 49.6 us -> 34.5 us
  blocking collectives: 42.7 us -> 49.8 us
  waiting for transfers between devices: 20 us -> 26.6 us
    all_to_all x1, blocking collectives: 26.4 us -> 33.4 us  [shards(): heads = lax.all_to_all(heads, 'z', 0, 0)]
    ppermute x0 -> x1, waiting for transfers between devices: none -> 6.83 us  [shards(): lax.ppermute(near, 'z', [(i, i ^ 1) for i in range(NZ)])]
    ppermute x16 -> x12, starting transfers between devices: 32.7 us -> 26.5 us  [along(): lax.ppermute(value, axis, [(i, (i + shift) % count) for i in range(count)])]
    ppermute x1, starting transfers between devices: 6.64 us -> 2.14 us  [shards(): other = lax.ppermute(other, 'k', CORES)]
    ppermute x1, starting transfers between devices: 3.61 us -> 0.39 us  [shards(): taken = lax.ppermute(given, 'k', CORES)]
    ppermute x16 -> x12, waiting for transfers between devices: 15.8 us -> 17.1 us  [along(): lax.ppermute(value, axis, [(i, (i + shift) % count) for i in range(count)])]
    unnamed x35 -> x32, local copies, waits for them, and re-layouts: 3.12 us -> 3.86 us
  transfers between devices with their start and end apart: 22 -> 19, of which waited for: 12 -> 8; matrix products, arithmetic and copies ran while one was open for 5% -> 5% of each run, Pallas kernels for 12% -> 12%
where the time goes in v14:
time: 158 us; the launch traced here: 157 us
  blocking collectives  49.8 us (32%)
  starting transfers between devices  34.5 us (22%)
  waiting for transfers between devices  26.6 us (17%)
  Pallas kernels  20.8 us (13%)
  between operations  13.4 us (8%)
  local copies, waits for them, and re-layouts  6.89 us (4%)
  other arithmetic  5.19 us (3%)
    all_to_all x1, blocking collectives, shards(): heads = lax.all_to_all(heads, 'z', 0, 0)  33.4 us
    ppermute x12, starting transfers between devices, along(): lax.ppermute(value, axis, [(i, (i + shift) % count) for i in range(count)])  26.5 us
    ppermute x12, waiting for transfers between devices, along(): lax.ppermute(value, axis, [(i, (i + shift) % count) for i in range(count)])  17.1 us
    all_to_all x1, blocking collectives, shards(): rows = lax.all_to_all(rows.reshape(NZ, NK, 16, 512), 'z', 0, 0)  16.4 us
    pallas_call x1, Pallas kernels, attend(): pl.pallas_call(attend_kernel, out_shape=jax.ShapeDtypeStruct((NZ, rows, H...  7.46 us
    ppermute x1, waiting for transfers between devices, shards(): lax.ppermute(near, 'z', [(i, i ^ 1) for i in range(NZ)])  6.83 us
    all_to_all x1, starting transfers between devices, shards(): rows = lax.all_to_all(rows.reshape(NX * NY, 16, 512), ('x', 'y'), 0, 0)  5.31 us
    pallas_call x1, Pallas kernels, project(): pl.pallas_call(project_kernel, out_shape=[jax.ShapeDtypeStruct((NX * BLOC...  5.25 us
  transfers between devices with their start and end apart: 19, of which 8 were waited for; matrix products, arithmetic and copies ran while one was open for 5% of the time, Pallas kernels for 12%

profile of v14, /device:TPU:1, one launch (start us, length us, event | category | flops | bytes accessed | tf_op | source)
XLA Modules:
  0.0 157.2 jit_solution(10577314385382802234)
XLA Ops:
  8.0 3.3 %pick.1 = (f32[64,2048]{1,0:T(8,128)}, f32[64,2048]{1,0:T(8,128)}, f32[64,2048]{1,0:T(8,128)}) custom-call(s32[4]{0:T(128)} %pad_add_fusion.where, f32[128,8192]{1,0:T(8,128)} %rows.3), custom_call_target="tpu_custom_call" | custom-call | tf_op jit(solution)/shard_map/pick/pallas_call | solution.py:55
  11.3 2.1 %collective-permute-start.5 = (f32[64,2048]{1,0:T(8,128)}, f32[64,2048]{1,0:T(8,128)S(1)}, u32[]{:S(2)}, u32[]{:S(2)}) collective-permute-start(f32[64,2048]{1,0:T(8,128)} %get-tuple-element.33), channel_id=1, source_target_pairs={{0,64},{64,128},{128,192},{192,0},{1,65},{65,129},{129,193},{193,1... | collective-permute-start | bytes 1572872 | tf_op jit(solution)/shard_map/ppermute | solution.py:278
  13.5 2.5 %collective-permute-start.6 = (f32[64,2048]{1,0:T(8,128)}, f32[64,2048]{1,0:T(8,128)S(1)}, u32[]{:S(2)}, u32[]{:S(2)}) collective-permute-start(f32[64,2048]{1,0:T(8,128)} %get-tuple-element.34), channel_id=1, source_target_pairs={{0,128},{64,192},{128,0},{192,64},{1,129},{65,193},{129,1},{193,65... | collective-permute-start | bytes 1572872 | tf_op jit(solution)/shard_map/ppermute | solution.py:278
  15.9 2.3 %pick_keys.1 = (f32[2,64,128]{2,1,0:T(8,128)}, f32[2,64,128]{2,1,0:T(8,128)}, f32[2,64,128]{2,1,0:T(8,128)}, f32[2,64,128]{2,1,0:T(8,128)}) custom-call(s32[4]{0:T(128)} %pad_add_fusion.where, f32[256,512]{1,0:T(8,128)} %keys.1, f32[256,512]{1,0:T(8,128)} %values.1), custom_call_target="tpu_custom_call" | custom-call | bytes 67108864 | tf_op jit(solution)/shard_map/pick_keys/pallas_call | solution.py:87
  18.2 7.0 %collective-permute-start.2 = (f32[2,64,128]{2,1,0:T(8,128)}, f32[2,64,128]{2,1,0:T(8,128)S(1)}, u32[]{:S(2)}, u32[]{:S(2)}) collective-permute-start(f32[2,64,128]{2,1,0:T(8,128)} %get-tuple-element.39), channel_id=1, source_target_pairs={{0,8},{2,10},{4,12},{6,14},{8,0},{10,2},{12,4},{14,6},{1,9},{3,11}... | collective-permute-start | bytes 196616 | tf_op jit(solution)/shard_map/ppermute | solution.py:278
  25.2 2.4 %collective-permute-start.1 = (f32[2,64,128]{2,1,0:T(8,128)}, f32[2,64,128]{2,1,0:T(8,128)S(1)}, u32[]{:S(2)}, u32[]{:S(2)}) collective-permute-start(f32[2,64,128]{2,1,0:T(8,128)} %get-tuple-element.38), channel_id=1, source_target_pairs={{0,4},{2,6},{4,8},{6,10},{8,12},{10,14},{12,0},{14,2},{1,5},{3,7},... | collective-permute-start | bytes 196616 | tf_op jit(solution)/shard_map/ppermute | solution.py:278
  29.7 3.5 %collective-permute-done.3 = f32[2,64,128]{2,1,0:T(8,128)S(1)} collective-permute-done((f32[2,64,128]{2,1,0:T(8,128)}, f32[2,64,128]{2,1,0:T(8,128)S(1)}, u32[]{:S(2)}, u32[]{:S(2)}) %collective-permute-start.3) | collective-permute-done | bytes 65568 | tf_op jit(solution)/shard_map/ppermute | solution.py:278
  35.6 6.8 %collective-permute-done.4 = f32[4,2,64,128]{3,2,1,0:T(8,128)S(1)} collective-permute-done((f32[4,2,64,128]{3,2,1,0:T(8,128)S(1)}, f32[4,2,64,128]{3,2,1,0:T(8,128)S(1)}, u32[]{:S(2)}, u32[]{:S(2)}) %collective-permute-start.4) | collective-permute-done | bytes 262176 | tf_op jit(solution)/shard_map/ppermute | solution.py:300
  46.6 5.3 %all-to-all-start = ((f32[16,16,512]{2,1,0:T(8,128)}), f32[16,16,512]{2,1,0:T(8,128)S(1)}, u32[]{:S(2)}, u32[]{:S(2)}) async-start(f32[16,16,512]{2,1,0:T(8,128)} %bitcast.12), calls=%async_computation | async-start | bytes 1048576 | tf_op jit(solution)/shard_map/all_to_all | solution.py:307
  52.1 5.2 %project.1 = (f32[256,128]{1,0:T(8,128)}, f32[256,128]{1,0:T(8,128)}, f32[256,128]{1,0:T(8,128)}, f32[256,128]{1,0:T(8,128)}) custom-call(s32[4]{0:T(128)} %pad_add_fusion.where, f32[128,8192]{1,0:T(8,128)} %rows.3, f32[64,2048]{1,0:T(8,128)} %copy-done.3, f32[64,2048]{1,0:T(8,128)} %copy-done.4, f32[64,2048]{1,0:T(8,128)} %copy-done.5, f32[8,512,256]{2,1,0:T(8,128)} %bitcast.43), custom_call_target="tpu_custom_call" | custom-call | flops 1610612736 | bytes 7340032 | tf_op jit(solution)/shard_map/project/pallas_call | solution.py:137
  57.4 2.7 %collective-permute-start.10 = (f32[256,128]{1,0:T(8,128)}, f32[256,128]{1,0:T(8,128)S(1)}, u32[]{:S(2)}, u32[]{:S(2)}) collective-permute-start(f32[256,128]{1,0:T(8,128)} %get-tuple-element.48), channel_id=1, source_target_pairs={{0,192},{64,0},{128,64},{192,128},{1,193},{65,1},{129,65},{193,129... | collective-permute-start | bytes 393224 | tf_op jit(solution)/shard_map/ppermute | solution.py:278
  60.0 1.7 %collective-permute-start.9 = (f32[256,128]{1,0:T(8,128)}, f32[256,128]{1,0:T(8,128)S(1)}, u32[]{:S(2)}, u32[]{:S(2)}) collective-permute-start(f32[256,128]{1,0:T(8,128)} %get-tuple-element.47), channel_id=1, source_target_pairs={{0,128},{64,192},{128,0},{192,64},{1,129},{65,193},{129,1},{193,65... | collective-permute-start | bytes 393224 | tf_op jit(solution)/shard_map/ppermute | solution.py:278
  63.5 4.1 %collective-permute-done.8.second = f32[256,128]{1,0:T(8,128)S(1)} collective-permute-done((f32[256,128]{1,0:T(8,128)}, f32[256,128]{1,0:T(8,128)S(1)}, u32[]{:S(2)}, u32[]{:S(2)}) %collective-permute-start.8) | collective-permute-done | bytes 131104 | tf_op jit(solution)/shard_map/ppermute | solution.py:278
  67.5 16.4 %all_to_all.15 = f32[8,2,16,512]{3,2,1,0:T(8,128)} all-to-all(f32[8,2,16,512]{3,2,1,0:T(8,128)S(1)} %bitcast.44), channel_id=1, replica_groups=mesh['x'=4,'y'=4,'z'=8,'k'=2] {'z'}, dimensions={0} | all-to-all | bytes 1048576 | tf_op jit(solution)/shard_map/all_to_all | solution.py:326
  84.7 7.5 %attend.1 = f32[8,256,128]{2,1,0:T(8,128)} custom-call(f32[256,128]{1,0:T(8,128)} %get-tuple-element.49.first, f32[256,128]{1,0:T(8,128)} %copy-done.10, f32[256,128]{1,0:T(8,128)} %copy-done.11, f32[256,128]{1,0:T(8,128)} %copy-done.9, f32[4,4096]{1,0:T(4,128)} %broadcast_in_dim.39.low, f32[4,4096]{1,0:T(4,128)} %broadcast_in_dim.41.up, ...), custom_call_target="tpu_custom_call" | custom-call | flops 1610612736 | bytes 6291456 | tf_op jit(solution)/shard_map/attend/pallas_call | solution.py:205
  92.2 33.4 %all_to_all.16.heads = f32[8,256,128]{2,1,0:T(8,128)S(1)} all-to-all(f32[8,256,128]{2,1,0:T(8,128)} %attend.1), channel_id=1, replica_groups=mesh['x'=4,'y'=4,'z'=8,'k'=2] {'z'}, dimensions={0} | all-to-all | bytes 2097152 | tf_op jit(solution)/shard_map/all_to_all | solution.py:329
  125.6 2.2 %copy-done.1 = f32[64,2,16,512]{3,2,1,0:T(8,128)S(1)} copy-done((f32[64,2,16,512]{3,2,1,0:T(8,128)S(1)}, f32[64,2,16,512]{3,2,1,0:T(8,128)}, u32[]{:S(2)}) %copy-start.1) | copy-done | bytes 4194328
  127.7 2.5 %mix.1 = (f32[2,64,512]{2,1,0:T(8,128)S(1)}, f32[2,64,512]{2,1,0:T(8,128)S(1)}, f32[2,64,512]{2,1,0:T(8,128)S(1)}, f32[2,64,512]{2,1,0:T(8,128)S(1)}) custom-call(s32[4]{0:T(128)S(1)} %copy-done, f32[8,256,128]{2,1,0:T(8,128)S(1)} %all_to_all.16.heads, f32[8,8,2,16,512]{4,3,2,1,0:T(8,128)S(1)} %bitcast.42), custom_call_target="tpu_custom_call" | custom-call | flops 1610612736 | bytes 6291456 | tf_op jit(solution)/shard_map/mix/pallas_call | solution.py:242
  130.2 3.3 %collective-permute-start.11 = (f32[2,64,512]{2,1,0:T(8,128)S(1)}, f32[2,64,512]{2,1,0:T(8,128)S(1)}, u32[]{:S(2)}, u32[]{:S(2)}) collective-permute-start(f32[2,64,512]{2,1,0:T(8,128)S(1)} %get-tuple-element.58), channel_id=1, source_target_pairs={{0,64},{64,128},{128,192},{192,0},{1,65},{65,129},{129,193},{193,1... | collective-permute-start | bytes 786440 | tf_op jit(solution)/shard_map/ppermute | solution.py:278
  133.5 2.3 %collective-permute-start.12 = (f32[2,64,512]{2,1,0:T(8,128)S(1)}, f32[2,64,512]{2,1,0:T(8,128)S(1)}, u32[]{:S(2)}, u32[]{:S(2)}) collective-permute-start(f32[2,64,512]{2,1,0:T(8,128)S(1)} %get-tuple-element.59), channel_id=1, source_target_pairs={{0,128},{64,192},{128,0},{192,64},{1,129},{65,193},{129,1},{193,65... | collective-permute-start | bytes 786440 | tf_op jit(solution)/shard_map/ppermute | solution.py:278
  135.8 1.3 collective-permute-start.13
  137.1 2.5 %collective-permute-done.11 = f32[2,64,512]{2,1,0:T(8,128)S(1)} collective-permute-done((f32[2,64,512]{2,1,0:T(8,128)S(1)}, f32[2,64,512]{2,1,0:T(8,128)S(1)}, u32[]{:S(2)}, u32[]{:S(2)}) %collective-permute-start.11) | collective-permute-done | bytes 262176 | tf_op jit(solution)/shard_map/ppermute | solution.py:278
  139.6 7.1 %collective-permute-done.12 = f32[2,64,512]{2,1,0:T(8,128)S(1)} collective-permute-done((f32[2,64,512]{2,1,0:T(8,128)S(1)}, f32[2,64,512]{2,1,0:T(8,128)S(1)}, u32[]{:S(2)}, u32[]{:S(2)}) %collective-permute-start.12) | collective-permute-done | bytes 262176 | tf_op jit(solution)/shard_map/ppermute | solution.py:278
  146.8 2.1 %collective-permute-start.14 = (f32[64,512]{1,0:T(8,128)S(1)}, f32[64,512]{1,0:T(8,128)S(1)}, u32[]{:S(2)}, u32[]{:S(2)}) collective-permute-start(f32[64,512]{1,0:T(8,128)S(1)} %dynamic-slice_bitcast_fusion.2), channel_id=1, source_target_pairs={{0,1},{1,0},{2,3},{3,2},{4,5},{5,4},{6,7},{7,6},{8,9},{9,8},{10,11... | collective-permute-start | bytes 393224 | tf_op jit(solution)/shard_map/ppermute | solution.py:335
  (86 shorter events, 14.4 us)
Async XLA Ops:
  6.5 45.6 %all-gather.7.cloned.1.call-start = ((), (), s32[]{:S(2)}) async-start(), calls=%async_computation.3 | async-start | bytes 4718592 | tf_op jit(solution)/shard_map/all_gather | solution.py:294
  7.3 77.5 %all-gather.9.cloned.1.call-start = ((), (), s32[]{:S(2)}) async-start(), calls=%async_computation.4 | async-start | bytes 4718592 | tf_op jit(solution)/shard_map/all_gather | solution.py:308
  8.0 35.4 %copy-start.12 = (s32[32]{0:T(128)S(1)}, s32[32]{0:T(128)}, u32[]{:S(2)}) copy-start(s32[32]{0:T(128)} %param.14) | copy-start | bytes 388
  8.0 36.0 %copy-start.13 = (s32[32]{0:T(128)S(1)}, s32[32]{0:T(128)}, u32[]{:S(2)}) copy-start(s32[32]{0:T(128)} %param.16) | copy-start | bytes 388
  8.0 36.9 %copy-start.7 = (s32[32,16]{0,1:T(8,128)S(1)}, s32[32,16]{0,1:T(8,128)}, u32[]{:S(2)}) copy-start(s32[32,16]{0,1:T(8,128)} %param.15) | copy-start | bytes 6148
  8.0 36.9 %copy-start.8 = (s32[32,16]{0,1:T(8,128)S(1)}, s32[32,16]{0,1:T(8,128)}, u32[]{:S(2)}) copy-start(s32[32,16]{0,1:T(8,128)} %param.13) | copy-start | bytes 6148
  11.3 31.2 %collective-permute-start.5 = (f32[64,2048]{1,0:T(8,128)}, f32[64,2048]{1,0:T(8,128)S(1)}, u32[]{:S(2)}, u32[]{:S(2)}) collective-permute-start(f32[64,2048]{1,0:T(8,128)} %get-tuple-element.33), channel_id=1, source_target_pairs={{0,64},{64,128},{128,192},{192,0},{1,65},{65,129},{129,193},{193,1... | collective-permute-start | bytes 1572872 | tf_op jit(solution)/shard_map/ppermute | solution.py:278
  13.5 29.1 %collective-permute-start.6 = (f32[64,2048]{1,0:T(8,128)}, f32[64,2048]{1,0:T(8,128)S(1)}, u32[]{:S(2)}, u32[]{:S(2)}) collective-permute-start(f32[64,2048]{1,0:T(8,128)} %get-tuple-element.34), channel_id=1, source_target_pairs={{0,128},{64,192},{128,0},{192,64},{1,129},{65,193},{129,1},{193,65... | collective-permute-start | bytes 1572872 | tf_op jit(solution)/shard_map/ppermute | solution.py:278
  18.2 10.3 %collective-permute-start.2 = (f32[2,64,128]{2,1,0:T(8,128)}, f32[2,64,128]{2,1,0:T(8,128)S(1)}, u32[]{:S(2)}, u32[]{:S(2)}) collective-permute-start(f32[2,64,128]{2,1,0:T(8,128)} %get-tuple-element.39), channel_id=1, source_target_pairs={{0,8},{2,10},{4,12},{6,14},{8,0},{10,2},{12,4},{14,6},{1,9},{3,11}... | collective-permute-start | bytes 196616 | tf_op jit(solution)/shard_map/ppermute | solution.py:278
  25.2 8.0 %collective-permute-start.3 = (f32[2,64,128]{2,1,0:T(8,128)}, f32[2,64,128]{2,1,0:T(8,128)S(1)}, u32[]{:S(2)}, u32[]{:S(2)}) collective-permute-start(f32[2,64,128]{2,1,0:T(8,128)} %get-tuple-element.40), channel_id=1, source_target_pairs={{0,12},{2,14},{4,0},{6,2},{8,4},{10,6},{12,8},{14,10},{1,13},{3,15... | collective-permute-start | bytes 196616 | tf_op jit(solution)/shard_map/ppermute | solution.py:278
  25.2 8.4 %collective-permute-start.1 = (f32[2,64,128]{2,1,0:T(8,128)}, f32[2,64,128]{2,1,0:T(8,128)S(1)}, u32[]{:S(2)}, u32[]{:S(2)}) collective-permute-start(f32[2,64,128]{2,1,0:T(8,128)} %get-tuple-element.38), channel_id=1, source_target_pairs={{0,4},{2,6},{4,8},{6,10},{8,12},{10,14},{12,0},{14,2},{1,5},{3,7},... | collective-permute-start | bytes 196616 | tf_op jit(solution)/shard_map/ppermute | solution.py:278
  28.5 14.0 %collective-permute-start.7 = (f32[64,2048]{1,0:T(8,128)}, f32[64,2048]{1,0:T(8,128)S(1)}, u32[]{:S(2)}, u32[]{:S(2)}) collective-permute-start(f32[64,2048]{1,0:T(8,128)} %get-tuple-element.35), channel_id=1, source_target_pairs={{0,192},{64,0},{128,64},{192,128},{1,193},{65,1},{129,65},{193,129... | collective-permute-start | bytes 1572872 | tf_op jit(solution)/shard_map/ppermute | solution.py:278
  33.3 1.6 collective-permute-start
  34.5 8.0 %collective-permute-start.4 = (f32[4,2,64,128]{3,2,1,0:T(8,128)S(1)}, f32[4,2,64,128]{3,2,1,0:T(8,128)S(1)}, u32[]{:S(2)}, u32[]{:S(2)}) collective-permute-start(f32[4,2,64,128]{3,2,1,0:T(8,128)S(1)} %pad_maximum_fusion), channel_id=1, source_target_pairs={{0,2},{2,0},{4,6},{6,4},{8,10},{10,8},{12,14},{14,12},{1,3},{3,1},... | collective-permute-start | bytes 786440 | tf_op jit(solution)/shard_map/ppermute | solution.py:300
  46.6 16.8 %all-to-all-start = ((f32[16,16,512]{2,1,0:T(8,128)}), f32[16,16,512]{2,1,0:T(8,128)S(1)}, u32[]{:S(2)}, u32[]{:S(2)}) async-start(f32[16,16,512]{2,1,0:T(8,128)} %bitcast.12), calls=%async_computation | async-start | bytes 1048576 | tf_op jit(solution)/shard_map/all_to_all | solution.py:307
  51.9 73.6 %all-gather.11.cloned.1.call-start = ((), (), s32[]{:S(2)}) async-start(), calls=%async_computation.5 | async-start | bytes 4718592 | tf_op jit(solution)/shard_map/all_gather | solution.py:327
  57.4 6.1 %collective-permute-start.10 = (f32[256,128]{1,0:T(8,128)}, f32[256,128]{1,0:T(8,128)S(1)}, u32[]{:S(2)}, u32[]{:S(2)}) collective-permute-start(f32[256,128]{1,0:T(8,128)} %get-tuple-element.48), channel_id=1, source_target_pairs={{0,192},{64,0},{128,64},{192,128},{1,193},{65,1},{129,65},{193,129... | collective-permute-start | bytes 393224 | tf_op jit(solution)/shard_map/ppermute | solution.py:278
  60.0 7.5 %collective-permute-start.8 = (f32[256,128]{1,0:T(8,128)}, f32[256,128]{1,0:T(8,128)S(1)}, u32[]{:S(2)}, u32[]{:S(2)}) collective-permute-start(f32[256,128]{1,0:T(8,128)} %get-tuple-element.46), channel_id=1, source_target_pairs={{0,64},{64,128},{128,192},{192,0},{1,65},{65,129},{129,193},{193,1... | collective-permute-start | bytes 393224 | tf_op jit(solution)/shard_map/ppermute | solution.py:278
  60.0 7.5 %collective-permute-start.9 = (f32[256,128]{1,0:T(8,128)}, f32[256,128]{1,0:T(8,128)S(1)}, u32[]{:S(2)}, u32[]{:S(2)}) collective-permute-start(f32[256,128]{1,0:T(8,128)} %get-tuple-element.47), channel_id=1, source_target_pairs={{0,128},{64,192},{128,0},{192,64},{1,129},{65,193},{129,1},{193,65... | collective-permute-start | bytes 393224 | tf_op jit(solution)/shard_map/ppermute | solution.py:278
  83.9 41.6 %copy-start = (s32[4]{0:T(128)S(1)}, s32[4]{0:T(128)}, u32[]{:S(2)}) copy-start(s32[4]{0:T(128)} %pad_add_fusion.where) | copy-start | bytes 52
  130.2 9.4 %collective-permute-start.11 = (f32[2,64,512]{2,1,0:T(8,128)S(1)}, f32[2,64,512]{2,1,0:T(8,128)S(1)}, u32[]{:S(2)}, u32[]{:S(2)}) collective-permute-start(f32[2,64,512]{2,1,0:T(8,128)S(1)} %get-tuple-element.58), channel_id=1, source_target_pairs={{0,64},{64,128},{128,192},{192,0},{1,65},{65,129},{129,193},{193,1... | collective-permute-start | bytes 786440 | tf_op jit(solution)/shard_map/ppermute | solution.py:278
  133.5 13.1 %collective-permute-start.12 = (f32[2,64,512]{2,1,0:T(8,128)S(1)}, f32[2,64,512]{2,1,0:T(8,128)S(1)}, u32[]{:S(2)}, u32[]{:S(2)}) collective-permute-start(f32[2,64,512]{2,1,0:T(8,128)S(1)} %get-tuple-element.59), channel_id=1, source_target_pairs={{0,128},{64,192},{128,0},{192,64},{1,129},{65,193},{129,1},{193,65... | collective-permute-start | bytes 786440 | tf_op jit(solution)/shard_map/ppermute | solution.py:278
  135.8 10.8 %collective-permute-start.13 = (f32[2,64,512]{2,1,0:T(8,128)S(1)}, f32[2,64,512]{2,1,0:T(8,128)S(1)}, u32[]{:S(2)}, u32[]{:S(2)}) collective-permute-start(f32[2,64,512]{2,1,0:T(8,128)S(1)} %get-tuple-element.60), channel_id=1, source_target_pairs={{0,192},{64,0},{128,64},{192,128},{1,193},{65,1},{129,65},{193,129... | collective-permute-start | bytes 786440 | tf_op jit(solution)/shard_map/ppermute | solution.py:278
  146.8 3.1 %collective-permute-start.14 = (f32[64,512]{1,0:T(8,128)S(1)}, f32[64,512]{1,0:T(8,128)S(1)}, u32[]{:S(2)}, u32[]{:S(2)}) collective-permute-start(f32[64,512]{1,0:T(8,128)S(1)} %dynamic-slice_bitcast_fusion.2), channel_id=1, source_target_pairs={{0,1},{1,0},{2,3},{3,2},{4,5},{5,4},{6,7},{7,6},{8,9},{9,8},{10,11... | collective-permute-start | bytes 393224 | tf_op jit(solution)/shard_map/ppermute | solution.py:335
  (9 other events, 109.3 us)
Sparse Core Ops, SparseCore 0:
  9.2 38.8 all-gather.6
  50.0 34.6 all-gather.8
  86.6 34.6 all-gather.10

commit v15 on v14

--- a/solution.py
+++ b/solution.py
@@ -195,16 +195,14 @@
         term = term[:, :HD] + (term[:, HD:] + dot(weight_low, value_high, MM))
         total = weight if total is None else total + weight
         summed = term if summed is None else summed + term
-    attended = summed / jnp.sum(total, axis=1, keepdims=True)
-    for z in range(NZ):
-        out[z] = attended
+    out[...] = summed / jnp.sum(total, axis=1, keepdims=True)
 
 
 def attend(partial, low, up, gathered):
     rows = NX * BLOCK
     return pl.pallas_call(
         attend_kernel,
-        out_shape=jax.ShapeDtypeStruct((NZ, rows, HD), jnp.float32),
+        out_shape=jax.ShapeDtypeStruct((rows, HD), jnp.float32),
         in_specs=[VMEM] * 6 + [ANY],
         out_specs=VMEM,
         scratch_shapes=[
@@ -220,14 +218,24 @@
     )(*partial, low, up, gathered)
 
 
-def mix_kernel(where, heads, weights, *refs):
-    outs, total_buf = refs[:NX], refs[NX]
+OFFSETS = (0, -1, 1, -2, 2, -3, 3, 4)
+
+
+def mix_kernel(where, *refs):
+    heads, weights, outs, total_buf = refs[:9], refs[9], refs[10 : 10 + NX], refs[10 + NX]
+    blocks = [head[...] for head in heads[:7]]
+    blocks.append(jnp.concatenate([heads[7][...], heads[8][...]], axis=0))
+    places = [lax.rem(where[3] + offset + NZ, NZ) for offset in OFFSETS]
     totals = [None, None]
     for step in range(NZ // 2):
-        left = split(jnp.concatenate([heads[2 * step], heads[2 * step + 1]], axis=1))
+        left = split(jnp.concatenate(blocks[2 * step : 2 * step + 2], axis=1))
         for core in range(NK):
             right = jnp.concatenate(
-                [weights[:, 2 * step + z, core].reshape(HD, 512) for z in range(2)], axis=0
+                [
+                    weights[:, spot, core].reshape(HD, 512)
+                    for spot in places[2 * step : 2 * step + 2]
+                ],
+                axis=0,
             )
             term = dot3(left, split(right), MM)
             totals[core] = term if totals[core] is None else totals[core] + term
@@ -242,7 +250,7 @@
     return pl.pallas_call(
         mix_kernel,
         out_shape=[jax.ShapeDtypeStruct((NK, BLOCK, 512), jnp.float32)] * NX,
-        in_specs=[SMEM, VMEM, VMEM],
+        in_specs=[SMEM] + [VMEM] * 10,
         out_specs=[VMEM] * NX,
         scratch_shapes=[pltpu.VMEM((NX, NK, BLOCK, 512), jnp.float32)],
         compiler_params=pltpu.CompilerParams(vmem_limit_bytes=24 << 20),
@@ -250,7 +258,7 @@
             flops=6 * 256 * 1024 * 1024, bytes_accessed=6 << 20, transcendentals=0
         ),
         name="mix",
-    )(where, heads, weights)
+    )(where, *heads, weights)
 
 
 def allowed_rows(
@@ -325,15 +333,22 @@
     rows, partial, low, up = lax.optimization_barrier((rows, partial, low, up))
     rows = lax.all_to_all(rows.reshape(NZ, NK, 16, 512), "z", 0, 0)
     out_weight = lax.all_gather(rows, ("y", "k"), axis=0)
-    heads = attend(partial, low, up, kv)
-    heads = lax.all_to_all(heads, "z", 0, 0)
+    own = attend(partial, low, up, kv)
+    near_up, near_down = along("z", own, 1), along("z", own, -1)
+    far_up, far_down = along("z", own, 2), along("z", own, -2)
+    heads = [own, near_up, near_down, far_up, far_down]
+    heads += [along("z", far_up, 1), along("z", far_down, -1)]
+    heads += [along("z", far_up[:128], 2), along("z", far_down[128:], -2)]
     mixed = mix(where, heads, out_weight)
     mixed = [mixed[0]] + [along("x", mixed[s], s) for s in range(1, NX)]
-    mixed = (mixed[0] + mixed[1]) + (mixed[2] + mixed[3])
-    own = lax.dynamic_index_in_dim(mixed, k, 0, keepdims=False)
-    other = lax.dynamic_index_in_dim(mixed, 1 - k, 0, keepdims=False)
-    other = lax.ppermute(other, "k", CORES)
-    return jnp.concatenate([jnp.where(k == 0, own, other), jnp.where(k == 0, other, own)])
+    first, second = (
+        sum(lax.dynamic_index_in_dim(part, core, 0, keepdims=False) for part in mixed)
+        for core in (1 - k, k)
+    )
+    other = lax.ppermute(first, "k", CORES)
+    return jnp.concatenate(
+        [jnp.where(k == 0, second, other), jnp.where(k == 0, other, second)]
+    )
 
 
 def solution(mesh):

time: 158 us -> 152 us (0.962)
  blocking collectives: 49.8 us -> 16.4 us
  waiting for transfers between devices: 26.6 us -> 45.1 us
  starting transfers between devices: 34.5 us -> 43.4 us
    all_to_all x1 -> x0, blocking collectives: 33.4 us -> none  [shards(): heads = lax.all_to_all(heads, 'z', 0, 0)]
    ppermute x12 -> x20, waiting for transfers between devices: 17.1 us -> 28.3 us  [along(): lax.ppermute(value, axis, [(i, (i + shift) % count) for i in range(count)])]
    ppermute x12 -> x20, starting transfers between devices: 26.5 us -> 36.3 us  [along(): lax.ppermute(value, axis, [(i, (i + shift) % count) for i in range(count)])]
    all_gather x1, waiting for transfers between devices: 0.01 us -> 7.44 us  [shards(): out_weight = lax.all_gather(rows, ('y', 'k'), axis=0)]
    unnamed x32 -> x34, local copies, waits for them, and re-layouts: 3.86 us -> 4.76 us
  transfers between devices with their start and end apart: 19 -> 27, of which waited for: 8 -> 13; matrix products, arithmetic and copies ran while one was open for 5% -> 5% of each run, Pallas kernels for 12% -> 12%
where the time goes in v15:
time: 152 us
  waiting for transfers between devices  45.1 us (30%)
  starting transfers between devices  43.4 us (29%)
  Pallas kernels  20.5 us (13%)
  blocking collectives  16.4 us (11%)
  between operations  13.4 us (9%)
  local copies, waits for them, and re-layouts  7.76 us (5%)
  other arithmetic  5.19 us (3%)
    ppermute x20, starting transfers between devices, along(): lax.ppermute(value, axis, [(i, (i + shift) % count) for i in range(count)])  36.3 us
    ppermute x20, waiting for transfers between devices, along(): lax.ppermute(value, axis, [(i, (i + shift) % count) for i in range(count)])  28.3 us
    all_to_all x1, blocking collectives, shards(): rows = lax.all_to_all(rows.reshape(NZ, NK, 16, 512), 'z', 0, 0)  16.4 us
    all_gather x1, waiting for transfers between devices, shards(): out_weight = lax.all_gather(rows, ('y', 'k'), axis=0)  7.44 us
    pallas_call x1, Pallas kernels, attend(): pl.pallas_call(attend_kernel, out_shape=jax.ShapeDtypeStruct((rows, HD),...  7.11 us
    ppermute x1, waiting for transfers between devices, shards(): lax.ppermute(near, 'z', [(i, i ^ 1) for i in range(NZ)])  6.82 us
    all_to_all x1, starting transfers between devices, shards(): rows = lax.all_to_all(rows.reshape(NX * NY, 16, 512), ('x', 'y'), 0, 0)  5.33 us
    pallas_call x1, Pallas kernels, project(): pl.pallas_call(project_kernel, out_shape=[jax.ShapeDtypeStruct((NX * BLOC...  5.25 us
  transfers between devices with their start and end apart: 27, of which 13 were waited for; matrix products, arithmetic and copies ran while one was open for 5% of the time, Pallas kernels for 12%

profile of v15, /device:TPU:1, one launch (start us, length us, event | category | flops | bytes accessed | tf_op | source)
XLA Modules:
  0.0 151.9 jit_solution(1710900023178010476)
XLA Ops:
  8.0 3.4 %pick.1 = (f32[64,2048]{1,0:T(8,128)}, f32[64,2048]{1,0:T(8,128)}, f32[64,2048]{1,0:T(8,128)}) custom-call(s32[4]{0:T(128)} %pad_add_fusion.where, f32[128,8192]{1,0:T(8,128)} %rows.3), custom_call_target="tpu_custom_call" | custom-call | tf_op jit(solution)/shard_map/pick/pallas_call | solution.py:55
  13.5 2.5 %collective-permute-start.6 = (f32[64,2048]{1,0:T(8,128)}, f32[64,2048]{1,0:T(8,128)S(1)}, u32[]{:S(2)}, u32[]{:S(2)}) collective-permute-start(f32[64,2048]{1,0:T(8,128)} %get-tuple-element.34), channel_id=1, source_target_pairs={{0,128},{64,192},{128,0},{192,64},{1,129},{65,193},{129,1},{193,65... | collective-permute-start | bytes 1572872 | tf_op jit(solution)/shard_map/ppermute | solution.py:286
  15.9 2.3 %pick_keys.1 = (f32[2,64,128]{2,1,0:T(8,128)}, f32[2,64,128]{2,1,0:T(8,128)}, f32[2,64,128]{2,1,0:T(8,128)}, f32[2,64,128]{2,1,0:T(8,128)}) custom-call(s32[4]{0:T(128)} %pad_add_fusion.where, f32[256,512]{1,0:T(8,128)} %keys.1, f32[256,512]{1,0:T(8,128)} %values.1), custom_call_target="tpu_custom_call" | custom-call | bytes 67108864 | tf_op jit(solution)/shard_map/pick_keys/pallas_call | solution.py:87
  18.3 7.0 %collective-permute-start.2 = (f32[2,64,128]{2,1,0:T(8,128)}, f32[2,64,128]{2,1,0:T(8,128)S(1)}, u32[]{:S(2)}, u32[]{:S(2)}) collective-permute-start(f32[2,64,128]{2,1,0:T(8,128)} %get-tuple-element.39), channel_id=1, source_target_pairs={{0,8},{2,10},{4,12},{6,14},{8,0},{10,2},{12,4},{14,6},{1,9},{3,11}... | collective-permute-start | bytes 196616 | tf_op jit(solution)/shard_map/ppermute | solution.py:286
  25.3 2.4 %collective-permute-start.1 = (f32[2,64,128]{2,1,0:T(8,128)}, f32[2,64,128]{2,1,0:T(8,128)S(1)}, u32[]{:S(2)}, u32[]{:S(2)}) collective-permute-start(f32[2,64,128]{2,1,0:T(8,128)} %get-tuple-element.38), channel_id=1, source_target_pairs={{0,4},{2,6},{4,8},{6,10},{8,12},{10,14},{12,0},{14,2},{1,5},{3,7},... | collective-permute-start | bytes 196616 | tf_op jit(solution)/shard_map/ppermute | solution.py:286
  29.8 3.5 %collective-permute-done.3 = f32[2,64,128]{2,1,0:T(8,128)S(1)} collective-permute-done((f32[2,64,128]{2,1,0:T(8,128)}, f32[2,64,128]{2,1,0:T(8,128)S(1)}, u32[]{:S(2)}, u32[]{:S(2)}) %collective-permute-start.3) | collective-permute-done | bytes 65568 | tf_op jit(solution)/shard_map/ppermute | solution.py:286
  35.7 6.8 %collective-permute-done.4 = f32[4,2,64,128]{3,2,1,0:T(8,128)S(1)} collective-permute-done((f32[4,2,64,128]{3,2,1,0:T(8,128)S(1)}, f32[4,2,64,128]{3,2,1,0:T(8,128)S(1)}, u32[]{:S(2)}, u32[]{:S(2)}) %collective-permute-start.4) | collective-permute-done | bytes 262176 | tf_op jit(solution)/shard_map/ppermute | solution.py:308
  46.6 5.3 %all-to-all-start = ((f32[16,16,512]{2,1,0:T(8,128)}), f32[16,16,512]{2,1,0:T(8,128)S(1)}, u32[]{:S(2)}, u32[]{:S(2)}) async-start(f32[16,16,512]{2,1,0:T(8,128)} %bitcast.12), calls=%async_computation | async-start | bytes 1048576 | tf_op jit(solution)/shard_map/all_to_all | solution.py:315
  52.1 5.2 %project.1 = (f32[256,128]{1,0:T(8,128)}, f32[256,128]{1,0:T(8,128)}, f32[256,128]{1,0:T(8,128)}, f32[256,128]{1,0:T(8,128)}) custom-call(s32[4]{0:T(128)} %pad_add_fusion.where, f32[128,8192]{1,0:T(8,128)} %rows.3, f32[64,2048]{1,0:T(8,128)} %copy-done.4, f32[64,2048]{1,0:T(8,128)} %copy-done.5, f32[64,2048]{1,0:T(8,128)} %copy-done.6, f32[8,512,256]{2,1,0:T(8,128)} %bitcast.43), custom_call_target="tpu_custom_call" | custom-call | flops 1610612736 | bytes 7340032 | tf_op jit(solution)/shard_map/project/pallas_call | solution.py:137
  57.4 2.7 %collective-permute-start.10 = (f32[256,128]{1,0:T(8,128)}, f32[256,128]{1,0:T(8,128)S(1)}, u32[]{:S(2)}, u32[]{:S(2)}) collective-permute-start(f32[256,128]{1,0:T(8,128)} %get-tuple-element.48), channel_id=1, source_target_pairs={{0,192},{64,0},{128,64},{192,128},{1,193},{65,1},{129,65},{193,129... | collective-permute-start | bytes 393224 | tf_op jit(solution)/shard_map/ppermute | solution.py:286
  63.5 4.0 %collective-permute-done.8.second = f32[256,128]{1,0:T(8,128)S(1)} collective-permute-done((f32[256,128]{1,0:T(8,128)}, f32[256,128]{1,0:T(8,128)S(1)}, u32[]{:S(2)}, u32[]{:S(2)}) %collective-permute-start.8) | collective-permute-done | bytes 131104 | tf_op jit(solution)/shard_map/ppermute | solution.py:286
  67.5 16.4 %all_to_all.10 = f32[8,2,16,512]{3,2,1,0:T(8,128)} all-to-all(f32[8,2,16,512]{3,2,1,0:T(8,128)S(1)} %bitcast.44), channel_id=1, replica_groups=mesh['x'=4,'y'=4,'z'=8,'k'=2] {'z'}, dimensions={0} | all-to-all | bytes 1048576 | tf_op jit(solution)/shard_map/all_to_all | solution.py:334
  84.7 7.1 %attend.1.refs_0_ = f32[256,128]{1,0:T(8,128)} custom-call(f32[256,128]{1,0:T(8,128)} %get-tuple-element.49.first, f32[256,128]{1,0:T(8,128)} %copy-done.11, f32[256,128]{1,0:T(8,128)} %copy-done.12, f32[256,128]{1,0:T(8,128)} %copy-done.10, f32[4,4096]{1,0:T(4,128)} %broadcast_in_dim.39.low, f32[4,4096]{1,0:T(4,128)} %broadcast_in_dim.41.up, ...), custom_call_target="tpu_custom_call" | custom-call | flops 1610612736 | bytes 6291456 | tf_op jit(solution)/shard_map/attend/pallas_call | solution.py:203
  91.8 2.3 %collective-permute-start.13 = (f32[256,128]{1,0:T(8,128)}, f32[256,128]{1,0:T(8,128)S(1)}, u32[]{:S(2)}, u32[]{:S(2)}) collective-permute-start(f32[256,128]{1,0:T(8,128)} %attend.1.refs_0_), channel_id=1, source_target_pairs={{0,4},{2,6},{4,8},{6,10},{8,12},{10,14},{12,0},{14,2},{1,5},{3,7},... | collective-permute-start | bytes 393224 | tf_op jit(solution)/shard_map/ppermute | solution.py:286
  100.8 3.5 %collective-permute-done.14.refs_4_ = f32[256,128]{1,0:T(8,128)S(1)} collective-permute-done((f32[256,128]{1,0:T(8,128)}, f32[256,128]{1,0:T(8,128)S(1)}, u32[]{:S(2)}, u32[]{:S(2)}) %collective-permute-start.14) | collective-permute-done | bytes 131104 | tf_op jit(solution)/shard_map/ppermute | solution.py:286
  104.2 2.3 %collective-permute-start.17 = (f32[128,128]{1,0:T(8,128)S(1)}, f32[128,128]{1,0:T(8,128)S(1)}, u32[]{:S(2)}, u32[]{:S(2)}) collective-permute-start(f32[128,128]{1,0:T(8,128)S(1)} %slice.28), channel_id=1, source_target_pairs={{0,4},{2,6},{4,8},{6,10},{8,12},{10,14},{12,0},{14,2},{1,5},{3,7},... | collective-permute-start | bytes 196616 | tf_op jit(solution)/shard_map/ppermute | solution.py:286
  108.0 2.7 %collective-permute-done.17.refs_7_ = f32[128,128]{1,0:T(8,128)S(1)} collective-permute-done((f32[128,128]{1,0:T(8,128)S(1)}, f32[128,128]{1,0:T(8,128)S(1)}, u32[]{:S(2)}, u32[]{:S(2)}) %collective-permute-start.17) | collective-permute-done | bytes 65568 | tf_op jit(solution)/shard_map/ppermute | solution.py:286
  110.7 3.1 %collective-permute-done.18.refs_8_ = f32[128,128]{1,0:T(8,128)S(1)} collective-permute-done((f32[128,128]{1,0:T(8,128)S(1)}, f32[128,128]{1,0:T(8,128)S(1)}, u32[]{:S(2)}, u32[]{:S(2)}) %collective-permute-start.18) | collective-permute-done | bytes 65568 | tf_op jit(solution)/shard_map/ppermute | solution.py:286
  113.8 7.4 %all-gather.11.cloned.1.call-done = f32[64,2,16,512]{3,2,1,0:T(8,128)} async-done(((f32[8,2,16,512]{3,2,1,0:T(8,128)}), f32[64,2,16,512]{3,2,1,0:T(8,128)}) %all-gather.11.cloned.1.call-update) | async-done | bytes 4194320 | tf_op jit(solution)/shard_map/all_gather | solution.py:335
  121.3 2.2 %copy-done.1 = f32[64,2,16,512]{3,2,1,0:T(8,128)S(1)} copy-done((f32[64,2,16,512]{3,2,1,0:T(8,128)S(1)}, f32[64,2,16,512]{3,2,1,0:T(8,128)}, u32[]{:S(2)}) %copy-start.1) | copy-done | bytes 4194328
  124.4 2.5 %mix.1 = (f32[2,64,512]{2,1,0:T(8,128)S(1)}, f32[2,64,512]{2,1,0:T(8,128)S(1)}, f32[2,64,512]{2,1,0:T(8,128)S(1)}, f32[2,64,512]{2,1,0:T(8,128)S(1)}) custom-call(s32[4]{0:T(128)S(1)} %copy-done, f32[256,128]{1,0:T(8,128)S(1)} %copy-done.2, f32[256,128]{1,0:T(8,128)S(1)} %collective-permute-done.11.refs_1_, f32[256,128]{1,0:T(8,128)S(1)} %collective-permute-done.12.refs_2_, ...), custom_call_target="tpu_custom_call" | custom-call | flops 1610612736 | bytes 6291456 | tf_op jit(solution)/shard_map/mix/pallas_call | solution.py:250
  128.1 2.4 %collective-permute-start.20 = (f32[2,64,512]{2,1,0:T(8,128)S(1)}, f32[2,64,512]{2,1,0:T(8,128)S(1)}, u32[]{:S(2)}, u32[]{:S(2)}) collective-permute-start(f32[2,64,512]{2,1,0:T(8,128)S(1)} %get-tuple-element.59), channel_id=1, source_target_pairs={{0,128},{64,192},{128,0},{192,64},{1,129},{65,193},{129,1},{193,65... | collective-permute-start | bytes 786440 | tf_op jit(solution)/shard_map/ppermute | solution.py:286
  131.7 4.1 %collective-permute-done.19 = f32[2,64,512]{2,1,0:T(8,128)S(1)} collective-permute-done((f32[2,64,512]{2,1,0:T(8,128)S(1)}, f32[2,64,512]{2,1,0:T(8,128)S(1)}, u32[]{:S(2)}, u32[]{:S(2)}) %collective-permute-start.19) | collective-permute-done | bytes 262176 | tf_op jit(solution)/shard_map/ppermute | solution.py:286
  135.8 6.5 %collective-permute-done.20 = f32[2,64,512]{2,1,0:T(8,128)S(1)} collective-permute-done((f32[2,64,512]{2,1,0:T(8,128)S(1)}, f32[2,64,512]{2,1,0:T(8,128)S(1)}, u32[]{:S(2)}, u32[]{:S(2)}) %collective-permute-start.20) | collective-permute-done | bytes 262176 | tf_op jit(solution)/shard_map/ppermute | solution.py:286
  (105 shorter events, 30.8 us)
Async XLA Ops:
  6.5 45.6 %all-gather.7.cloned.1.call-start = ((), (), s32[]{:S(2)}) async-start(), calls=%async_computation.2 | async-start | bytes 4718592 | tf_op jit(solution)/shard_map/all_gather | solution.py:302
  7.3 77.5 %all-gather.9.cloned.1.call-start = ((), (), s32[]{:S(2)}) async-start(), calls=%async_computation.3 | async-start | bytes 4718592 | tf_op jit(solution)/shard_map/all_gather | solution.py:316
  11.4 31.2 %collective-permute-start.5 = (f32[64,2048]{1,0:T(8,128)}, f32[64,2048]{1,0:T(8,128)S(1)}, u32[]{:S(2)}, u32[]{:S(2)}) collective-permute-start(f32[64,2048]{1,0:T(8,128)} %get-tuple-element.33), channel_id=1, source_target_pairs={{0,64},{64,128},{128,192},{192,0},{1,65},{65,129},{129,193},{193,1... | collective-permute-start | bytes 1572872 | tf_op jit(solution)/shard_map/ppermute | solution.py:286
  13.5 29.1 %collective-permute-start.6 = (f32[64,2048]{1,0:T(8,128)}, f32[64,2048]{1,0:T(8,128)S(1)}, u32[]{:S(2)}, u32[]{:S(2)}) collective-permute-start(f32[64,2048]{1,0:T(8,128)} %get-tuple-element.34), channel_id=1, source_target_pairs={{0,128},{64,192},{128,0},{192,64},{1,129},{65,193},{129,1},{193,65... | collective-permute-start | bytes 1572872 | tf_op jit(solution)/shard_map/ppermute | solution.py:286
  18.3 10.3 %collective-permute-start.2 = (f32[2,64,128]{2,1,0:T(8,128)}, f32[2,64,128]{2,1,0:T(8,128)S(1)}, u32[]{:S(2)}, u32[]{:S(2)}) collective-permute-start(f32[2,64,128]{2,1,0:T(8,128)} %get-tuple-element.39), channel_id=1, source_target_pairs={{0,8},{2,10},{4,12},{6,14},{8,0},{10,2},{12,4},{14,6},{1,9},{3,11}... | collective-permute-start | bytes 196616 | tf_op jit(solution)/shard_map/ppermute | solution.py:286
  25.3 8.0 %collective-permute-start.3 = (f32[2,64,128]{2,1,0:T(8,128)}, f32[2,64,128]{2,1,0:T(8,128)S(1)}, u32[]{:S(2)}, u32[]{:S(2)}) collective-permute-start(f32[2,64,128]{2,1,0:T(8,128)} %get-tuple-element.40), channel_id=1, source_target_pairs={{0,12},{2,14},{4,0},{6,2},{8,4},{10,6},{12,8},{14,10},{1,13},{3,15... | collective-permute-start | bytes 196616 | tf_op jit(solution)/shard_map/ppermute | solution.py:286
  25.3 8.4 %collective-permute-start.1 = (f32[2,64,128]{2,1,0:T(8,128)}, f32[2,64,128]{2,1,0:T(8,128)S(1)}, u32[]{:S(2)}, u32[]{:S(2)}) collective-permute-start(f32[2,64,128]{2,1,0:T(8,128)} %get-tuple-element.38), channel_id=1, source_target_pairs={{0,4},{2,6},{4,8},{6,10},{8,12},{10,14},{12,0},{14,2},{1,5},{3,7},... | collective-permute-start | bytes 196616 | tf_op jit(solution)/shard_map/ppermute | solution.py:286
  28.5 14.0 %collective-permute-start.7 = (f32[64,2048]{1,0:T(8,128)}, f32[64,2048]{1,0:T(8,128)S(1)}, u32[]{:S(2)}, u32[]{:S(2)}) collective-permute-start(f32[64,2048]{1,0:T(8,128)} %get-tuple-element.35), channel_id=1, source_target_pairs={{0,192},{64,0},{128,64},{192,128},{1,193},{65,1},{129,65},{193,129... | collective-permute-start | bytes 1572872 | tf_op jit(solution)/shard_map/ppermute | solution.py:286
  34.5 8.0 %collective-permute-start.4 = (f32[4,2,64,128]{3,2,1,0:T(8,128)S(1)}, f32[4,2,64,128]{3,2,1,0:T(8,128)S(1)}, u32[]{:S(2)}, u32[]{:S(2)}) collective-permute-start(f32[4,2,64,128]{3,2,1,0:T(8,128)S(1)} %pad_maximum_fusion), channel_id=1, source_target_pairs={{0,2},{2,0},{4,6},{6,4},{8,10},{10,8},{12,14},{14,12},{1,3},{3,1},... | collective-permute-start | bytes 786440 | tf_op jit(solution)/shard_map/ppermute | solution.py:308
  46.6 16.9 %all-to-all-start = ((f32[16,16,512]{2,1,0:T(8,128)}), f32[16,16,512]{2,1,0:T(8,128)S(1)}, u32[]{:S(2)}, u32[]{:S(2)}) async-start(f32[16,16,512]{2,1,0:T(8,128)} %bitcast.12), calls=%async_computation | async-start | bytes 1048576 | tf_op jit(solution)/shard_map/all_to_all | solution.py:315
  52.0 69.3 %all-gather.11.cloned.1.call-start = ((), (), s32[]{:S(2)}) async-start(), calls=%async_computation.4 | async-start | bytes 4718592 | tf_op jit(solution)/shard_map/all_gather | solution.py:335
  60.1 7.5 %collective-permute-start.8 = (f32[256,128]{1,0:T(8,128)}, f32[256,128]{1,0:T(8,128)S(1)}, u32[]{:S(2)}, u32[]{:S(2)}) collective-permute-start(f32[256,128]{1,0:T(8,128)} %get-tuple-element.46), channel_id=1, source_target_pairs={{0,64},{64,128},{128,192},{192,0},{1,65},{65,129},{129,193},{193,1... | collective-permute-start | bytes 393224 | tf_op jit(solution)/shard_map/ppermute | solution.py:286
  60.1 7.5 %collective-permute-start.9 = (f32[256,128]{1,0:T(8,128)}, f32[256,128]{1,0:T(8,128)S(1)}, u32[]{:S(2)}, u32[]{:S(2)}) collective-permute-start(f32[256,128]{1,0:T(8,128)} %get-tuple-element.47), channel_id=1, source_target_pairs={{0,128},{64,192},{128,0},{192,64},{1,129},{65,193},{129,1},{193,65... | collective-permute-start | bytes 393224 | tf_op jit(solution)/shard_map/ppermute | solution.py:286
  91.8 7.4 %collective-permute-start.13 = (f32[256,128]{1,0:T(8,128)}, f32[256,128]{1,0:T(8,128)S(1)}, u32[]{:S(2)}, u32[]{:S(2)}) collective-permute-start(f32[256,128]{1,0:T(8,128)} %attend.1.refs_0_), channel_id=1, source_target_pairs={{0,4},{2,6},{4,8},{6,10},{8,12},{10,14},{12,0},{14,2},{1,5},{3,7},... | collective-permute-start | bytes 393224 | tf_op jit(solution)/shard_map/ppermute | solution.py:286
  94.2 10.1 %collective-permute-start.14 = (f32[256,128]{1,0:T(8,128)}, f32[256,128]{1,0:T(8,128)S(1)}, u32[]{:S(2)}, u32[]{:S(2)}) collective-permute-start(f32[256,128]{1,0:T(8,128)} %attend.1.refs_0_), channel_id=1, source_target_pairs={{0,12},{2,14},{4,0},{6,2},{8,4},{10,6},{12,8},{14,10},{1,13},{3,15... | collective-permute-start | bytes 393224 | tf_op jit(solution)/shard_map/ppermute | solution.py:286
  95.8 10.7 %collective-permute-start.11 = (f32[256,128]{1,0:T(8,128)}, f32[256,128]{1,0:T(8,128)S(1)}, u32[]{:S(2)}, u32[]{:S(2)}) collective-permute-start(f32[256,128]{1,0:T(8,128)} %attend.1.refs_0_), channel_id=1, source_target_pairs={{0,2},{2,4},{4,6},{6,8},{8,10},{10,12},{12,14},{14,0},{1,3},{3,5},... | collective-permute-start | bytes 393224 | tf_op jit(solution)/shard_map/ppermute | solution.py:286
  96.8 11.2 %collective-permute-start.12 = (f32[256,128]{1,0:T(8,128)}, f32[256,128]{1,0:T(8,128)S(1)}, u32[]{:S(2)}, u32[]{:S(2)}) collective-permute-start(f32[256,128]{1,0:T(8,128)} %attend.1.refs_0_), channel_id=1, source_target_pairs={{0,14},{2,0},{4,2},{6,4},{8,6},{10,8},{12,10},{14,12},{1,15},{3,1}... | collective-permute-start | bytes 393224 | tf_op jit(solution)/shard_map/ppermute | solution.py:286
  99.3 14.6 %collective-permute-start.15 = (f32[256,128]{1,0:T(8,128)S(1)}, f32[256,128]{1,0:T(8,128)S(1)}, u32[]{:S(2)}, u32[]{:S(2)}) collective-permute-start(f32[256,128]{1,0:T(8,128)S(1)} %collective-permute-done.13.refs_3_), channel_id=1, source_target_pairs={{0,2},{2,4},{4,6},{6,8},{8,10},{10,12},{12,14},{14,0},{1,3},{3,5},... | collective-permute-start | bytes 393224 | tf_op jit(solution)/shard_map/ppermute | solution.py:286
  104.2 9.6 %collective-permute-start.16 = (f32[256,128]{1,0:T(8,128)S(1)}, f32[256,128]{1,0:T(8,128)S(1)}, u32[]{:S(2)}, u32[]{:S(2)}) collective-permute-start(f32[256,128]{1,0:T(8,128)S(1)} %collective-permute-done.14.refs_4_), channel_id=1, source_target_pairs={{0,14},{2,0},{4,2},{6,4},{8,6},{10,8},{12,10},{14,12},{1,15},{3,1}... | collective-permute-start | bytes 393224 | tf_op jit(solution)/shard_map/ppermute | solution.py:286
  104.2 6.4 %collective-permute-start.17 = (f32[128,128]{1,0:T(8,128)S(1)}, f32[128,128]{1,0:T(8,128)S(1)}, u32[]{:S(2)}, u32[]{:S(2)}) collective-permute-start(f32[128,128]{1,0:T(8,128)S(1)} %slice.28), channel_id=1, source_target_pairs={{0,4},{2,6},{4,8},{6,10},{8,12},{10,14},{12,0},{14,2},{1,5},{3,7},... | collective-permute-start | bytes 196616 | tf_op jit(solution)/shard_map/ppermute | solution.py:286
  106.5 7.3 %collective-permute-start.18 = (f32[128,128]{1,0:T(8,128)S(1)}, f32[128,128]{1,0:T(8,128)S(1)}, u32[]{:S(2)}, u32[]{:S(2)}) collective-permute-start(f32[128,128]{1,0:T(8,128)S(1)} %slice.29), channel_id=1, source_target_pairs={{0,12},{2,14},{4,0},{6,2},{8,4},{10,6},{12,8},{14,10},{1,13},{3,15... | collective-permute-start | bytes 196616 | tf_op jit(solution)/shard_map/ppermute | solution.py:286
  126.8 8.9 %collective-permute-start.19 = (f32[2,64,512]{2,1,0:T(8,128)S(1)}, f32[2,64,512]{2,1,0:T(8,128)S(1)}, u32[]{:S(2)}, u32[]{:S(2)}) collective-permute-start(f32[2,64,512]{2,1,0:T(8,128)S(1)} %get-tuple-element.58), channel_id=1, source_target_pairs={{0,64},{64,128},{128,192},{192,0},{1,65},{65,129},{129,193},{193,1... | collective-permute-start | bytes 786440 | tf_op jit(solution)/shard_map/ppermute | solution.py:286
  128.1 14.2 %collective-permute-start.20 = (f32[2,64,512]{2,1,0:T(8,128)S(1)}, f32[2,64,512]{2,1,0:T(8,128)S(1)}, u32[]{:S(2)}, u32[]{:S(2)}) collective-permute-start(f32[2,64,512]{2,1,0:T(8,128)S(1)} %get-tuple-element.59), channel_id=1, source_target_pairs={{0,128},{64,192},{128,0},{192,64},{1,129},{65,193},{129,1},{193,65... | collective-permute-start | bytes 786440 | tf_op jit(solution)/shard_map/ppermute | solution.py:286
  130.5 11.8 %collective-permute-start.21 = (f32[2,64,512]{2,1,0:T(8,128)S(1)}, f32[2,64,512]{2,1,0:T(8,128)S(1)}, u32[]{:S(2)}, u32[]{:S(2)}) collective-permute-start(f32[2,64,512]{2,1,0:T(8,128)S(1)} %get-tuple-element.60), channel_id=1, source_target_pairs={{0,192},{64,0},{128,64},{192,128},{1,193},{65,1},{129,65},{193,129... | collective-permute-start | bytes 786440 | tf_op jit(solution)/shard_map/ppermute | solution.py:286
  (18 other events, 324.5 us)
Sparse Core Ops, SparseCore 0:
  9.2 38.8 all-gather.6
  50.0 34.6 all-gather.8
  86.6 34.6 all-gather.10

commit v16 on v15

--- a/solution.py
+++ b/solution.py
@@ -210,7 +210,7 @@
             pltpu.VMEM((8, rows, NZ * BLOCK), jnp.float32),
             pltpu.SemaphoreType.DMA((8,)),
         ],
-        compiler_params=pltpu.CompilerParams(vmem_limit_bytes=LIMIT),
+        compiler_params=pltpu.CompilerParams(vmem_limit_bytes=40 << 20),
         cost_estimate=pl.CostEstimate(
             flops=12 * 256 * 4096 * HD, bytes_accessed=6 << 20, transcendentals=256 * 4096
         ),
@@ -222,21 +222,32 @@
 
 
 def mix_kernel(where, *refs):
-    heads, weights, outs, total_buf = refs[:9], refs[9], refs[10 : 10 + NX], refs[10 + NX]
+    heads, weights, outs = refs[:9], refs[9], refs[10 : 10 + NX]
+    total_buf, buf, sems = refs[10 + NX :]
+    places = [lax.rem(where[3] + offset + NZ, NZ) for offset in OFFSETS]
+    copies = [
+        [
+            pltpu.make_async_copy(
+                weights.at[part, spot], buf.at[index, :, pl.ds(16 * part, 16)], sems.at[index, part]
+            )
+            for part in range(8)
+        ]
+        for index, spot in enumerate(places)
+    ]
+    for group in copies:
+        for copy in group:
+            copy.start()
     blocks = [head[...] for head in heads[:7]]
     blocks.append(jnp.concatenate([heads[7][...], heads[8][...]], axis=0))
-    places = [lax.rem(where[3] + offset + NZ, NZ) for offset in OFFSETS]
     totals = [None, None]
     for step in range(NZ // 2):
-        left = split(jnp.concatenate(blocks[2 * step : 2 * step + 2], axis=1))
+        pair = (2 * step, 2 * step + 1)
+        left = split(jnp.concatenate([blocks[index] for index in pair], axis=1))
+        for index in pair:
+            for copy in copies[index]:
+                copy.wait()
         for core in range(NK):
-            right = jnp.concatenate(
-                [
-                    weights[:, spot, core].reshape(HD, 512)
-                    for spot in places[2 * step : 2 * step + 2]
-                ],
-                axis=0,
-            )
+            right = jnp.concatenate([buf[index, core] for index in pair], axis=0)
             term = dot3(left, split(right), MM)
             totals[core] = term if totals[core] is None else totals[core] + term
     for core in range(NK):
@@ -250,10 +261,14 @@
     return pl.pallas_call(
         mix_kernel,
         out_shape=[jax.ShapeDtypeStruct((NK, BLOCK, 512), jnp.float32)] * NX,
-        in_specs=[SMEM] + [VMEM] * 10,
+        in_specs=[SMEM] + [VMEM] * 9 + [ANY],
         out_specs=[VMEM] * NX,
-        scratch_shapes=[pltpu.VMEM((NX, NK, BLOCK, 512), jnp.float32)],
-        compiler_params=pltpu.CompilerParams(vmem_limit_bytes=24 << 20),
+        scratch_shapes=[
+            pltpu.VMEM((NX, NK, BLOCK, 512), jnp.float32),
+            pltpu.VMEM((NZ, NK, HD, 512), jnp.float32),
+            pltpu.SemaphoreType.DMA((NZ, 8)),
+        ],
+        compiler_params=pltpu.CompilerParams(vmem_limit_bytes=48 << 20),
         cost_estimate=pl.CostEstimate(
             flops=6 * 256 * 1024 * 1024, bytes_accessed=6 << 20, transcendentals=0
         ),

time: 152 us -> 151 us (level)
    pallas_call x1, Pallas kernels: 7.11 us -> 4.64 us  [attend(): pl.pallas_call(attend_kernel, out_shape=jax.ShapeDtypeStruct((rows, HD),...]
    pallas_call x1, Pallas kernels: 2.48 us -> 4.53 us  [mix(): pl.pallas_call(mix_kernel, out_shape=[jax.ShapeDtypeStruct((NK, BLOCK, 51...]
    unnamed x34 -> x28, local copies, waits for them, and re-layouts: 4.76 us -> 4.76 us
  transfers between devices with their start and end apart: 27 -> 27, of which waited for: 13 -> 14; matrix products, arithmetic and copies ran while one was open for 5% -> 5% of each run, Pallas kernels for 12% -> 10%
where the time goes in v16:
time: 151 us
  waiting for transfers between devices  45.8 us (30%)
  starting transfers between devices  43.4 us (29%)
  Pallas kernels  20.1 us (13%)
  blocking collectives  16.4 us (11%)
  between operations  13.4 us (9%)
  local copies, waits for them, and re-layouts  6.53 us (4%)
  other arithmetic  5.12 us (3%)
    ppermute x20, starting transfers between devices, along(): lax.ppermute(value, axis, [(i, (i + shift) % count) for i in range(count)])  36.3 us
    ppermute x20, waiting for transfers between devices, along(): lax.ppermute(value, axis, [(i, (i + shift) % count) for i in range(count)])  29.3 us
    all_to_all x1, blocking collectives, shards(): rows = lax.all_to_all(rows.reshape(NZ, NK, 16, 512), 'z', 0, 0)  16.4 us
    all_gather x1, waiting for transfers between devices, shards(): out_weight = lax.all_gather(rows, ('y', 'k'), axis=0)  7.02 us
    ppermute x1, waiting for transfers between devices, shards(): lax.ppermute(near, 'z', [(i, i ^ 1) for i in range(NZ)])  6.81 us
    all_to_all x1, starting transfers between devices, shards(): rows = lax.all_to_all(rows.reshape(NX * NY, 16, 512), ('x', 'y'), 0, 0)  5.33 us
    pallas_call x1, Pallas kernels, project(): pl.pallas_call(project_kernel, out_shape=[jax.ShapeDtypeStruct((NX * BLOC...  5.25 us
    unnamed x28, local copies, waits for them, and re-layouts  4.76 us
  transfers between devices with their start and end apart: 27, of which 14 were waited for; matrix products, arithmetic and copies ran while one was open for 5% of the time, Pallas kernels for 10%

profile of v16, /device:TPU:1, one launch (start us, length us, event | category | flops | bytes accessed | tf_op | source)
XLA Modules:
  0.0 150.8 jit_solution(4275256175119601929)
XLA Ops:
  7.9 3.3 %pick.1 = (f32[64,2048]{1,0:T(8,128)}, f32[64,2048]{1,0:T(8,128)}, f32[64,2048]{1,0:T(8,128)}) custom-call(s32[4]{0:T(128)} %pad_add_fusion.where, f32[128,8192]{1,0:T(8,128)} %rows.3), custom_call_target="tpu_custom_call" | custom-call | tf_op jit(solution)/shard_map/pick/pallas_call | solution.py:55
  11.3 2.1 %collective-permute-start.5 = (f32[64,2048]{1,0:T(8,128)}, f32[64,2048]{1,0:T(8,128)S(1)}, u32[]{:S(2)}, u32[]{:S(2)}) collective-permute-start(f32[64,2048]{1,0:T(8,128)} %get-tuple-element.33), channel_id=1, source_target_pairs={{0,64},{64,128},{128,192},{192,0},{1,65},{65,129},{129,193},{193,1... | collective-permute-start | bytes 1572872 | tf_op jit(solution)/shard_map/ppermute | solution.py:301
  13.4 2.5 %collective-permute-start.6 = (f32[64,2048]{1,0:T(8,128)}, f32[64,2048]{1,0:T(8,128)S(1)}, u32[]{:S(2)}, u32[]{:S(2)}) collective-permute-start(f32[64,2048]{1,0:T(8,128)} %get-tuple-element.34), channel_id=1, source_target_pairs={{0,128},{64,192},{128,0},{192,64},{1,129},{65,193},{129,1},{193,65... | collective-permute-start | bytes 1572872 | tf_op jit(solution)/shard_map/ppermute | solution.py:301
  15.8 2.3 %pick_keys.1 = (f32[2,64,128]{2,1,0:T(8,128)}, f32[2,64,128]{2,1,0:T(8,128)}, f32[2,64,128]{2,1,0:T(8,128)}, f32[2,64,128]{2,1,0:T(8,128)}) custom-call(s32[4]{0:T(128)} %pad_add_fusion.where, f32[256,512]{1,0:T(8,128)} %keys.1, f32[256,512]{1,0:T(8,128)} %values.1), custom_call_target="tpu_custom_call" | custom-call | bytes 67108864 | tf_op jit(solution)/shard_map/pick_keys/pallas_call | solution.py:87
  18.2 7.0 %collective-permute-start.2 = (f32[2,64,128]{2,1,0:T(8,128)}, f32[2,64,128]{2,1,0:T(8,128)S(1)}, u32[]{:S(2)}, u32[]{:S(2)}) collective-permute-start(f32[2,64,128]{2,1,0:T(8,128)} %get-tuple-element.39), channel_id=1, source_target_pairs={{0,8},{2,10},{4,12},{6,14},{8,0},{10,2},{12,4},{14,6},{1,9},{3,11}... | collective-permute-start | bytes 196616 | tf_op jit(solution)/shard_map/ppermute | solution.py:301
  25.2 2.4 %collective-permute-start.1 = (f32[2,64,128]{2,1,0:T(8,128)}, f32[2,64,128]{2,1,0:T(8,128)S(1)}, u32[]{:S(2)}, u32[]{:S(2)}) collective-permute-start(f32[2,64,128]{2,1,0:T(8,128)} %get-tuple-element.38), channel_id=1, source_target_pairs={{0,4},{2,6},{4,8},{6,10},{8,12},{10,14},{12,0},{14,2},{1,5},{3,7},... | collective-permute-start | bytes 196616 | tf_op jit(solution)/shard_map/ppermute | solution.py:301
  29.7 3.5 %collective-permute-done.3 = f32[2,64,128]{2,1,0:T(8,128)S(1)} collective-permute-done((f32[2,64,128]{2,1,0:T(8,128)}, f32[2,64,128]{2,1,0:T(8,128)S(1)}, u32[]{:S(2)}, u32[]{:S(2)}) %collective-permute-start.3) | collective-permute-done | bytes 65568 | tf_op jit(solution)/shard_map/ppermute | solution.py:301
  35.6 6.8 %collective-permute-done.4 = f32[4,2,64,128]{3,2,1,0:T(8,128)S(1)} collective-permute-done((f32[4,2,64,128]{3,2,1,0:T(8,128)S(1)}, f32[4,2,64,128]{3,2,1,0:T(8,128)S(1)}, u32[]{:S(2)}, u32[]{:S(2)}) %collective-permute-start.4) | collective-permute-done | bytes 262176 | tf_op jit(solution)/shard_map/ppermute | solution.py:323
  46.5 5.3 %all-to-all-start = ((f32[16,16,512]{2,1,0:T(8,128)}), f32[16,16,512]{2,1,0:T(8,128)S(1)}, u32[]{:S(2)}, u32[]{:S(2)}) async-start(f32[16,16,512]{2,1,0:T(8,128)} %bitcast.12), calls=%async_computation | async-start | bytes 1048576 | tf_op jit(solution)/shard_map/all_to_all | solution.py:330
  52.1 5.3 %project.1 = (f32[256,128]{1,0:T(8,128)}, f32[256,128]{1,0:T(8,128)}, f32[256,128]{1,0:T(8,128)}, f32[256,128]{1,0:T(8,128)}) custom-call(s32[4]{0:T(128)} %pad_add_fusion.where, f32[128,8192]{1,0:T(8,128)} %rows.3, f32[64,2048]{1,0:T(8,128)} %copy-done.4, f32[64,2048]{1,0:T(8,128)} %copy-done.5, f32[64,2048]{1,0:T(8,128)} %copy-done.6, f32[8,512,256]{2,1,0:T(8,128)} %bitcast.43), custom_call_target="tpu_custom_call" | custom-call | flops 1610612736 | bytes 7340032 | tf_op jit(solution)/shard_map/project/pallas_call | solution.py:137
  57.3 2.7 %collective-permute-start.10 = (f32[256,128]{1,0:T(8,128)}, f32[256,128]{1,0:T(8,128)S(1)}, u32[]{:S(2)}, u32[]{:S(2)}) collective-permute-start(f32[256,128]{1,0:T(8,128)} %get-tuple-element.48), channel_id=1, source_target_pairs={{0,192},{64,0},{128,64},{192,128},{1,193},{65,1},{129,65},{193,129... | collective-permute-start | bytes 393224 | tf_op jit(solution)/shard_map/ppermute | solution.py:301
  62.2 5.2 %collective-permute-done.8.second = f32[256,128]{1,0:T(8,128)S(1)} collective-permute-done((f32[256,128]{1,0:T(8,128)}, f32[256,128]{1,0:T(8,128)S(1)}, u32[]{:S(2)}, u32[]{:S(2)}) %collective-permute-start.8) | collective-permute-done | bytes 131104 | tf_op jit(solution)/shard_map/ppermute | solution.py:301
  67.5 16.4 %all_to_all.10 = f32[8,2,16,512]{3,2,1,0:T(8,128)} all-to-all(f32[8,2,16,512]{3,2,1,0:T(8,128)S(1)} %bitcast.44), channel_id=1, replica_groups=mesh['x'=4,'y'=4,'z'=8,'k'=2] {'z'}, dimensions={0} | all-to-all | bytes 1048576 | tf_op jit(solution)/shard_map/all_to_all | solution.py:349
  84.7 2.2 %copy-done.1 = f32[64,2,64,128]{3,2,1,0:T(8,128)S(1)} copy-done((f32[64,2,64,128]{3,2,1,0:T(8,128)S(1)}, f32[64,2,64,128]{3,2,1,0:T(8,128)}, u32[]{:S(2)}) %copy-start.1) | copy-done | bytes 4194328
  87.8 4.6 %attend.1.refs_0_ = f32[256,128]{1,0:T(8,128)S(1)} custom-call(f32[256,128]{1,0:T(8,128)S(1)} %copy-done.2, f32[256,128]{1,0:T(8,128)S(1)} %collective-permute-done.8.second, f32[256,128]{1,0:T(8,128)S(1)} %collective-permute-done.9.third, f32[256,128]{1,0:T(8,128)S(1)} %collective-permute-done.10.fourth, f32[4,4096]{1,0:T(4,128)S(1)} %broadcast_in_dim.39.low, ...), custom_call_target="tpu_custom_call" | custom-call | flops 1610612736 | bytes 6291456 | tf_op jit(solution)/shard_map/attend/pallas_call | solution.py:203
  92.5 2.3 %collective-permute-start.13 = (f32[256,128]{1,0:T(8,128)S(1)}, f32[256,128]{1,0:T(8,128)S(1)}, u32[]{:S(2)}, u32[]{:S(2)}) collective-permute-start(f32[256,128]{1,0:T(8,128)S(1)} %attend.1.refs_0_), channel_id=1, source_target_pairs={{0,4},{2,6},{4,8},{6,10},{8,12},{10,14},{12,0},{14,2},{1,5},{3,7},... | collective-permute-start | bytes 393224 | tf_op jit(solution)/shard_map/ppermute | solution.py:301
  101.2 3.5 %collective-permute-done.14.refs_4_ = f32[256,128]{1,0:T(8,128)S(1)} collective-permute-done((f32[256,128]{1,0:T(8,128)S(1)}, f32[256,128]{1,0:T(8,128)S(1)}, u32[]{:S(2)}, u32[]{:S(2)}) %collective-permute-start.14) | collective-permute-done | bytes 131104 | tf_op jit(solution)/shard_map/ppermute | solution.py:301
  108.4 2.6 %collective-permute-done.17.refs_7_ = f32[128,128]{1,0:T(8,128)S(1)} collective-permute-done((f32[128,128]{1,0:T(8,128)S(1)}, f32[128,128]{1,0:T(8,128)S(1)}, u32[]{:S(2)}, u32[]{:S(2)}) %collective-permute-start.17) | collective-permute-done | bytes 65568 | tf_op jit(solution)/shard_map/ppermute | solution.py:301
  111.1 3.2 %collective-permute-done.18.refs_8_ = f32[128,128]{1,0:T(8,128)S(1)} collective-permute-done((f32[128,128]{1,0:T(8,128)S(1)}, f32[128,128]{1,0:T(8,128)S(1)}, u32[]{:S(2)}, u32[]{:S(2)}) %collective-permute-start.18) | collective-permute-done | bytes 65568 | tf_op jit(solution)/shard_map/ppermute | solution.py:301
  114.2 7.0 %all-gather.11.cloned.1.call-done = f32[64,2,16,512]{3,2,1,0:T(8,128)} async-done(((f32[8,2,16,512]{3,2,1,0:T(8,128)}), f32[64,2,16,512]{3,2,1,0:T(8,128)}) %all-gather.11.cloned.1.call-update) | async-done | bytes 4194320 | tf_op jit(solution)/shard_map/all_gather | solution.py:350
  121.3 4.5 %mix.1 = (f32[2,64,512]{2,1,0:T(8,128)S(1)}, f32[2,64,512]{2,1,0:T(8,128)S(1)}, f32[2,64,512]{2,1,0:T(8,128)S(1)}, f32[2,64,512]{2,1,0:T(8,128)S(1)}) custom-call(s32[4]{0:T(128)S(1)} %copy-done, f32[256,128]{1,0:T(8,128)S(1)} %attend.1.refs_0_, f32[256,128]{1,0:T(8,128)S(1)} %collective-permute-done.11.refs_1_, ...), custom_call_target="tpu_custom_call" | custom-call | flops 1610612736 | bytes 6291456 | tf_op jit(solution)/shard_map/mix/pallas_call | solution.py:261
  127.1 2.4 %collective-permute-start.20 = (f32[2,64,512]{2,1,0:T(8,128)S(1)}, f32[2,64,512]{2,1,0:T(8,128)S(1)}, u32[]{:S(2)}, u32[]{:S(2)}) collective-permute-start(f32[2,64,512]{2,1,0:T(8,128)S(1)} %get-tuple-element.59), channel_id=1, source_target_pairs={{0,128},{64,192},{128,0},{192,64},{1,129},{65,193},{129,1},{193,65... | collective-permute-start | bytes 786440 | tf_op jit(solution)/shard_map/ppermute | solution.py:301
  130.6 4.1 %collective-permute-done.19 = f32[2,64,512]{2,1,0:T(8,128)S(1)} collective-permute-done((f32[2,64,512]{2,1,0:T(8,128)S(1)}, f32[2,64,512]{2,1,0:T(8,128)S(1)}, u32[]{:S(2)}, u32[]{:S(2)}) %collective-permute-start.19) | collective-permute-done | bytes 262176 | tf_op jit(solution)/shard_map/ppermute | solution.py:301
  134.8 6.5 %collective-permute-done.20 = f32[2,64,512]{2,1,0:T(8,128)S(1)} collective-permute-done((f32[2,64,512]{2,1,0:T(8,128)S(1)}, f32[2,64,512]{2,1,0:T(8,128)S(1)}, u32[]{:S(2)}, u32[]{:S(2)}) %collective-permute-start.20) | collective-permute-done | bytes 262176 | tf_op jit(solution)/shard_map/ppermute | solution.py:301
  (99 shorter events, 29.5 us)
Async XLA Ops:
  6.5 45.5 %all-gather.7.cloned.1.call-start = ((), (), s32[]{:S(2)}) async-start(), calls=%async_computation.2 | async-start | bytes 4718592 | tf_op jit(solution)/shard_map/all_gather | solution.py:317
  7.3 77.5 %all-gather.9.cloned.1.call-start = ((), (), s32[]{:S(2)}) async-start(), calls=%async_computation.3 | async-start | bytes 4718592 | tf_op jit(solution)/shard_map/all_gather | solution.py:331
  11.3 31.2 %collective-permute-start.5 = (f32[64,2048]{1,0:T(8,128)}, f32[64,2048]{1,0:T(8,128)S(1)}, u32[]{:S(2)}, u32[]{:S(2)}) collective-permute-start(f32[64,2048]{1,0:T(8,128)} %get-tuple-element.33), channel_id=1, source_target_pairs={{0,64},{64,128},{128,192},{192,0},{1,65},{65,129},{129,193},{193,1... | collective-permute-start | bytes 1572872 | tf_op jit(solution)/shard_map/ppermute | solution.py:301
  13.4 29.1 %collective-permute-start.6 = (f32[64,2048]{1,0:T(8,128)}, f32[64,2048]{1,0:T(8,128)S(1)}, u32[]{:S(2)}, u32[]{:S(2)}) collective-permute-start(f32[64,2048]{1,0:T(8,128)} %get-tuple-element.34), channel_id=1, source_target_pairs={{0,128},{64,192},{128,0},{192,64},{1,129},{65,193},{129,1},{193,65... | collective-permute-start | bytes 1572872 | tf_op jit(solution)/shard_map/ppermute | solution.py:301
  18.2 10.3 %collective-permute-start.2 = (f32[2,64,128]{2,1,0:T(8,128)}, f32[2,64,128]{2,1,0:T(8,128)S(1)}, u32[]{:S(2)}, u32[]{:S(2)}) collective-permute-start(f32[2,64,128]{2,1,0:T(8,128)} %get-tuple-element.39), channel_id=1, source_target_pairs={{0,8},{2,10},{4,12},{6,14},{8,0},{10,2},{12,4},{14,6},{1,9},{3,11}... | collective-permute-start | bytes 196616 | tf_op jit(solution)/shard_map/ppermute | solution.py:301
  25.2 8.0 %collective-permute-start.3 = (f32[2,64,128]{2,1,0:T(8,128)}, f32[2,64,128]{2,1,0:T(8,128)S(1)}, u32[]{:S(2)}, u32[]{:S(2)}) collective-permute-start(f32[2,64,128]{2,1,0:T(8,128)} %get-tuple-element.40), channel_id=1, source_target_pairs={{0,12},{2,14},{4,0},{6,2},{8,4},{10,6},{12,8},{14,10},{1,13},{3,15... | collective-permute-start | bytes 196616 | tf_op jit(solution)/shard_map/ppermute | solution.py:301
  25.2 8.4 %collective-permute-start.1 = (f32[2,64,128]{2,1,0:T(8,128)}, f32[2,64,128]{2,1,0:T(8,128)S(1)}, u32[]{:S(2)}, u32[]{:S(2)}) collective-permute-start(f32[2,64,128]{2,1,0:T(8,128)} %get-tuple-element.38), channel_id=1, source_target_pairs={{0,4},{2,6},{4,8},{6,10},{8,12},{10,14},{12,0},{14,2},{1,5},{3,7},... | collective-permute-start | bytes 196616 | tf_op jit(solution)/shard_map/ppermute | solution.py:301
  28.4 14.0 %collective-permute-start.7 = (f32[64,2048]{1,0:T(8,128)}, f32[64,2048]{1,0:T(8,128)S(1)}, u32[]{:S(2)}, u32[]{:S(2)}) collective-permute-start(f32[64,2048]{1,0:T(8,128)} %get-tuple-element.35), channel_id=1, source_target_pairs={{0,192},{64,0},{128,64},{192,128},{1,193},{65,1},{129,65},{193,129... | collective-permute-start | bytes 1572872 | tf_op jit(solution)/shard_map/ppermute | solution.py:301
  34.4 8.0 %collective-permute-start.4 = (f32[4,2,64,128]{3,2,1,0:T(8,128)S(1)}, f32[4,2,64,128]{3,2,1,0:T(8,128)S(1)}, u32[]{:S(2)}, u32[]{:S(2)}) collective-permute-start(f32[4,2,64,128]{3,2,1,0:T(8,128)S(1)} %pad_maximum_fusion), channel_id=1, source_target_pairs={{0,2},{2,0},{4,6},{6,4},{8,10},{10,8},{12,14},{14,12},{1,3},{3,1},... | collective-permute-start | bytes 786440 | tf_op jit(solution)/shard_map/ppermute | solution.py:323
  46.5 15.6 %all-to-all-start = ((f32[16,16,512]{2,1,0:T(8,128)}), f32[16,16,512]{2,1,0:T(8,128)S(1)}, u32[]{:S(2)}, u32[]{:S(2)}) async-start(f32[16,16,512]{2,1,0:T(8,128)} %bitcast.12), calls=%async_computation | async-start | bytes 1048576 | tf_op jit(solution)/shard_map/all_to_all | solution.py:330
  51.9 69.4 %all-gather.11.cloned.1.call-start = ((), (), s32[]{:S(2)}) async-start(), calls=%async_computation.4 | async-start | bytes 4718592 | tf_op jit(solution)/shard_map/all_gather | solution.py:350
  60.0 7.5 %collective-permute-start.8 = (f32[256,128]{1,0:T(8,128)}, f32[256,128]{1,0:T(8,128)S(1)}, u32[]{:S(2)}, u32[]{:S(2)}) collective-permute-start(f32[256,128]{1,0:T(8,128)} %get-tuple-element.46), channel_id=1, source_target_pairs={{0,64},{64,128},{128,192},{192,0},{1,65},{65,129},{129,193},{193,1... | collective-permute-start | bytes 393224 | tf_op jit(solution)/shard_map/ppermute | solution.py:301
  60.0 7.5 %collective-permute-start.9 = (f32[256,128]{1,0:T(8,128)}, f32[256,128]{1,0:T(8,128)S(1)}, u32[]{:S(2)}, u32[]{:S(2)}) collective-permute-start(f32[256,128]{1,0:T(8,128)} %get-tuple-element.47), channel_id=1, source_target_pairs={{0,128},{64,192},{128,0},{192,64},{1,129},{65,193},{129,1},{193,65... | collective-permute-start | bytes 393224 | tf_op jit(solution)/shard_map/ppermute | solution.py:301
  92.5 7.2 %collective-permute-start.13 = (f32[256,128]{1,0:T(8,128)S(1)}, f32[256,128]{1,0:T(8,128)S(1)}, u32[]{:S(2)}, u32[]{:S(2)}) collective-permute-start(f32[256,128]{1,0:T(8,128)S(1)} %attend.1.refs_0_), channel_id=1, source_target_pairs={{0,4},{2,6},{4,8},{6,10},{8,12},{10,14},{12,0},{14,2},{1,5},{3,7},... | collective-permute-start | bytes 393224 | tf_op jit(solution)/shard_map/ppermute | solution.py:301
  94.8 9.9 %collective-permute-start.14 = (f32[256,128]{1,0:T(8,128)S(1)}, f32[256,128]{1,0:T(8,128)S(1)}, u32[]{:S(2)}, u32[]{:S(2)}) collective-permute-start(f32[256,128]{1,0:T(8,128)S(1)} %attend.1.refs_0_), channel_id=1, source_target_pairs={{0,12},{2,14},{4,0},{6,2},{8,4},{10,6},{12,8},{14,10},{1,13},{3,15... | collective-permute-start | bytes 393224 | tf_op jit(solution)/shard_map/ppermute | solution.py:301
  96.5 10.3 %collective-permute-start.11 = (f32[256,128]{1,0:T(8,128)S(1)}, f32[256,128]{1,0:T(8,128)S(1)}, u32[]{:S(2)}, u32[]{:S(2)}) collective-permute-start(f32[256,128]{1,0:T(8,128)S(1)} %attend.1.refs_0_), channel_id=1, source_target_pairs={{0,2},{2,4},{4,6},{6,8},{8,10},{10,12},{12,14},{14,0},{1,3},{3,5},... | collective-permute-start | bytes 393224 | tf_op jit(solution)/shard_map/ppermute | solution.py:301
  97.4 11.1 %collective-permute-start.12 = (f32[256,128]{1,0:T(8,128)S(1)}, f32[256,128]{1,0:T(8,128)S(1)}, u32[]{:S(2)}, u32[]{:S(2)}) collective-permute-start(f32[256,128]{1,0:T(8,128)S(1)} %attend.1.refs_0_), channel_id=1, source_target_pairs={{0,14},{2,0},{4,2},{6,4},{8,6},{10,8},{12,10},{14,12},{1,15},{3,1}... | collective-permute-start | bytes 393224 | tf_op jit(solution)/shard_map/ppermute | solution.py:301
  99.7 14.6 %collective-permute-start.15 = (f32[256,128]{1,0:T(8,128)S(1)}, f32[256,128]{1,0:T(8,128)S(1)}, u32[]{:S(2)}, u32[]{:S(2)}) collective-permute-start(f32[256,128]{1,0:T(8,128)S(1)} %collective-permute-done.13.refs_3_), channel_id=1, source_target_pairs={{0,2},{2,4},{4,6},{6,8},{8,10},{10,12},{12,14},{14,0},{1,3},{3,5},... | collective-permute-start | bytes 393224 | tf_op jit(solution)/shard_map/ppermute | solution.py:301
  104.7 9.6 %collective-permute-start.16 = (f32[256,128]{1,0:T(8,128)S(1)}, f32[256,128]{1,0:T(8,128)S(1)}, u32[]{:S(2)}, u32[]{:S(2)}) collective-permute-start(f32[256,128]{1,0:T(8,128)S(1)} %collective-permute-done.14.refs_4_), channel_id=1, source_target_pairs={{0,14},{2,0},{4,2},{6,4},{8,6},{10,8},{12,10},{14,12},{1,15},{3,1}... | collective-permute-start | bytes 393224 | tf_op jit(solution)/shard_map/ppermute | solution.py:301
  104.7 6.4 %collective-permute-start.17 = (f32[128,128]{1,0:T(8,128)S(1)}, f32[128,128]{1,0:T(8,128)S(1)}, u32[]{:S(2)}, u32[]{:S(2)}) collective-permute-start(f32[128,128]{1,0:T(8,128)S(1)} %slice.28), channel_id=1, source_target_pairs={{0,4},{2,6},{4,8},{6,10},{8,12},{10,14},{12,0},{14,2},{1,5},{3,7},... | collective-permute-start | bytes 196616 | tf_op jit(solution)/shard_map/ppermute | solution.py:301
  106.8 7.4 %collective-permute-start.18 = (f32[128,128]{1,0:T(8,128)S(1)}, f32[128,128]{1,0:T(8,128)S(1)}, u32[]{:S(2)}, u32[]{:S(2)}) collective-permute-start(f32[128,128]{1,0:T(8,128)S(1)} %slice.29), channel_id=1, source_target_pairs={{0,12},{2,14},{4,0},{6,2},{8,4},{10,6},{12,8},{14,10},{1,13},{3,15... | collective-permute-start | bytes 196616 | tf_op jit(solution)/shard_map/ppermute | solution.py:301
  125.8 9.0 %collective-permute-start.19 = (f32[2,64,512]{2,1,0:T(8,128)S(1)}, f32[2,64,512]{2,1,0:T(8,128)S(1)}, u32[]{:S(2)}, u32[]{:S(2)}) collective-permute-start(f32[2,64,512]{2,1,0:T(8,128)S(1)} %get-tuple-element.58), channel_id=1, source_target_pairs={{0,64},{64,128},{128,192},{192,0},{1,65},{65,129},{129,193},{193,1... | collective-permute-start | bytes 786440 | tf_op jit(solution)/shard_map/ppermute | solution.py:301
  127.1 14.2 %collective-permute-start.20 = (f32[2,64,512]{2,1,0:T(8,128)S(1)}, f32[2,64,512]{2,1,0:T(8,128)S(1)}, u32[]{:S(2)}, u32[]{:S(2)}) collective-permute-start(f32[2,64,512]{2,1,0:T(8,128)S(1)} %get-tuple-element.59), channel_id=1, source_target_pairs={{0,128},{64,192},{128,0},{192,64},{1,129},{65,193},{129,1},{193,65... | collective-permute-start | bytes 786440 | tf_op jit(solution)/shard_map/ppermute | solution.py:301
  129.5 11.8 %collective-permute-start.21 = (f32[2,64,512]{2,1,0:T(8,128)S(1)}, f32[2,64,512]{2,1,0:T(8,128)S(1)}, u32[]{:S(2)}, u32[]{:S(2)}) collective-permute-start(f32[2,64,512]{2,1,0:T(8,128)S(1)} %get-tuple-element.60), channel_id=1, source_target_pairs={{0,192},{64,0},{128,64},{192,128},{1,193},{65,1},{129,65},{193,129... | collective-permute-start | bytes 786440 | tf_op jit(solution)/shard_map/ppermute | solution.py:301
  (15 other events, 267.7 us)
Sparse Core Ops, SparseCore 0:
  9.2 38.9 all-gather.6
  50.0 34.6 all-gather.8
  86.6 34.6 all-gather.10

commit v17 on v16

--- a/solution.py
+++ b/solution.py
@@ -145,7 +145,7 @@
             pltpu.VMEM((NX, NX * BLOCK, HD), jnp.float32),
             pltpu.SemaphoreType.DMA((NY, NX + 1)),
         ],
-        compiler_params=pltpu.CompilerParams(vmem_limit_bytes=LIMIT),
+        compiler_params=pltpu.CompilerParams(vmem_limit_bytes=48 << 20),
         cost_estimate=pl.CostEstimate(
             flops=6 * 256 * 2048 * 512, bytes_accessed=7 << 20, transcendentals=0
         ),
@@ -345,7 +345,7 @@
     )
     partial = project(where, hidden_rows, hidden, weights)
     partial = [partial[0]] + [along("x", partial[s], s) for s in range(1, NX)]
-    rows, partial, low, up = lax.optimization_barrier((rows, partial, low, up))
+    rows, partial = lax.optimization_barrier((rows, partial))
     rows = lax.all_to_all(rows.reshape(NZ, NK, 16, 512), "z", 0, 0)
     out_weight = lax.all_gather(rows, ("y", "k"), axis=0)
     own = attend(partial, low, up, kv)

time: 151 us -> 151 us (level)
  blocking collectives: 16.4 us -> 20 us
    ppermute x20, waiting for transfers between devices: 29.3 us -> 25.3 us  [along(): lax.ppermute(value, axis, [(i, (i + shift) % count) for i in range(count)])]
    all_to_all x1, blocking collectives: 16.4 us -> 20 us  [shards(): rows = lax.all_to_all(rows.reshape(NZ, NK, 16, 512), 'z', 0, 0)]
    all_gather x1, waiting for transfers between devices: 7.02 us -> 9.16 us  [shards(): out_weight = lax.all_gather(rows, ('y', 'k'), axis=0)]
    unnamed x28 -> x20, local copies, waits for them, and re-layouts: 4.76 us -> 3.87 us
where the time goes in v17:
time: 151 us
  waiting for transfers between devices  44.4 us (29%)
  starting transfers between devices  43.4 us (29%)
  blocking collectives  20 us (13%)
  Pallas kernels  18.8 us (12%)
  between operations  13.4 us (9%)
  local copies, waits for them, and re-layouts  5.62 us (4%)
  other arithmetic  5.14 us (3%)
    ppermute x20, starting transfers between devices, along(): lax.ppermute(value, axis, [(i, (i + shift) % count) for i in range(count)])  36.3 us
    ppermute x20, waiting for transfers between devices, along(): lax.ppermute(value, axis, [(i, (i + shift) % count) for i in range(count)])  25.3 us
    all_to_all x1, blocking collectives, shards(): rows = lax.all_to_all(rows.reshape(NZ, NK, 16, 512), 'z', 0, 0)  20 us
    all_gather x1, waiting for transfers between devices, shards(): out_weight = lax.all_gather(rows, ('y', 'k'), axis=0)  9.16 us
    ppermute x1, waiting for transfers between devices, shards(): lax.ppermute(near, 'z', [(i, i ^ 1) for i in range(NZ)])  6.82 us
    all_to_all x1, starting transfers between devices, shards(): rows = lax.all_to_all(rows.reshape(NX * NY, 16, 512), ('x', 'y'), 0, 0)  5.32 us
    pallas_call x1, Pallas kernels, attend(): pl.pallas_call(attend_kernel, out_shape=jax.ShapeDtypeStruct((rows, HD),...  4.64 us
    pallas_call x1, Pallas kernels, mix(): pl.pallas_call(mix_kernel, out_shape=[jax.ShapeDtypeStruct((NK, BLOCK, 51...  4.52 us
  transfers between devices with their start and end apart: 27, of which 14 were waited for; matrix products, arithmetic and copies ran while one was open for 5% of the time, Pallas kernels for 10%

profile of v17, /device:TPU:1, one launch (start us, length us, event | category | flops | bytes accessed | tf_op | source)
XLA Modules:
  0.0 150.8 jit_solution(17629311734326787392)
XLA Ops:
  7.9 3.2 %pick.1 = (f32[64,2048]{1,0:T(8,128)}, f32[64,2048]{1,0:T(8,128)}, f32[64,2048]{1,0:T(8,128)}) custom-call(s32[4]{0:T(128)} %pad_add_fusion.where, f32[128,8192]{1,0:T(8,128)} %rows.3), custom_call_target="tpu_custom_call" | custom-call | tf_op jit(solution)/shard_map/pick/pallas_call | solution.py:55
  13.3 2.5 %collective-permute-start.6 = (f32[64,2048]{1,0:T(8,128)}, f32[64,2048]{1,0:T(8,128)S(1)}, u32[]{:S(2)}, u32[]{:S(2)}) collective-permute-start(f32[64,2048]{1,0:T(8,128)} %get-tuple-element.32), channel_id=1, source_target_pairs={{0,128},{64,192},{128,0},{192,64},{1,129},{65,193},{129,1},{193,65... | collective-permute-start | bytes 1572872 | tf_op jit(solution)/shard_map/ppermute | solution.py:301
  15.7 2.3 %pick_keys.1 = (f32[2,64,128]{2,1,0:T(8,128)}, f32[2,64,128]{2,1,0:T(8,128)}, f32[2,64,128]{2,1,0:T(8,128)}, f32[2,64,128]{2,1,0:T(8,128)}) custom-call(s32[4]{0:T(128)} %pad_add_fusion.where, f32[256,512]{1,0:T(8,128)} %keys.1, f32[256,512]{1,0:T(8,128)} %values.1), custom_call_target="tpu_custom_call" | custom-call | bytes 67108864 | tf_op jit(solution)/shard_map/pick_keys/pallas_call | solution.py:87
  18.0 7.0 %collective-permute-start.2 = (f32[2,64,128]{2,1,0:T(8,128)}, f32[2,64,128]{2,1,0:T(8,128)S(1)}, u32[]{:S(2)}, u32[]{:S(2)}) collective-permute-start(f32[2,64,128]{2,1,0:T(8,128)} %get-tuple-element.37), channel_id=1, source_target_pairs={{0,8},{2,10},{4,12},{6,14},{8,0},{10,2},{12,4},{14,6},{1,9},{3,11}... | collective-permute-start | bytes 196616 | tf_op jit(solution)/shard_map/ppermute | solution.py:301
  25.0 2.4 %collective-permute-start.1 = (f32[2,64,128]{2,1,0:T(8,128)}, f32[2,64,128]{2,1,0:T(8,128)S(1)}, u32[]{:S(2)}, u32[]{:S(2)}) collective-permute-start(f32[2,64,128]{2,1,0:T(8,128)} %get-tuple-element.36), channel_id=1, source_target_pairs={{0,4},{2,6},{4,8},{6,10},{8,12},{10,14},{12,0},{14,2},{1,5},{3,7},... | collective-permute-start | bytes 196616 | tf_op jit(solution)/shard_map/ppermute | solution.py:301
  29.6 3.5 %collective-permute-done.3 = f32[2,64,128]{2,1,0:T(8,128)S(1)} collective-permute-done((f32[2,64,128]{2,1,0:T(8,128)}, f32[2,64,128]{2,1,0:T(8,128)S(1)}, u32[]{:S(2)}, u32[]{:S(2)}) %collective-permute-start.3) | collective-permute-done | bytes 65568 | tf_op jit(solution)/shard_map/ppermute | solution.py:301
  35.5 6.8 %collective-permute-done.4 = f32[4,2,64,128]{3,2,1,0:T(8,128)S(1)} collective-permute-done((f32[4,2,64,128]{3,2,1,0:T(8,128)S(1)}, f32[4,2,64,128]{3,2,1,0:T(8,128)S(1)}, u32[]{:S(2)}, u32[]{:S(2)}) %collective-permute-start.4) | collective-permute-done | bytes 262176 | tf_op jit(solution)/shard_map/ppermute | solution.py:323
  43.2 5.3 %all-to-all-start = ((f32[16,16,512]{2,1,0:T(8,128)}), f32[16,16,512]{2,1,0:T(8,128)S(1)}, u32[]{:S(2)}, u32[]{:S(2)}) async-start(f32[16,16,512]{2,1,0:T(8,128)} %bitcast.12), calls=%async_computation | async-start | bytes 1048576 | tf_op jit(solution)/shard_map/all_to_all | solution.py:330
  48.6 4.2 %project.1 = (f32[256,128]{1,0:T(8,128)S(1)}, f32[256,128]{1,0:T(8,128)S(1)}, f32[256,128]{1,0:T(8,128)S(1)}, f32[256,128]{1,0:T(8,128)S(1)}) custom-call(s32[4]{0:T(128)S(1)} %copy-done, f32[128,8192]{1,0:T(8,128)} %rows.3, f32[64,2048]{1,0:T(8,128)S(1)} %collective-permute-done.5.first, f32[64,2048]{1,0:T(8,128)S(1)} %collective-permute-done.6.second, ...), custom_call_target="tpu_custom_call" | custom-call | flops 1610612736 | bytes 7340032 | tf_op jit(solution)/shard_map/project/pallas_call | solution.py:137
  52.8 2.7 %collective-permute-start.10 = (f32[256,128]{1,0:T(8,128)S(1)}, f32[256,128]{1,0:T(8,128)S(1)}, u32[]{:S(2)}, u32[]{:S(2)}) collective-permute-start(f32[256,128]{1,0:T(8,128)S(1)} %get-tuple-element.46), channel_id=1, source_target_pairs={{0,192},{64,0},{128,64},{192,128},{1,193},{65,1},{129,65},{193,129... | collective-permute-start | bytes 393224 | tf_op jit(solution)/shard_map/ppermute | solution.py:301
  58.5 4.1 %collective-permute-done.8.second = f32[256,128]{1,0:T(8,128)S(1)} collective-permute-done((f32[256,128]{1,0:T(8,128)S(1)}, f32[256,128]{1,0:T(8,128)S(1)}, u32[]{:S(2)}, u32[]{:S(2)}) %collective-permute-start.8) | collective-permute-done | bytes 131104 | tf_op jit(solution)/shard_map/ppermute | solution.py:301
  62.6 20.0 %all_to_all.10 = f32[8,2,16,512]{3,2,1,0:T(8,128)} all-to-all(f32[8,2,16,512]{3,2,1,0:T(8,128)S(1)} %bitcast.44), channel_id=1, replica_groups=mesh['x'=4,'y'=4,'z'=8,'k'=2] {'z'}, dimensions={0} | all-to-all | bytes 1048576 | tf_op jit(solution)/shard_map/all_to_all | solution.py:349
  86.4 2.2 %copy-done.1 = f32[64,2,64,128]{3,2,1,0:T(8,128)S(1)} copy-done((f32[64,2,64,128]{3,2,1,0:T(8,128)S(1)}, f32[64,2,64,128]{3,2,1,0:T(8,128)}, u32[]{:S(2)}) %copy-start.1) | copy-done | bytes 4194328
  88.6 4.6 %attend.1.refs_0_ = f32[256,128]{1,0:T(8,128)S(1)} custom-call(f32[256,128]{1,0:T(8,128)S(1)} %get-tuple-element.47.first, f32[256,128]{1,0:T(8,128)S(1)} %collective-permute-done.8.second, f32[256,128]{1,0:T(8,128)S(1)} %collective-permute-done.9.third, f32[256,128]{1,0:T(8,128)S(1)} %collective-permute-done.10.fourth, f32[4,4096]{1,0:T(4,128)S(1)} %broadcast_in_dim.39.low, ...), custom_call_target="tpu_custom_call" | custom-call | flops 1610612736 | bytes 6291456 | tf_op jit(solution)/shard_map/attend/pallas_call | solution.py:203
  93.9 3.0 %collective-permute-start.14 = (f32[256,128]{1,0:T(8,128)S(1)}, f32[256,128]{1,0:T(8,128)S(1)}, u32[]{:S(2)}, u32[]{:S(2)}) collective-permute-start(f32[256,128]{1,0:T(8,128)S(1)} %attend.1.refs_0_), channel_id=1, source_target_pairs={{0,12},{2,14},{4,0},{6,2},{8,4},{10,6},{12,8},{14,10},{1,13},{3,15... | collective-permute-start | bytes 393224 | tf_op jit(solution)/shard_map/ppermute | solution.py:301
  96.9 2.7 %collective-permute-start.12 = (f32[256,128]{1,0:T(8,128)S(1)}, f32[256,128]{1,0:T(8,128)S(1)}, u32[]{:S(2)}, u32[]{:S(2)}) collective-permute-start(f32[256,128]{1,0:T(8,128)S(1)} %attend.1.refs_0_), channel_id=1, source_target_pairs={{0,14},{2,0},{4,2},{6,4},{8,6},{10,8},{12,10},{14,12},{1,15},{3,1}... | collective-permute-start | bytes 393224 | tf_op jit(solution)/shard_map/ppermute | solution.py:301
  104.3 2.5 %collective-permute-start.18 = (f32[128,128]{1,0:T(8,128)S(1)}, f32[128,128]{1,0:T(8,128)S(1)}, u32[]{:S(2)}, u32[]{:S(2)}) collective-permute-start(f32[128,128]{1,0:T(8,128)S(1)} %slice.29), channel_id=1, source_target_pairs={{0,12},{2,14},{4,0},{6,2},{8,4},{10,6},{12,8},{14,10},{1,13},{3,15... | collective-permute-start | bytes 196616 | tf_op jit(solution)/shard_map/ppermute | solution.py:301
  106.8 2.8 %collective-permute-done.17.refs_7_ = f32[128,128]{1,0:T(8,128)S(1)} collective-permute-done((f32[128,128]{1,0:T(8,128)S(1)}, f32[128,128]{1,0:T(8,128)S(1)}, u32[]{:S(2)}, u32[]{:S(2)}) %collective-permute-start.17) | collective-permute-done | bytes 65568 | tf_op jit(solution)/shard_map/ppermute | solution.py:301
  109.6 2.5 %collective-permute-done.18.refs_8_ = f32[128,128]{1,0:T(8,128)S(1)} collective-permute-done((f32[128,128]{1,0:T(8,128)S(1)}, f32[128,128]{1,0:T(8,128)S(1)}, u32[]{:S(2)}, u32[]{:S(2)}) %collective-permute-start.18) | collective-permute-done | bytes 65568 | tf_op jit(solution)/shard_map/ppermute | solution.py:301
  112.1 9.2 %all-gather.11.cloned.1.call-done = f32[64,2,16,512]{3,2,1,0:T(8,128)} async-done(((f32[8,2,16,512]{3,2,1,0:T(8,128)}), f32[64,2,16,512]{3,2,1,0:T(8,128)}) %all-gather.11.cloned.1.call-update) | async-done | bytes 4194320 | tf_op jit(solution)/shard_map/all_gather | solution.py:350
  121.3 4.5 %mix.1 = (f32[2,64,512]{2,1,0:T(8,128)S(1)}, f32[2,64,512]{2,1,0:T(8,128)S(1)}, f32[2,64,512]{2,1,0:T(8,128)S(1)}, f32[2,64,512]{2,1,0:T(8,128)S(1)}) custom-call(s32[4]{0:T(128)S(1)} %copy-done, f32[256,128]{1,0:T(8,128)S(1)} %attend.1.refs_0_, f32[256,128]{1,0:T(8,128)S(1)} %collective-permute-done.11.refs_1_, ...), custom_call_target="tpu_custom_call" | custom-call | flops 1610612736 | bytes 6291456 | tf_op jit(solution)/shard_map/mix/pallas_call | solution.py:261
  127.1 2.4 %collective-permute-start.20 = (f32[2,64,512]{2,1,0:T(8,128)S(1)}, f32[2,64,512]{2,1,0:T(8,128)S(1)}, u32[]{:S(2)}, u32[]{:S(2)}) collective-permute-start(f32[2,64,512]{2,1,0:T(8,128)S(1)} %get-tuple-element.55), channel_id=1, source_target_pairs={{0,128},{64,192},{128,0},{192,64},{1,129},{65,193},{129,1},{193,65... | collective-permute-start | bytes 786440 | tf_op jit(solution)/shard_map/ppermute | solution.py:301
  130.7 4.1 %collective-permute-done.19 = f32[2,64,512]{2,1,0:T(8,128)S(1)} collective-permute-done((f32[2,64,512]{2,1,0:T(8,128)S(1)}, f32[2,64,512]{2,1,0:T(8,128)S(1)}, u32[]{:S(2)}, u32[]{:S(2)}) %collective-permute-start.19) | collective-permute-done | bytes 262176 | tf_op jit(solution)/shard_map/ppermute | solution.py:301
  134.8 6.5 %collective-permute-done.20 = f32[2,64,512]{2,1,0:T(8,128)S(1)} collective-permute-done((f32[2,64,512]{2,1,0:T(8,128)S(1)}, f32[2,64,512]{2,1,0:T(8,128)S(1)}, u32[]{:S(2)}, u32[]{:S(2)}) %collective-permute-start.20) | collective-permute-done | bytes 262176 | tf_op jit(solution)/shard_map/ppermute | solution.py:301
  (91 shorter events, 26.5 us)
Async XLA Ops:
  6.5 42.0 %all-gather.7.cloned.1.call-start = ((), (), s32[]{:S(2)}) async-start(), calls=%async_computation.2 | async-start | bytes 4718592 | tf_op jit(solution)/shard_map/all_gather | solution.py:317
  7.3 79.1 %all-gather.9.cloned.1.call-start = ((), (), s32[]{:S(2)}) async-start(), calls=%async_computation.3 | async-start | bytes 4718592 | tf_op jit(solution)/shard_map/all_gather | solution.py:331
  11.1 31.2 %collective-permute-start.5 = (f32[64,2048]{1,0:T(8,128)}, f32[64,2048]{1,0:T(8,128)S(1)}, u32[]{:S(2)}, u32[]{:S(2)}) collective-permute-start(f32[64,2048]{1,0:T(8,128)} %get-tuple-element.31), channel_id=1, source_target_pairs={{0,64},{64,128},{128,192},{192,0},{1,65},{65,129},{129,193},{193,1... | collective-permute-start | bytes 1572872 | tf_op jit(solution)/shard_map/ppermute | solution.py:301
  13.3 29.1 %collective-permute-start.6 = (f32[64,2048]{1,0:T(8,128)}, f32[64,2048]{1,0:T(8,128)S(1)}, u32[]{:S(2)}, u32[]{:S(2)}) collective-permute-start(f32[64,2048]{1,0:T(8,128)} %get-tuple-element.32), channel_id=1, source_target_pairs={{0,128},{64,192},{128,0},{192,64},{1,129},{65,193},{129,1},{193,65... | collective-permute-start | bytes 1572872 | tf_op jit(solution)/shard_map/ppermute | solution.py:301
  18.0 10.3 %collective-permute-start.2 = (f32[2,64,128]{2,1,0:T(8,128)}, f32[2,64,128]{2,1,0:T(8,128)S(1)}, u32[]{:S(2)}, u32[]{:S(2)}) collective-permute-start(f32[2,64,128]{2,1,0:T(8,128)} %get-tuple-element.37), channel_id=1, source_target_pairs={{0,8},{2,10},{4,12},{6,14},{8,0},{10,2},{12,4},{14,6},{1,9},{3,11}... | collective-permute-start | bytes 196616 | tf_op jit(solution)/shard_map/ppermute | solution.py:301
  25.0 8.0 %collective-permute-start.3 = (f32[2,64,128]{2,1,0:T(8,128)}, f32[2,64,128]{2,1,0:T(8,128)S(1)}, u32[]{:S(2)}, u32[]{:S(2)}) collective-permute-start(f32[2,64,128]{2,1,0:T(8,128)} %get-tuple-element.38), channel_id=1, source_target_pairs={{0,12},{2,14},{4,0},{6,2},{8,4},{10,6},{12,8},{14,10},{1,13},{3,15... | collective-permute-start | bytes 196616 | tf_op jit(solution)/shard_map/ppermute | solution.py:301
  25.0 8.4 %collective-permute-start.1 = (f32[2,64,128]{2,1,0:T(8,128)}, f32[2,64,128]{2,1,0:T(8,128)S(1)}, u32[]{:S(2)}, u32[]{:S(2)}) collective-permute-start(f32[2,64,128]{2,1,0:T(8,128)} %get-tuple-element.36), channel_id=1, source_target_pairs={{0,4},{2,6},{4,8},{6,10},{8,12},{10,14},{12,0},{14,2},{1,5},{3,7},... | collective-permute-start | bytes 196616 | tf_op jit(solution)/shard_map/ppermute | solution.py:301
  28.3 14.0 %collective-permute-start.7 = (f32[64,2048]{1,0:T(8,128)}, f32[64,2048]{1,0:T(8,128)S(1)}, u32[]{:S(2)}, u32[]{:S(2)}) collective-permute-start(f32[64,2048]{1,0:T(8,128)} %get-tuple-element.33), channel_id=1, source_target_pairs={{0,192},{64,0},{128,64},{192,128},{1,193},{65,1},{129,65},{193,129... | collective-permute-start | bytes 1572872 | tf_op jit(solution)/shard_map/ppermute | solution.py:301
  34.3 8.0 %collective-permute-start.4 = (f32[4,2,64,128]{3,2,1,0:T(8,128)S(1)}, f32[4,2,64,128]{3,2,1,0:T(8,128)S(1)}, u32[]{:S(2)}, u32[]{:S(2)}) collective-permute-start(f32[4,2,64,128]{3,2,1,0:T(8,128)S(1)} %pad_maximum_fusion), channel_id=1, source_target_pairs={{0,2},{2,0},{4,6},{6,4},{8,10},{10,8},{12,14},{14,12},{1,3},{3,1},... | collective-permute-start | bytes 786440 | tf_op jit(solution)/shard_map/ppermute | solution.py:323
  43.2 15.2 %all-to-all-start = ((f32[16,16,512]{2,1,0:T(8,128)}), f32[16,16,512]{2,1,0:T(8,128)S(1)}, u32[]{:S(2)}, u32[]{:S(2)}) async-start(f32[16,16,512]{2,1,0:T(8,128)} %bitcast.12), calls=%async_computation | async-start | bytes 1048576 | tf_op jit(solution)/shard_map/all_to_all | solution.py:330
  48.5 72.8 %all-gather.11.cloned.1.call-start = ((), (), s32[]{:S(2)}) async-start(), calls=%async_computation.4 | async-start | bytes 4718592 | tf_op jit(solution)/shard_map/all_gather | solution.py:350
  55.5 7.2 %collective-permute-start.8 = (f32[256,128]{1,0:T(8,128)S(1)}, f32[256,128]{1,0:T(8,128)S(1)}, u32[]{:S(2)}, u32[]{:S(2)}) collective-permute-start(f32[256,128]{1,0:T(8,128)S(1)} %get-tuple-element.44), channel_id=1, source_target_pairs={{0,64},{64,128},{128,192},{192,0},{1,65},{65,129},{129,193},{193,1... | collective-permute-start | bytes 393224 | tf_op jit(solution)/shard_map/ppermute | solution.py:301
  55.5 7.2 %collective-permute-start.9 = (f32[256,128]{1,0:T(8,128)S(1)}, f32[256,128]{1,0:T(8,128)S(1)}, u32[]{:S(2)}, u32[]{:S(2)}) collective-permute-start(f32[256,128]{1,0:T(8,128)S(1)} %get-tuple-element.45), channel_id=1, source_target_pairs={{0,128},{64,192},{128,0},{192,64},{1,129},{65,193},{129,1},{193,65... | collective-permute-start | bytes 393224 | tf_op jit(solution)/shard_map/ppermute | solution.py:301
  93.2 7.2 %collective-permute-start.13 = (f32[256,128]{1,0:T(8,128)S(1)}, f32[256,128]{1,0:T(8,128)S(1)}, u32[]{:S(2)}, u32[]{:S(2)}) collective-permute-start(f32[256,128]{1,0:T(8,128)S(1)} %attend.1.refs_0_), channel_id=1, source_target_pairs={{0,4},{2,6},{4,8},{6,10},{8,12},{10,14},{12,0},{14,2},{1,5},{3,7},... | collective-permute-start | bytes 393224 | tf_op jit(solution)/shard_map/ppermute | solution.py:301
  93.9 7.3 %collective-permute-start.14 = (f32[256,128]{1,0:T(8,128)S(1)}, f32[256,128]{1,0:T(8,128)S(1)}, u32[]{:S(2)}, u32[]{:S(2)}) collective-permute-start(f32[256,128]{1,0:T(8,128)S(1)} %attend.1.refs_0_), channel_id=1, source_target_pairs={{0,12},{2,14},{4,0},{6,2},{8,4},{10,6},{12,8},{14,10},{1,13},{3,15... | collective-permute-start | bytes 393224 | tf_op jit(solution)/shard_map/ppermute | solution.py:301
  96.9 7.4 %collective-permute-start.11 = (f32[256,128]{1,0:T(8,128)S(1)}, f32[256,128]{1,0:T(8,128)S(1)}, u32[]{:S(2)}, u32[]{:S(2)}) collective-permute-start(f32[256,128]{1,0:T(8,128)S(1)} %attend.1.refs_0_), channel_id=1, source_target_pairs={{0,2},{2,4},{4,6},{6,8},{8,10},{10,12},{12,14},{14,0},{1,3},{3,5},... | collective-permute-start | bytes 393224 | tf_op jit(solution)/shard_map/ppermute | solution.py:301
  96.9 9.9 %collective-permute-start.12 = (f32[256,128]{1,0:T(8,128)S(1)}, f32[256,128]{1,0:T(8,128)S(1)}, u32[]{:S(2)}, u32[]{:S(2)}) collective-permute-start(f32[256,128]{1,0:T(8,128)S(1)} %attend.1.refs_0_), channel_id=1, source_target_pairs={{0,14},{2,0},{4,2},{6,4},{8,6},{10,8},{12,10},{14,12},{1,15},{3,1}... | collective-permute-start | bytes 393224 | tf_op jit(solution)/shard_map/ppermute | solution.py:301
  100.4 11.7 %collective-permute-start.15 = (f32[256,128]{1,0:T(8,128)S(1)}, f32[256,128]{1,0:T(8,128)S(1)}, u32[]{:S(2)}, u32[]{:S(2)}) collective-permute-start(f32[256,128]{1,0:T(8,128)S(1)} %collective-permute-done.13.refs_3_), channel_id=1, source_target_pairs={{0,2},{2,4},{4,6},{6,8},{8,10},{10,12},{12,14},{14,0},{1,3},{3,5},... | collective-permute-start | bytes 393224 | tf_op jit(solution)/shard_map/ppermute | solution.py:301
  101.2 10.9 %collective-permute-start.16 = (f32[256,128]{1,0:T(8,128)S(1)}, f32[256,128]{1,0:T(8,128)S(1)}, u32[]{:S(2)}, u32[]{:S(2)}) collective-permute-start(f32[256,128]{1,0:T(8,128)S(1)} %collective-permute-done.14.refs_4_), channel_id=1, source_target_pairs={{0,14},{2,0},{4,2},{6,4},{8,6},{10,8},{12,10},{14,12},{1,15},{3,1}... | collective-permute-start | bytes 393224 | tf_op jit(solution)/shard_map/ppermute | solution.py:301
  103.1 6.5 %collective-permute-start.17 = (f32[128,128]{1,0:T(8,128)S(1)}, f32[128,128]{1,0:T(8,128)S(1)}, u32[]{:S(2)}, u32[]{:S(2)}) collective-permute-start(f32[128,128]{1,0:T(8,128)S(1)} %slice.28), channel_id=1, source_target_pairs={{0,4},{2,6},{4,8},{6,10},{8,12},{10,14},{12,0},{14,2},{1,5},{3,7},... | collective-permute-start | bytes 196616 | tf_op jit(solution)/shard_map/ppermute | solution.py:301
  104.3 7.9 %collective-permute-start.18 = (f32[128,128]{1,0:T(8,128)S(1)}, f32[128,128]{1,0:T(8,128)S(1)}, u32[]{:S(2)}, u32[]{:S(2)}) collective-permute-start(f32[128,128]{1,0:T(8,128)S(1)} %slice.29), channel_id=1, source_target_pairs={{0,12},{2,14},{4,0},{6,2},{8,4},{10,6},{12,8},{14,10},{1,13},{3,15... | collective-permute-start | bytes 196616 | tf_op jit(solution)/shard_map/ppermute | solution.py:301
  125.8 8.9 %collective-permute-start.19 = (f32[2,64,512]{2,1,0:T(8,128)S(1)}, f32[2,64,512]{2,1,0:T(8,128)S(1)}, u32[]{:S(2)}, u32[]{:S(2)}) collective-permute-start(f32[2,64,512]{2,1,0:T(8,128)S(1)} %get-tuple-element.54), channel_id=1, source_target_pairs={{0,64},{64,128},{128,192},{192,0},{1,65},{65,129},{129,193},{193,1... | collective-permute-start | bytes 786440 | tf_op jit(solution)/shard_map/ppermute | solution.py:301
  127.1 14.2 %collective-permute-start.20 = (f32[2,64,512]{2,1,0:T(8,128)S(1)}, f32[2,64,512]{2,1,0:T(8,128)S(1)}, u32[]{:S(2)}, u32[]{:S(2)}) collective-permute-start(f32[2,64,512]{2,1,0:T(8,128)S(1)} %get-tuple-element.55), channel_id=1, source_target_pairs={{0,128},{64,192},{128,0},{192,64},{1,129},{65,193},{129,1},{193,65... | collective-permute-start | bytes 786440 | tf_op jit(solution)/shard_map/ppermute | solution.py:301
  129.5 11.8 %collective-permute-start.21 = (f32[2,64,512]{2,1,0:T(8,128)S(1)}, f32[2,64,512]{2,1,0:T(8,128)S(1)}, u32[]{:S(2)}, u32[]{:S(2)}) collective-permute-start(f32[2,64,512]{2,1,0:T(8,128)S(1)} %get-tuple-element.56), channel_id=1, source_target_pairs={{0,192},{64,0},{128,64},{192,128},{1,193},{65,1},{129,65},{193,129... | collective-permute-start | bytes 786440 | tf_op jit(solution)/shard_map/ppermute | solution.py:301
  (11 other events, 211.2 us)
Sparse Core Ops, SparseCore 0:
  9.2 38.8 all-gather.6
  50.0 34.6 all-gather.8
  86.6 34.6 all-gather.10

commit v18 on v17

--- a/solution.py
+++ b/solution.py
@@ -222,58 +222,62 @@
 
 
 def mix_kernel(where, *refs):
-    heads, weights, outs = refs[:9], refs[9], refs[10 : 10 + NX]
-    total_buf, buf, sems = refs[10 + NX :]
+    own, other, weights, outs = refs[:9], refs[9:18], refs[18], refs[19 : 19 + NX]
+    total_buf, buf, sems = refs[19 + NX :]
     places = [lax.rem(where[3] + offset + NZ, NZ) for offset in OFFSETS]
     copies = [
         [
             pltpu.make_async_copy(
-                weights.at[part, spot], buf.at[index, :, pl.ds(16 * part, 16)], sems.at[index, part]
+                weights.at[y, pl.ds(2 * spot, 2)], buf.at[index, y], sems.at[index, y]
             )
-            for part in range(8)
+            for y in range(NY)
         ]
         for index, spot in enumerate(places)
     ]
     for group in copies:
         for copy in group:
             copy.start()
-    blocks = [head[...] for head in heads[:7]]
-    blocks.append(jnp.concatenate([heads[7][...], heads[8][...]], axis=0))
+    blocks = [
+        [head[...] for head in heads[:7]]
+        + [jnp.concatenate([heads[7][...], heads[8][...]], axis=0)]
+        for heads in (own, other)
+    ]
     totals = [None, None]
     for step in range(NZ // 2):
         pair = (2 * step, 2 * step + 1)
-        left = split(jnp.concatenate([blocks[index] for index in pair], axis=1))
         for index in pair:
             for copy in copies[index]:
                 copy.wait()
-        for core in range(NK):
-            right = jnp.concatenate([buf[index, core] for index in pair], axis=0)
-            term = dot3(left, split(right), MM)
-            totals[core] = term if totals[core] is None else totals[core] + term
-    for core in range(NK):
+        right = split(jnp.concatenate([buf[index].reshape(HD, 512) for index in pair], axis=0))
+        for side in range(2):
+            left = split(jnp.concatenate([blocks[side][index] for index in pair], axis=1))
+            term = dot3(left, right, MM)
+            totals[side] = term if totals[side] is None else totals[side] + term
+    for side in range(2):
+        core = where[2] if side == 0 else 1 - where[2]
         for x in range(NX):
-            total_buf[x, core] = totals[core][x * BLOCK : (x + 1) * BLOCK]
+            total_buf[x, core] = totals[side][x * BLOCK : (x + 1) * BLOCK]
     for shift in range(NX):
         outs[shift][...] = total_buf[lax.rem(where[0] + shift, NX)]
 
 
-def mix(where, heads, weights):
+def mix(where, own, other, weights):
     return pl.pallas_call(
         mix_kernel,
         out_shape=[jax.ShapeDtypeStruct((NK, BLOCK, 512), jnp.float32)] * NX,
-        in_specs=[SMEM] + [VMEM] * 9 + [ANY],
+        in_specs=[SMEM] + [VMEM] * 18 + [ANY],
         out_specs=[VMEM] * NX,
         scratch_shapes=[
             pltpu.VMEM((NX, NK, BLOCK, 512), jnp.float32),
-            pltpu.VMEM((NZ, NK, HD, 512), jnp.float32),
-            pltpu.SemaphoreType.DMA((NZ, 8)),
+            pltpu.VMEM((NZ, NY, 2, 16, 512), jnp.float32),
+            pltpu.SemaphoreType.DMA((NZ, NY)),
         ],
-        compiler_params=pltpu.CompilerParams(vmem_limit_bytes=48 << 20),
+        compiler_params=pltpu.CompilerParams(vmem_limit_bytes=50 << 20),
         cost_estimate=pl.CostEstimate(
             flops=6 * 256 * 1024 * 1024, bytes_accessed=6 << 20, transcendentals=0
         ),
         name="mix",
-    )(where, *heads, weights)
+    )(where, *own, *other, weights)
 
 
 def allowed_rows(
@@ -346,24 +350,18 @@
     partial = project(where, hidden_rows, hidden, weights)
     partial = [partial[0]] + [along("x", partial[s], s) for s in range(1, NX)]
     rows, partial = lax.optimization_barrier((rows, partial))
-    rows = lax.all_to_all(rows.reshape(NZ, NK, 16, 512), "z", 0, 0)
-    out_weight = lax.all_gather(rows, ("y", "k"), axis=0)
+    rows = lax.all_to_all(rows, ("z", "k"), 0, 0)
+    out_weight = lax.all_gather(rows, "y", axis=0)
     own = attend(partial, low, up, kv)
     near_up, near_down = along("z", own, 1), along("z", own, -1)
     far_up, far_down = along("z", own, 2), along("z", own, -2)
     heads = [own, near_up, near_down, far_up, far_down]
     heads += [along("z", far_up, 1), along("z", far_down, -1)]
     heads += [along("z", far_up[:128], 2), along("z", far_down[128:], -2)]
-    mixed = mix(where, heads, out_weight)
+    swapped = [lax.ppermute(head, "k", CORES) for head in heads]
+    mixed = mix(where, heads, swapped, out_weight)
     mixed = [mixed[0]] + [along("x", mixed[s], s) for s in range(1, NX)]
-    first, second = (
-        sum(lax.dynamic_index_in_dim(part, core, 0, keepdims=False) for part in mixed)
-        for core in (1 - k, k)
-    )
-    other = lax.ppermute(first, "k", CORES)
-    return jnp.concatenate(
-        [jnp.where(k == 0, second, other), jnp.where(k == 0, other, second)]
-    )
+    return ((mixed[0] + mixed[1]) + (mixed[2] + mixed[3])).reshape(NK * BLOCK, 512)
 
 
 def solution(mesh):

time: 151 us -> 149 us (0.987)
  waiting for transfers between devices: 44.4 us -> 32.7 us
  blocking collectives: 20 us -> 26.3 us
  starting transfers between devices: 43.4 us -> 47.2 us
    all_gather x1, waiting for transfers between devices: 9.16 us -> 0.01 us  [shards(): out_weight = lax.all_gather(rows, 'y', axis=0)]
    all_to_all x1, blocking collectives: 20 us -> 26.3 us  [shards(): rows = lax.all_to_all(rows, ('z', 'k'), 0, 0)]
    ppermute x1 -> x9, starting transfers between devices: 1.17 us -> 6.69 us  [shards(): swapped = [lax.ppermute(head, 'k', CORES) for head in heads]]
    ppermute x20, waiting for transfers between devices: 25.3 us -> 22.3 us  [along(): lax.ppermute(value, axis, [(i, (i + shift) % count) for i in range(count)])]
    ppermute x20, starting transfers between devices: 36.3 us -> 34.6 us  [along(): lax.ppermute(value, axis, [(i, (i + shift) % count) for i in range(count)])]
  transfers between devices with their start and end apart: 27 -> 35, of which waited for: 14 -> 14; matrix products, arithmetic and copies ran while one was open for 5% -> 5% of each run, Pallas kernels for 10% -> 10%
where the time goes in v18:
time: 149 us
  starting transfers between devices  47.2 us (32%)
  waiting for transfers between devices  32.7 us (22%)
  blocking collectives  26.3 us (18%)
  Pallas kernels  18.4 us (12%)
  between operations  13.4 us (9%)
  local copies, waits for them, and re-layouts  5.62 us (4%)
  other arithmetic  5.16 us (3%)
    ppermute x20, starting transfers between devices, along(): lax.ppermute(value, axis, [(i, (i + shift) % count) for i in range(count)])  34.6 us
    all_to_all x1, blocking collectives, shards(): rows = lax.all_to_all(rows, ('z', 'k'), 0, 0)  26.3 us
    ppermute x20, waiting for transfers between devices, along(): lax.ppermute(value, axis, [(i, (i + shift) % count) for i in range(count)])  22.3 us
    ppermute x1, waiting for transfers between devices, shards(): lax.ppermute(near, 'z', [(i, i ^ 1) for i in range(NZ)])  6.82 us
    ppermute x9, starting transfers between devices, shards(): swapped = [lax.ppermute(head, 'k', CORES) for head in heads]  6.69 us
    all_to_all x1, starting transfers between devices, shards(): rows = lax.all_to_all(rows.reshape(NX * NY, 16, 512), ('x', 'y'), 0, 0)  5.32 us
    pallas_call x1, Pallas kernels, attend(): pl.pallas_call(attend_kernel, out_shape=jax.ShapeDtypeStruct((rows, HD),...  4.64 us
    pallas_call x1, Pallas kernels, project(): pl.pallas_call(project_kernel, out_shape=[jax.ShapeDtypeStruct((NX * BLOC...  4.17 us
  transfers between devices with their start and end apart: 35, of which 14 were waited for; matrix products, arithmetic and copies ran while one was open for 5% of the time, Pallas kernels for 10%

profile of v18, /device:TPU:1, one launch (start us, length us, event | category | flops | bytes accessed | tf_op | source)
XLA Modules:
  0.0 148.8 jit_solution(9972546032977271380)
XLA Ops:
  8.0 3.2 %pick.1 = (f32[64,2048]{1,0:T(8,128)}, f32[64,2048]{1,0:T(8,128)}, f32[64,2048]{1,0:T(8,128)}) custom-call(s32[4]{0:T(128)} %pad_add_fusion.where, f32[128,8192]{1,0:T(8,128)} %rows.3), custom_call_target="tpu_custom_call" | custom-call | tf_op jit(solution)/shard_map/pick/pallas_call | solution.py:55
  11.2 2.1 %collective-permute-start.5 = (f32[64,2048]{1,0:T(8,128)}, f32[64,2048]{1,0:T(8,128)S(1)}, u32[]{:S(2)}, u32[]{:S(2)}) collective-permute-start(f32[64,2048]{1,0:T(8,128)} %get-tuple-element.31), channel_id=1, source_target_pairs={{0,64},{64,128},{128,192},{192,0},{1,65},{65,129},{129,193},{193,1... | collective-permute-start | bytes 1572872 | tf_op jit(solution)/shard_map/ppermute | solution.py:305
  13.4 2.5 %collective-permute-start.6 = (f32[64,2048]{1,0:T(8,128)}, f32[64,2048]{1,0:T(8,128)S(1)}, u32[]{:S(2)}, u32[]{:S(2)}) collective-permute-start(f32[64,2048]{1,0:T(8,128)} %get-tuple-element.32), channel_id=1, source_target_pairs={{0,128},{64,192},{128,0},{192,64},{1,129},{65,193},{129,1},{193,65... | collective-permute-start | bytes 1572872 | tf_op jit(solution)/shard_map/ppermute | solution.py:305
  15.8 2.3 %pick_keys.1 = (f32[2,64,128]{2,1,0:T(8,128)}, f32[2,64,128]{2,1,0:T(8,128)}, f32[2,64,128]{2,1,0:T(8,128)}, f32[2,64,128]{2,1,0:T(8,128)}) custom-call(s32[4]{0:T(128)} %pad_add_fusion.where, f32[256,512]{1,0:T(8,128)} %keys.1, f32[256,512]{1,0:T(8,128)} %values.1), custom_call_target="tpu_custom_call" | custom-call | bytes 67108864 | tf_op jit(solution)/shard_map/pick_keys/pallas_call | solution.py:87
  18.1 7.0 %collective-permute-start.2 = (f32[2,64,128]{2,1,0:T(8,128)}, f32[2,64,128]{2,1,0:T(8,128)S(1)}, u32[]{:S(2)}, u32[]{:S(2)}) collective-permute-start(f32[2,64,128]{2,1,0:T(8,128)} %get-tuple-element.37), channel_id=1, source_target_pairs={{0,8},{2,10},{4,12},{6,14},{8,0},{10,2},{12,4},{14,6},{1,9},{3,11}... | collective-permute-start | bytes 196616 | tf_op jit(solution)/shard_map/ppermute | solution.py:305
  25.1 2.4 %collective-permute-start.1 = (f32[2,64,128]{2,1,0:T(8,128)}, f32[2,64,128]{2,1,0:T(8,128)S(1)}, u32[]{:S(2)}, u32[]{:S(2)}) collective-permute-start(f32[2,64,128]{2,1,0:T(8,128)} %get-tuple-element.36), channel_id=1, source_target_pairs={{0,4},{2,6},{4,8},{6,10},{8,12},{10,14},{12,0},{14,2},{1,5},{3,7},... | collective-permute-start | bytes 196616 | tf_op jit(solution)/shard_map/ppermute | solution.py:305
  29.7 3.5 %collective-permute-done.3 = f32[2,64,128]{2,1,0:T(8,128)S(1)} collective-permute-done((f32[2,64,128]{2,1,0:T(8,128)}, f32[2,64,128]{2,1,0:T(8,128)S(1)}, u32[]{:S(2)}, u32[]{:S(2)}) %collective-permute-start.3) | collective-permute-done | bytes 65568 | tf_op jit(solution)/shard_map/ppermute | solution.py:305
  35.6 6.8 %collective-permute-done.4 = f32[4,2,64,128]{3,2,1,0:T(8,128)S(1)} collective-permute-done((f32[4,2,64,128]{3,2,1,0:T(8,128)S(1)}, f32[4,2,64,128]{3,2,1,0:T(8,128)S(1)}, u32[]{:S(2)}, u32[]{:S(2)}) %collective-permute-start.4) | collective-permute-done | bytes 262176 | tf_op jit(solution)/shard_map/ppermute | solution.py:327
  43.3 5.3 %all-to-all-start = ((f32[16,16,512]{2,1,0:T(8,128)}), f32[16,16,512]{2,1,0:T(8,128)S(1)}, u32[]{:S(2)}, u32[]{:S(2)}) async-start(f32[16,16,512]{2,1,0:T(8,128)} %bitcast.12), calls=%async_computation | async-start | bytes 1048576 | tf_op jit(solution)/shard_map/all_to_all | solution.py:334
  48.7 4.2 %project.1 = (f32[256,128]{1,0:T(8,128)S(1)}, f32[256,128]{1,0:T(8,128)S(1)}, f32[256,128]{1,0:T(8,128)S(1)}, f32[256,128]{1,0:T(8,128)S(1)}) custom-call(s32[4]{0:T(128)S(1)} %copy-done, f32[128,8192]{1,0:T(8,128)} %rows.3, f32[64,2048]{1,0:T(8,128)S(1)} %collective-permute-done.5.first, f32[64,2048]{1,0:T(8,128)S(1)} %collective-permute-done.6.second, ...), custom_call_target="tpu_custom_call" | custom-call | flops 1610612736 | bytes 7340032 | tf_op jit(solution)/shard_map/project/pallas_call | solution.py:137
  52.9 2.7 %collective-permute-start.10 = (f32[256,128]{1,0:T(8,128)S(1)}, f32[256,128]{1,0:T(8,128)S(1)}, u32[]{:S(2)}, u32[]{:S(2)}) collective-permute-start(f32[256,128]{1,0:T(8,128)S(1)} %get-tuple-element.46), channel_id=1, source_target_pairs={{0,192},{64,0},{128,64},{192,128},{1,193},{65,1},{129,65},{193,129... | collective-permute-start | bytes 393224 | tf_op jit(solution)/shard_map/ppermute | solution.py:305
  58.6 4.1 %collective-permute-done.8.second = f32[256,128]{1,0:T(8,128)S(1)} collective-permute-done((f32[256,128]{1,0:T(8,128)S(1)}, f32[256,128]{1,0:T(8,128)S(1)}, u32[]{:S(2)}, u32[]{:S(2)}) %collective-permute-start.8) | collective-permute-done | bytes 131104 | tf_op jit(solution)/shard_map/ppermute | solution.py:305
  62.7 26.3 %all_to_all.10 = f32[16,16,512]{2,1,0:T(8,128)} all-to-all(f32[16,16,512]{2,1,0:T(8,128)S(1)} %all-to-all-done), channel_id=1, replica_groups=mesh['x'=4,'y'=4,'z'=8,'k'=2] {'z','k'}, dimensions={0} | all-to-all | bytes 1048576 | tf_op jit(solution)/shard_map/all_to_all | solution.py:353
  92.8 2.2 %copy-done.1 = f32[64,2,64,128]{3,2,1,0:T(8,128)S(1)} copy-done((f32[64,2,64,128]{3,2,1,0:T(8,128)S(1)}, f32[64,2,64,128]{3,2,1,0:T(8,128)}, u32[]{:S(2)}) %copy-start.1) | copy-done | bytes 4194328
  95.0 4.6 %attend.1.refs_0_ = f32[256,128]{1,0:T(8,128)S(1)} custom-call(f32[256,128]{1,0:T(8,128)S(1)} %get-tuple-element.47.first, f32[256,128]{1,0:T(8,128)S(1)} %collective-permute-done.8.second, f32[256,128]{1,0:T(8,128)S(1)} %collective-permute-done.9.third, f32[256,128]{1,0:T(8,128)S(1)} %collective-permute-done.10.fourth, f32[4,4096]{1,0:T(4,128)S(1)} %broadcast_in_dim.39.low, ...), custom_call_target="tpu_custom_call" | custom-call | flops 1610612736 | bytes 6291456 | tf_op jit(solution)/shard_map/attend/pallas_call | solution.py:203
  99.8 3.6 %collective-permute-start.14 = (f32[256,128]{1,0:T(8,128)S(1)}, f32[256,128]{1,0:T(8,128)S(1)}, u32[]{:S(2)}, u32[]{:S(2)}) collective-permute-start(f32[256,128]{1,0:T(8,128)S(1)} %attend.1.refs_0_), channel_id=1, source_target_pairs={{0,12},{2,14},{4,0},{6,2},{8,4},{10,6},{12,8},{14,10},{1,13},{3,15... | collective-permute-start | bytes 393224 | tf_op jit(solution)/shard_map/ppermute | solution.py:305
  103.3 2.7 %collective-permute-start.12 = (f32[256,128]{1,0:T(8,128)S(1)}, f32[256,128]{1,0:T(8,128)S(1)}, u32[]{:S(2)}, u32[]{:S(2)}) collective-permute-start(f32[256,128]{1,0:T(8,128)S(1)} %attend.1.refs_0_), channel_id=1, source_target_pairs={{0,14},{2,0},{4,2},{6,4},{8,6},{10,8},{12,10},{14,12},{1,15},{3,1}... | collective-permute-start | bytes 393224 | tf_op jit(solution)/shard_map/ppermute | solution.py:305
  106.0 1.9 %collective-permute-done.13.refs_3_ = f32[256,128]{1,0:T(8,128)S(1)} collective-permute-done((f32[256,128]{1,0:T(8,128)S(1)}, f32[256,128]{1,0:T(8,128)S(1)}, u32[]{:S(2)}, u32[]{:S(2)}) %collective-permute-start.13) | collective-permute-done | bytes 131104 | tf_op jit(solution)/shard_map/ppermute | solution.py:305
  108.4 2.2 %collective-permute-start.16 = (f32[256,128]{1,0:T(8,128)S(1)}, f32[256,128]{1,0:T(8,128)S(1)}, u32[]{:S(2)}, u32[]{:S(2)}) collective-permute-start(f32[256,128]{1,0:T(8,128)S(1)} %collective-permute-done.14.refs_4_), channel_id=1, source_target_pairs={{0,14},{2,0},{4,2},{6,4},{8,6},{10,8},{12,10},{14,12},{1,15},{3,1}... | collective-permute-start | bytes 393224 | tf_op jit(solution)/shard_map/ppermute | solution.py:305
  111.6 2.7 %collective-permute-start.18 = (f32[128,128]{1,0:T(8,128)S(1)}, f32[128,128]{1,0:T(8,128)S(1)}, u32[]{:S(2)}, u32[]{:S(2)}) collective-permute-start(f32[128,128]{1,0:T(8,128)S(1)} %slice.29), channel_id=1, source_target_pairs={{0,12},{2,14},{4,0},{6,2},{8,4},{10,6},{12,8},{14,10},{1,13},{3,15... | collective-permute-start | bytes 196616 | tf_op jit(solution)/shard_map/ppermute | solution.py:305
  114.4 2.0 %collective-permute-start.20 = (f32[256,128]{1,0:T(8,128)S(1)}, f32[256,128]{1,0:T(8,128)S(1)}, u32[]{:S(2)}, u32[]{:S(2)}) collective-permute-start(f32[256,128]{1,0:T(8,128)S(1)} %collective-permute-done.11.refs_1_), channel_id=1, source_target_pairs={{0,1},{1,0},{2,3},{3,2},{4,5},{5,4},{6,7},{7,6},{8,9},{9,8},{10,11... | collective-permute-start | bytes 393224 | tf_op jit(solution)/shard_map/ppermute | solution.py:361
  116.3 2.5 %collective-permute-start.26 = (f32[128,128]{1,0:T(8,128)S(1)}, f32[128,128]{1,0:T(8,128)S(1)}, u32[]{:S(2)}, u32[]{:S(2)}) collective-permute-start(f32[128,128]{1,0:T(8,128)S(1)} %collective-permute-done.17.refs_7_), channel_id=1, source_target_pairs={{0,1},{1,0},{2,3},{3,2},{4,5},{5,4},{6,7},{7,6},{8,9},{9,8},{10,11... | collective-permute-start | bytes 196616 | tf_op jit(solution)/shard_map/ppermute | solution.py:361
  122.5 4.0 %mix.1 = (f32[2,64,512]{2,1,0:T(8,128)S(1)}, f32[2,64,512]{2,1,0:T(8,128)S(1)}, f32[2,64,512]{2,1,0:T(8,128)S(1)}, f32[2,64,512]{2,1,0:T(8,128)S(1)}) custom-call(s32[4]{0:T(128)S(1)} %copy-done, f32[256,128]{1,0:T(8,128)S(1)} %attend.1.refs_0_, f32[256,128]{1,0:T(8,128)S(1)} %collective-permute-done.11.refs_1_, ...), custom_call_target="tpu_custom_call" | custom-call | flops 1610612736 | bytes 6291456 | tf_op jit(solution)/shard_map/mix/pallas_call | solution.py:265
  129.3 11.9 %collective-permute-done.28 = f32[2,64,512]{2,1,0:T(8,128)S(1)} collective-permute-done((f32[2,64,512]{2,1,0:T(8,128)S(1)}, f32[2,64,512]{2,1,0:T(8,128)S(1)}, u32[]{:S(2)}, u32[]{:S(2)}) %collective-permute-start.28) | collective-permute-done | bytes 262176 | tf_op jit(solution)/shard_map/ppermute | solution.py:305
  (104 shorter events, 22.6 us)
Async XLA Ops:
  6.5 42.1 %all-gather.7.cloned.1.call-start = ((), (), s32[]{:S(2)}) async-start(), calls=%async_computation.2 | async-start | bytes 4718592 | tf_op jit(solution)/shard_map/all_gather | solution.py:321
  7.3 85.6 %all-gather.9.cloned.1.call-start = ((), (), s32[]{:S(2)}) async-start(), calls=%async_computation.3 | async-start | bytes 4718592 | tf_op jit(solution)/shard_map/all_gather | solution.py:335
  11.2 31.2 %collective-permute-start.5 = (f32[64,2048]{1,0:T(8,128)}, f32[64,2048]{1,0:T(8,128)S(1)}, u32[]{:S(2)}, u32[]{:S(2)}) collective-permute-start(f32[64,2048]{1,0:T(8,128)} %get-tuple-element.31), channel_id=1, source_target_pairs={{0,64},{64,128},{128,192},{192,0},{1,65},{65,129},{129,193},{193,1... | collective-permute-start | bytes 1572872 | tf_op jit(solution)/shard_map/ppermute | solution.py:305
  13.4 29.1 %collective-permute-start.6 = (f32[64,2048]{1,0:T(8,128)}, f32[64,2048]{1,0:T(8,128)S(1)}, u32[]{:S(2)}, u32[]{:S(2)}) collective-permute-start(f32[64,2048]{1,0:T(8,128)} %get-tuple-element.32), channel_id=1, source_target_pairs={{0,128},{64,192},{128,0},{192,64},{1,129},{65,193},{129,1},{193,65... | collective-permute-start | bytes 1572872 | tf_op jit(solution)/shard_map/ppermute | solution.py:305
  18.1 10.3 %collective-permute-start.2 = (f32[2,64,128]{2,1,0:T(8,128)}, f32[2,64,128]{2,1,0:T(8,128)S(1)}, u32[]{:S(2)}, u32[]{:S(2)}) collective-permute-start(f32[2,64,128]{2,1,0:T(8,128)} %get-tuple-element.37), channel_id=1, source_target_pairs={{0,8},{2,10},{4,12},{6,14},{8,0},{10,2},{12,4},{14,6},{1,9},{3,11}... | collective-permute-start | bytes 196616 | tf_op jit(solution)/shard_map/ppermute | solution.py:305
  25.1 8.0 %collective-permute-start.3 = (f32[2,64,128]{2,1,0:T(8,128)}, f32[2,64,128]{2,1,0:T(8,128)S(1)}, u32[]{:S(2)}, u32[]{:S(2)}) collective-permute-start(f32[2,64,128]{2,1,0:T(8,128)} %get-tuple-element.38), channel_id=1, source_target_pairs={{0,12},{2,14},{4,0},{6,2},{8,4},{10,6},{12,8},{14,10},{1,13},{3,15... | collective-permute-start | bytes 196616 | tf_op jit(solution)/shard_map/ppermute | solution.py:305
  25.1 8.4 %collective-permute-start.1 = (f32[2,64,128]{2,1,0:T(8,128)}, f32[2,64,128]{2,1,0:T(8,128)S(1)}, u32[]{:S(2)}, u32[]{:S(2)}) collective-permute-start(f32[2,64,128]{2,1,0:T(8,128)} %get-tuple-element.36), channel_id=1, source_target_pairs={{0,4},{2,6},{4,8},{6,10},{8,12},{10,14},{12,0},{14,2},{1,5},{3,7},... | collective-permute-start | bytes 196616 | tf_op jit(solution)/shard_map/ppermute | solution.py:305
  28.4 14.0 %collective-permute-start.7 = (f32[64,2048]{1,0:T(8,128)}, f32[64,2048]{1,0:T(8,128)S(1)}, u32[]{:S(2)}, u32[]{:S(2)}) collective-permute-start(f32[64,2048]{1,0:T(8,128)} %get-tuple-element.33), channel_id=1, source_target_pairs={{0,192},{64,0},{128,64},{192,128},{1,193},{65,1},{129,65},{193,129... | collective-permute-start | bytes 1572872 | tf_op jit(solution)/shard_map/ppermute | solution.py:305
  34.4 8.0 %collective-permute-start.4 = (f32[4,2,64,128]{3,2,1,0:T(8,128)S(1)}, f32[4,2,64,128]{3,2,1,0:T(8,128)S(1)}, u32[]{:S(2)}, u32[]{:S(2)}) collective-permute-start(f32[4,2,64,128]{3,2,1,0:T(8,128)S(1)} %pad_maximum_fusion), channel_id=1, source_target_pairs={{0,2},{2,0},{4,6},{6,4},{8,10},{10,8},{12,14},{14,12},{1,3},{3,1},... | collective-permute-start | bytes 786440 | tf_op jit(solution)/shard_map/ppermute | solution.py:327
  43.3 15.2 %all-to-all-start = ((f32[16,16,512]{2,1,0:T(8,128)}), f32[16,16,512]{2,1,0:T(8,128)S(1)}, u32[]{:S(2)}, u32[]{:S(2)}) async-start(f32[16,16,512]{2,1,0:T(8,128)} %bitcast.12), calls=%async_computation | async-start | bytes 1048576 | tf_op jit(solution)/shard_map/all_to_all | solution.py:334
  48.6 74.0 %all-gather.11.cloned.1.call-start = ((), (), s32[]{:S(2)}) async-start(), calls=%async_computation.4 | async-start | bytes 2621440 | tf_op jit(solution)/shard_map/all_gather | solution.py:354
  55.6 7.2 %collective-permute-start.8 = (f32[256,128]{1,0:T(8,128)S(1)}, f32[256,128]{1,0:T(8,128)S(1)}, u32[]{:S(2)}, u32[]{:S(2)}) collective-permute-start(f32[256,128]{1,0:T(8,128)S(1)} %get-tuple-element.44), channel_id=1, source_target_pairs={{0,64},{64,128},{128,192},{192,0},{1,65},{65,129},{129,193},{193,1... | collective-permute-start | bytes 393224 | tf_op jit(solution)/shard_map/ppermute | solution.py:305
  55.6 7.2 %collective-permute-start.9 = (f32[256,128]{1,0:T(8,128)S(1)}, f32[256,128]{1,0:T(8,128)S(1)}, u32[]{:S(2)}, u32[]{:S(2)}) collective-permute-start(f32[256,128]{1,0:T(8,128)S(1)} %get-tuple-element.45), channel_id=1, source_target_pairs={{0,128},{64,192},{128,0},{192,64},{1,129},{65,193},{129,1},{193,65... | collective-permute-start | bytes 393224 | tf_op jit(solution)/shard_map/ppermute | solution.py:305
  99.7 8.2 %collective-permute-start.13 = (f32[256,128]{1,0:T(8,128)S(1)}, f32[256,128]{1,0:T(8,128)S(1)}, u32[]{:S(2)}, u32[]{:S(2)}) collective-permute-start(f32[256,128]{1,0:T(8,128)S(1)} %attend.1.refs_0_), channel_id=1, source_target_pairs={{0,4},{2,6},{4,8},{6,10},{8,12},{10,14},{12,0},{14,2},{1,5},{3,7},... | collective-permute-start | bytes 393224 | tf_op jit(solution)/shard_map/ppermute | solution.py:305
  99.8 8.7 %collective-permute-start.14 = (f32[256,128]{1,0:T(8,128)S(1)}, f32[256,128]{1,0:T(8,128)S(1)}, u32[]{:S(2)}, u32[]{:S(2)}) collective-permute-start(f32[256,128]{1,0:T(8,128)S(1)} %attend.1.refs_0_), channel_id=1, source_target_pairs={{0,12},{2,14},{4,0},{6,2},{8,4},{10,6},{12,8},{14,10},{1,13},{3,15... | collective-permute-start | bytes 393224 | tf_op jit(solution)/shard_map/ppermute | solution.py:305
  103.3 7.4 %collective-permute-start.11 = (f32[256,128]{1,0:T(8,128)S(1)}, f32[256,128]{1,0:T(8,128)S(1)}, u32[]{:S(2)}, u32[]{:S(2)}) collective-permute-start(f32[256,128]{1,0:T(8,128)S(1)} %attend.1.refs_0_), channel_id=1, source_target_pairs={{0,2},{2,4},{4,6},{6,8},{8,10},{10,12},{12,14},{14,0},{1,3},{3,5},... | collective-permute-start | bytes 393224 | tf_op jit(solution)/shard_map/ppermute | solution.py:305
  103.3 8.3 %collective-permute-start.12 = (f32[256,128]{1,0:T(8,128)S(1)}, f32[256,128]{1,0:T(8,128)S(1)}, u32[]{:S(2)}, u32[]{:S(2)}) collective-permute-start(f32[256,128]{1,0:T(8,128)S(1)} %attend.1.refs_0_), channel_id=1, source_target_pairs={{0,14},{2,0},{4,2},{6,4},{8,6},{10,8},{12,10},{14,12},{1,15},{3,1}... | collective-permute-start | bytes 393224 | tf_op jit(solution)/shard_map/ppermute | solution.py:305
  106.0 8.4 %collective-permute-start.19 = (f32[256,128]{1,0:T(8,128)S(1)}, f32[256,128]{1,0:T(8,128)S(1)}, u32[]{:S(2)}, u32[]{:S(2)}) collective-permute-start(f32[256,128]{1,0:T(8,128)S(1)} %attend.1.refs_0_), channel_id=1, source_target_pairs={{0,1},{1,0},{2,3},{3,2},{4,5},{5,4},{6,7},{7,6},{8,9},{9,8},{10,11... | collective-permute-start | bytes 393224 | tf_op jit(solution)/shard_map/ppermute | solution.py:361
  107.9 12.0 %collective-permute-start.15 = (f32[256,128]{1,0:T(8,128)S(1)}, f32[256,128]{1,0:T(8,128)S(1)}, u32[]{:S(2)}, u32[]{:S(2)}) collective-permute-start(f32[256,128]{1,0:T(8,128)S(1)} %collective-permute-done.13.refs_3_), channel_id=1, source_target_pairs={{0,2},{2,4},{4,6},{6,8},{8,10},{10,12},{12,14},{14,0},{1,3},{3,5},... | collective-permute-start | bytes 393224 | tf_op jit(solution)/shard_map/ppermute | solution.py:305
  108.4 11.5 %collective-permute-start.16 = (f32[256,128]{1,0:T(8,128)S(1)}, f32[256,128]{1,0:T(8,128)S(1)}, u32[]{:S(2)}, u32[]{:S(2)}) collective-permute-start(f32[256,128]{1,0:T(8,128)S(1)} %collective-permute-done.14.refs_4_), channel_id=1, source_target_pairs={{0,14},{2,0},{4,2},{6,4},{8,6},{10,8},{12,10},{14,12},{1,15},{3,1}... | collective-permute-start | bytes 393224 | tf_op jit(solution)/shard_map/ppermute | solution.py:305
  111.6 7.3 %collective-permute-start.18 = (f32[128,128]{1,0:T(8,128)S(1)}, f32[128,128]{1,0:T(8,128)S(1)}, u32[]{:S(2)}, u32[]{:S(2)}) collective-permute-start(f32[128,128]{1,0:T(8,128)S(1)} %slice.29), channel_id=1, source_target_pairs={{0,12},{2,14},{4,0},{6,2},{8,4},{10,6},{12,8},{14,10},{1,13},{3,15... | collective-permute-start | bytes 196616 | tf_op jit(solution)/shard_map/ppermute | solution.py:305
  126.5 14.6 %collective-permute-start.28 = (f32[2,64,512]{2,1,0:T(8,128)S(1)}, f32[2,64,512]{2,1,0:T(8,128)S(1)}, u32[]{:S(2)}, u32[]{:S(2)}) collective-permute-start(f32[2,64,512]{2,1,0:T(8,128)S(1)} %get-tuple-element.54), channel_id=1, source_target_pairs={{0,64},{64,128},{128,192},{192,0},{1,65},{65,129},{129,193},{193,1... | collective-permute-start | bytes 786440 | tf_op jit(solution)/shard_map/ppermute | solution.py:305
  126.6 14.6 %collective-permute-start.29 = (f32[2,64,512]{2,1,0:T(8,128)S(1)}, f32[2,64,512]{2,1,0:T(8,128)S(1)}, u32[]{:S(2)}, u32[]{:S(2)}) collective-permute-start(f32[2,64,512]{2,1,0:T(8,128)S(1)} %get-tuple-element.55), channel_id=1, source_target_pairs={{0,128},{64,192},{128,0},{192,64},{1,129},{65,193},{129,1},{193,65... | collective-permute-start | bytes 786440 | tf_op jit(solution)/shard_map/ppermute | solution.py:305
  128.4 13.0 %collective-permute-start.30 = (f32[2,64,512]{2,1,0:T(8,128)S(1)}, f32[2,64,512]{2,1,0:T(8,128)S(1)}, u32[]{:S(2)}, u32[]{:S(2)}) collective-permute-start(f32[2,64,512]{2,1,0:T(8,128)S(1)} %get-tuple-element.56), channel_id=1, source_target_pairs={{0,192},{64,0},{128,64},{192,128},{1,193},{65,1},{129,65},{193,129... | collective-permute-start | bytes 786440 | tf_op jit(solution)/shard_map/ppermute | solution.py:305
  (19 other events, 260.8 us)
Sparse Core Ops, SparseCore 0:
  9.2 38.8 all-gather.6
  50.0 34.6 all-gather.8
  89.2 30.3 all-gather.10

commit v19 on v18

--- a/solution.py
+++ b/solution.py
@@ -210,7 +210,7 @@
             pltpu.VMEM((8, rows, NZ * BLOCK), jnp.float32),
             pltpu.SemaphoreType.DMA((8,)),
         ],
-        compiler_params=pltpu.CompilerParams(vmem_limit_bytes=40 << 20),
+        compiler_params=pltpu.CompilerParams(vmem_limit_bytes=50 << 20),
         cost_estimate=pl.CostEstimate(
             flops=12 * 256 * 4096 * HD, bytes_accessed=6 << 20, transcendentals=256 * 4096
         ),
@@ -330,9 +330,6 @@
     given = lax.dynamic_index_in_dim(rows, 1 - k, 2, keepdims=False)
     taken = lax.ppermute(given, "k", CORES)
     rows = jnp.where(k == 0, jnp.stack([kept, taken]), jnp.stack([taken, kept]))
-    rows, near, hidden = lax.optimization_barrier((rows, near, hidden))
-    rows = lax.all_to_all(rows.reshape(NX * NY, 16, 512), ("x", "y"), 0, 0)
-    kv = lax.all_gather(near, ("y", "k"), axis=0)
     key_block = jnp.arange(NY, dtype=jnp.int32)[:, None, None]
     key_block = key_block + 4 * jnp.arange(NK, dtype=jnp.int32)[None, :, None]
     turns = 2 * jnp.arange(NZ // 2, dtype=jnp.int32)
@@ -347,6 +344,9 @@
         slash_offsets,
         slash_count,
     )
+    rows, near, hidden, low, up = lax.optimization_barrier((rows, near, hidden, low, up))
+    rows = lax.all_to_all(rows.reshape(NX * NY, 16, 512), ("x", "y"), 0, 0)
+    kv = lax.all_gather(near, ("y", "k"), axis=0)
     partial = project(where, hidden_rows, hidden, weights)
     partial = [partial[0]] + [along("x", partial[s], s) for s in range(1, NX)]
     rows, partial = lax.optimization_barrier((rows, partial))

time: 149 us -> 146 us (0.980)
  waiting for transfers between devices: 32.7 us -> 27.3 us
  starting transfers between devices: 47.2 us -> 51.4 us
  local copies, waits for them, and re-layouts: 5.62 us -> 3.48 us
    ppermute x20, waiting for transfers between devices: 22.3 us -> 17.5 us  [along(): lax.ppermute(value, axis, [(i, (i + shift) % count) for i in range(count)])]
    unnamed x20 -> x18, local copies, waits for them, and re-layouts: 3.87 us -> 1.68 us
    ppermute x20, starting transfers between devices: 34.6 us -> 36.6 us  [along(): lax.ppermute(value, axis, [(i, (i + shift) % count) for i in range(count)])]
    ppermute x1, starting transfers between devices: 0.39 us -> 2.37 us  [shards(): taken = lax.ppermute(given, 'k', CORES)]
  transfers between devices with their start and end apart: 35 -> 35, of which waited for: 14 -> 13; matrix products, arithmetic and copies ran while one was open for 5% -> 5% of each run, Pallas kernels for 10% -> 10%
where the time goes in v19:
time: 146 us
  starting transfers between devices  51.4 us (35%)
  waiting for transfers between devices  27.3 us (19%)
  blocking collectives  26.2 us (18%)
  Pallas kernels  19 us (13%)
  between operations  13.4 us (9%)
  other arithmetic  5.12 us (4%)
  local copies, waits for them, and re-layouts  3.48 us (2%)
    ppermute x20, starting transfers between devices, along(): lax.ppermute(value, axis, [(i, (i + shift) % count) for i in range(count)])  36.6 us
    all_to_all x1, blocking collectives, shards(): rows = lax.all_to_all(rows, ('z', 'k'), 0, 0)  26.2 us
    ppermute x20, waiting for transfers between devices, along(): lax.ppermute(value, axis, [(i, (i + shift) % count) for i in range(count)])  17.5 us
    ppermute x9, starting transfers between devices, shards(): swapped = [lax.ppermute(head, 'k', CORES) for head in heads]  6.96 us
    ppermute x1, waiting for transfers between devices, shards(): lax.ppermute(near, 'z', [(i, i ^ 1) for i in range(NZ)])  6.42 us
    pallas_call x1, Pallas kernels, attend(): pl.pallas_call(attend_kernel, out_shape=jax.ShapeDtypeStruct((rows, HD),...  5.34 us
    all_to_all x1, starting transfers between devices, shards(): rows = lax.all_to_all(rows.reshape(NX * NY, 16, 512), ('x', 'y'), 0, 0)  4.57 us
    pallas_call x1, Pallas kernels, project(): pl.pallas_call(project_kernel, out_shape=[jax.ShapeDtypeStruct((NX * BLOC...  4.17 us
  transfers between devices with their start and end apart: 35, of which 13 were waited for; matrix products, arithmetic and copies ran while one was open for 5% of the time, Pallas kernels for 10%

profile of v19, /device:TPU:1, one launch (start us, length us, event | category | flops | bytes accessed | tf_op | source)
XLA Modules:
  0.0 145.9 jit_solution(2284295537311458054)
XLA Ops:
  8.0 3.2 %pick.1 = (f32[64,2048]{1,0:T(8,128)}, f32[64,2048]{1,0:T(8,128)}, f32[64,2048]{1,0:T(8,128)}) custom-call(s32[4]{0:T(128)} %pad_add_fusion.where, f32[128,8192]{1,0:T(8,128)} %rows.3), custom_call_target="tpu_custom_call" | custom-call | tf_op jit(solution)/shard_map/pick/pallas_call | solution.py:55
  11.2 2.1 %collective-permute-start.5 = (f32[64,2048]{1,0:T(8,128)}, f32[64,2048]{1,0:T(8,128)S(1)}, u32[]{:S(2)}, u32[]{:S(2)}) collective-permute-start(f32[64,2048]{1,0:T(8,128)} %get-tuple-element.33), channel_id=1, source_target_pairs={{0,64},{64,128},{128,192},{192,0},{1,65},{65,129},{129,193},{193,1... | collective-permute-start | bytes 1572872 | tf_op jit(solution)/shard_map/ppermute | solution.py:305
  13.4 2.5 %collective-permute-start.6 = (f32[64,2048]{1,0:T(8,128)}, f32[64,2048]{1,0:T(8,128)S(1)}, u32[]{:S(2)}, u32[]{:S(2)}) collective-permute-start(f32[64,2048]{1,0:T(8,128)} %get-tuple-element.34), channel_id=1, source_target_pairs={{0,128},{64,192},{128,0},{192,64},{1,129},{65,193},{129,1},{193,65... | collective-permute-start | bytes 1572872 | tf_op jit(solution)/shard_map/ppermute | solution.py:305
  15.8 2.3 %pick_keys.1 = (f32[2,64,128]{2,1,0:T(8,128)}, f32[2,64,128]{2,1,0:T(8,128)}, f32[2,64,128]{2,1,0:T(8,128)}, f32[2,64,128]{2,1,0:T(8,128)}) custom-call(s32[4]{0:T(128)} %pad_add_fusion.where, f32[256,512]{1,0:T(8,128)} %keys.1, f32[256,512]{1,0:T(8,128)} %values.1), custom_call_target="tpu_custom_call" | custom-call | bytes 67108864 | tf_op jit(solution)/shard_map/pick_keys/pallas_call | solution.py:87
  18.1 7.0 %collective-permute-start.2 = (f32[2,64,128]{2,1,0:T(8,128)}, f32[2,64,128]{2,1,0:T(8,128)S(1)}, u32[]{:S(2)}, u32[]{:S(2)}) collective-permute-start(f32[2,64,128]{2,1,0:T(8,128)} %get-tuple-element.39), channel_id=1, source_target_pairs={{0,8},{2,10},{4,12},{6,14},{8,0},{10,2},{12,4},{14,6},{1,9},{3,11}... | collective-permute-start | bytes 196616 | tf_op jit(solution)/shard_map/ppermute | solution.py:305
  25.1 2.4 %collective-permute-start.1 = (f32[2,64,128]{2,1,0:T(8,128)}, f32[2,64,128]{2,1,0:T(8,128)S(1)}, u32[]{:S(2)}, u32[]{:S(2)}) collective-permute-start(f32[2,64,128]{2,1,0:T(8,128)} %get-tuple-element.38), channel_id=1, source_target_pairs={{0,4},{2,6},{4,8},{6,10},{8,12},{10,14},{12,0},{14,2},{1,5},{3,7},... | collective-permute-start | bytes 196616 | tf_op jit(solution)/shard_map/ppermute | solution.py:305
  33.4 2.4 %collective-permute-start = (f32[2,4,16,512]{3,2,1,0:T(8,128)S(1)}, f32[2,4,16,512]{3,2,1,0:T(8,128)S(1)}, u32[]{:S(2)}, u32[]{:S(2)}) collective-permute-start(f32[2,4,16,512]{3,2,1,0:T(8,128)S(1)} %get-tuple-element.64), channel_id=1, source_target_pairs={{0,1},{1,0},{2,3},{3,2},{4,5},{5,4},{6,7},{7,6},{8,9},{9,8},{10,11... | collective-permute-start | bytes 786440 | tf_op jit(solution)/shard_map/ppermute | solution.py:331
  38.3 6.4 %collective-permute-done.4 = f32[4,2,64,128]{3,2,1,0:T(8,128)S(1)} collective-permute-done((f32[4,2,64,128]{3,2,1,0:T(8,128)S(1)}, f32[4,2,64,128]{3,2,1,0:T(8,128)S(1)}, u32[]{:S(2)}, u32[]{:S(2)}) %collective-permute-start.4) | collective-permute-done | bytes 262176 | tf_op jit(solution)/shard_map/ppermute | solution.py:327
  45.6 4.6 %all-to-all-start = ((f32[16,16,512]{2,1,0:T(8,128)}), f32[16,16,512]{2,1,0:T(8,128)S(1)}, u32[]{:S(2)}, u32[]{:S(2)}) async-start(f32[16,16,512]{2,1,0:T(8,128)} %bitcast.18), calls=%async_computation | async-start | bytes 1048576 | tf_op jit(solution)/shard_map/all_to_all | solution.py:348
  50.3 4.2 %project.1 = (f32[256,128]{1,0:T(8,128)S(1)}, f32[256,128]{1,0:T(8,128)S(1)}, f32[256,128]{1,0:T(8,128)S(1)}, f32[256,128]{1,0:T(8,128)S(1)}) custom-call(s32[4]{0:T(128)S(1)} %copy-done, f32[128,8192]{1,0:T(8,128)} %rows.3, f32[64,2048]{1,0:T(8,128)S(1)} %collective-permute-done.5.first, f32[64,2048]{1,0:T(8,128)S(1)} %collective-permute-done.6.second, ...), custom_call_target="tpu_custom_call" | custom-call | flops 1610612736 | bytes 7340032 | tf_op jit(solution)/shard_map/project/pallas_call | solution.py:137
  54.5 2.7 %collective-permute-start.10 = (f32[256,128]{1,0:T(8,128)S(1)}, f32[256,128]{1,0:T(8,128)S(1)}, u32[]{:S(2)}, u32[]{:S(2)}) collective-permute-start(f32[256,128]{1,0:T(8,128)S(1)} %get-tuple-element.48), channel_id=1, source_target_pairs={{0,192},{64,0},{128,64},{192,128},{1,193},{65,1},{129,65},{193,129... | collective-permute-start | bytes 393224 | tf_op jit(solution)/shard_map/ppermute | solution.py:305
  60.0 4.0 %collective-permute-done.8.second = f32[256,128]{1,0:T(8,128)S(1)} collective-permute-done((f32[256,128]{1,0:T(8,128)S(1)}, f32[256,128]{1,0:T(8,128)S(1)}, u32[]{:S(2)}, u32[]{:S(2)}) %collective-permute-start.8) | collective-permute-done | bytes 131104 | tf_op jit(solution)/shard_map/ppermute | solution.py:305
  64.0 26.2 %all_to_all.10 = f32[16,16,512]{2,1,0:T(8,128)} all-to-all(f32[16,16,512]{2,1,0:T(8,128)S(1)} %all-to-all-done), channel_id=1, replica_groups=mesh['x'=4,'y'=4,'z'=8,'k'=2] {'z','k'}, dimensions={0} | all-to-all | bytes 1048576 | tf_op jit(solution)/shard_map/all_to_all | solution.py:353
  90.2 5.3 %attend.1.refs_0_ = f32[256,128]{1,0:T(8,128)S(1)} custom-call(f32[256,128]{1,0:T(8,128)S(1)} %get-tuple-element.49.first, f32[256,128]{1,0:T(8,128)S(1)} %collective-permute-done.8.second, f32[256,128]{1,0:T(8,128)S(1)} %collective-permute-done.9.third, f32[256,128]{1,0:T(8,128)S(1)} %collective-permute-done.10.fourth, f32[4,4096]{1,0:T(4,128)S(1)} %broadcast_in_dim.39.low, ...), custom_call_target="tpu_custom_call" | custom-call | flops 1610612736 | bytes 6291456 | tf_op jit(solution)/shard_map/attend/pallas_call | solution.py:203
  95.7 3.6 %collective-permute-start.14 = (f32[256,128]{1,0:T(8,128)S(1)}, f32[256,128]{1,0:T(8,128)S(1)}, u32[]{:S(2)}, u32[]{:S(2)}) collective-permute-start(f32[256,128]{1,0:T(8,128)S(1)} %attend.1.refs_0_), channel_id=1, source_target_pairs={{0,12},{2,14},{4,0},{6,2},{8,4},{10,6},{12,8},{14,10},{1,13},{3,15... | collective-permute-start | bytes 393224 | tf_op jit(solution)/shard_map/ppermute | solution.py:305
  99.2 2.7 %collective-permute-start.12 = (f32[256,128]{1,0:T(8,128)S(1)}, f32[256,128]{1,0:T(8,128)S(1)}, u32[]{:S(2)}, u32[]{:S(2)}) collective-permute-start(f32[256,128]{1,0:T(8,128)S(1)} %attend.1.refs_0_), channel_id=1, source_target_pairs={{0,14},{2,0},{4,2},{6,4},{8,6},{10,8},{12,10},{14,12},{1,15},{3,1}... | collective-permute-start | bytes 393224 | tf_op jit(solution)/shard_map/ppermute | solution.py:305
  104.3 2.2 %collective-permute-start.16 = (f32[256,128]{1,0:T(8,128)S(1)}, f32[256,128]{1,0:T(8,128)S(1)}, u32[]{:S(2)}, u32[]{:S(2)}) collective-permute-start(f32[256,128]{1,0:T(8,128)S(1)} %collective-permute-done.14.refs_4_), channel_id=1, source_target_pairs={{0,14},{2,0},{4,2},{6,4},{8,6},{10,8},{12,10},{14,12},{1,15},{3,1}... | collective-permute-start | bytes 393224 | tf_op jit(solution)/shard_map/ppermute | solution.py:305
  107.5 2.7 %collective-permute-start.18 = (f32[128,128]{1,0:T(8,128)S(1)}, f32[128,128]{1,0:T(8,128)S(1)}, u32[]{:S(2)}, u32[]{:S(2)}) collective-permute-start(f32[128,128]{1,0:T(8,128)S(1)} %slice.29), channel_id=1, source_target_pairs={{0,12},{2,14},{4,0},{6,2},{8,4},{10,6},{12,8},{14,10},{1,13},{3,15... | collective-permute-start | bytes 196616 | tf_op jit(solution)/shard_map/ppermute | solution.py:305
  110.2 2.1 %collective-permute-start.20 = (f32[256,128]{1,0:T(8,128)S(1)}, f32[256,128]{1,0:T(8,128)S(1)}, u32[]{:S(2)}, u32[]{:S(2)}) collective-permute-start(f32[256,128]{1,0:T(8,128)S(1)} %collective-permute-done.11.refs_1_), channel_id=1, source_target_pairs={{0,1},{1,0},{2,3},{3,2},{4,5},{5,4},{6,7},{7,6},{8,9},{9,8},{10,11... | collective-permute-start | bytes 393224 | tf_op jit(solution)/shard_map/ppermute | solution.py:361
  112.3 2.5 %collective-permute-start.26 = (f32[128,128]{1,0:T(8,128)S(1)}, f32[128,128]{1,0:T(8,128)S(1)}, u32[]{:S(2)}, u32[]{:S(2)}) collective-permute-start(f32[128,128]{1,0:T(8,128)S(1)} %collective-permute-done.17.refs_7_), channel_id=1, source_target_pairs={{0,1},{1,0},{2,3},{3,2},{4,5},{5,4},{6,7},{7,6},{8,9},{9,8},{10,11... | collective-permute-start | bytes 196616 | tf_op jit(solution)/shard_map/ppermute | solution.py:361
  119.6 4.0 %mix.1 = (f32[2,64,512]{2,1,0:T(8,128)S(1)}, f32[2,64,512]{2,1,0:T(8,128)S(1)}, f32[2,64,512]{2,1,0:T(8,128)S(1)}, f32[2,64,512]{2,1,0:T(8,128)S(1)}) custom-call(s32[4]{0:T(128)S(1)} %copy-done, f32[256,128]{1,0:T(8,128)S(1)} %attend.1.refs_0_, f32[256,128]{1,0:T(8,128)S(1)} %collective-permute-done.11.refs_1_, ...), custom_call_target="tpu_custom_call" | custom-call | flops 1610612736 | bytes 6291456 | tf_op jit(solution)/shard_map/mix/pallas_call | solution.py:265
  124.8 2.4 %collective-permute-start.29 = (f32[2,64,512]{2,1,0:T(8,128)S(1)}, f32[2,64,512]{2,1,0:T(8,128)S(1)}, u32[]{:S(2)}, u32[]{:S(2)}) collective-permute-start(f32[2,64,512]{2,1,0:T(8,128)S(1)} %get-tuple-element.59), channel_id=1, source_target_pairs={{0,128},{64,192},{128,0},{192,64},{1,129},{65,193},{129,1},{193,65... | collective-permute-start | bytes 786440 | tf_op jit(solution)/shard_map/ppermute | solution.py:305
  128.4 3.6 %collective-permute-done.28 = f32[2,64,512]{2,1,0:T(8,128)S(1)} collective-permute-done((f32[2,64,512]{2,1,0:T(8,128)S(1)}, f32[2,64,512]{2,1,0:T(8,128)S(1)}, u32[]{:S(2)}, u32[]{:S(2)}) %collective-permute-start.28) | collective-permute-done | bytes 262176 | tf_op jit(solution)/shard_map/ppermute | solution.py:305
  132.0 6.5 %collective-permute-done.29 = f32[2,64,512]{2,1,0:T(8,128)S(1)} collective-permute-done((f32[2,64,512]{2,1,0:T(8,128)S(1)}, f32[2,64,512]{2,1,0:T(8,128)S(1)}, u32[]{:S(2)}, u32[]{:S(2)}) %collective-permute-start.29) | collective-permute-done | bytes 262176 | tf_op jit(solution)/shard_map/ppermute | solution.py:305
  (102 shorter events, 25.0 us)
Async XLA Ops:
  6.5 43.7 %all-gather.7.cloned.1.call-start = ((), (), s32[]{:S(2)}) async-start(), calls=%async_computation.2 | async-start | bytes 4718592 | tf_op jit(solution)/shard_map/all_gather | solution.py:321
  7.3 82.9 %all-gather.9.cloned.1.call-start = ((), (), s32[]{:S(2)}) async-start(), calls=%async_computation.3 | async-start | bytes 4718592 | tf_op jit(solution)/shard_map/all_gather | solution.py:349
  11.2 33.5 %collective-permute-start.5 = (f32[64,2048]{1,0:T(8,128)}, f32[64,2048]{1,0:T(8,128)S(1)}, u32[]{:S(2)}, u32[]{:S(2)}) collective-permute-start(f32[64,2048]{1,0:T(8,128)} %get-tuple-element.33), channel_id=1, source_target_pairs={{0,64},{64,128},{128,192},{192,0},{1,65},{65,129},{129,193},{193,1... | collective-permute-start | bytes 1572872 | tf_op jit(solution)/shard_map/ppermute | solution.py:305
  13.4 31.4 %collective-permute-start.6 = (f32[64,2048]{1,0:T(8,128)}, f32[64,2048]{1,0:T(8,128)S(1)}, u32[]{:S(2)}, u32[]{:S(2)}) collective-permute-start(f32[64,2048]{1,0:T(8,128)} %get-tuple-element.34), channel_id=1, source_target_pairs={{0,128},{64,192},{128,0},{192,64},{1,129},{65,193},{129,1},{193,65... | collective-permute-start | bytes 1572872 | tf_op jit(solution)/shard_map/ppermute | solution.py:305
  18.1 14.0 %collective-permute-start.2 = (f32[2,64,128]{2,1,0:T(8,128)}, f32[2,64,128]{2,1,0:T(8,128)S(1)}, u32[]{:S(2)}, u32[]{:S(2)}) collective-permute-start(f32[2,64,128]{2,1,0:T(8,128)} %get-tuple-element.39), channel_id=1, source_target_pairs={{0,8},{2,10},{4,12},{6,14},{8,0},{10,2},{12,4},{14,6},{1,9},{3,11}... | collective-permute-start | bytes 196616 | tf_op jit(solution)/shard_map/ppermute | solution.py:305
  25.1 8.3 %collective-permute-start.3 = (f32[2,64,128]{2,1,0:T(8,128)}, f32[2,64,128]{2,1,0:T(8,128)S(1)}, u32[]{:S(2)}, u32[]{:S(2)}) collective-permute-start(f32[2,64,128]{2,1,0:T(8,128)} %get-tuple-element.40), channel_id=1, source_target_pairs={{0,12},{2,14},{4,0},{6,2},{8,4},{10,6},{12,8},{14,10},{1,13},{3,15... | collective-permute-start | bytes 196616 | tf_op jit(solution)/shard_map/ppermute | solution.py:305
  25.1 10.6 %collective-permute-start.1 = (f32[2,64,128]{2,1,0:T(8,128)}, f32[2,64,128]{2,1,0:T(8,128)S(1)}, u32[]{:S(2)}, u32[]{:S(2)}) collective-permute-start(f32[2,64,128]{2,1,0:T(8,128)} %get-tuple-element.38), channel_id=1, source_target_pairs={{0,4},{2,6},{4,8},{6,10},{8,12},{10,14},{12,0},{14,2},{1,5},{3,7},... | collective-permute-start | bytes 196616 | tf_op jit(solution)/shard_map/ppermute | solution.py:305
  32.1 12.7 %collective-permute-start.7 = (f32[64,2048]{1,0:T(8,128)}, f32[64,2048]{1,0:T(8,128)S(1)}, u32[]{:S(2)}, u32[]{:S(2)}) collective-permute-start(f32[64,2048]{1,0:T(8,128)} %get-tuple-element.35), channel_id=1, source_target_pairs={{0,192},{64,0},{128,64},{192,128},{1,193},{65,1},{129,65},{193,129... | collective-permute-start | bytes 1572872 | tf_op jit(solution)/shard_map/ppermute | solution.py:305
  36.6 8.1 %collective-permute-start.4 = (f32[4,2,64,128]{3,2,1,0:T(8,128)S(1)}, f32[4,2,64,128]{3,2,1,0:T(8,128)S(1)}, u32[]{:S(2)}, u32[]{:S(2)}) collective-permute-start(f32[4,2,64,128]{3,2,1,0:T(8,128)S(1)} %pad_maximum_fusion), channel_id=1, source_target_pairs={{0,2},{2,0},{4,6},{6,4},{8,10},{10,8},{12,14},{14,12},{1,3},{3,1},... | collective-permute-start | bytes 786440 | tf_op jit(solution)/shard_map/ppermute | solution.py:327
  45.6 13.5 %all-to-all-start = ((f32[16,16,512]{2,1,0:T(8,128)}), f32[16,16,512]{2,1,0:T(8,128)S(1)}, u32[]{:S(2)}, u32[]{:S(2)}) async-start(f32[16,16,512]{2,1,0:T(8,128)} %bitcast.18), calls=%async_computation | async-start | bytes 1048576 | tf_op jit(solution)/shard_map/all_to_all | solution.py:348
  50.2 69.4 %all-gather.11.cloned.1.call-start = ((), (), s32[]{:S(2)}) async-start(), calls=%async_computation.4 | async-start | bytes 2621440 | tf_op jit(solution)/shard_map/all_gather | solution.py:354
  57.1 6.9 %collective-permute-start.8 = (f32[256,128]{1,0:T(8,128)S(1)}, f32[256,128]{1,0:T(8,128)S(1)}, u32[]{:S(2)}, u32[]{:S(2)}) collective-permute-start(f32[256,128]{1,0:T(8,128)S(1)} %get-tuple-element.46), channel_id=1, source_target_pairs={{0,64},{64,128},{128,192},{192,0},{1,65},{65,129},{129,193},{193,1... | collective-permute-start | bytes 393224 | tf_op jit(solution)/shard_map/ppermute | solution.py:305
  57.1 6.9 %collective-permute-start.9 = (f32[256,128]{1,0:T(8,128)S(1)}, f32[256,128]{1,0:T(8,128)S(1)}, u32[]{:S(2)}, u32[]{:S(2)}) collective-permute-start(f32[256,128]{1,0:T(8,128)S(1)} %get-tuple-element.47), channel_id=1, source_target_pairs={{0,128},{64,192},{128,0},{192,64},{1,129},{65,193},{129,1},{193,65... | collective-permute-start | bytes 393224 | tf_op jit(solution)/shard_map/ppermute | solution.py:305
  95.6 8.2 %collective-permute-start.13 = (f32[256,128]{1,0:T(8,128)S(1)}, f32[256,128]{1,0:T(8,128)S(1)}, u32[]{:S(2)}, u32[]{:S(2)}) collective-permute-start(f32[256,128]{1,0:T(8,128)S(1)} %attend.1.refs_0_), channel_id=1, source_target_pairs={{0,4},{2,6},{4,8},{6,10},{8,12},{10,14},{12,0},{14,2},{1,5},{3,7},... | collective-permute-start | bytes 393224 | tf_op jit(solution)/shard_map/ppermute | solution.py:305
  95.7 8.7 %collective-permute-start.14 = (f32[256,128]{1,0:T(8,128)S(1)}, f32[256,128]{1,0:T(8,128)S(1)}, u32[]{:S(2)}, u32[]{:S(2)}) collective-permute-start(f32[256,128]{1,0:T(8,128)S(1)} %attend.1.refs_0_), channel_id=1, source_target_pairs={{0,12},{2,14},{4,0},{6,2},{8,4},{10,6},{12,8},{14,10},{1,13},{3,15... | collective-permute-start | bytes 393224 | tf_op jit(solution)/shard_map/ppermute | solution.py:305
  99.2 7.3 %collective-permute-start.11 = (f32[256,128]{1,0:T(8,128)S(1)}, f32[256,128]{1,0:T(8,128)S(1)}, u32[]{:S(2)}, u32[]{:S(2)}) collective-permute-start(f32[256,128]{1,0:T(8,128)S(1)} %attend.1.refs_0_), channel_id=1, source_target_pairs={{0,2},{2,4},{4,6},{6,8},{8,10},{10,12},{12,14},{14,0},{1,3},{3,5},... | collective-permute-start | bytes 393224 | tf_op jit(solution)/shard_map/ppermute | solution.py:305
  99.2 8.3 %collective-permute-start.12 = (f32[256,128]{1,0:T(8,128)S(1)}, f32[256,128]{1,0:T(8,128)S(1)}, u32[]{:S(2)}, u32[]{:S(2)}) collective-permute-start(f32[256,128]{1,0:T(8,128)S(1)} %attend.1.refs_0_), channel_id=1, source_target_pairs={{0,14},{2,0},{4,2},{6,4},{8,6},{10,8},{12,10},{14,12},{1,15},{3,1}... | collective-permute-start | bytes 393224 | tf_op jit(solution)/shard_map/ppermute | solution.py:305
  101.9 8.3 %collective-permute-start.19 = (f32[256,128]{1,0:T(8,128)S(1)}, f32[256,128]{1,0:T(8,128)S(1)}, u32[]{:S(2)}, u32[]{:S(2)}) collective-permute-start(f32[256,128]{1,0:T(8,128)S(1)} %attend.1.refs_0_), channel_id=1, source_target_pairs={{0,1},{1,0},{2,3},{3,2},{4,5},{5,4},{6,7},{7,6},{8,9},{9,8},{10,11... | collective-permute-start | bytes 393224 | tf_op jit(solution)/shard_map/ppermute | solution.py:361
  103.8 12.1 %collective-permute-start.15 = (f32[256,128]{1,0:T(8,128)S(1)}, f32[256,128]{1,0:T(8,128)S(1)}, u32[]{:S(2)}, u32[]{:S(2)}) collective-permute-start(f32[256,128]{1,0:T(8,128)S(1)} %collective-permute-done.13.refs_3_), channel_id=1, source_target_pairs={{0,2},{2,4},{4,6},{6,8},{8,10},{10,12},{12,14},{14,0},{1,3},{3,5},... | collective-permute-start | bytes 393224 | tf_op jit(solution)/shard_map/ppermute | solution.py:305
  104.3 11.5 %collective-permute-start.16 = (f32[256,128]{1,0:T(8,128)S(1)}, f32[256,128]{1,0:T(8,128)S(1)}, u32[]{:S(2)}, u32[]{:S(2)}) collective-permute-start(f32[256,128]{1,0:T(8,128)S(1)} %collective-permute-done.14.refs_4_), channel_id=1, source_target_pairs={{0,14},{2,0},{4,2},{6,4},{8,6},{10,8},{12,10},{14,12},{1,15},{3,1}... | collective-permute-start | bytes 393224 | tf_op jit(solution)/shard_map/ppermute | solution.py:305
  107.5 7.3 %collective-permute-start.18 = (f32[128,128]{1,0:T(8,128)S(1)}, f32[128,128]{1,0:T(8,128)S(1)}, u32[]{:S(2)}, u32[]{:S(2)}) collective-permute-start(f32[128,128]{1,0:T(8,128)S(1)} %slice.29), channel_id=1, source_target_pairs={{0,12},{2,14},{4,0},{6,2},{8,4},{10,6},{12,8},{14,10},{1,13},{3,15... | collective-permute-start | bytes 196616 | tf_op jit(solution)/shard_map/ppermute | solution.py:305
  123.5 8.5 %collective-permute-start.28 = (f32[2,64,512]{2,1,0:T(8,128)S(1)}, f32[2,64,512]{2,1,0:T(8,128)S(1)}, u32[]{:S(2)}, u32[]{:S(2)}) collective-permute-start(f32[2,64,512]{2,1,0:T(8,128)S(1)} %get-tuple-element.58), channel_id=1, source_target_pairs={{0,64},{64,128},{128,192},{192,0},{1,65},{65,129},{129,193},{193,1... | collective-permute-start | bytes 786440 | tf_op jit(solution)/shard_map/ppermute | solution.py:305
  124.8 13.7 %collective-permute-start.29 = (f32[2,64,512]{2,1,0:T(8,128)S(1)}, f32[2,64,512]{2,1,0:T(8,128)S(1)}, u32[]{:S(2)}, u32[]{:S(2)}) collective-permute-start(f32[2,64,512]{2,1,0:T(8,128)S(1)} %get-tuple-element.59), channel_id=1, source_target_pairs={{0,128},{64,192},{128,0},{192,64},{1,129},{65,193},{129,1},{193,65... | collective-permute-start | bytes 786440 | tf_op jit(solution)/shard_map/ppermute | solution.py:305
  127.2 11.3 %collective-permute-start.30 = (f32[2,64,512]{2,1,0:T(8,128)S(1)}, f32[2,64,512]{2,1,0:T(8,128)S(1)}, u32[]{:S(2)}, u32[]{:S(2)}) collective-permute-start(f32[2,64,512]{2,1,0:T(8,128)S(1)} %get-tuple-element.60), channel_id=1, source_target_pairs={{0,192},{64,0},{128,64},{192,128},{1,193},{65,1},{129,65},{193,129... | collective-permute-start | bytes 786440 | tf_op jit(solution)/shard_map/ppermute | solution.py:305
  (18 other events, 188.8 us)
Sparse Core Ops, SparseCore 0:
  9.2 38.8 all-gather.6
  50.0 34.6 all-gather.8
  90.3 29.1 all-gather.10

commit v20 on v19

--- a/solution.py
+++ b/solution.py
@@ -350,7 +350,11 @@
     partial = project(where, hidden_rows, hidden, weights)
     partial = [partial[0]] + [along("x", partial[s], s) for s in range(1, NX)]
     rows, partial = lax.optimization_barrier((rows, partial))
-    rows = lax.all_to_all(rows, ("z", "k"), 0, 0)
+    rows = lax.all_to_all(rows.reshape(NZ, NK, 16, 512), "z", 0, 0)
+    kept = lax.dynamic_index_in_dim(rows, k, 1, keepdims=False)
+    taken = lax.ppermute(lax.dynamic_index_in_dim(rows, 1 - k, 1, keepdims=False), "k", CORES)
+    rows = jnp.where(k == 0, jnp.stack([kept, taken], 1), jnp.stack([taken, kept], 1))
+    rows = rows.reshape(NZ * NK, 16, 512)
     out_weight = lax.all_gather(rows, "y", axis=0)
     own = attend(partial, low, up, kv)
     near_up, near_down = along("z", own, 1), along("z", own, -1)

time: 146 us -> 146 us (level)
  blocking collectives: 26.2 us -> 16.3 us
  starting transfers between devices: 51.4 us -> 59.6 us
    all_to_all x1, blocking collectives: 26.2 us -> 16.3 us  [shards(): rows = lax.all_to_all(rows.reshape(NZ, NK, 16, 512), 'z', 0, 0)]
    ppermute x0 -> x1, starting transfers between devices: none -> 6.29 us  [shards(): lax.ppermute(lax.dynamic_index_in_dim(rows, 1 - k, 1, keepdims=False), 'k...]
  transfers between devices with their start and end apart: 35 -> 36, of which waited for: 13 -> 13; matrix products, arithmetic and copies ran while one was open for 5% -> 5% of each run, Pallas kernels for 10% -> 10%
where the time goes in v20:
time: 146 us
  starting transfers between devices  59.6 us (41%)
  waiting for transfers between devices  27.9 us (19%)
  Pallas kernels  19 us (13%)
  blocking collectives  16.3 us (11%)
  between operations  13.4 us (9%)
  other arithmetic  5.99 us (4%)
  local copies, waits for them, and re-layouts  3.47 us (2%)
    ppermute x20, starting transfers between devices, along(): lax.ppermute(value, axis, [(i, (i + shift) % count) for i in range(count)])  37.1 us
    ppermute x20, waiting for transfers between devices, along(): lax.ppermute(value, axis, [(i, (i + shift) % count) for i in range(count)])  16.9 us
    all_to_all x1, blocking collectives, shards(): rows = lax.all_to_all(rows.reshape(NZ, NK, 16, 512), 'z', 0, 0)  16.3 us
    ppermute x9, starting transfers between devices, shards(): swapped = [lax.ppermute(head, 'k', CORES) for head in heads]  8.37 us
    ppermute x1, waiting for transfers between devices, shards(): lax.ppermute(near, 'z', [(i, i ^ 1) for i in range(NZ)])  6.42 us
    ppermute x1, starting transfers between devices, shards(): lax.ppermute(lax.dynamic_index_in_dim(rows, 1 - k, 1, keepdims=False), 'k...  6.29 us
    pallas_call x1, Pallas kernels, attend(): pl.pallas_call(attend_kernel, out_shape=jax.ShapeDtypeStruct((rows, HD),...  5.34 us
    all_to_all x1, starting transfers between devices, shards(): rows = lax.all_to_all(rows.reshape(NX * NY, 16, 512), ('x', 'y'), 0, 0)  4.58 us
  transfers between devices with their start and end apart: 36, of which 13 were waited for; matrix products, arithmetic and copies ran while one was open for 5% of the time, Pallas kernels for 10%

profile of v20, /device:TPU:1, one launch (start us, length us, event | category | flops | bytes accessed | tf_op | source)
XLA Modules:
  0.0 145.9 jit_solution(15479115945689694111)
XLA Ops:
  8.0 3.2 %pick.1 = (f32[64,2048]{1,0:T(8,128)}, f32[64,2048]{1,0:T(8,128)}, f32[64,2048]{1,0:T(8,128)}) custom-call(s32[4]{0:T(128)} %pad_add_fusion.where, f32[128,8192]{1,0:T(8,128)} %rows.3), custom_call_target="tpu_custom_call" | custom-call | tf_op jit(solution)/shard_map/pick/pallas_call | solution.py:55
  13.4 2.5 %collective-permute-start.6 = (f32[64,2048]{1,0:T(8,128)}, f32[64,2048]{1,0:T(8,128)S(1)}, u32[]{:S(2)}, u32[]{:S(2)}) collective-permute-start(f32[64,2048]{1,0:T(8,128)} %get-tuple-element.34), channel_id=1, source_target_pairs={{0,128},{64,192},{128,0},{192,64},{1,129},{65,193},{129,1},{193,65... | collective-permute-start | bytes 1572872 | tf_op jit(solution)/shard_map/ppermute | solution.py:305
  15.8 2.3 %pick_keys.1 = (f32[2,64,128]{2,1,0:T(8,128)}, f32[2,64,128]{2,1,0:T(8,128)}, f32[2,64,128]{2,1,0:T(8,128)}, f32[2,64,128]{2,1,0:T(8,128)}) custom-call(s32[4]{0:T(128)} %pad_add_fusion.where, f32[256,512]{1,0:T(8,128)} %keys.1, f32[256,512]{1,0:T(8,128)} %values.1), custom_call_target="tpu_custom_call" | custom-call | bytes 67108864 | tf_op jit(solution)/shard_map/pick_keys/pallas_call | solution.py:87
  18.1 7.0 %collective-permute-start.2 = (f32[2,64,128]{2,1,0:T(8,128)}, f32[2,64,128]{2,1,0:T(8,128)S(1)}, u32[]{:S(2)}, u32[]{:S(2)}) collective-permute-start(f32[2,64,128]{2,1,0:T(8,128)} %get-tuple-element.39), channel_id=1, source_target_pairs={{0,8},{2,10},{4,12},{6,14},{8,0},{10,2},{12,4},{14,6},{1,9},{3,11}... | collective-permute-start | bytes 196616 | tf_op jit(solution)/shard_map/ppermute | solution.py:305
  25.1 2.4 %collective-permute-start.1 = (f32[2,64,128]{2,1,0:T(8,128)}, f32[2,64,128]{2,1,0:T(8,128)S(1)}, u32[]{:S(2)}, u32[]{:S(2)}) collective-permute-start(f32[2,64,128]{2,1,0:T(8,128)} %get-tuple-element.38), channel_id=1, source_target_pairs={{0,4},{2,6},{4,8},{6,10},{8,12},{10,14},{12,0},{14,2},{1,5},{3,7},... | collective-permute-start | bytes 196616 | tf_op jit(solution)/shard_map/ppermute | solution.py:305
  33.4 2.4 %collective-permute-start = (f32[2,4,16,512]{3,2,1,0:T(8,128)S(1)}, f32[2,4,16,512]{3,2,1,0:T(8,128)S(1)}, u32[]{:S(2)}, u32[]{:S(2)}) collective-permute-start(f32[2,4,16,512]{3,2,1,0:T(8,128)S(1)} %get-tuple-element.66), channel_id=1, source_target_pairs={{0,1},{1,0},{2,3},{3,2},{4,5},{5,4},{6,7},{7,6},{8,9},{9,8},{10,11... | collective-permute-start | bytes 786440 | tf_op jit(solution)/shard_map/ppermute | solution.py:331
  38.3 6.4 %collective-permute-done.4 = f32[4,2,64,128]{3,2,1,0:T(8,128)S(1)} collective-permute-done((f32[4,2,64,128]{3,2,1,0:T(8,128)S(1)}, f32[4,2,64,128]{3,2,1,0:T(8,128)S(1)}, u32[]{:S(2)}, u32[]{:S(2)}) %collective-permute-start.4) | collective-permute-done | bytes 262176 | tf_op jit(solution)/shard_map/ppermute | solution.py:327
  45.6 4.6 %all-to-all-start = ((f32[16,16,512]{2,1,0:T(8,128)}), f32[16,16,512]{2,1,0:T(8,128)S(1)}, u32[]{:S(2)}, u32[]{:S(2)}) async-start(f32[16,16,512]{2,1,0:T(8,128)} %bitcast.18), calls=%async_computation | async-start | bytes 1048576 | tf_op jit(solution)/shard_map/all_to_all | solution.py:348
  50.2 4.2 %project.1 = (f32[256,128]{1,0:T(8,128)S(1)}, f32[256,128]{1,0:T(8,128)S(1)}, f32[256,128]{1,0:T(8,128)S(1)}, f32[256,128]{1,0:T(8,128)S(1)}) custom-call(s32[4]{0:T(128)S(1)} %copy-done, f32[128,8192]{1,0:T(8,128)} %rows.3, f32[64,2048]{1,0:T(8,128)S(1)} %collective-permute-done.5.first, f32[64,2048]{1,0:T(8,128)S(1)} %collective-permute-done.6.second, ...), custom_call_target="tpu_custom_call" | custom-call | flops 1610612736 | bytes 7340032 | tf_op jit(solution)/shard_map/project/pallas_call | solution.py:137
  54.4 2.7 %collective-permute-start.10 = (f32[256,128]{1,0:T(8,128)S(1)}, f32[256,128]{1,0:T(8,128)S(1)}, u32[]{:S(2)}, u32[]{:S(2)}) collective-permute-start(f32[256,128]{1,0:T(8,128)S(1)} %get-tuple-element.48), channel_id=1, source_target_pairs={{0,192},{64,0},{128,64},{192,128},{1,193},{65,1},{129,65},{193,129... | collective-permute-start | bytes 393224 | tf_op jit(solution)/shard_map/ppermute | solution.py:305
  59.9 4.0 %collective-permute-done.8.second = f32[256,128]{1,0:T(8,128)S(1)} collective-permute-done((f32[256,128]{1,0:T(8,128)S(1)}, f32[256,128]{1,0:T(8,128)S(1)}, u32[]{:S(2)}, u32[]{:S(2)}) %collective-permute-start.8) | collective-permute-done | bytes 131104 | tf_op jit(solution)/shard_map/ppermute | solution.py:305
  64.0 16.3 %all_to_all.10 = f32[8,2,16,512]{3,2,1,0:T(8,128)S(1)} all-to-all(f32[8,2,16,512]{3,2,1,0:T(8,128)S(1)} %bitcast.43), channel_id=1, replica_groups=mesh['x'=4,'y'=4,'z'=8,'k'=2] {'z'}, dimensions={0} | all-to-all | bytes 1048576 | tf_op jit(solution)/shard_map/all_to_all | solution.py:353
  80.4 6.3 %collective-permute-start.28 = (f32[8,16,512]{2,1,0:T(8,128)S(1)}, f32[8,16,512]{2,1,0:T(8,128)S(1)}, u32[]{:S(2)}, u32[]{:S(2)}) collective-permute-start(f32[8,16,512]{2,1,0:T(8,128)S(1)} %get-tuple-element.64), channel_id=1, source_target_pairs={{0,1},{1,0},{2,3},{3,2},{4,5},{5,4},{6,7},{7,6},{8,9},{9,8},{10,11... | collective-permute-start | bytes 786440 | tf_op jit(solution)/shard_map/ppermute | solution.py:355
  88.8 5.3 %attend.1.refs_0_ = f32[256,128]{1,0:T(8,128)S(1)} custom-call(f32[256,128]{1,0:T(8,128)S(1)} %get-tuple-element.49.first, f32[256,128]{1,0:T(8,128)S(1)} %collective-permute-done.8.second, f32[256,128]{1,0:T(8,128)S(1)} %collective-permute-done.9.third, f32[256,128]{1,0:T(8,128)S(1)} %collective-permute-done.10.fourth, f32[4,4096]{1,0:T(4,128)S(1)} %broadcast_in_dim.39.low, ...), custom_call_target="tpu_custom_call" | custom-call | flops 1610612736 | bytes 6291456 | tf_op jit(solution)/shard_map/attend/pallas_call | solution.py:203
  94.2 3.6 %collective-permute-start.14 = (f32[256,128]{1,0:T(8,128)S(1)}, f32[256,128]{1,0:T(8,128)S(1)}, u32[]{:S(2)}, u32[]{:S(2)}) collective-permute-start(f32[256,128]{1,0:T(8,128)S(1)} %attend.1.refs_0_), channel_id=1, source_target_pairs={{0,12},{2,14},{4,0},{6,2},{8,4},{10,6},{12,8},{14,10},{1,13},{3,15... | collective-permute-start | bytes 393224 | tf_op jit(solution)/shard_map/ppermute | solution.py:305
  98.0 2.4 %collective-permute-start.12 = (f32[256,128]{1,0:T(8,128)S(1)}, f32[256,128]{1,0:T(8,128)S(1)}, u32[]{:S(2)}, u32[]{:S(2)}) collective-permute-start(f32[256,128]{1,0:T(8,128)S(1)} %attend.1.refs_0_), channel_id=1, source_target_pairs={{0,14},{2,0},{4,2},{6,4},{8,6},{10,8},{12,10},{14,12},{1,15},{3,1}... | collective-permute-start | bytes 393224 | tf_op jit(solution)/shard_map/ppermute | solution.py:305
  103.8 2.7 %collective-permute-start.16 = (f32[256,128]{1,0:T(8,128)S(1)}, f32[256,128]{1,0:T(8,128)S(1)}, u32[]{:S(2)}, u32[]{:S(2)}) collective-permute-start(f32[256,128]{1,0:T(8,128)S(1)} %collective-permute-done.14.refs_4_), channel_id=1, source_target_pairs={{0,14},{2,0},{4,2},{6,4},{8,6},{10,8},{12,10},{14,12},{1,15},{3,1}... | collective-permute-start | bytes 393224 | tf_op jit(solution)/shard_map/ppermute | solution.py:305
  106.7 3.6 %collective-permute-start.18 = (f32[128,128]{1,0:T(8,128)S(1)}, f32[128,128]{1,0:T(8,128)S(1)}, u32[]{:S(2)}, u32[]{:S(2)}) collective-permute-start(f32[128,128]{1,0:T(8,128)S(1)} %slice.29), channel_id=1, source_target_pairs={{0,12},{2,14},{4,0},{6,2},{8,4},{10,6},{12,8},{14,10},{1,13},{3,15... | collective-permute-start | bytes 196616 | tf_op jit(solution)/shard_map/ppermute | solution.py:305
  110.2 3.0 %collective-permute-start.20 = (f32[256,128]{1,0:T(8,128)S(1)}, f32[256,128]{1,0:T(8,128)S(1)}, u32[]{:S(2)}, u32[]{:S(2)}) collective-permute-start(f32[256,128]{1,0:T(8,128)S(1)} %collective-permute-done.11.refs_1_), channel_id=1, source_target_pairs={{0,1},{1,0},{2,3},{3,2},{4,5},{5,4},{6,7},{7,6},{8,9},{9,8},{10,11... | collective-permute-start | bytes 393224 | tf_op jit(solution)/shard_map/ppermute | solution.py:365
  113.2 2.2 %collective-permute-start.26 = (f32[128,128]{1,0:T(8,128)S(1)}, f32[128,128]{1,0:T(8,128)S(1)}, u32[]{:S(2)}, u32[]{:S(2)}) collective-permute-start(f32[128,128]{1,0:T(8,128)S(1)} %collective-permute-done.17.refs_7_), channel_id=1, source_target_pairs={{0,1},{1,0},{2,3},{3,2},{4,5},{5,4},{6,7},{7,6},{8,9},{9,8},{10,11... | collective-permute-start | bytes 196616 | tf_op jit(solution)/shard_map/ppermute | solution.py:365
  119.6 4.0 %mix.1 = (f32[2,64,512]{2,1,0:T(8,128)S(1)}, f32[2,64,512]{2,1,0:T(8,128)S(1)}, f32[2,64,512]{2,1,0:T(8,128)S(1)}, f32[2,64,512]{2,1,0:T(8,128)S(1)}) custom-call(s32[4]{0:T(128)S(1)} %copy-done, f32[256,128]{1,0:T(8,128)S(1)} %attend.1.refs_0_, f32[256,128]{1,0:T(8,128)S(1)} %collective-permute-done.11.refs_1_, ...), custom_call_target="tpu_custom_call" | custom-call | flops 1610612736 | bytes 6291456 | tf_op jit(solution)/shard_map/mix/pallas_call | solution.py:265
  124.8 2.4 %collective-permute-start.30 = (f32[2,64,512]{2,1,0:T(8,128)S(1)}, f32[2,64,512]{2,1,0:T(8,128)S(1)}, u32[]{:S(2)}, u32[]{:S(2)}) collective-permute-start(f32[2,64,512]{2,1,0:T(8,128)S(1)} %get-tuple-element.59), channel_id=1, source_target_pairs={{0,128},{64,192},{128,0},{192,64},{1,129},{65,193},{129,1},{193,65... | collective-permute-start | bytes 786440 | tf_op jit(solution)/shard_map/ppermute | solution.py:305
  128.4 3.6 %collective-permute-done.29 = f32[2,64,512]{2,1,0:T(8,128)S(1)} collective-permute-done((f32[2,64,512]{2,1,0:T(8,128)S(1)}, f32[2,64,512]{2,1,0:T(8,128)S(1)}, u32[]{:S(2)}, u32[]{:S(2)}) %collective-permute-start.29) | collective-permute-done | bytes 262176 | tf_op jit(solution)/shard_map/ppermute | solution.py:305
  132.0 6.5 %collective-permute-done.30 = f32[2,64,512]{2,1,0:T(8,128)S(1)} collective-permute-done((f32[2,64,512]{2,1,0:T(8,128)S(1)}, f32[2,64,512]{2,1,0:T(8,128)S(1)}, u32[]{:S(2)}, u32[]{:S(2)}) %collective-permute-start.30) | collective-permute-done | bytes 262176 | tf_op jit(solution)/shard_map/ppermute | solution.py:305
  (106 shorter events, 28.9 us)
Async XLA Ops:
  6.5 43.7 %all-gather.8.cloned.1.call-start = ((), (), s32[]{:S(2)}) async-start(), calls=%async_computation.3 | async-start | bytes 4718592 | tf_op jit(solution)/shard_map/all_gather | solution.py:321
  7.3 81.5 %all-gather.10.cloned.1.call-start = ((), (), s32[]{:S(2)}) async-start(), calls=%async_computation.4 | async-start | bytes 4718592 | tf_op jit(solution)/shard_map/all_gather | solution.py:349
  11.2 33.5 %collective-permute-start.5 = (f32[64,2048]{1,0:T(8,128)}, f32[64,2048]{1,0:T(8,128)S(1)}, u32[]{:S(2)}, u32[]{:S(2)}) collective-permute-start(f32[64,2048]{1,0:T(8,128)} %get-tuple-element.33), channel_id=1, source_target_pairs={{0,64},{64,128},{128,192},{192,0},{1,65},{65,129},{129,193},{193,1... | collective-permute-start | bytes 1572872 | tf_op jit(solution)/shard_map/ppermute | solution.py:305
  13.4 31.4 %collective-permute-start.6 = (f32[64,2048]{1,0:T(8,128)}, f32[64,2048]{1,0:T(8,128)S(1)}, u32[]{:S(2)}, u32[]{:S(2)}) collective-permute-start(f32[64,2048]{1,0:T(8,128)} %get-tuple-element.34), channel_id=1, source_target_pairs={{0,128},{64,192},{128,0},{192,64},{1,129},{65,193},{129,1},{193,65... | collective-permute-start | bytes 1572872 | tf_op jit(solution)/shard_map/ppermute | solution.py:305
  18.1 14.0 %collective-permute-start.2 = (f32[2,64,128]{2,1,0:T(8,128)}, f32[2,64,128]{2,1,0:T(8,128)S(1)}, u32[]{:S(2)}, u32[]{:S(2)}) collective-permute-start(f32[2,64,128]{2,1,0:T(8,128)} %get-tuple-element.39), channel_id=1, source_target_pairs={{0,8},{2,10},{4,12},{6,14},{8,0},{10,2},{12,4},{14,6},{1,9},{3,11}... | collective-permute-start | bytes 196616 | tf_op jit(solution)/shard_map/ppermute | solution.py:305
  25.1 8.2 %collective-permute-start.3 = (f32[2,64,128]{2,1,0:T(8,128)}, f32[2,64,128]{2,1,0:T(8,128)S(1)}, u32[]{:S(2)}, u32[]{:S(2)}) collective-permute-start(f32[2,64,128]{2,1,0:T(8,128)} %get-tuple-element.40), channel_id=1, source_target_pairs={{0,12},{2,14},{4,0},{6,2},{8,4},{10,6},{12,8},{14,10},{1,13},{3,15... | collective-permute-start | bytes 196616 | tf_op jit(solution)/shard_map/ppermute | solution.py:305
  25.1 10.6 %collective-permute-start.1 = (f32[2,64,128]{2,1,0:T(8,128)}, f32[2,64,128]{2,1,0:T(8,128)S(1)}, u32[]{:S(2)}, u32[]{:S(2)}) collective-permute-start(f32[2,64,128]{2,1,0:T(8,128)} %get-tuple-element.38), channel_id=1, source_target_pairs={{0,4},{2,6},{4,8},{6,10},{8,12},{10,14},{12,0},{14,2},{1,5},{3,7},... | collective-permute-start | bytes 196616 | tf_op jit(solution)/shard_map/ppermute | solution.py:305
  32.1 12.7 %collective-permute-start.7 = (f32[64,2048]{1,0:T(8,128)}, f32[64,2048]{1,0:T(8,128)S(1)}, u32[]{:S(2)}, u32[]{:S(2)}) collective-permute-start(f32[64,2048]{1,0:T(8,128)} %get-tuple-element.35), channel_id=1, source_target_pairs={{0,192},{64,0},{128,64},{192,128},{1,193},{65,1},{129,65},{193,129... | collective-permute-start | bytes 1572872 | tf_op jit(solution)/shard_map/ppermute | solution.py:305
  36.6 8.1 %collective-permute-start.4 = (f32[4,2,64,128]{3,2,1,0:T(8,128)S(1)}, f32[4,2,64,128]{3,2,1,0:T(8,128)S(1)}, u32[]{:S(2)}, u32[]{:S(2)}) collective-permute-start(f32[4,2,64,128]{3,2,1,0:T(8,128)S(1)} %pad_maximum_fusion), channel_id=1, source_target_pairs={{0,2},{2,0},{4,6},{6,4},{8,10},{10,8},{12,14},{14,12},{1,3},{3,1},... | collective-permute-start | bytes 786440 | tf_op jit(solution)/shard_map/ppermute | solution.py:327
  45.6 13.5 %all-to-all-start = ((f32[16,16,512]{2,1,0:T(8,128)}), f32[16,16,512]{2,1,0:T(8,128)S(1)}, u32[]{:S(2)}, u32[]{:S(2)}) async-start(f32[16,16,512]{2,1,0:T(8,128)} %bitcast.18), calls=%async_computation | async-start | bytes 1048576 | tf_op jit(solution)/shard_map/all_to_all | solution.py:348
  50.2 69.4 %all-gather.6.cloned.1.call-start = ((), (), s32[]{:S(2)}) async-start(), calls=%async_computation.2 | async-start | bytes 2621440 | tf_op jit(solution)/shard_map/all_gather | solution.py:358
  57.1 6.9 %collective-permute-start.8 = (f32[256,128]{1,0:T(8,128)S(1)}, f32[256,128]{1,0:T(8,128)S(1)}, u32[]{:S(2)}, u32[]{:S(2)}) collective-permute-start(f32[256,128]{1,0:T(8,128)S(1)} %get-tuple-element.46), channel_id=1, source_target_pairs={{0,64},{64,128},{128,192},{192,0},{1,65},{65,129},{129,193},{193,1... | collective-permute-start | bytes 393224 | tf_op jit(solution)/shard_map/ppermute | solution.py:305
  80.4 7.4 %collective-permute-start.28 = (f32[8,16,512]{2,1,0:T(8,128)S(1)}, f32[8,16,512]{2,1,0:T(8,128)S(1)}, u32[]{:S(2)}, u32[]{:S(2)}) collective-permute-start(f32[8,16,512]{2,1,0:T(8,128)S(1)} %get-tuple-element.64), channel_id=1, source_target_pairs={{0,1},{1,0},{2,3},{3,2},{4,5},{5,4},{6,7},{7,6},{8,9},{9,8},{10,11... | collective-permute-start | bytes 786440 | tf_op jit(solution)/shard_map/ppermute | solution.py:355
  94.1 9.7 %collective-permute-start.13 = (f32[256,128]{1,0:T(8,128)S(1)}, f32[256,128]{1,0:T(8,128)S(1)}, u32[]{:S(2)}, u32[]{:S(2)}) collective-permute-start(f32[256,128]{1,0:T(8,128)S(1)} %attend.1.refs_0_), channel_id=1, source_target_pairs={{0,4},{2,6},{4,8},{6,10},{8,12},{10,14},{12,0},{14,2},{1,5},{3,7},... | collective-permute-start | bytes 393224 | tf_op jit(solution)/shard_map/ppermute | solution.py:305
  94.2 9.6 %collective-permute-start.14 = (f32[256,128]{1,0:T(8,128)S(1)}, f32[256,128]{1,0:T(8,128)S(1)}, u32[]{:S(2)}, u32[]{:S(2)}) collective-permute-start(f32[256,128]{1,0:T(8,128)S(1)} %attend.1.refs_0_), channel_id=1, source_target_pairs={{0,12},{2,14},{4,0},{6,2},{8,4},{10,6},{12,8},{14,10},{1,13},{3,15... | collective-permute-start | bytes 393224 | tf_op jit(solution)/shard_map/ppermute | solution.py:305
  97.8 8.8 %collective-permute-start.11 = (f32[256,128]{1,0:T(8,128)S(1)}, f32[256,128]{1,0:T(8,128)S(1)}, u32[]{:S(2)}, u32[]{:S(2)}) collective-permute-start(f32[256,128]{1,0:T(8,128)S(1)} %attend.1.refs_0_), channel_id=1, source_target_pairs={{0,2},{2,4},{4,6},{6,8},{8,10},{10,12},{12,14},{14,0},{1,3},{3,5},... | collective-permute-start | bytes 393224 | tf_op jit(solution)/shard_map/ppermute | solution.py:305
  98.0 8.6 %collective-permute-start.12 = (f32[256,128]{1,0:T(8,128)S(1)}, f32[256,128]{1,0:T(8,128)S(1)}, u32[]{:S(2)}, u32[]{:S(2)}) collective-permute-start(f32[256,128]{1,0:T(8,128)S(1)} %attend.1.refs_0_), channel_id=1, source_target_pairs={{0,14},{2,0},{4,2},{6,4},{8,6},{10,8},{12,10},{14,12},{1,15},{3,1}... | collective-permute-start | bytes 393224 | tf_op jit(solution)/shard_map/ppermute | solution.py:305
  100.4 9.8 %collective-permute-start.19 = (f32[256,128]{1,0:T(8,128)S(1)}, f32[256,128]{1,0:T(8,128)S(1)}, u32[]{:S(2)}, u32[]{:S(2)}) collective-permute-start(f32[256,128]{1,0:T(8,128)S(1)} %attend.1.refs_0_), channel_id=1, source_target_pairs={{0,1},{1,0},{2,3},{3,2},{4,5},{5,4},{6,7},{7,6},{8,9},{9,8},{10,11... | collective-permute-start | bytes 393224 | tf_op jit(solution)/shard_map/ppermute | solution.py:365
  103.8 11.6 %collective-permute-start.15 = (f32[256,128]{1,0:T(8,128)S(1)}, f32[256,128]{1,0:T(8,128)S(1)}, u32[]{:S(2)}, u32[]{:S(2)}) collective-permute-start(f32[256,128]{1,0:T(8,128)S(1)} %collective-permute-done.13.refs_3_), channel_id=1, source_target_pairs={{0,2},{2,4},{4,6},{6,8},{8,10},{10,12},{12,14},{14,0},{1,3},{3,5},... | collective-permute-start | bytes 393224 | tf_op jit(solution)/shard_map/ppermute | solution.py:305
  103.8 12.1 %collective-permute-start.16 = (f32[256,128]{1,0:T(8,128)S(1)}, f32[256,128]{1,0:T(8,128)S(1)}, u32[]{:S(2)}, u32[]{:S(2)}) collective-permute-start(f32[256,128]{1,0:T(8,128)S(1)} %collective-permute-done.14.refs_4_), channel_id=1, source_target_pairs={{0,14},{2,0},{4,2},{6,4},{8,6},{10,8},{12,10},{14,12},{1,15},{3,1}... | collective-permute-start | bytes 393224 | tf_op jit(solution)/shard_map/ppermute | solution.py:305
  106.7 8.8 %collective-permute-start.18 = (f32[128,128]{1,0:T(8,128)S(1)}, f32[128,128]{1,0:T(8,128)S(1)}, u32[]{:S(2)}, u32[]{:S(2)}) collective-permute-start(f32[128,128]{1,0:T(8,128)S(1)} %slice.29), channel_id=1, source_target_pairs={{0,12},{2,14},{4,0},{6,2},{8,4},{10,6},{12,8},{14,10},{1,13},{3,15... | collective-permute-start | bytes 196616 | tf_op jit(solution)/shard_map/ppermute | solution.py:305
  123.5 8.5 %collective-permute-start.29 = (f32[2,64,512]{2,1,0:T(8,128)S(1)}, f32[2,64,512]{2,1,0:T(8,128)S(1)}, u32[]{:S(2)}, u32[]{:S(2)}) collective-permute-start(f32[2,64,512]{2,1,0:T(8,128)S(1)} %get-tuple-element.58), channel_id=1, source_target_pairs={{0,64},{64,128},{128,192},{192,0},{1,65},{65,129},{129,193},{193,1... | collective-permute-start | bytes 786440 | tf_op jit(solution)/shard_map/ppermute | solution.py:305
  124.8 13.7 %collective-permute-start.30 = (f32[2,64,512]{2,1,0:T(8,128)S(1)}, f32[2,64,512]{2,1,0:T(8,128)S(1)}, u32[]{:S(2)}, u32[]{:S(2)}) collective-permute-start(f32[2,64,512]{2,1,0:T(8,128)S(1)} %get-tuple-element.59), channel_id=1, source_target_pairs={{0,128},{64,192},{128,0},{192,64},{1,129},{65,193},{129,1},{193,65... | collective-permute-start | bytes 786440 | tf_op jit(solution)/shard_map/ppermute | solution.py:305
  127.2 11.3 %collective-permute-start.31 = (f32[2,64,512]{2,1,0:T(8,128)S(1)}, f32[2,64,512]{2,1,0:T(8,128)S(1)}, u32[]{:S(2)}, u32[]{:S(2)}) collective-permute-start(f32[2,64,512]{2,1,0:T(8,128)S(1)} %get-tuple-element.60), channel_id=1, source_target_pairs={{0,192},{64,0},{128,64},{192,128},{1,193},{65,1},{129,65},{193,129... | collective-permute-start | bytes 786440 | tf_op jit(solution)/shard_map/ppermute | solution.py:305
  (19 other events, 194.9 us)
Sparse Core Ops, SparseCore 0:
  9.2 38.8 all-gather.7
  50.0 34.6 all-gather.9
  88.8 30.6 all-gather.5
